TPU v7x, 32 devices: a whole 2x2x4 slice. The times are simulated.
32 devices in a mesh: seq: 8 (over z, y), mem: 4 (over x, core).
Axes of the slice: x: 2, y: 2, z: 4, core: 2. Of those that a mesh axis runs over, the one named last changes fastest.
Arguments:
- tokens: bfloat16 [32768, 1024], P(('seq', 'mem')), may hold values from -6 to 6
- memory: bfloat16 [32, 588, 1024], P('seq', 'mem'), may hold values from -6 to 6
- page_lengths: int32 [32], P(('seq', 'mem')), may hold values from 256 to 1024, as said below
- slot_masks: int32 [32, 588], P('seq'), may hold values from 0 to 1, as said below
- upstream: bfloat16 [32768, 1024], P(('seq', 'mem')), may hold values from -6 to 6
- weights: float32 [1024, 16384], P(None, ('seq', 'mem'))
- weight_average: float32 [1024, 16384], P(None, ('seq', 'mem'))
- weight_moment1: float32 [1024, 16384], P(None, ('seq', 'mem'))
- weight_moment2: float32 [1024, 16384], P(None, ('seq', 'mem')), as said below
- stats: float32 [128, 128, 128], P(('seq', 'mem')), as said below
- bases: float32 [128, 128, 128], P(('seq', 'mem'))
- vectors: float32 [17, 1024], P(None, ('seq', 'mem'))
- vector_average: float32 [17, 1024], P(None, ('seq', 'mem'))
- vector_moment1: float32 [17, 1024], P(None, ('seq', 'mem'))
- vector_moment2: float32 [17, 1024], P(None, ('seq', 'mem')), as said below
Outputs:
- mixed: bfloat16 [32768, 1024], P(('seq', 'mem'))
- input_grad: float32 [32768, 1024], P(('seq', 'mem'))
- memory_grad: float32 [32, 588, 1024], P('seq', 'mem')
- weight_grad: float32 [1024, 16384], P(None, ('seq', 'mem'))
- weight_first: float32 [1024, 16384], P(None, ('seq', 'mem'))
- weight_second: float32 [1024, 16384], P(None, ('seq', 'mem'))
- new_weights: float32 [1024, 16384], P(None, ('seq', 'mem'))
- new_average: float32 [1024, 16384], P(None, ('seq', 'mem'))
- weights_copy: bfloat16 [1024, 16384], P(None, ('seq', 'mem'))
- new_stats: float32 [128, 128, 128], P(('seq', 'mem'))
- new_bases: float32 [128, 128, 128], P(('seq', 'mem'))
- vector_grad: float32 [17, 1024], P(None, ('seq', 'mem'))
- vector_first: float32 [17, 1024], P(None, ('seq', 'mem'))
- vector_second: float32 [17, 1024], P(None, ('seq', 'mem'))
- new_vectors: float32 [17, 1024], P(None, ('seq', 'mem'))
- new_vector_average: float32 [17, 1024], P(None, ('seq', 'mem'))
- vectors_copy: bfloat16 [17, 1024], P(None, ('seq', 'mem'))
- down_bias_grad: float32 [1024], P(('seq', 'mem'))
Inputs may be any that keep to these rules, and one draw needn't show every extreme that they name: `page_lengths`: in every aligned group of 4 pages one page has length 1024. `slot_masks`: A page's memory is either full, all 588 slots real, or half, exactly 154 real slots among its first 196 and none after; every aligned group of 4 pages has a full one. `weight_moment2`: every entry is positive. `vector_moment2`: every entry is positive. `stats`: each block is symmetric positive definite.
All inputs are finite; a program needn't handle non-finite values.
Results may differ from a plain program's by a relative error of at most 0.024.
The roundings to bfloat16 on the way count: a program that leaves them out, or rounds other values in their place, can miss the bound.
Values may be sent and summed in bfloat16 or wider, within the bound.
No kernel may reach another device: no remote copies, remote signals or barrier semaphores. Data moves between devices by JAX's collectives and lax.ppermute only.
A program may use at most 384 MiB of HBM per device.

v0:
```python
import jax
import jax.numpy as jnp
from jax import lax
from jax.sharding import PartitionSpec as P

HEADS = 16
HEAD = 64
BLK = 128
STEP = 10


HIGHEST = lax.Precision.HIGHEST
NORM_EPS = 1e-05
ADAM_EPS = 1e-08
BETA_ONE = 0.9
BETA_TWO = 0.95
RATE = 0.04
VECTOR_RATE = 0.4
DECAY = 0.01
AVERAGE = 0.999
MASKED = -1e30
CONTRACT_ROWS = (((0,), (0,)), ((), ()))
CONTRACT_LAST = (((1,), (1,)), ((), ()))


def normalize(values, scale_gain, offset):
    centre = jnp.mean(values, axis=-1, keepdims=True)
    centred = values - centre
    variance = jnp.mean(centred * centred, axis=-1, keepdims=True)
    return centred * lax.rsqrt(variance + NORM_EPS) * scale_gain + offset


def gelu_tanh(values):
    return jax.nn.gelu(values, approximate=True)


def softmax_rows(scores):
    largest = jnp.max(scores, axis=-1, keepdims=True)
    raised = jnp.exp(scores - largest)
    summed = jnp.sum(raised, axis=-1, keepdims=True)
    return (raised / summed, largest[..., 0] + jnp.log(summed[..., 0]))


def split_heads(values):
    return values.reshape(values.shape[:-1] + (HEADS, HEAD))


def column_total(values):
    return jnp.sum(values.astype(jnp.float32), axis=0)


def self_scores(query_part, keys_in, start):
    scores = jnp.einsum("qhd,khd->hqk", query_part, keys_in, preferred_element_type=jnp.float32)
    query_pos = start + jnp.arange(query_part.shape[0])
    key_pos = jnp.arange(keys_in.shape[0])
    return jnp.where(key_pos[None, None, :] <= query_pos[None, :, None], scores, MASKED)


def self_forward(queries, keys_in, values_in):
    row_count = queries.shape[0]
    block_rows = min(512, row_count)
    block_count = row_count // block_rows
    pieces = queries.reshape((block_count, block_rows) + queries.shape[1:])

    def one_block(item_tuple):
        position, query_part = item_tuple
        chance, log_total = softmax_rows(self_scores(query_part, keys_in, position * block_rows))
        attended = jnp.einsum(
            "hqk,khd->qhd",
            chance.astype(jnp.bfloat16),
            values_in,
            preferred_element_type=jnp.float32,
        )
        return (attended, log_total)

    attended, log_total = lax.map(one_block, (jnp.arange(block_count), pieces))
    return (attended.reshape(row_count, -1), log_total)


def self_backward(queries, keys_in, values_in, log_total, grad_out):
    row_count = queries.shape[0]
    block_rows = min(512, row_count)
    block_count = row_count // block_rows
    query_pieces = queries.reshape((block_count, block_rows) + queries.shape[1:])
    grad_pieces = grad_out.reshape((block_count, block_rows) + grad_out.shape[1:])

    def one_block(running, item_tuple):
        keys_sum, values_sum = running
        position, query_part, grad_part, log_part = item_tuple
        scores = self_scores(query_part, keys_in, position * block_rows)
        chance = jnp.exp(scores - log_part[..., None])
        grad_chance = jnp.einsum(
            "qhd,khd->hqk", grad_part, values_in, preferred_element_type=jnp.float32
        )
        inner = jnp.sum(chance * grad_chance, axis=-1, keepdims=True)
        grad_scores = (chance * (grad_chance - inner)).astype(jnp.bfloat16)
        grad_query = jnp.einsum(
            "hqk,khd->qhd", grad_scores, keys_in, preferred_element_type=jnp.float32
        )
        keys_sum = keys_sum + jnp.einsum(
            "hqk,qhd->khd", grad_scores, query_part, preferred_element_type=jnp.float32
        )
        values_sum = values_sum + jnp.einsum(
            "hqk,qhd->khd",
            chance.astype(jnp.bfloat16),
            grad_part,
            preferred_element_type=jnp.float32,
        )
        return ((keys_sum, values_sum), grad_query)

    empty_sum = jnp.zeros(keys_in.shape, jnp.float32)
    (grad_keys, grad_values), grad_query = lax.scan(
        one_block,
        (empty_sum, empty_sum),
        (jnp.arange(block_count), query_pieces, grad_pieces, log_total),
    )
    return (
        grad_query.reshape(row_count, -1),
        grad_keys.reshape(row_count, -1),
        grad_values.reshape(row_count, -1),
    )


def cross_part(item_tuple):
    query_in, keys_in, values_in, slot_live = item_tuple
    scores = jnp.einsum("qhd,khd->hqk", query_in, keys_in, preferred_element_type=jnp.float32)
    scores = jnp.where(slot_live[None, None, :] > 0, scores, MASKED)
    chance, log_total = softmax_rows(scores)
    partials = jnp.einsum(
        "hqk,khd->qhd", chance.astype(jnp.bfloat16), values_in, preferred_element_type=jnp.float32
    )
    return (partials, log_total)


def cross_back(item_tuple):
    query_in, keys_in, values_in, slot_live, log_part, shares, log_grad, grad_out = item_tuple
    scores = jnp.einsum("qhd,khd->hqk", query_in, keys_in, preferred_element_type=jnp.float32)
    scores = jnp.where(slot_live[None, None, :] > 0, scores, MASKED)
    chance = jnp.exp(scores - log_part[..., None])
    grad_chance = shares[..., None] * jnp.einsum(
        "qhd,khd->hqk", grad_out, values_in, preferred_element_type=jnp.float32
    )
    inner = jnp.sum(chance * grad_chance, axis=-1, keepdims=True)
    grad_scores = (chance * (grad_chance - inner + log_grad[..., None])).astype(jnp.bfloat16)
    grad_query = jnp.einsum(
        "hqk,khd->qhd", grad_scores, keys_in, preferred_element_type=jnp.float32
    )
    grad_keys = jnp.einsum(
        "hqk,qhd->khd", grad_scores, query_in, preferred_element_type=jnp.float32
    )
    weighted = chance.astype(jnp.bfloat16).astype(jnp.float32) * shares[..., None]
    grad_values = jnp.einsum(
        "hqk,qhd->khd", weighted, grad_out.astype(jnp.float32), precision=HIGHEST
    )
    return (grad_query, grad_keys, grad_values)


def rotated_update(grad, weights, moment1, moment2, stats, bases):
    block_count = stats.shape[0]
    grads_three = grad.reshape(grad.shape[0], block_count, BLK)
    turned = jnp.einsum("dnb,nbc->dnc", grads_three, bases, precision=HIGHEST)
    first_moment = BETA_ONE * moment1.reshape(grads_three.shape) + (1.0 - BETA_ONE) * turned
    second_moment = (
        BETA_TWO * moment2.reshape(grads_three.shape) + (1.0 - BETA_TWO) * turned * turned
    )
    direction = (
        first_moment
        / (1.0 - BETA_ONE**STEP)
        / (jnp.sqrt(second_moment / (1.0 - BETA_TWO**STEP)) + ADAM_EPS)
    )
    returned = jnp.einsum("dnc,nbc->dnb", direction, bases, precision=HIGHEST).reshape(grad.shape)
    updated = weights - RATE * (returned + DECAY * weights)
    renewed = BETA_TWO * stats + (1.0 - BETA_TWO) * jnp.einsum(
        "dnb,dnc->nbc", grads_three, grads_three, precision=HIGHEST
    )
    product = jnp.einsum("nbc,ncd->nbd", renewed, bases, precision=HIGHEST)
    gram_matrix = jnp.einsum("nbc,nbd->ncd", product, product, precision=HIGHEST)
    factor = jnp.linalg.cholesky(gram_matrix)
    solved = jax.scipy.linalg.solve_triangular(factor, jnp.swapaxes(product, 1, 2), lower=True)
    return (
        first_moment.reshape(grad.shape),
        second_moment.reshape(grad.shape),
        updated,
        renewed,
        jnp.swapaxes(solved, 1, 2),
    )


def adam_update(grad, values, moment1, moment2):
    first_moment = BETA_ONE * moment1 + (1.0 - BETA_ONE) * grad
    second_moment = BETA_TWO * moment2 + (1.0 - BETA_TWO) * grad * grad
    updated = values - VECTOR_RATE * (first_moment / (1.0 - BETA_ONE**STEP)) / (
        jnp.sqrt(second_moment / (1.0 - BETA_TWO**STEP)) + ADAM_EPS
    )
    return (first_moment, second_moment, updated)


def local(
    tokens,
    memory,
    page_lengths,
    slot_masks,
    upstream,
    weights,
    weight_average,
    weight_moment1,
    weight_moment2,
    stats,
    bases,
    vectors,
    vector_average,
    vector_moment1,
    vector_moment2,
):
    row_count, model_width = tokens.shape
    group_size = lax.axis_size("mem")
    member = lax.axis_index("mem")
    quarter = memory.shape[1]
    scale_q = HEAD ** (-0.5)
    full_weights, full_vectors = (
        lax.all_gather(weights.astype(jnp.bfloat16), ("seq", "mem"), axis=1, tiled=True),
        lax.all_gather(vectors.astype(jnp.bfloat16), ("seq", "mem"), axis=1, tiled=True),
    )
    vector_rows = full_vectors.astype(jnp.float32)

    def block_columns(source, first, count):
        return source[:, first * model_width : (first + count) * model_width]

    inputs = tokens.astype(jnp.float32)
    live_rows = (jnp.arange(row_count) < page_lengths[0]).astype(jnp.float32)[:, None]
    normed_one, pull_one = jax.vjp(normalize, inputs, vector_rows[0], vector_rows[1])
    low_one = normed_one.astype(jnp.bfloat16)
    projected = jnp.dot(
        low_one, block_columns(full_weights, 0, 3), preferred_element_type=jnp.float32
    )
    queries_self = ((projected[:, :model_width] + vector_rows[6]) * scale_q).astype(jnp.bfloat16)
    keys_self = projected[:, model_width : 2 * model_width].astype(jnp.bfloat16)
    values_self = (projected[:, 2 * model_width :] + vector_rows[7]).astype(jnp.bfloat16)
    attended, self_log = self_forward(
        split_heads(queries_self), split_heads(keys_self), split_heads(values_self)
    )
    attended_low = attended.astype(jnp.bfloat16)
    after_self = (
        inputs
        + jnp.dot(
            attended_low, block_columns(full_weights, 3, 1), preferred_element_type=jnp.float32
        )
        + vector_rows[8]
    )
    normed_two, pull_two = jax.vjp(normalize, after_self, vector_rows[2], vector_rows[3])
    low_two = normed_two.astype(jnp.bfloat16)
    queries_cross = (
        (
            jnp.dot(low_two, block_columns(full_weights, 4, 1), preferred_element_type=jnp.float32)
            + vector_rows[9]
        )
        * scale_q
    ).astype(jnp.bfloat16)
    memory_here = lax.all_to_all(memory, "mem", split_axis=0, concat_axis=0, tiled=True)
    queries_all = jnp.broadcast_to(
        split_heads(queries_cross)[None], (group_size, row_count, HEADS, HEAD)
    )
    slots_here = lax.dynamic_slice_in_dim(slot_masks, member, 1, 0).reshape(group_size, quarter)
    key_value = jnp.einsum(
        "gsd,de->gse",
        memory_here,
        block_columns(full_weights, 5, 2),
        preferred_element_type=jnp.float32,
    )
    keys_cross = key_value[..., :model_width].astype(jnp.bfloat16)
    values_cross = (key_value[..., model_width:] + vector_rows[10]).astype(jnp.bfloat16)
    keys_heads = split_heads(keys_cross)
    values_heads = split_heads(values_cross)
    partials, log_part = lax.map(cross_part, (queries_all, keys_heads, values_heads, slots_here))
    partials_own, log_own = (partials, log_part)
    largest = jnp.max(log_own, axis=0)
    log_all = largest + jnp.log(jnp.sum(jnp.exp(log_own - largest), axis=0))
    shares_own = jnp.exp(log_own - log_all)
    merged = jnp.sum(jnp.transpose(shares_own, (0, 2, 1))[..., None] * partials_own, axis=0)
    merged_low = merged.reshape(row_count, model_width).astype(jnp.bfloat16)
    after_cross = (
        after_self
        + jnp.dot(merged_low, block_columns(full_weights, 7, 1), preferred_element_type=jnp.float32)
        + vector_rows[11]
    )
    normed_three, pull_three = jax.vjp(normalize, after_cross, vector_rows[4], vector_rows[5])
    low_three = normed_three.astype(jnp.bfloat16)
    bias_up = vector_rows[13:17].reshape(-1)
    hidden = (
        jnp.dot(low_three, block_columns(full_weights, 8, 4), preferred_element_type=jnp.float32)
        + bias_up
    )
    activated, pull_act = jax.vjp(gelu_tanh, hidden)
    activated_low = activated.astype(jnp.bfloat16)
    branch_down = lax.dot_general(
        activated_low,
        block_columns(full_weights, 12, 4),
        CONTRACT_LAST,
        preferred_element_type=jnp.float32,
    )
    result = (after_cross + branch_down + vector_rows[12]) * live_rows
    mixed = result.astype(jnp.bfloat16)
    grad_result = upstream.astype(jnp.float32) * live_rows
    grad_low_three = grad_result.astype(jnp.bfloat16)
    up_weight = block_columns(full_weights, 8, 4)
    grad_down = lax.dot_general(
        grad_low_three, activated_low, CONTRACT_ROWS, preferred_element_type=jnp.float32
    )
    grad_act = jnp.dot(
        grad_low_three, block_columns(full_weights, 12, 4), preferred_element_type=jnp.float32
    )
    (grad_hidden,) = pull_act(grad_act)
    hidden_low = grad_hidden.astype(jnp.bfloat16)
    grad_up = lax.dot_general(
        low_three, hidden_low, CONTRACT_ROWS, preferred_element_type=jnp.float32
    )
    grad_normed_three = lax.dot_general(
        hidden_low, up_weight, CONTRACT_LAST, preferred_element_type=jnp.float32
    )
    back_three, gain_three, shift_three = pull_three(grad_normed_three)
    grad_two = grad_result + back_three
    grad_low_two = grad_two.astype(jnp.bfloat16)
    grad_out_cross = lax.dot_general(
        merged_low, grad_low_two, CONTRACT_ROWS, preferred_element_type=jnp.float32
    )
    grad_merged = lax.dot_general(
        grad_low_two,
        block_columns(full_weights, 7, 1),
        CONTRACT_LAST,
        preferred_element_type=jnp.float32,
    ).astype(jnp.bfloat16)
    grad_merged_wide = grad_merged.astype(jnp.float32)
    dot_own = jnp.transpose(jnp.sum(split_heads(grad_merged_wide) * merged, axis=-1))
    grad_items = jnp.broadcast_to(
        split_heads(grad_merged)[None], (group_size, row_count, HEADS, HEAD)
    )
    log_items = log_all[None]
    dot_items = dot_own[None]
    shares_here = jnp.exp(log_part - log_items)
    dot_part = jnp.transpose(jnp.sum(grad_items.astype(jnp.float32) * partials, axis=-1), (0, 2, 1))
    log_grad = shares_here * (dot_part - dot_items)
    grad_query_items, grad_keys_items, grad_values_items = lax.map(
        cross_back,
        (
            queries_all,
            keys_heads,
            values_heads,
            slots_here,
            log_part,
            shares_here,
            log_grad,
            grad_items,
        ),
    )
    grad_query_cross = jnp.sum(grad_query_items, axis=0).reshape(row_count, model_width)
    query_cross_low = grad_query_cross.astype(jnp.bfloat16) * scale_q
    keys_grad_low = grad_keys_items.reshape(group_size, quarter, model_width).astype(jnp.bfloat16)
    values_grad_low = grad_values_items.reshape(group_size, quarter, model_width).astype(
        jnp.bfloat16
    )
    grad_query_weight = lax.dot_general(
        low_two, query_cross_low, CONTRACT_ROWS, preferred_element_type=jnp.float32
    )
    grad_key_cross = jnp.einsum(
        "gsd,gse->de", memory_here, keys_grad_low, preferred_element_type=jnp.float32
    )
    grad_value_cross = jnp.einsum(
        "gsd,gse->de", memory_here, values_grad_low, preferred_element_type=jnp.float32
    )
    memory_back = jnp.einsum(
        "gse,de->gsd",
        keys_grad_low,
        block_columns(full_weights, 5, 1),
        preferred_element_type=jnp.float32,
    )
    memory_back = memory_back + jnp.einsum(
        "gse,de->gsd",
        values_grad_low,
        block_columns(full_weights, 6, 1),
        preferred_element_type=jnp.float32,
    )
    memory_back = lax.all_to_all(memory_back, "mem", split_axis=0, concat_axis=0, tiled=True)
    grad_normed_two = lax.dot_general(
        query_cross_low,
        block_columns(full_weights, 4, 1),
        CONTRACT_LAST,
        preferred_element_type=jnp.float32,
    )
    back_two, gain_two, shift_two = pull_two(grad_normed_two)
    grad_one = grad_two + back_two
    grad_low_one = grad_one.astype(jnp.bfloat16)
    grad_out_self = lax.dot_general(
        attended_low, grad_low_one, CONTRACT_ROWS, preferred_element_type=jnp.float32
    )
    grad_attended = lax.dot_general(
        grad_low_one,
        block_columns(full_weights, 3, 1),
        CONTRACT_LAST,
        preferred_element_type=jnp.float32,
    ).astype(jnp.bfloat16)
    grad_query_self, grad_keys_self, grad_values_self = self_backward(
        split_heads(queries_self),
        split_heads(keys_self),
        split_heads(values_self),
        self_log,
        split_heads(grad_attended),
    )
    stacked = jnp.concatenate(
        [
            grad_query_self.astype(jnp.bfloat16) * scale_q,
            grad_keys_self.astype(jnp.bfloat16),
            grad_values_self.astype(jnp.bfloat16),
        ],
        axis=1,
    )
    grad_projection = lax.dot_general(
        low_one, stacked, CONTRACT_ROWS, preferred_element_type=jnp.float32
    )
    grad_normed_one = lax.dot_general(
        stacked,
        block_columns(full_weights, 0, 3),
        CONTRACT_LAST,
        preferred_element_type=jnp.float32,
    )
    back_one, gain_one, shift_one = pull_one(grad_normed_one)
    input_grad = grad_one + back_one
    weight_terms = jnp.concatenate(
        [
            grad_projection,
            grad_out_self,
            grad_query_weight,
            grad_key_cross,
            grad_value_cross,
            grad_out_cross,
            grad_up,
            grad_down,
        ],
        axis=1,
    )
    vector_head = jnp.stack(
        [
            gain_one,
            shift_one,
            gain_two,
            shift_two,
            gain_three,
            shift_three,
            column_total(stacked[:, :model_width]),
            column_total(stacked[:, 2 * model_width :]),
            column_total(grad_low_one),
            column_total(query_cross_low),
            jnp.sum(values_grad_low.astype(jnp.float32), axis=(0, 1)),
            column_total(grad_low_two),
            column_total(grad_low_three),
        ],
        axis=0,
    )
    vector_terms = jnp.concatenate(
        [vector_head, column_total(hidden_low).reshape(4, model_width)], axis=0
    )
    weight_grad, vector_grad = (
        lax.psum_scatter(weight_terms, ("seq", "mem"), scatter_dimension=1, tiled=True),
        lax.psum_scatter(vector_terms, ("seq", "mem"), scatter_dimension=1, tiled=True),
    )
    weight_first, weight_second, new_weights, new_stats, new_bases = rotated_update(
        weight_grad, weights, weight_moment1, weight_moment2, stats, bases
    )
    new_average = AVERAGE * weight_average + (1.0 - AVERAGE) * new_weights
    vector_first, vector_second, new_vectors = adam_update(
        vector_grad, vectors, vector_moment1, vector_moment2
    )
    new_vector_average = AVERAGE * vector_average + (1.0 - AVERAGE) * new_vectors
    return (
        mixed,
        input_grad,
        memory_back,
        weight_grad,
        weight_first,
        weight_second,
        new_weights,
        new_average,
        new_weights.astype(jnp.bfloat16),
        new_stats,
        new_bases,
        vector_grad,
        vector_first,
        vector_second,
        new_vectors,
        new_vector_average,
        new_vectors.astype(jnp.bfloat16),
        vector_grad[12],
    )


def solution(mesh):
    return jax.shard_map(
        local,
        mesh=mesh,
        in_specs=(
            P(("seq", "mem"), None),
            P("seq", "mem", None),
            P(("seq", "mem")),
            P("seq", None),
            P(("seq", "mem"), None),
            P(None, ("seq", "mem")),
            P(None, ("seq", "mem")),
            P(None, ("seq", "mem")),
            P(None, ("seq", "mem")),
            P(("seq", "mem"), None, None),
            P(("seq", "mem"), None, None),
            P(None, ("seq", "mem")),
            P(None, ("seq", "mem")),
            P(None, ("seq", "mem")),
            P(None, ("seq", "mem")),
        ),
        out_specs=(
            P(("seq", "mem"), None),
            P(("seq", "mem"), None),
            P("seq", "mem", None),
            P(None, ("seq", "mem")),
            P(None, ("seq", "mem")),
            P(None, ("seq", "mem")),
            P(None, ("seq", "mem")),
            P(None, ("seq", "mem")),
            P(None, ("seq", "mem")),
            P(("seq", "mem"), None, None),
            P(("seq", "mem"), None, None),
            P(None, ("seq", "mem")),
            P(None, ("seq", "mem")),
            P(None, ("seq", "mem")),
            P(None, ("seq", "mem")),
            P(None, ("seq", "mem")),
            P(None, ("seq", "mem")),
            P(("seq", "mem")),
        ),
        check_vma=False,
    )
```

profile of v0, /device:TPU:0, one launch (start us, length us, event | category | flops | bytes accessed | tf_op | source)
XLA Modules:
  0.0 2157.0 jit_solution(12346818881156182433)
XLA Ops:
  15.9 60.3 %all-gather = bf16[32,32,17]{1,2,0:T(8,128)(2,1)S(1)} all-gather(bf16[1,32,17]{1,2,0:T(8,128)(2,1)S(1)} %convert_bitcast_fusion), channel_id=1, replica_groups=mesh['seq'=8,'mem'=4] {'seq','mem'}, dimensions={0}, use_global_device_ids=true | all-gather | bytes 35904 | tf_op jit(solution)/shard_map/all_gather | solution.py:222
  88.9 150.4 %all-gather.3.cloned.1.call-done = bf16[1024,16384]{1,0:T(8,128)(2,1)} async-done(((bf16[1024,512]{1,0:T(8,128)(2,1)}), bf16[1024,16384]{1,0:T(8,128)(2,1)}) %all-gather.3.cloned.1.call-update) | async-done | bytes 33554448 | tf_op jit(solution)/shard_map/all_gather | solution.py:221
  270.6 93.9 %while.53 = (s32[]{:T(128)}, bf16[2,512,16,64]{1,3,2,0:T(8,128)(2,1)}, f32[2,16,512]{2,1,0:T(8,128)S(1)}, s32[2]{0:T(128)S(1)}, bf16[2,512,16,64]{1,3,2,0:T(8,12...) while((s32[]{:T(128)}, ...), condition=%wide.region_5.6_spmd, body=%wide.region_2.5_spmd.sunk | while | flops 2223497728 | bytes 135532752 | solution.py:76
  272.4 14.7 select_reduce_fusion.5
  287.1 15.0 fusion.305
  302.2 14.1 bitcast_dynamic-update-slice_fusion.12
  319.2 14.7 select_reduce_fusion.5
  334.0 15.0 fusion.305
  349.0 14.1 bitcast_dynamic-update-slice_fusion.12
  412.8 42.3 %while.54 = (s32[]{:T(128)}, f32[4,1024,16,64]{1,3,2,0:T(8,128)}, f32[4,16,1024]{2,1,0:T(8,128)S(1)}, bf16[4,147,16,64]{1,3,2,0:T(8,128)(2,1)}, s32[4,147]{1,0:T...) while((s32[]{:T(128)}, f32[4,1024,16,64]{1,3,2,0:T(8,128)}, ...), condition=%wide.region_11.12_spmd, body=%wide.region_8.11_spmd.sunk | while | flops 638222464 | bytes 36769384 | solution.py:274
  455.4 10.9 multiply_reduce_fusion.3
  474.8 16.4 fusion.143
  491.2 26.4 %convert_reduce_fusion = (f32[4096]{0:T(1024)}, bf16[1024,4096]{1,0:T(8,128)(2,1)}) fusion(f32[1024,4096]{1,0:T(8,128)} %fusion.143, f32[4096]{0:T(1024)S(1)} %bitcast.392, bf16[1024,16384]{1,0:T(8,128)(2,1)} %all-gather.3.cloned.1.call-done, bf16[1024,1024]{0,1:T(8,128)(2,1)S(1)} %copy-done.23, f32[1024]{0:T(1024)S(1)} %copy-done.71), kind=kOutput, calls=%fused_computation.133 | convolution fusion | flops 8689545216 | bytes 35688448 | tf_op jit(solution)/shard_map/dot_general | solution.py:309
  517.7 16.2 fusion.237
  570.8 252.9 %while.55 = (s32[]{:T(128)}, f32[4,1024,16,64]{1,3,2,0:T(8,128)}, bf16[4,147,16,64]{1,3,2,0:T(8,128)(2,1)}, bf16[4,147,16,64]{1,3,2,0:T(8,128)(2,1)}, bf16[4,147...) while((s32[]{:T(128)}, f32[4,1024,16,64]{1,3,2,0:T(8,128)}, ...), condition=%wide.region_23.24_spmd, body=%wide.region_21.23_spmd.sunk | while | flops 3147874816 | bytes 126361600 | solution.py:342
  584.8 19.9 bitcast_dynamic-update-slice_fusion.16
  604.7 16.9 fusion.320
  621.6 12.4 fusion.321
  647.8 19.9 bitcast_dynamic-update-slice_fusion.16
  667.8 17.0 fusion.320
  684.8 12.4 fusion.321
  711.0 19.9 bitcast_dynamic-update-slice_fusion.16
  730.9 17.1 fusion.320
  747.9 12.4 fusion.321
  774.1 19.9 bitcast_dynamic-update-slice_fusion.16
  794.0 16.9 fusion.320
  811.0 12.4 fusion.321
  875.1 216.0 %while.56 = (s32[]{:T(128)}, f32[1024,16,64]{0,2,1:T(8,128)}, f32[1024,16,64]{0,2,1:T(8,128)}, bf16[2,512,16,64]{1,3,2,0:T(8,128)(2,1)}, bf16[2,512,16,64]{1,3,2...) while((s32[]{:T(128)}, f32[1024,16,64]{0,2,1:T(8,128)}, ...), condition=%wide.region_29.30_spmd.clone, body=%wide.region_27.29_spmd.clone.sunk | while | flops 5474083328 | bytes 300126432 | solution.py:112
  875.3 14.6 fusion.331
  891.5 24.7 %multiply_reduce_fusion.12 = (f32[16,512]{1,0:T(8,128)S(1)}, f32[16,512,1024]{2,1,0:T(8,128)}) fusion(f32[16,512,1024]{2,1,0:T(8,128)} %fusion.331, f32[16,512]{1,0:T(8,128)S(1)} %dynamic-slice_bitcast_fusion.9, pred[512,1024]{1,0:T(8,128)(4,1)S(1)} %iota_compare_fusion.8, bf16[1024,16,64]{0,2,1:T(8,128)(2,1)S(1)} %copy-done.5, ...), kind=kOutput, calls=%fused_computation.15.clone.1 | convolution fusion | flops 1107288064 | bytes 70844416 | tf_op jit(solution)/shard_map/while/body/eval_jaxpr/qhd,khd->hqk/dot_general | solution.py:92
  916.1 27.9 %multiply_convert_fusion.8 = bf16[16,512,1024]{2,1,0:T(8,128)(2,1)} fusion(f32[16,512,1024]{2,1,0:T(8,128)} %get-tuple-element.895, f32[16,512,1024]{2,1,0:T(8,128)} %fusion.331, f32[16,512]{1,0:T(8,128)S(1)} %get-tuple-element.896, f32[16,512]{1,0:T(8,128)S(1)} %dynamic-slice_bitcast_fusion.9, pred[512,1024]{1,0:T(8,128)(4,1)S(1)} %iota_compare_fusion.8), kind=kLoop, calls=%fused_computation.14.clone.1 | loop fusion | flops 41943040 | bytes 84475904 | tf_op jit(solution)/shard_map/while/body/eval_jaxpr/convert_element_type | solution.py:96
  944.0 11.1 bitcast_add_fusion.5
  955.1 17.0 bitcast_add_fusion.6
  972.1 9.7 bitcast_dynamic-update-slice_fusion.17
  981.8 14.6 fusion.331
  998.0 24.7 %multiply_reduce_fusion.12 = (f32[16,512]{1,0:T(8,128)S(1)}, f32[16,512,1024]{2,1,0:T(8,128)}) fusion(f32[16,512,1024]{2,1,0:T(8,128)} %fusion.331, f32[16,512]{1,0:T(8,128)S(1)} %dynamic-slice_bitcast_fusion.9, pred[512,1024]{1,0:T(8,128)(4,1)S(1)} %iota_compare_fusion.8, bf16[1024,16,64]{0,2,1:T(8,128)(2,1)S(1)} %copy-done.5, ...), kind=kOutput, calls=%fused_computation.15.clone.1 | convolution fusion | flops 1107288064 | bytes 70844416 | tf_op jit(solution)/shard_map/while/body/eval_jaxpr/qhd,khd->hqk/dot_general | solution.py:92
  1022.6 27.9 %multiply_convert_fusion.8 = bf16[16,512,1024]{2,1,0:T(8,128)(2,1)} fusion(f32[16,512,1024]{2,1,0:T(8,128)} %get-tuple-element.895, f32[16,512,1024]{2,1,0:T(8,128)} %fusion.331, f32[16,512]{1,0:T(8,128)S(1)} %get-tuple-element.896, f32[16,512]{1,0:T(8,128)S(1)} %dynamic-slice_bitcast_fusion.9, pred[512,1024]{1,0:T(8,128)(4,1)S(1)} %iota_compare_fusion.8), kind=kLoop, calls=%fused_computation.14.clone.1 | loop fusion | flops 41943040 | bytes 84475904 | tf_op jit(solution)/shard_map/while/body/eval_jaxpr/convert_element_type | solution.py:96
  1050.5 12.3 bitcast_add_fusion.5
  1062.8 18.3 bitcast_add_fusion.6
  1099.0 11.4 convolution_dynamic-update-slice_fusion.2
  1110.3 11.6 fusion.235
  1179.4 12.5 convolution_dynamic-update-slice_fusion.1
  1193.6 17.0 convolution_dynamic-update-slice_fusion
  1237.9 16.7 multiply_convert_fusion.3
  1270.7 55.9 %reduce-scatter.7.cloned.1.call-done = f32[32,17]{1,0:T(8,128)} async-done(((f32[1024,17]{1,0:T(8,128)}), f32[32,17]{1,0:T(8,128)}) %reduce-scatter.7.cloned.1.call-update) | async-done | bytes 2192
  1333.8 694.4 %reduce-scatter.5.cloned.1.call-done = f32[1024,512]{1,0:T(8,128)} async-done(((f32[1024,16384]{1,0:T(8,128)}), f32[1024,512]{1,0:T(8,128)}) %reduce-scatter.5.cloned.1.call-update) | async-done | bytes 2097168 | tf_op jit(solution)/shard_map/reduce_scatter | solution.py:462
  2057.9 47.9 %custom-call.8 = f32[4,128,128]{2,1,0:T(8,128)S(1)} custom-call(f32[4,128,128]{2,1,0:T(8,128)} %fusion.210), custom_call_target="Cholesky" | custom-call | tf_op jit(solution)/shard_map/jit(cholesky)/cholesky | solution.py:178
  2106.1 39.3 %custom-call.9 = f32[4,1,128,128]{2,3,1,0:T(8,128)S(1)} custom-call(f32[4,1,128,128]{3,2,1,0:T(8,128)S(1)} %select_bitcast_fusion), custom_call_target="InvertDiagBlocksLowerTriangular" | custom-call | tf_op jit(solution)/shard_map/jit(_solve_triangular)/vmap()/triangular_solve | solution.py:179
  (455 shorter events, 461.7 us)
Async XLA Ops:
  7.2 2021.0 %copy-start = (f32[4,128,128]{2,1,0:T(8,128)S(1)}, f32[4,128,128]{2,1,0:T(8,128)}, u32[]{:S(2)}) copy-start(f32[4,128,128]{2,1,0:T(8,128)} %param.33) | copy-start | bytes 786436
  7.2 232.1 %all-gather.3.cloned.1.call-start = ((), (), s32[]{:S(2)}) async-start(), calls=%async_computation.4 | async-start | bytes 34603008 | tf_op jit(solution)/shard_map/all_gather | solution.py:221
  11.5 359.4 %all-to-all-start = ((bf16[4,147,1024]{2,1,0:T(8,128)(2,1)}), bf16[4,147,1024]{2,1,0:T(8,128)(2,1)}, u32[]{:S(2)}, u32[]{:S(2)}) async-start(bf16[4,147,1024]{2,1,0:T(8,128)(2,1)} %copy.241), calls=%async_computation | async-start | bytes 2490368 | tf_op jit(solution)/shard_map/all_to_all | solution.py:259
  15.8 1310.7 %reduce-scatter.7.cloned.1.call-start = ((), (), s32[]{:S(2)}) async-start(), calls=%async_computation.6 | async-start | bytes 540672
  79.3 160.0 %copy-start.7 = (bf16[1024,1024]{0,1:T(8,128)(2,1)}, bf16[1024,1024]{0,1:T(8,128)(2,1)S(1)}, u32[]{:S(2)}) copy-start(bf16[1024,1024]{0,1:T(8,128)(2,1)S(1)} %copy.234) | copy-start | bytes 6291460
  87.0 161.6 %copy-start.52 = (f32[1024]{0:T(1024)}, f32[1024]{0:T(1024)S(1)}, u32[]{:S(2)}) copy-start(f32[1024]{0:T(1024)S(1)} %broadcast_multiply_fusion.4) | copy-start | bytes 12292
  88.2 160.4 %copy-start.69 = (f32[1024]{0:T(1024)}, f32[1024]{0:T(1024)S(1)}, u32[]{:S(2)}) copy-start(f32[1024]{0:T(1024)S(1)} %fusion.214) | copy-start | bytes 12292
  88.9 159.8 %copy-start.59 = (f32[1,1024]{1,0:T(1,128)}, f32[1,1024]{1,0:T(1,128)S(1)}, u32[]{:S(2)}) copy-start(f32[1,1024]{1,0:T(1,128)S(1)} %get-tuple-element.646) | copy-start | bytes 12292
  88.9 159.8 %copy-start.102 = (f32[1,1024]{1,0:T(1,128)}, f32[1,1024]{1,0:T(1,128)S(1)}, u32[]{:S(2)}) copy-start(f32[1,1024]{1,0:T(1,128)S(1)} %get-tuple-element.645) | copy-start | bytes 12292
  287.1 15.0 copy-start.4
  287.1 15.0 copy-start.33
  334.0 15.0 copy-start.4
  334.0 15.0 copy-start.33
  474.0 17.2 copy-start.16
  474.0 70.6 %copy-start.57 = (f32[1024]{0:T(1024)}, f32[1024]{0:T(1024)S(1)}, u32[]{:S(2)}) copy-start(f32[1024]{0:T(1024)S(1)} %broadcast_multiply_fusion.2) | copy-start | bytes 12292
  474.5 70.1 %copy-start.74 = (f32[1024]{0:T(1024)}, f32[1024]{0:T(1024)S(1)}, u32[]{:S(2)}) copy-start(f32[1024]{0:T(1024)S(1)} %fusion.216) | copy-start | bytes 12292
  474.8 16.4 copy-start.23
  474.8 16.4 copy-start.71
  474.8 16.5 copy-start.90
  545.1 8.7 slice-start
  545.1 8.8 slice-start.1
  875.2 16.2 copy-start.5
  875.3 16.2 copy-start.6
  981.8 16.2 copy-start.5
  981.8 16.2 copy-start.6
  1165.8 13.4 slice-start.4
  1179.2 12.8 copy-start.84
  1179.2 12.9 copy-start.92
  1179.3 12.9 copy-start.85
  1179.3 12.9 copy-start.86
  1179.3 12.9 copy-start.87
  1179.3 12.9 copy-start.88
  1179.3 12.9 copy-start.89
  1179.3 12.9 copy-start.107
  1179.3 12.9 copy-start.108
  1179.3 14.3 copy-start.73
  1179.3 14.3 copy-start.91
  1193.5 834.6 %reduce-scatter.5.cloned.1.call-start = ((), (), s32[]{:S(2)}) async-start(), calls=%async_computation.5 | async-start | bytes 69206016 | tf_op jit(solution)/shard_map/reduce_scatter | solution.py:462
  1233.0 96.1 %all-to-all-start.1 = ((f32[4,147,1024]{2,1,0:T(8,128)}), f32[4,147,1024]{2,1,0:T(8,128)}, u32[]{:S(2)}, u32[]{:S(2)}) async-start(f32[4,147,1024]{2,1,0:T(8,128)} %fusion.197), calls=%async_computation.1 | async-start | bytes 4980736 | tf_op jit(solution)/shard_map/all_to_all | solution.py:382
  1265.3 62.6 %copy-start.64 = (f32[17,32]{1,0:T(8,128)S(1)}, f32[17,32]{1,0:T(8,128)}, u32[]{:S(2)}) copy-start(f32[17,32]{1,0:T(8,128)} %param.34) | copy-start | bytes 6532
  1265.3 62.6 %copy-start.95 = (f32[17,32]{1,0:T(8,128)S(1)}, f32[17,32]{1,0:T(8,128)}, u32[]{:S(2)}) copy-start(f32[17,32]{1,0:T(8,128)} %param.37) | copy-start | bytes 6532
  1265.3 62.6 %copy-start.96 = (f32[17,32]{1,0:T(8,128)S(1)}, f32[17,32]{1,0:T(8,128)}, u32[]{:S(2)}) copy-start(f32[17,32]{1,0:T(8,128)} %param.36) | copy-start | bytes 6532
  1265.3 63.2 %copy-start.94 = (f32[17,32]{1,0:T(8,128)S(1)}, f32[17,32]{1,0:T(8,128)}, u32[]{:S(2)}) copy-start(f32[17,32]{1,0:T(8,128)} %param.35) | copy-start | bytes 6532
  1270.7 757.5 %copy-start.35 = (f32[1024,512]{0,1:T(8,128)S(1)}, f32[1024,512]{0,1:T(8,128)}, u32[]{:S(2)}) copy-start(f32[1024,512]{0,1:T(8,128)} %copy.269) | copy-start | bytes 6291460
  1327.3 707.4 %copy-start.62 = (f32[17,32]{1,0:T(8,128)}, f32[17,32]{1,0:T(8,128)S(1)}, u32[]{:S(2)}) copy-start(f32[17,32]{1,0:T(8,128)S(1)} %copy.301) | copy-start | bytes 6532
  1328.5 706.2 %copy-start.65 = (f32[17,32]{1,0:T(8,128)}, f32[17,32]{1,0:T(8,128)S(1)}, u32[]{:S(2)}) copy-start(f32[17,32]{1,0:T(8,128)S(1)} %get-tuple-element.604) | copy-start | bytes 6532
  2052.4 97.5 %copy-start.30 = (f32[1024,512]{1,0:T(8,128)}, f32[1024,512]{1,0:T(8,128)S(1)}, u32[]{:S(2)}) copy-start(f32[1024,512]{1,0:T(8,128)S(1)} %get-tuple-element.618) | copy-start | bytes 6291460
  2056.0 93.9 %copy-start.45 = (f32[4,128,128]{2,1,0:T(8,128)}, f32[4,128,128]{2,1,0:T(8,128)S(1)}, u32[]{:S(2)}) copy-start(f32[4,128,128]{2,1,0:T(8,128)S(1)} %fusion.201) | copy-start | bytes 786436
  (79 other events, 318.6 us)
Sparse Core Ops, SparseCore 0:
  11.5 227.7 all-gather.2
  1193.7 132.8 reduce-scatter.6
  1329.6 698.5 reduce-scatter.4
where the time goes:
time: 2170 us; the launch traced here: 2160 us
  waiting for transfers between devices  901 us (42%)
  matrix products  726 us (33%)
  other arithmetic  270 us (12%)
  local copies, waits for them, and re-layouts  170 us (8%)
  blocking collectives  60.3 us (3%)
    reduce_scatter x1, waiting for transfers between devices, local(): lax.psum_scatter(weight_terms, ('seq', 'mem'), scatter_dimension=1, tiled...  694 us
    all_gather x1, waiting for transfers between devices, local(): lax.all_gather(weights.astype(jnp.bfloat16), ('seq', 'mem'), axis=1, tile...  150 us
    dot_general x4, matrix products, cross_back(): jnp.einsum('hqk,khd->qhd', grad_scores, keys_in, preferred_element_type=j...  79.6 us
    dot_general x4, matrix products, cross_back(): jnp.einsum('hqk,qhd->khd', grad_scores, query_in, preferred_element_type=...  67.9 us
    all_gather x1, blocking collectives, local(): lax.all_gather(vectors.astype(jnp.bfloat16), ('seq', 'mem'), axis=1, tile...  60.3 us
    dot_general x4, matrix products, self_scores(): jnp.einsum('qhd,khd->hqk', query_part, keys_in, preferred_element_type=jn...  58.6 us
    unnamed x241, local copies, waits for them, and re-layouts  58 us
    unnamed x4, waiting for transfers between devices  55.9 us
  transfers between devices with their start and end apart: 5, of which 3 were waited for; matrix products, arithmetic and copies ran while one was open for 10% of the time, Pallas kernels for 0%

commit v1 on v0

v1 whole, which is shorter than its diff:
```python
import functools

import jax
import jax.numpy as jnp
from jax import lax
from jax.experimental import pallas as pl
from jax.experimental.pallas import tpu as pltpu
from jax.sharding import PartitionSpec as P

HEADS = 16
HEAD = 64
BLK = 128
STEP = 10
LANES = 128
QUERY_ROWS = 256
SLOT_PAD = 160
VECTOR_PAD = 16
GROUPS = 4
AXES = ("seq", "mem")

F32 = jnp.float32
BF16 = jnp.bfloat16
HIGHEST = lax.Precision.HIGHEST
NORM_EPS = 1e-05
ADAM_EPS = 1e-08
BETA_ONE = 0.9
BETA_TWO = 0.95
RATE = 0.04
VECTOR_RATE = 0.4
DECAY = 0.01
AVERAGE = 0.999
MASKED = -1e30
CONTRACT_ROWS = (((0,), (0,)), ((), ()))
CONTRACT_LAST = (((1,), (1,)), ((), ()))


def dot(left, right):
    return jnp.dot(left, right, preferred_element_type=F32)


def dot_last(left, right):
    return lax.dot_general(left, right, CONTRACT_LAST, preferred_element_type=F32)


def dot_rows(left, right):
    return lax.dot_general(left, right, CONTRACT_ROWS, preferred_element_type=F32)


def normalize(values, scale_gain, offset):
    centre = jnp.mean(values, axis=-1, keepdims=True)
    centred = values - centre
    variance = jnp.mean(centred * centred, axis=-1, keepdims=True)
    return centred * lax.rsqrt(variance + NORM_EPS) * scale_gain + offset


def column_total(values):
    return jnp.sum(values.astype(F32), axis=0)


def causal_mask(scores):
    key_pos = lax.broadcasted_iota(jnp.int32, scores.shape, 0)
    query_pos = lax.broadcasted_iota(jnp.int32, scores.shape, 1)
    return jnp.where(key_pos <= query_pos, scores, MASKED)


def head_of_lane(shape):
    return lax.broadcasted_iota(jnp.int32, shape, 1) // HEAD


def one_head(values, lane_head, head):
    return jnp.where(lane_head == head, values, jnp.zeros_like(values))


def widen(bias, columns):
    return jnp.concatenate([bias] * (columns // LANES), axis=1)


def attention_forward_kernel(*refs, causal):
    if causal:
        q_ref, k_ref, v_ref, out_ref, log_ref = refs
    else:
        q_ref, k_ref, v_ref, bias_ref, out_ref, log_ref = refs
    keys = k_ref[...]
    key_count = keys.shape[0]
    row_count = q_ref.shape[0]
    values_turned = v_ref[...].T
    lane_head = head_of_lane(keys.shape)
    for block in range(row_count // QUERY_ROWS):
        rows = slice(block * QUERY_ROWS, (block + 1) * QUERY_ROWS)
        seen = (block + 1) * QUERY_ROWS if causal else key_count
        queries = q_ref[rows, :]
        outs = []
        for head in range(2):
            scores = dot_last(one_head(keys[:seen], lane_head[:seen], head), queries)
            if causal:
                last = causal_mask(scores[seen - QUERY_ROWS :])
                if seen > QUERY_ROWS:
                    last = jnp.concatenate([scores[: seen - QUERY_ROWS], last], axis=0)
                scores = last
            else:
                scores = scores + widen(bias_ref[...], QUERY_ROWS)
            largest = jnp.max(scores, axis=0, keepdims=True)
            raised = jnp.exp(scores - largest)
            summed = jnp.sum(raised, axis=0, keepdims=True)
            turned = values_turned[head * HEAD : (head + 1) * HEAD, :seen]
            outs.append(dot(turned, raised.astype(BF16)) / summed)
            log_ref[0, head : head + 1, rows] = largest + jnp.log(summed)
        out_ref[rows, :] = jnp.concatenate(outs, axis=0).T.astype(BF16)


def attention_backward_kernel(*refs, causal):
    if causal:
        q_ref, k_ref, v_ref, grad_ref, out_ref, log_ref = refs[:6]
    else:
        q_ref, k_ref, v_ref, grad_ref, out_ref, log_ref, bias_ref = refs[:7]
    dq_ref, dk_ref, dv_ref, chance_ref, score_ref = refs[-5:]
    keys = k_ref[...]
    values = v_ref[...]
    queries = q_ref[...]
    grads = grad_ref[...]
    key_count = keys.shape[0]
    row_count = queries.shape[0]
    keys_turned = keys.T
    product = (grads.astype(F32) * out_ref[...].astype(F32)).T
    inner = [
        jnp.sum(product[head * HEAD : (head + 1) * HEAD], axis=0, keepdims=True)
        for head in range(2)
    ]
    key_rows = chance_ref.shape[1]
    lane_head = head_of_lane((key_rows, LANES))
    for piece in range(key_count // key_rows):
        slots = slice(piece * key_rows, (piece + 1) * key_rows)
        first = piece * key_rows if causal else 0
        grad_keys = []
        grad_values = []
        for head in range(2):
            key_part = one_head(keys[slots], lane_head, head)
            value_part = one_head(values[slots], lane_head, head)
            for block in range(first // QUERY_ROWS, row_count // QUERY_ROWS):
                rows = slice(block * QUERY_ROWS, (block + 1) * QUERY_ROWS)
                scores = dot_last(key_part, queries[rows])
                if causal and block == piece:
                    scores = causal_mask(scores)
                if not causal:
                    scores = scores + widen(bias_ref[slots, :], QUERY_ROWS)
                chance = jnp.exp(scores - log_ref[0, head : head + 1, rows])
                chance_ref[head, :, rows] = chance.astype(BF16)
                grad_chance = dot_last(value_part, grads[rows])
                score_ref[head, slots, rows] = (
                    chance * (grad_chance - inner[head][:, rows])
                ).astype(BF16)
            grad_values.append(dot(chance_ref[head, :, first:], grads[first:]))
            grad_keys.append(dot(score_ref[head, slots, first:], queries[first:]))
        dk_ref[slots, :] = jnp.where(lane_head == 0, grad_keys[0], grad_keys[1]).astype(BF16)
        dv_ref[slots, :] = jnp.where(lane_head == 0, grad_values[0], grad_values[1]).astype(BF16)
    for block in range(row_count // QUERY_ROWS):
        rows = slice(block * QUERY_ROWS, (block + 1) * QUERY_ROWS)
        seen = (block + 1) * QUERY_ROWS if causal else key_count
        parts = [
            dot(
                keys_turned[head * HEAD : (head + 1) * HEAD, :seen],
                score_ref[head, :seen, rows],
            )
            for head in range(2)
        ]
        grad_query = jnp.concatenate(parts, axis=0).T.astype(BF16)
        dq_ref[rows, :] = (grad_query.astype(F32) * HEAD ** (-0.5)).astype(BF16)


def head_pair(row_count, first):
    return pl.BlockSpec((row_count, LANES), lambda pair: (0, first + pair))


def attention_forward(queries, keys, values, firsts, bias=None):
    causal = bias is None
    row_count = queries.shape[0]
    key_count = keys.shape[0]
    pairs = HEADS // 2
    in_specs = [
        head_pair(row_count, firsts[0]),
        head_pair(key_count, firsts[1]),
        head_pair(key_count, firsts[2]),
    ]
    operands = [queries, keys, values]
    if not causal:
        in_specs.append(pl.BlockSpec((key_count, LANES), lambda pair: (0, 0)))
        operands.append(bias)
    return pl.pallas_call(
        functools.partial(attention_forward_kernel, causal=causal),
        grid=(pairs,),
        in_specs=in_specs,
        out_specs=[
            head_pair(row_count, 0),
            pl.BlockSpec((1, 8, row_count), lambda pair: (pair, 0, 0)),
        ],
        out_shape=[
            jax.ShapeDtypeStruct((row_count, pairs * LANES), BF16),
            jax.ShapeDtypeStruct((pairs, 8, row_count), F32),
        ],
        compiler_params=pltpu.CompilerParams(vmem_limit_bytes=40 << 20),
        cost_estimate=pl.CostEstimate(
            flops=16 * row_count * key_count * HEADS * HEAD,
            bytes_accessed=8 << 20,
            transcendentals=row_count * key_count * HEADS,
        ),
    )(*operands)


def attention_backward(queries, keys, values, firsts, grads, outs, log_total, bias=None):
    causal = bias is None
    row_count = queries.shape[0]
    key_count = keys.shape[0]
    pairs = HEADS // 2
    key_rows = QUERY_ROWS if causal else LANES
    in_specs = [
        head_pair(row_count, firsts[0]),
        head_pair(key_count, firsts[1]),
        head_pair(key_count, firsts[2]),
        head_pair(row_count, 0),
        head_pair(row_count, 0),
        pl.BlockSpec((1, 8, row_count), lambda pair: (pair, 0, 0)),
    ]
    operands = [queries, keys, values, grads, outs, log_total]
    if not causal:
        in_specs.append(pl.BlockSpec((key_count, LANES), lambda pair: (0, 0)))
        operands.append(bias)
    return pl.pallas_call(
        functools.partial(attention_backward_kernel, causal=causal),
        grid=(pairs,),
        in_specs=in_specs,
        out_specs=[
            head_pair(row_count, 0),
            head_pair(key_count, 0),
            head_pair(key_count, 0),
        ],
        out_shape=[
            jax.ShapeDtypeStruct((row_count, pairs * LANES), BF16),
            jax.ShapeDtypeStruct((key_count, pairs * LANES), BF16),
            jax.ShapeDtypeStruct((key_count, pairs * LANES), BF16),
        ],
        scratch_shapes=[
            pltpu.VMEM((2, key_rows, row_count), BF16),
            pltpu.VMEM((2, key_count, row_count), BF16),
        ],
        compiler_params=pltpu.CompilerParams(vmem_limit_bytes=40 << 20),
        cost_estimate=pl.CostEstimate(
            flops=20 * row_count * key_count * HEADS * HEAD,
            bytes_accessed=16 << 20,
            transcendentals=row_count * key_count * HEADS,
        ),
    )(*operands)


def gelu_parts(values):
    slope = 0.7978845608028654
    square = values * values
    turned = jnp.tanh(slope * values * (1.0 + 0.044715 * square))
    weight = 0.5 * (1.0 + turned)
    derivative = weight + 0.5 * values * (1.0 - turned * turned) * (
        slope + (3.0 * 0.044715 * slope) * square
    )
    return values * weight, derivative


def feed_kernel(
    half_ref,
    low_ref,
    grad_ref,
    up_ref,
    down_ref,
    bias_ref,
    out_ref,
    back_ref,
    grad_up_ref,
    grad_down_ref,
    grad_bias_ref,
    low_turned,
    grad_turned,
    active_ref,
    hidden_ref,
):
    @pl.when(pl.program_id(0) == 0)
    def _():
        low_turned[...] = low_ref[...].T
        grad_turned[...] = grad_ref[...].T
        out_ref[...] = jnp.zeros_like(out_ref)
        back_ref[...] = jnp.zeros_like(back_ref)

    up = up_ref[...]
    down = down_ref[...]
    total = jnp.zeros((1, up.shape[1]), F32)
    pieces = low_ref.shape[0] // QUERY_ROWS
    for piece in range(pieces):
        rows = slice(piece * QUERY_ROWS, (piece + 1) * QUERY_ROWS)
        active, derivative = gelu_parts(dot(low_ref[rows, :], up) + bias_ref[0])
        active_low = active.astype(BF16)
        hidden_low = (derivative * dot(grad_ref[rows, :], down)).astype(BF16)
        active_ref[rows, :] = active_low
        hidden_ref[rows, :] = hidden_low
        total = total + jnp.sum(hidden_low.astype(F32), axis=0, keepdims=True)
        out_ref[rows, :] += dot_last(active_low, down)
        back_ref[rows, :] += dot_last(hidden_low, up)
    grad_bias_ref[0] = total
    for piece in range(low_turned.shape[0] // QUERY_ROWS):
        rows = slice(piece * QUERY_ROWS, (piece + 1) * QUERY_ROWS)
        grad_down_ref[0, rows, :] = dot(grad_turned[rows, :], active_ref[...]).astype(BF16)
        grad_up_ref[0, rows, :] = dot(low_turned[rows, :], hidden_ref[...]).astype(BF16)


def feed_half(half, low, grad, full_weights, bias, width):
    row_count, model = low.shape
    hidden = bias.shape[0]
    steps = hidden // (2 * width)
    up_first = 2 * hidden // width
    down_first = 3 * hidden // width
    whole = pl.BlockSpec(
        (row_count, model), lambda step, side: (0, 0), pipeline_mode=pl.Buffered(1)
    )
    total = pl.BlockSpec((row_count, model), lambda step, side: (0, 0))
    terms = pl.BlockSpec((1, model, width), lambda step, side: (step, 0, 0))
    return pl.pallas_call(
        feed_kernel,
        grid_spec=pltpu.PrefetchScalarGridSpec(
            num_scalar_prefetch=1,
            grid=(steps,),
            in_specs=[
                whole,
                whole,
                pl.BlockSpec((model, width), lambda step, side: (0, up_first + 2 * step + side[0])),
                pl.BlockSpec(
                    (model, width), lambda step, side: (0, down_first + 2 * step + side[0])
                ),
                pl.BlockSpec((1, 1, width), lambda step, side: (2 * step + side[0], 0, 0)),
            ],
            out_specs=[
                total,
                total,
                terms,
                terms,
                pl.BlockSpec((1, 1, width), lambda step, side: (step, 0, 0)),
            ],
            scratch_shapes=[
                pltpu.VMEM((model, row_count), BF16),
                pltpu.VMEM((model, row_count), BF16),
                pltpu.VMEM((row_count, width), BF16),
                pltpu.VMEM((row_count, width), BF16),
            ],
        ),
        out_shape=[
            jax.ShapeDtypeStruct((row_count, model), F32),
            jax.ShapeDtypeStruct((row_count, model), F32),
            jax.ShapeDtypeStruct((steps, model, width), BF16),
            jax.ShapeDtypeStruct((steps, model, width), BF16),
            jax.ShapeDtypeStruct((steps, 1, width), F32),
        ],
        compiler_params=pltpu.CompilerParams(vmem_limit_bytes=56 << 20),
        cost_estimate=pl.CostEstimate(
            flops=6 * row_count * model * hidden,
            bytes_accessed=40 << 20,
            transcendentals=row_count * hidden // 2,
        ),
    )(half, low, grad, full_weights, full_weights, bias.reshape(-1, 1, width))


def swap_bit(values, device_count, bit):
    return lax.ppermute(values, AXES, [(item, item ^ bit) for item in range(device_count)])


def total_of(terms):
    result = terms[0].astype(F32)
    for term in terms[1:]:
        result = result + term.astype(F32)
    return result


def halve(terms, own_bits, position, device, device_count):
    bit = own_bits[position]
    mine = (device // bit) % 2
    sent = total_of(
        [lax.dynamic_index_in_dim(term, 1 - mine, position, keepdims=False) for term in terms]
    ).astype(BF16)
    got = swap_bit(sent, device_count, bit)
    kept = [lax.dynamic_index_in_dim(term, mine, position, keepdims=False) for term in terms]
    return kept + [got], own_bits[:position] + own_bits[position + 1 :]


def fold_planes(terms, group, plane_size):
    near = []
    for inner in range(plane_size):
        for plane in range(GROUPS):
            if (plane ^ group) & 1:
                near.append((plane * plane_size + inner, (plane ^ 1) * plane_size + inner))
    got = lax.ppermute(total_of(terms).astype(BF16), AXES, near)
    terms = terms + [got]
    other = group ^ 2
    far = [
        (other * plane_size + inner, group * plane_size + inner) for inner in range(plane_size)
    ]
    got = lax.ppermute(total_of(terms).astype(BF16), AXES, far)
    return terms + [got]


def sum_to_plane(sent, kept, group, device, device_count):
    plane_size = device_count // GROUPS
    got = swap_bit(sent, device_count, 1)
    bits = []
    bit = plane_size // 2
    while bit > 1:
        bits.append(bit)
        bit //= 2
    rows = kept.shape[1]
    parts = []
    for part in range(2):
        first = part * (rows // 2)
        terms = [
            term[:, first : first + rows // 2].reshape((2,) * len(bits) + (rows // 2, -1))
            for term in (kept, got)
        ]
        left = list(bits)
        while left:
            position = 0 if part == 0 else len(left) - 1
            terms, left = halve(terms, left, position, device, device_count)
        parts.append(total_of(fold_planes(terms, group, plane_size)))
    return jnp.concatenate(parts, axis=0)


def column_half(values, half, width):
    rows = values.shape[0]
    pieces = values.reshape(rows, -1, 2, width)
    return lax.dynamic_index_in_dim(pieces, half, 2, keepdims=False).reshape(rows, -1)


def weight_half(pairs, half, width):
    terms = []
    for left, right in pairs:
        product = dot_rows(left, column_half(right, half, width)).astype(BF16)
        terms.append(jnp.swapaxes(product.reshape(product.shape[0], -1, width), 0, 1))
    return jnp.concatenate(terms, axis=0)


def rotated_update(grad, weights, moment1, moment2, stats, bases):
    block_count = stats.shape[0]
    grads_three = grad.reshape(grad.shape[0], block_count, BLK)
    turned = jnp.einsum("dnb,nbc->dnc", grads_three, bases, precision=HIGHEST)
    first_moment = BETA_ONE * moment1.reshape(grads_three.shape) + (1.0 - BETA_ONE) * turned
    second_moment = (
        BETA_TWO * moment2.reshape(grads_three.shape) + (1.0 - BETA_TWO) * turned * turned
    )
    direction = (
        first_moment
        / (1.0 - BETA_ONE**STEP)
        / (jnp.sqrt(second_moment / (1.0 - BETA_TWO**STEP)) + ADAM_EPS)
    )
    returned = jnp.einsum("dnc,nbc->dnb", direction, bases, precision=HIGHEST).reshape(grad.shape)
    updated = weights - RATE * (returned + DECAY * weights)
    renewed = BETA_TWO * stats + (1.0 - BETA_TWO) * jnp.einsum(
        "dnb,dnc->nbc", grads_three, grads_three, precision=HIGHEST
    )
    product = jnp.einsum("nbc,ncd->nbd", renewed, bases, precision=HIGHEST)
    gram_matrix = jnp.einsum("nbc,nbd->ncd", product, product, precision=HIGHEST)
    factor = jnp.linalg.cholesky(gram_matrix)
    solved = jax.scipy.linalg.solve_triangular(factor, jnp.swapaxes(product, 1, 2), lower=True)
    return (
        first_moment.reshape(grad.shape),
        second_moment.reshape(grad.shape),
        updated,
        renewed,
        jnp.swapaxes(solved, 1, 2),
    )


def adam_update(grad, values, moment1, moment2):
    first_moment = BETA_ONE * moment1 + (1.0 - BETA_ONE) * grad
    second_moment = BETA_TWO * moment2 + (1.0 - BETA_TWO) * grad * grad
    updated = values - VECTOR_RATE * (first_moment / (1.0 - BETA_ONE**STEP)) / (
        jnp.sqrt(second_moment / (1.0 - BETA_TWO**STEP)) + ADAM_EPS
    )
    return (first_moment, second_moment, updated)


def gather_parameters(weights, vectors, device_count):
    model, width = weights.shape
    vector_rows, vector_width = vectors.shape
    flat = vectors.astype(BF16).reshape(-1)
    flat = jnp.pad(flat, (0, VECTOR_PAD * width - flat.shape[0]))
    packed = jnp.concatenate([weights.astype(BF16), flat.reshape(VECTOR_PAD, width)], axis=0)
    full = lax.all_gather(packed, AXES, axis=1, tiled=True)
    tail = full[model:].reshape(VECTOR_PAD, device_count, width)
    tail = jnp.swapaxes(tail, 0, 1).reshape(device_count, -1)[:, : vector_rows * vector_width]
    tail = jnp.swapaxes(tail.reshape(device_count, vector_rows, vector_width), 0, 1)
    return full, tail.reshape(vector_rows, -1).astype(F32)


def local(
    tokens,
    memory,
    page_lengths,
    slot_masks,
    upstream,
    weights,
    weight_average,
    weight_moment1,
    weight_moment2,
    stats,
    bases,
    vectors,
    vector_average,
    vector_moment1,
    vector_moment2,
):
    row_count, model = tokens.shape
    width = weights.shape[1]
    group_size = lax.axis_size("mem")
    device_count = lax.axis_size("seq") * group_size
    device = lax.axis_index(AXES)
    member = lax.axis_index("mem")
    core = device % 2
    quarter = memory.shape[1]
    scale_q = HEAD ** (-0.5)
    pairs = HEADS // 2

    memory_padded = jnp.pad(memory, ((0, 0), (0, SLOT_PAD - quarter), (0, 0)))
    memory_here = lax.all_to_all(memory_padded, "mem", split_axis=0, concat_axis=0, tiled=True)
    memory_here = memory_here.reshape(group_size * SLOT_PAD, model)
    full_weights, vector_rows = gather_parameters(weights, vectors, device_count)

    def block_columns(first, count):
        return full_weights[:model, first * model : (first + count) * model]

    inputs = tokens.astype(F32)
    live_rows = (jnp.arange(row_count) < page_lengths[0]).astype(F32)[:, None]
    slots_here = lax.dynamic_slice_in_dim(slot_masks, member, 1, 0).reshape(group_size, quarter)
    slots_here = jnp.pad(slots_here, ((0, 0), (0, SLOT_PAD - quarter))).reshape(-1, 1)
    slot_bias = jnp.broadcast_to(
        jnp.where(slots_here > 0, 0.0, MASKED).astype(F32), (group_size * SLOT_PAD, LANES)
    )

    normed_one, pull_one = jax.vjp(normalize, inputs, vector_rows[0], vector_rows[1])
    low_one = normed_one.astype(BF16)
    queries_self = ((dot(low_one, block_columns(0, 1)) + vector_rows[6]) * scale_q).astype(BF16)
    keys_self = dot(low_one, block_columns(1, 1)).astype(BF16)
    values_self = (dot(low_one, block_columns(2, 1)) + vector_rows[7]).astype(BF16)
    attended, self_log = attention_forward(queries_self, keys_self, values_self, (0, 0, 0))
    after_self = inputs + dot(attended, block_columns(3, 1)) + vector_rows[8]
    normed_two, pull_two = jax.vjp(normalize, after_self, vector_rows[2], vector_rows[3])
    low_two = normed_two.astype(BF16)
    queries_cross = ((dot(low_two, block_columns(4, 1)) + vector_rows[9]) * scale_q).astype(BF16)
    keys_cross = dot(memory_here, block_columns(5, 1)).astype(BF16)
    values_cross = (dot(memory_here, block_columns(6, 1)) + vector_rows[10]).astype(BF16)
    merged, cross_log = attention_forward(
        queries_cross, keys_cross, values_cross, (0, 0, 0), slot_bias
    )
    after_cross = after_self + dot(merged, block_columns(7, 1)) + vector_rows[11]
    normed_three, pull_three = jax.vjp(normalize, after_cross, vector_rows[4], vector_rows[5])
    low_three = normed_three.astype(BF16)
    bias_up = vector_rows[13:17].reshape(-1)

    grad_result = upstream.astype(F32) * live_rows
    grad_low_three = grad_result.astype(BF16)
    away = (1 - core).reshape(1).astype(jnp.int32)
    here = core.reshape(1).astype(jnp.int32)
    out_a, back_a, up_sent, down_sent, bias_sent = feed_half(
        away, low_three, grad_low_three, full_weights, bias_up, width
    )
    out_b, back_b, up_kept, down_kept, bias_kept = feed_half(
        here, low_three, grad_low_three, full_weights, bias_up, width
    )
    group_two = sum_to_plane(up_sent, up_kept, 2, device, device_count)
    group_three = sum_to_plane(down_sent, down_kept, 3, device, device_count)
    result = (after_cross + (out_a + out_b) + vector_rows[12]) * live_rows
    mixed = result.astype(BF16)
    bias_even = jnp.where(core == 0, bias_kept, bias_sent)
    bias_odd = jnp.where(core == 0, bias_sent, bias_kept)
    grad_bias_up = jnp.concatenate([bias_even, bias_odd], axis=1).reshape(4, model)
    back_three, gain_three, shift_three = pull_three(back_a + back_b)

    grad_two = grad_result + back_three
    grad_low_two = grad_two.astype(BF16)
    grad_merged = dot_last(grad_low_two, block_columns(7, 1)).astype(BF16)
    grad_queries_cross, grad_keys_cross, grad_values_cross = attention_backward(
        queries_cross,
        keys_cross,
        values_cross,
        (0, 0, 0),
        grad_merged,
        merged,
        cross_log,
        slot_bias,
    )
    cross_pairs = (
        (low_two, grad_queries_cross),
        (memory_here, grad_keys_cross),
        (memory_here, grad_values_cross),
        (merged, grad_low_two),
    )
    group_one = sum_to_plane(
        weight_half(cross_pairs, 1 - core, width),
        weight_half(cross_pairs, core, width),
        1,
        device,
        device_count,
    )
    grad_normed_two = dot_last(grad_queries_cross, block_columns(4, 1))
    back_two, gain_two, shift_two = pull_two(grad_normed_two)

    grad_one = grad_two + back_two
    grad_low_one = grad_one.astype(BF16)
    grad_attended = dot_last(grad_low_one, block_columns(3, 1)).astype(BF16)
    grad_queries_self, grad_keys_self, grad_values_self = attention_backward(
        queries_self,
        keys_self,
        values_self,
        (0, 0, 0),
        grad_attended,
        attended,
        self_log,
    )
    self_pairs = (
        (low_one, grad_queries_self),
        (low_one, grad_keys_self),
        (low_one, grad_values_self),
        (attended, grad_low_one),
    )
    group_zero = sum_to_plane(
        weight_half(self_pairs, 1 - core, width),
        weight_half(self_pairs, core, width),
        0,
        device,
        device_count,
    )
    grad_normed_one = (
        dot_last(grad_queries_self, block_columns(0, 1))
        + dot_last(grad_keys_self, block_columns(1, 1))
        + dot_last(grad_values_self, block_columns(2, 1))
    )
    back_one, gain_one, shift_one = pull_one(grad_normed_one)
    input_grad = grad_one + back_one
    memory_back = dot_last(grad_keys_cross, block_columns(5, 1)) + dot_last(
        grad_values_cross, block_columns(6, 1)
    )
    memory_back = lax.all_to_all(
        memory_back.astype(BF16).reshape(group_size, SLOT_PAD, model),
        "mem",
        split_axis=0,
        concat_axis=0,
        tiled=True,
    )
    memory_back = memory_back[:, :quarter].astype(F32)

    vector_head = jnp.stack(
        [
            gain_one,
            shift_one,
            gain_two,
            shift_two,
            gain_three,
            shift_three,
            column_total(grad_queries_self),
            column_total(grad_values_self),
            column_total(grad_low_one),
            column_total(grad_queries_cross),
            column_total(grad_values_cross),
            column_total(grad_low_two),
            column_total(grad_low_three),
        ],
        axis=0,
    )
    vector_terms = jnp.concatenate([vector_head, grad_bias_up], axis=0)
    vector_grad = lax.psum_scatter(vector_terms, AXES, scatter_dimension=1, tiled=True)

    plane = device // (device_count // GROUPS)
    weight_grad = jnp.where(
        plane < 2,
        jnp.where(plane == 0, group_zero, group_one),
        jnp.where(plane == 2, group_two, group_three),
    )
    weight_first, weight_second, new_weights, new_stats, new_bases = rotated_update(
        weight_grad, weights, weight_moment1, weight_moment2, stats, bases
    )
    new_average = AVERAGE * weight_average + (1.0 - AVERAGE) * new_weights
    vector_first, vector_second, new_vectors = adam_update(
        vector_grad, vectors, vector_moment1, vector_moment2
    )
    new_vector_average = AVERAGE * vector_average + (1.0 - AVERAGE) * new_vectors
    return (
        mixed,
        input_grad,
        memory_back,
        weight_grad,
        weight_first,
        weight_second,
        new_weights,
        new_average,
        new_weights.astype(BF16),
        new_stats,
        new_bases,
        vector_grad,
        vector_first,
        vector_second,
        new_vectors,
        new_vector_average,
        new_vectors.astype(BF16),
        vector_grad[12],
    )


def solution(mesh):
    return jax.shard_map(
        local,
        mesh=mesh,
        in_specs=(
            P(("seq", "mem"), None),
            P("seq", "mem", None),
            P(("seq", "mem")),
            P("seq", None),
            P(("seq", "mem"), None),
            P(None, ("seq", "mem")),
            P(None, ("seq", "mem")),
            P(None, ("seq", "mem")),
            P(None, ("seq", "mem")),
            P(("seq", "mem"), None, None),
            P(("seq", "mem"), None, None),
            P(None, ("seq", "mem")),
            P(None, ("seq", "mem")),
            P(None, ("seq", "mem")),
            P(None, ("seq", "mem")),
        ),
        out_specs=(
            P(("seq", "mem"), None),
            P(("seq", "mem"), None),
            P("seq", "mem", None),
            P(None, ("seq", "mem")),
            P(None, ("seq", "mem")),
            P(None, ("seq", "mem")),
            P(None, ("seq", "mem")),
            P(None, ("seq", "mem")),
            P(None, ("seq", "mem")),
            P(("seq", "mem"), None, None),
            P(("seq", "mem"), None, None),
            P(None, ("seq", "mem")),
            P(None, ("seq", "mem")),
            P(None, ("seq", "mem")),
            P(None, ("seq", "mem")),
            P(None, ("seq", "mem")),
            P(None, ("seq", "mem")),
            P(("seq", "mem")),
        ),
        check_vma=False,
    )
```

time: 2170 us -> 1140 us (0.53)
  matrix products: 726 us -> 115 us
  waiting for transfers between devices: 901 us -> 336 us
  Pallas kernels: 0 us -> 207 us
  other arithmetic: 270 us -> 199 us
  starting transfers between devices: 9.27 us -> 71.9 us
  blocking collectives: 60.3 us -> 0 us
    reduce_scatter x1 -> x0, waiting for transfers between devices: 694 us -> none  [local(): lax.psum_scatter(weight_terms, ('seq', 'mem'), scatter_dimension=1, tiled...]
    dot_general x65 -> x32, matrix products: 708 us -> 103 us  [the longest x8 38.2 us: dot(): return jnp.dot(left, right, preferred_element_type=F32)]
    pallas_call x0 -> x6, Pallas kernels: none -> 207 us  [the longest x2 73.3 us: feed_half(): pl.pallas_call(feed_kernel, grid_spec=pltpu.PrefetchScalarGridSpec(num_sc...]
    ppermute x0 -> x36, waiting for transfers between devices: none -> 123 us  [the longest x20 103 us: swap_bit(): lax.ppermute(values, AXES, [(item, item ^ bit) for item in range(device_c...]
    ppermute x0 -> x36, starting transfers between devices: none -> 63.2 us  [the longest x8 37.7 us: fold_planes(): got = lax.ppermute(total_of(terms).astype(BF16), AXES, far)]
    reduce_sum x17 -> x6, other arithmetic: 71.7 us -> 10.2 us  [column_total(): return jnp.sum(values.astype(F32), axis=0)]
    all_gather x1 -> x0, blocking collectives: 60.3 us -> none  [local(): lax.all_gather(vectors.astype(jnp.bfloat16), ('seq', 'mem'), axis=1, tile...]
    all_gather x1, waiting for transfers between devices: 150 us -> 208 us  [gather_parameters(): full = lax.all_gather(packed, AXES, axis=1, tiled=True)]
  transfers between devices with their start and end apart: 5 -> 40, of which waited for: 3 -> 15; matrix products, arithmetic and copies ran while one was open for 10% -> 20% of each run, Pallas kernels for 0% -> 3%
where the time goes in v1:
time: 1140 us; the launch traced here: 1130 us
  waiting for transfers between devices  336 us (29%)
  Pallas kernels  207 us (18%)
  other arithmetic  199 us (17%)
  local copies, waits for them, and re-layouts  185 us (16%)
  matrix products  115 us (10%)
  starting transfers between devices  71.9 us (6%)
  between operations  17.4 us (2%)
    all_gather x1, waiting for transfers between devices, gather_parameters(): full = lax.all_gather(packed, AXES, axis=1, tiled=True)  208 us
    ppermute x20, waiting for transfers between devices, swap_bit(): lax.ppermute(values, AXES, [(item, item ^ bit) for item in range(device_c...  103 us
    pallas_call x2, Pallas kernels, feed_half(): pl.pallas_call(feed_kernel, grid_spec=pltpu.PrefetchScalarGridSpec(num_sc...  73.3 us
    pallas_call x2, Pallas kernels, attention_forward(): pl.pallas_call(functools.partial(attention_forward_kernel, causal=causal)...  67.5 us
    pallas_call x2, Pallas kernels, attention_backward(): pl.pallas_call(functools.partial(attention_backward_kernel, causal=causal...  66.2 us
    unnamed x286, local copies, waits for them, and re-layouts  55.4 us
    another operation x4, other arithmetic, rotated_update(): factor = jnp.linalg.cholesky(gram_matrix)  48.7 us
    another operation x3, other arithmetic, rotated_update(): jax.scipy.linalg.solve_triangular(factor, jnp.swapaxes(product, 1, 2), lo...  40 us
  transfers between devices with their start and end apart: 40, of which 15 were waited for; matrix products, arithmetic and copies ran while one was open for 20% of the time, Pallas kernels for 3%

profile of v1, /device:TPU:0, one launch (start us, length us, event | category | flops | bytes accessed | tf_op | source)
XLA Modules:
  0.0 1131.5 jit_solution(7495718069697698498)
XLA Ops:
  12.2 4.3 all-to-all-start
  33.7 208.4 %all-gather.2.cloned.1.call-done.up_ref.down_ref = bf16[1040,16384]{1,0:T(8,128)(2,1)} async-done(((bf16[1040,512]{1,0:T(8,128)(2,1)}), bf16[1040,16384]{1,0:T(8,128)(2,1)}) %all-gather.2.cloned.1.call-update) | async-done | bytes 34078736 | tf_op jit(solution)/shard_map/all_gather | solution.py:487
  245.6 4.7 convolution_convert_fusion.2.refs_1_
  250.3 4.7 add_convert_fusion.2.refs_2_
  255.0 4.7 multiply_convert_fusion.2.refs_0_
  259.7 33.7 %shard_map.286 = (bf16[1024,1024]{1,0:T(8,128)(2,1)S(1)}, f32[8,8,1024]{2,1,0:T(8,128)S(1)}) custom-call(bf16[1024,1024]{1,0:T(8,128)(2,1)S(1)} %multiply_convert_fusion.2.refs_0_, bf16[1024,1024]{1,0:T(8,128)(2,1)S(1)} %convolution_convert_fusion.2.refs_1_, bf16[1024,1024]{1,0:T(8,128)(2,1)S(1)} %add_convert_fusion.2.refs_2_), custom_call_target="tpu_custom_call" | custom-call | flops 17179869184 | bytes 8388608 | tf_op jit(solution)/shard_map/pallas_call | solution.py:188
  293.5 6.8 fusion.152
  313.1 4.4 multiply_convert_fusion.1.refs_0_
  317.7 33.8 %shard_map.287 = (bf16[1024,1024]{1,0:T(8,128)(2,1)S(1)}, f32[8,8,1024]{2,1,0:T(8,128)S(1)}) custom-call(bf16[1024,1024]{1,0:T(8,128)(2,1)S(1)} %multiply_convert_fusion.1.refs_0_, bf16[640,1024]{1,0:T(8,128)(2,1)S(1)} %fusion.47.refs_1_, bf16[640,1024]{1,0:T(8,128)(2,1)S(1)} %add_convert_fusion.4.refs_2_, f32[640,128]{1,0:T(8,128)S(1)} %broadcast_in_dim.44.refs_3_.refs_6_), custom_call_target="tpu_custom_call" | custom-call | flops 10737418240 | bytes 8388608 | tf_op jit(solution)/shard_map/pallas_call | solution.py:188
  351.5 4.8 fusion.153
  363.3 36.7 %shard_map.289 = (f32[1024,1024]{1,0:T(8,128)}, f32[1024,1024]{1,0:T(8,128)}, bf16[4,1024,512]{2,1,0:T(8,128)(2,1)}, bf16[4,1024,512]{2,1,0:T(8,128)(2,1)}, f32[4,1,512]{2,1,0:T(1,128)}) custom-call(s32[1]{0:T(128)} %bitcast.5.half_ref, bf16[1024,1024]{1,0:T(8,128)(2,1)} %add_convert_fusion.low_ref, bf16[1024,1024]{1,0:T(8,128)(2,1)} %get-tuple-element.157.grad_ref, ...), custom_call_target="tpu_custom_call" | custom-call | flops 25769803776 | bytes 41943040 | tf_op jit(solution)/shard_map/pallas_call | solution.py:321
  400.1 36.6 %shard_map.288 = (f32[1024,1024]{1,0:T(8,128)}, f32[1024,1024]{1,0:T(8,128)}, bf16[4,1024,512]{2,1,0:T(8,128)(2,1)}, bf16[4,1024,512]{2,1,0:T(8,128)(2,1)}, f32[4,1,512]{2,1,0:T(1,128)}) custom-call(s32[1]{0:T(128)} %bitcast.3.half_ref, bf16[1024,1024]{1,0:T(8,128)(2,1)} %add_convert_fusion.low_ref, bf16[1024,1024]{1,0:T(8,128)(2,1)} %get-tuple-element.157.grad_ref, ...), custom_call_target="tpu_custom_call" | custom-call | flops 25769803776 | bytes 41943040 | tf_op jit(solution)/shard_map/pallas_call | solution.py:321
  436.6 5.8 multiply_reduce_fusion
  442.6 8.6 fusion.143
  453.1 4.8 convolution_convert_fusion.1.refs_3_
  457.9 33.5 %shard_map.290 = (bf16[1024,1024]{1,0:T(8,128)(2,1)S(1)}, bf16[640,1024]{1,0:T(8,128)(2,1)S(1)}, bf16[640,1024]{1,0:T(8,128)(2,1)S(1)}) custom-call(bf16[1024,1024]{1,0:T(8,128)(2,1)S(1)} %copy-done.25, bf16[640,1024]{1,0:T(8,128)(2,1)S(1)} %copy-done.15, bf16[640,1024]{1,0:T(8,128)(2,1)S(1)} %copy-done.19, ...), custom_call_target="tpu_custom_call" | custom-call | flops 13421772800 | bytes 16777216 | tf_op jit(solution)/shard_map/pallas_call | solution.py:227
  496.7 4.5 reshape.607
  502.7 4.4 reshape.605
  507.1 6.1 fusion.154
  513.2 5.7 copy.187
  519.0 4.5 multiply_reduce_fusion.1
  530.4 6.1 convolution_convert_fusion.refs_3_
  536.5 32.7 %shard_map.291 = (bf16[1024,1024]{1,0:T(8,128)(2,1)S(1)}, bf16[1024,1024]{1,0:T(8,128)(2,1)S(1)}, bf16[1024,1024]{1,0:T(8,128)(2,1)S(1)}) custom-call(bf16[1024,1024]{1,0:T(8,128)(2,1)S(1)} %copy-done.23, bf16[1024,1024]{1,0:T(8,128)(2,1)S(1)} %copy-done.17, bf16[1024,1024]{1,0:T(8,128)(2,1)S(1)} %copy-done.21, ...), custom_call_target="tpu_custom_call" | custom-call | flops 21474836480 | bytes 16777216 | tf_op jit(solution)/shard_map/pallas_call | solution.py:227
  571.8 4.5 reshape.585
  581.5 4.5 reshape.591
  586.0 4.6 reshape.587
  590.7 4.7 fusion.41
  599.7 4.6 fusion.120
  608.6 11.2 constant_dynamic-slice_fusion.5
  626.2 7.2 constant_dynamic-slice_fusion.6
  654.2 9.1 constant_dynamic-slice_fusion.21
  666.9 8.7 constant_dynamic-slice_fusion.19
  703.3 6.5 fusion.144
  738.5 4.9 reduce-scatter.4.cloned.1.call-done
  769.9 9.9 collective-permute-done.28
  782.8 19.5 %collective-permute-done.19 = bf16[2,512,512]{2,1,0:T(8,128)(2,1)S(1)} collective-permute-done((bf16[2,512,512]{2,1,0:T(8,128)(2,1)S(1)}, bf16[2,512,512]{2,1,0:T(8,128)(2,1)S(1)}, u32[]{:S(2)}, u32[]{:S(2)}) %collective-permute-start.19) | collective-permute-done | bytes 1048608 | tf_op jit(solution)/shard_map/ppermute | solution.py:366
  802.7 22.1 %collective-permute-done.10 = bf16[2,512,512]{2,1,0:T(8,128)(2,1)} collective-permute-done((bf16[2,512,512]{2,1,0:T(8,128)(2,1)S(1)}, bf16[2,512,512]{2,1,0:T(8,128)(2,1)}, u32[]{:S(2)}, u32[]{:S(2)}) %collective-permute-start.10) | collective-permute-done | bytes 1048608 | tf_op jit(solution)/shard_map/ppermute | solution.py:366
  828.8 18.4 %collective-permute-done.1 = bf16[2,512,512]{2,1,0:T(8,128)(2,1)S(1)} collective-permute-done((bf16[2,512,512]{2,1,0:T(8,128)(2,1)S(1)}, bf16[2,512,512]{2,1,0:T(8,128)(2,1)S(1)}, u32[]{:S(2)}, u32[]{:S(2)}) %collective-permute-start.1) | collective-permute-done | bytes 1048608 | tf_op jit(solution)/shard_map/ppermute | solution.py:366
  849.9 21.3 %collective-permute-done.11 = bf16[512,512]{1,0:T(8,128)(2,1)S(1)} collective-permute-done((bf16[512,512]{1,0:T(8,128)(2,1)S(1)}, bf16[512,512]{1,0:T(8,128)(2,1)S(1)}, u32[]{:S(2)}, u32[]{:S(2)}) %collective-permute-start.11) | collective-permute-done | bytes 524320 | tf_op jit(solution)/shard_map/ppermute | solution.py:366
  877.1 5.3 collective-permute-done.20
  891.7 4.6 collective-permute-start.12
  902.8 8.2 collective-permute-done.25
  917.1 28.0 %collective-permute-start.22 = (bf16[512,512]{1,0:T(8,128)(2,1)}, bf16[512,512]{1,0:T(8,128)(2,1)}, u32[]{:S(2)}, u32[]{:S(2)}) collective-permute-start(bf16[512,512]{1,0:T(8,128)(2,1)} %fusion.102), channel_id=1, source_target_pairs={{0,16},{1,17},{2,18},{3,19},{4,20},{5,21},{6,22},{7,23}} | collective-permute-start | bytes 1572872 | tf_op jit(solution)/shard_map/ppermute | solution.py:399
  989.7 7.5 collective-permute-done.8
  1002.2 5.0 fusion.15
  1012.6 47.9 %custom-call.8 = f32[4,128,128]{2,1,0:T(8,128)S(1)} custom-call(f32[4,128,128]{2,1,0:T(8,128)} %fusion.108), custom_call_target="Cholesky" | custom-call | tf_op jit(solution)/shard_map/jit(cholesky)/cholesky | solution.py:461
  1060.8 39.3 %custom-call.9 = f32[4,1,128,128]{2,3,1,0:T(8,128)S(1)} custom-call(f32[4,1,128,128]{3,2,1,0:T(8,128)S(1)} %select_bitcast_fusion), custom_call_target="InvertDiagBlocksLowerTriangular" | custom-call | tf_op jit(solution)/shard_map/jit(_solve_triangular)/vmap()/triangular_solve | solution.py:462
  1101.2 4.6 fusion.14
  (534 shorter events, 301.9 us)
Async XLA Ops:
  7.2 1003.5 %copy-start = (f32[4,128,128]{2,1,0:T(8,128)S(1)}, f32[4,128,128]{2,1,0:T(8,128)}, u32[]{:S(2)}) copy-start(f32[4,128,128]{2,1,0:T(8,128)} %param.25) | copy-start | bytes 786436
  7.2 235.0 %all-gather.2.cloned.1.call-start = ((), (), s32[]{:S(2)}) async-start(), calls=%async_computation.3 | async-start | bytes 35143680 | tf_op jit(solution)/shard_map/all_gather | solution.py:487
  12.2 292.7 %all-to-all-start = ((bf16[4,160,1024]{2,1,0:T(8,128)(2,1)}), bf16[4,160,1024]{2,1,0:T(8,128)(2,1)}, u32[]{:S(2)}, u32[]{:S(2)}) async-start(bf16[4,160,1024]{2,1,0:T(8,128)(2,1)} %pad.13), calls=%async_computation | async-start | bytes 2621440 | tf_op jit(solution)/shard_map/all_to_all | solution.py:523
  16.5 726.9 %reduce-scatter.4.cloned.1.call-start = ((), (), s32[]{:S(2)}) async-start(), calls=%async_computation.4 | async-start | bytes 540672
  30.0 214.7 %copy-start.113 = (f32[1024]{0:T(1024)}, f32[1024]{0:T(1024)S(1)}, u32[]{:S(2)}) copy-start(f32[1024]{0:T(1024)S(1)} %broadcast_multiply_fusion.4) | copy-start | bytes 12292
  31.3 213.5 %copy-start.119 = (f32[1024]{0:T(1024)}, f32[1024]{0:T(1024)S(1)}, u32[]{:S(2)}) copy-start(f32[1024]{0:T(1024)S(1)} %fusion.112) | copy-start | bytes 12292
  608.0 142.5 %collective-permute-start.27 = (bf16[4,1024,512]{2,1,0:T(8,128)(2,1)}, bf16[4,1024,512]{2,1,0:T(8,128)(2,1)}, u32[]{:S(2)}, u32[]{:S(2)}) collective-permute-start(bf16[4,1024,512]{2,1,0:T(8,128)(2,1)} %get-tuple-element.55), channel_id=1, source_target_pairs={{0,1},{1,0},{2,3},{3,2},{4,5},{5,4},{6,7},{7,6},{8,9},{9,8},{10,11... | collective-permute-start | bytes 12582920 | tf_op jit(solution)/shard_map/ppermute | solution.py:366
  608.4 146.8 %collective-permute-start.18 = (bf16[4,1024,512]{2,1,0:T(8,128)(2,1)}, bf16[4,1024,512]{2,1,0:T(8,128)(2,1)}, u32[]{:S(2)}, u32[]{:S(2)}) collective-permute-start(bf16[4,1024,512]{2,1,0:T(8,128)(2,1)} %get-tuple-element.53), channel_id=1, source_target_pairs={{0,1},{1,0},{2,3},{3,2},{4,5},{5,4},{6,7},{7,6},{8,9},{9,8},{10,11... | collective-permute-start | bytes 12582920 | tf_op jit(solution)/shard_map/ppermute | solution.py:366
  640.7 118.6 %collective-permute-start.9 = (bf16[4,1024,512]{2,1,0:T(8,128)(2,1)}, bf16[4,1024,512]{2,1,0:T(8,128)(2,1)}, u32[]{:S(2)}, u32[]{:S(2)}) collective-permute-start(bf16[4,1024,512]{2,1,0:T(8,128)(2,1)} %pad_maximum_fusion.3), channel_id=1, source_target_pairs={{0,1},{1,0},{2,3},{3,2},{4,5},{5,4},{6,7},{7,6},{8,9},{9,8},{10,11... | collective-permute-start | bytes 12582920 | tf_op jit(solution)/shard_map/ppermute | solution.py:366
  680.6 83.0 %collective-permute-start = (bf16[4,1024,512]{2,1,0:T(8,128)(2,1)}, bf16[4,1024,512]{2,1,0:T(8,128)(2,1)}, u32[]{:S(2)}, u32[]{:S(2)}) collective-permute-start(bf16[4,1024,512]{2,1,0:T(8,128)(2,1)} %pad_maximum_fusion.1), channel_id=1, source_target_pairs={{0,1},{1,0},{2,3},{3,2},{4,5},{5,4},{6,7},{7,6},{8,9},{9,8},{10,11... | collective-permute-start | bytes 12582920 | tf_op jit(solution)/shard_map/ppermute | solution.py:366
  699.0 46.9 %all-to-all-start.1 = ((bf16[4,160,1024]{2,1,0:T(8,128)(2,1)}), bf16[4,160,1024]{2,1,0:T(8,128)(2,1)}, u32[]{:S(2)}, u32[]{:S(2)}) async-start(bf16[4,160,1024]{2,1,0:T(8,128)(2,1)} %bitcast.373), calls=%async_computation.1 | async-start | bytes 2621440 | tf_op jit(solution)/shard_map/all_to_all | solution.py:641
  753.7 26.2 %collective-permute-start.28 = (bf16[2,512,512]{2,1,0:T(8,128)(2,1)S(1)}, bf16[2,512,512]{2,1,0:T(8,128)(2,1)S(1)}, u32[]{:S(2)}, u32[]{:S(2)}) collective-permute-start(bf16[2,512,512]{2,1,0:T(8,128)(2,1)S(1)} %fusion.77), channel_id=1, source_target_pairs={{0,4},{1,5},{2,6},{3,7},{4,0},{5,1},{6,2},{7,3},{8,12},{9,13},{10,... | collective-permute-start | bytes 3145736 | tf_op jit(solution)/shard_map/ppermute | solution.py:366
  755.1 26.2 %collective-permute-start.32 = (bf16[2,512,512]{2,1,0:T(8,128)(2,1)S(1)}, bf16[2,512,512]{2,1,0:T(8,128)(2,1)S(1)}, u32[]{:S(2)}, u32[]{:S(2)}) collective-permute-start(bf16[2,512,512]{2,1,0:T(8,128)(2,1)S(1)} %fusion.78), channel_id=1, source_target_pairs={{0,2},{1,3},{2,0},{3,1},{4,6},{5,7},{6,4},{7,5},{8,10},{9,11},{10,... | collective-permute-start | bytes 3145736 | tf_op jit(solution)/shard_map/ppermute | solution.py:366
  758.3 44.0 %collective-permute-start.19 = (bf16[2,512,512]{2,1,0:T(8,128)(2,1)S(1)}, bf16[2,512,512]{2,1,0:T(8,128)(2,1)S(1)}, u32[]{:S(2)}, u32[]{:S(2)}) collective-permute-start(bf16[2,512,512]{2,1,0:T(8,128)(2,1)S(1)} %fusion.75), channel_id=1, source_target_pairs={{0,4},{1,5},{2,6},{3,7},{4,0},{5,1},{6,2},{7,3},{8,12},{9,13},{10,... | collective-permute-start | bytes 3145736 | tf_op jit(solution)/shard_map/ppermute | solution.py:366
  762.2 62.7 %collective-permute-start.10 = (bf16[2,512,512]{2,1,0:T(8,128)(2,1)S(1)}, bf16[2,512,512]{2,1,0:T(8,128)(2,1)}, u32[]{:S(2)}, u32[]{:S(2)}) collective-permute-start(bf16[2,512,512]{2,1,0:T(8,128)(2,1)S(1)} %fusion.73), channel_id=1, source_target_pairs={{0,4},{1,5},{2,6},{3,7},{4,0},{5,1},{6,2},{7,3},{8,12},{9,13},{10,... | collective-permute-start | bytes 3145736 | tf_op jit(solution)/shard_map/ppermute | solution.py:366
  763.7 62.5 %collective-permute-start.14 = (bf16[2,512,512]{2,1,0:T(8,128)(2,1)S(1)}, bf16[2,512,512]{2,1,0:T(8,128)(2,1)S(1)}, u32[]{:S(2)}, u32[]{:S(2)}) collective-permute-start(bf16[2,512,512]{2,1,0:T(8,128)(2,1)S(1)} %fusion.74), channel_id=1, source_target_pairs={{0,2},{1,3},{2,0},{3,1},{4,6},{5,7},{6,4},{7,5},{8,10},{9,11},{10,... | collective-permute-start | bytes 3145736 | tf_op jit(solution)/shard_map/ppermute | solution.py:366
  779.8 46.7 %collective-permute-start.23 = (bf16[2,512,512]{2,1,0:T(8,128)(2,1)S(1)}, bf16[2,512,512]{2,1,0:T(8,128)(2,1)S(1)}, u32[]{:S(2)}, u32[]{:S(2)}) collective-permute-start(bf16[2,512,512]{2,1,0:T(8,128)(2,1)S(1)} %fusion.76), channel_id=1, source_target_pairs={{0,2},{1,3},{2,0},{3,1},{4,6},{5,7},{6,4},{7,5},{8,10},{9,11},{10,... | collective-permute-start | bytes 3145736 | tf_op jit(solution)/shard_map/ppermute | solution.py:366
  781.3 66.0 %collective-permute-start.1 = (bf16[2,512,512]{2,1,0:T(8,128)(2,1)S(1)}, bf16[2,512,512]{2,1,0:T(8,128)(2,1)S(1)}, u32[]{:S(2)}, u32[]{:S(2)}) collective-permute-start(bf16[2,512,512]{2,1,0:T(8,128)(2,1)S(1)} %fusion.71), channel_id=1, source_target_pairs={{0,4},{1,5},{2,6},{3,7},{4,0},{5,1},{6,2},{7,3},{8,12},{9,13},{10,... | collective-permute-start | bytes 3145736 | tf_op jit(solution)/shard_map/ppermute | solution.py:366
  802.3 46.4 %collective-permute-start.5 = (bf16[2,512,512]{2,1,0:T(8,128)(2,1)S(1)}, bf16[2,512,512]{2,1,0:T(8,128)(2,1)S(1)}, u32[]{:S(2)}, u32[]{:S(2)}) collective-permute-start(bf16[2,512,512]{2,1,0:T(8,128)(2,1)S(1)} %fusion.72), channel_id=1, source_target_pairs={{0,2},{1,3},{2,0},{3,1},{4,6},{5,7},{6,4},{7,5},{8,10},{9,11},{10,... | collective-permute-start | bytes 3145736 | tf_op jit(solution)/shard_map/ppermute | solution.py:366
  824.9 49.1 %collective-permute-start.29 = (bf16[512,512]{1,0:T(8,128)(2,1)S(1)}, bf16[512,512]{1,0:T(8,128)(2,1)S(1)}, u32[]{:S(2)}, u32[]{:S(2)}) collective-permute-start(bf16[512,512]{1,0:T(8,128)(2,1)S(1)} %fusion.81), channel_id=1, source_target_pairs={{0,2},{1,3},{2,0},{3,1},{4,6},{5,7},{6,4},{7,5},{8,10},{9,11},{10,... | collective-permute-start | bytes 1572872 | tf_op jit(solution)/shard_map/ppermute | solution.py:366
  826.2 49.2 %collective-permute-start.33 = (bf16[512,512]{1,0:T(8,128)(2,1)S(1)}, bf16[512,512]{1,0:T(8,128)(2,1)S(1)}, u32[]{:S(2)}, u32[]{:S(2)}) collective-permute-start(bf16[512,512]{1,0:T(8,128)(2,1)S(1)} %fusion.79), channel_id=1, source_target_pairs={{0,4},{1,5},{2,6},{3,7},{4,0},{5,1},{6,2},{7,3},{8,12},{9,13},{10,... | collective-permute-start | bytes 1572872 | tf_op jit(solution)/shard_map/ppermute | solution.py:366
  826.5 44.7 %collective-permute-start.11 = (bf16[512,512]{1,0:T(8,128)(2,1)S(1)}, bf16[512,512]{1,0:T(8,128)(2,1)S(1)}, u32[]{:S(2)}, u32[]{:S(2)}) collective-permute-start(bf16[512,512]{1,0:T(8,128)(2,1)S(1)} %fusion.89), channel_id=1, source_target_pairs={{0,2},{1,3},{2,0},{3,1},{4,6},{5,7},{6,4},{7,5},{8,10},{9,11},{10,... | collective-permute-start | bytes 1572872 | tf_op jit(solution)/shard_map/ppermute | solution.py:366
  828.8 43.3 %copy-start.95 = (bf16[1,1,512,512]{3,2,1,0:T(8,128)(2,1)S(1)}, bf16[1,1,512,512]{3,2,1,0:T(8,128)(2,1)}, u32[]{:S(2)}) copy-start(bf16[1,1,512,512]{3,2,1,0:T(8,128)(2,1)} %copy.274) | copy-start | bytes 1572868
  847.2 35.2 %collective-permute-start.20 = (bf16[512,512]{1,0:T(8,128)(2,1)S(1)}, bf16[512,512]{1,0:T(8,128)(2,1)S(1)}, u32[]{:S(2)}, u32[]{:S(2)}) collective-permute-start(bf16[512,512]{1,0:T(8,128)(2,1)S(1)} %fusion.85), channel_id=1, source_target_pairs={{0,2},{1,3},{2,0},{3,1},{4,6},{5,7},{6,4},{7,5},{8,10},{9,11},{10,... | collective-permute-start | bytes 1572872 | tf_op jit(solution)/shard_map/ppermute | solution.py:366
  848.7 24.8 %collective-permute-start.15 = (bf16[512,512]{1,0:T(8,128)(2,1)S(1)}, bf16[512,512]{1,0:T(8,128)(2,1)S(1)}, u32[]{:S(2)}, u32[]{:S(2)}) collective-permute-start(bf16[512,512]{1,0:T(8,128)(2,1)S(1)} %fusion.87), channel_id=1, source_target_pairs={{0,4},{1,5},{2,6},{3,7},{4,0},{5,1},{6,2},{7,3},{8,12},{9,13},{10,... | collective-permute-start | bytes 1572872 | tf_op jit(solution)/shard_map/ppermute | solution.py:366
  871.2 12.9 %collective-permute-start.24 = (bf16[512,512]{1,0:T(8,128)(2,1)S(1)}, bf16[512,512]{1,0:T(8,128)(2,1)S(1)}, u32[]{:S(2)}, u32[]{:S(2)}) collective-permute-start(bf16[512,512]{1,0:T(8,128)(2,1)S(1)} %fusion.83), channel_id=1, source_target_pairs={{0,4},{1,5},{2,6},{3,7},{4,0},{5,1},{6,2},{7,3},{8,12},{9,13},{10,... | collective-permute-start | bytes 1572872 | tf_op jit(solution)/shard_map/ppermute | solution.py:366
  873.5 16.4 %collective-permute-start.2 = (bf16[512,512]{1,0:T(8,128)(2,1)S(1)}, bf16[512,512]{1,0:T(8,128)(2,1)S(1)}, u32[]{:S(2)}, u32[]{:S(2)}) collective-permute-start(bf16[512,512]{1,0:T(8,128)(2,1)S(1)} %fusion.93), channel_id=1, source_target_pairs={{0,2},{1,3},{2,0},{3,1},{4,6},{5,7},{6,4},{7,5},{8,10},{9,11},{10,... | collective-permute-start | bytes 1572872 | tf_op jit(solution)/shard_map/ppermute | solution.py:366
  874.0 17.8 %collective-permute-start.6 = (bf16[512,512]{1,0:T(8,128)(2,1)S(1)}, bf16[512,512]{1,0:T(8,128)(2,1)S(1)}, u32[]{:S(2)}, u32[]{:S(2)}) collective-permute-start(bf16[512,512]{1,0:T(8,128)(2,1)S(1)} %fusion.91), channel_id=1, source_target_pairs={{0,4},{1,5},{2,6},{3,7},{4,0},{5,1},{6,2},{7,3},{8,12},{9,13},{10,... | collective-permute-start | bytes 1572872 | tf_op jit(solution)/shard_map/ppermute | solution.py:366
  875.4 21.3 %collective-permute-start.30 = (bf16[512,512]{1,0:T(8,128)(2,1)S(1)}, bf16[512,512]{1,0:T(8,128)(2,1)S(1)}, u32[]{:S(2)}, u32[]{:S(2)}) collective-permute-start(bf16[512,512]{1,0:T(8,128)(2,1)S(1)} %get-tuple-element.165), channel_id=1, source_target_pairs={{0,8},{16,24},{1,9},{17,25},{2,10},{18,26},{3,11},{19,27},{4,12},{... | collective-permute-start | bytes 1572872 | tf_op jit(solution)/shard_map/ppermute | solution.py:393
  882.4 15.8 %collective-permute-start.34 = (bf16[512,512]{1,0:T(8,128)(2,1)S(1)}, bf16[512,512]{1,0:T(8,128)(2,1)S(1)}, u32[]{:S(2)}, u32[]{:S(2)}) collective-permute-start(bf16[512,512]{1,0:T(8,128)(2,1)S(1)} %get-tuple-element.167), channel_id=1, source_target_pairs={{0,8},{16,24},{1,9},{17,25},{2,10},{18,26},{3,11},{19,27},{4,12},{... | collective-permute-start | bytes 1572872 | tf_op jit(solution)/shard_map/ppermute | solution.py:393
  884.1 16.4 %collective-permute-start.21 = (bf16[512,512]{1,0:T(8,128)(2,1)S(1)}, bf16[512,512]{1,0:T(8,128)(2,1)S(1)}, u32[]{:S(2)}, u32[]{:S(2)}) collective-permute-start(bf16[512,512]{1,0:T(8,128)(2,1)S(1)} %get-tuple-element.169), channel_id=1, source_target_pairs={{8,0},{24,16},{9,1},{25,17},{10,2},{26,18},{11,3},{27,19},{12,4},{... | collective-permute-start | bytes 1572872 | tf_op jit(solution)/shard_map/ppermute | solution.py:393
  889.9 21.1 %collective-permute-start.25 = (bf16[512,512]{1,0:T(8,128)(2,1)S(1)}, bf16[512,512]{1,0:T(8,128)(2,1)S(1)}, u32[]{:S(2)}, u32[]{:S(2)}) collective-permute-start(bf16[512,512]{1,0:T(8,128)(2,1)S(1)} %get-tuple-element.171), channel_id=1, source_target_pairs={{8,0},{24,16},{9,1},{25,17},{10,2},{26,18},{11,3},{27,19},{12,4},{... | collective-permute-start | bytes 1572872 | tf_op jit(solution)/shard_map/ppermute | solution.py:393
  891.7 20.9 %collective-permute-start.12 = (bf16[512,512]{1,0:T(8,128)(2,1)S(1)}, bf16[512,512]{1,0:T(8,128)(2,1)S(1)}, u32[]{:S(2)}, u32[]{:S(2)}) collective-permute-start(bf16[512,512]{1,0:T(8,128)(2,1)S(1)} %get-tuple-element.173), channel_id=1, source_target_pairs={{0,8},{16,24},{1,9},{17,25},{2,10},{18,26},{3,11},{19,27},{4,12},{... | collective-permute-start | bytes 1572872 | tf_op jit(solution)/shard_map/ppermute | solution.py:393
  896.7 53.9 %copy-start.51 = (f32[512,512]{1,0:T(8,128)}, f32[512,512]{1,0:T(8,128)S(1)}, u32[]{:S(2)}) copy-start(f32[512,512]{1,0:T(8,128)S(1)} %get-tuple-element.180) | copy-start | bytes 3145732
  896.7 20.4 %collective-permute-start.16 = (bf16[512,512]{1,0:T(8,128)(2,1)S(1)}, bf16[512,512]{1,0:T(8,128)(2,1)S(1)}, u32[]{:S(2)}, u32[]{:S(2)}) collective-permute-start(bf16[512,512]{1,0:T(8,128)(2,1)S(1)} %get-tuple-element.175), channel_id=1, source_target_pairs={{0,8},{16,24},{1,9},{17,25},{2,10},{18,26},{3,11},{19,27},{4,12},{... | collective-permute-start | bytes 1572872 | tf_op jit(solution)/shard_map/ppermute | solution.py:393
  898.2 47.8 %collective-permute-start.3 = (bf16[512,512]{1,0:T(8,128)(2,1)S(1)}, bf16[512,512]{1,0:T(8,128)(2,1)S(1)}, u32[]{:S(2)}, u32[]{:S(2)}) collective-permute-start(bf16[512,512]{1,0:T(8,128)(2,1)S(1)} %get-tuple-element.177), channel_id=1, source_target_pairs={{8,0},{24,16},{9,1},{25,17},{10,2},{26,18},{11,3},{27,19},{12,4},{... | collective-permute-start | bytes 1572872 | tf_op jit(solution)/shard_map/ppermute | solution.py:393
  900.5 48.6 %collective-permute-start.7 = (bf16[512,512]{1,0:T(8,128)(2,1)S(1)}, bf16[512,512]{1,0:T(8,128)(2,1)S(1)}, u32[]{:S(2)}, u32[]{:S(2)}) collective-permute-start(bf16[512,512]{1,0:T(8,128)(2,1)S(1)} %get-tuple-element.179), channel_id=1, source_target_pairs={{8,0},{24,16},{9,1},{25,17},{10,2},{26,18},{11,3},{27,19},{12,4},{... | collective-permute-start | bytes 1572872 | tf_op jit(solution)/shard_map/ppermute | solution.py:393
  911.0 40.6 %collective-permute-start.31 = (bf16[512,512]{1,0:T(8,128)(2,1)S(1)}, bf16[512,512]{1,0:T(8,128)(2,1)S(1)}, u32[]{:S(2)}, u32[]{:S(2)}) collective-permute-start(bf16[512,512]{1,0:T(8,128)(2,1)S(1)} %fusion.104), channel_id=1, source_target_pairs={{8,24},{9,25},{10,26},{11,27},{12,28},{13,29},{14,30},{15,31}} | collective-permute-start | bytes 1572872 | tf_op jit(solution)/shard_map/ppermute | solution.py:399
  912.7 44.2 %collective-permute-start.35 = (bf16[512,512]{1,0:T(8,128)(2,1)}, bf16[512,512]{1,0:T(8,128)(2,1)}, u32[]{:S(2)}, u32[]{:S(2)}) collective-permute-start(bf16[512,512]{1,0:T(8,128)(2,1)} %fusion.105), channel_id=1, source_target_pairs={{8,24},{9,25},{10,26},{11,27},{12,28},{13,29},{14,30},{15,31}} | collective-permute-start | bytes 1572872 | tf_op jit(solution)/shard_map/ppermute | solution.py:399
  917.1 46.3 %collective-permute-start.22 = (bf16[512,512]{1,0:T(8,128)(2,1)}, bf16[512,512]{1,0:T(8,128)(2,1)}, u32[]{:S(2)}, u32[]{:S(2)}) collective-permute-start(bf16[512,512]{1,0:T(8,128)(2,1)} %fusion.102), channel_id=1, source_target_pairs={{0,16},{1,17},{2,18},{3,19},{4,20},{5,21},{6,22},{7,23}} | collective-permute-start | bytes 1572872 | tf_op jit(solution)/shard_map/ppermute | solution.py:399
  946.0 23.9 %collective-permute-start.26 = (bf16[512,512]{1,0:T(8,128)(2,1)}, bf16[512,512]{1,0:T(8,128)(2,1)}, u32[]{:S(2)}, u32[]{:S(2)}) collective-permute-start(bf16[512,512]{1,0:T(8,128)(2,1)} %fusion.103), channel_id=1, source_target_pairs={{0,16},{1,17},{2,18},{3,19},{4,20},{5,21},{6,22},{7,23}} | collective-permute-start | bytes 1572872 | tf_op jit(solution)/shard_map/ppermute | solution.py:399
  949.1 26.1 %collective-permute-start.13 = (bf16[512,512]{1,0:T(8,128)(2,1)}, bf16[512,512]{1,0:T(8,128)(2,1)}, u32[]{:S(2)}, u32[]{:S(2)}) collective-permute-start(bf16[512,512]{1,0:T(8,128)(2,1)} %fusion.100), channel_id=1, source_target_pairs={{24,8},{25,9},{26,10},{27,11},{28,12},{29,13},{30,14},{31,15}} | collective-permute-start | bytes 1572872 | tf_op jit(solution)/shard_map/ppermute | solution.py:399
  951.6 28.5 %collective-permute-start.17 = (bf16[512,512]{1,0:T(8,128)(2,1)}, bf16[512,512]{1,0:T(8,128)(2,1)}, u32[]{:S(2)}, u32[]{:S(2)}) collective-permute-start(bf16[512,512]{1,0:T(8,128)(2,1)} %fusion.101), channel_id=1, source_target_pairs={{24,8},{25,9},{26,10},{27,11},{28,12},{29,13},{30,14},{31,15}} | collective-permute-start | bytes 1572872 | tf_op jit(solution)/shard_map/ppermute | solution.py:399
  956.8 29.1 %collective-permute-start.4 = (bf16[512,512]{1,0:T(8,128)(2,1)}, bf16[512,512]{1,0:T(8,128)(2,1)}, u32[]{:S(2)}, u32[]{:S(2)}) collective-permute-start(bf16[512,512]{1,0:T(8,128)(2,1)} %fusion.98), channel_id=1, source_target_pairs={{16,0},{17,1},{18,2},{19,3},{20,4},{21,5},{22,6},{23,7}} | collective-permute-start | bytes 1572872 | tf_op jit(solution)/shard_map/ppermute | solution.py:399
  963.4 33.8 %collective-permute-start.8 = (bf16[512,512]{1,0:T(8,128)(2,1)}, bf16[512,512]{1,0:T(8,128)(2,1)}, u32[]{:S(2)}, u32[]{:S(2)}) collective-permute-start(bf16[512,512]{1,0:T(8,128)(2,1)} %fusion.99), channel_id=1, source_target_pairs={{16,0},{17,1},{18,2},{19,3},{20,4},{21,5},{22,6},{23,7}} | collective-permute-start | bytes 1572872 | tf_op jit(solution)/shard_map/ppermute | solution.py:399
  1010.7 90.5 %copy-start.107 = (f32[4,128,128]{2,1,0:T(8,128)}, f32[4,128,128]{2,1,0:T(8,128)S(1)}, u32[]{:S(2)}) copy-start(f32[4,128,128]{2,1,0:T(8,128)S(1)} %fusion.70) | copy-start | bytes 786436
  1010.7 49.8 %copy-start.116 = (pred[128,128]{1,0:T(8,128)(4,1)S(1)}, pred[128,128]{1,0:T(8,128)(4,1)}, u32[]{:S(2)}) copy-start(pred[128,128]{1,0:T(8,128)(4,1)} %iota_compare_fusion) | copy-start | bytes 49156
  1010.7 49.9 %copy-start.115 = (pred[128,128]{1,0:T(8,128)(4,1)S(1)}, pred[128,128]{1,0:T(8,128)(4,1)}, u32[]{:S(2)}) copy-start(pred[128,128]{1,0:T(8,128)(4,1)} %iota_compare_fusion.1) | copy-start | bytes 49156
  (125 other events, 934.3 us)
Sparse Core Ops, SparseCore 0:
  11.5 230.6 all-gather.1
  608.2 135.1 reduce-scatter.3

commit v2 on v1

--- a/solution.py
+++ b/solution.py
@@ -15,6 +15,7 @@
 QUERY_ROWS = 256
 SLOT_PAD = 160
 VECTOR_PAD = 16
+PANEL = 8
 GROUPS = 4
 AXES = ("seq", "mem")
 
@@ -109,11 +110,9 @@
 
 
 def attention_backward_kernel(*refs, causal):
-    if causal:
-        q_ref, k_ref, v_ref, grad_ref, out_ref, log_ref = refs[:6]
-    else:
-        q_ref, k_ref, v_ref, grad_ref, out_ref, log_ref, bias_ref = refs[:7]
-    dq_ref, dk_ref, dv_ref, chance_ref, score_ref = refs[-5:]
+    _, q_ref, k_ref, v_ref, grad_ref, out_ref, log_ref = refs[:7]
+    bias_ref = None if causal else refs[7]
+    dq_ref, dk_ref, dv_ref, dq_half, dk_half, dv_half, chance_ref, score_ref = refs[-8:]
     keys = k_ref[...]
     values = v_ref[...]
     queries = q_ref[...]
@@ -151,8 +150,12 @@
                 ).astype(BF16)
             grad_values.append(dot(chance_ref[head, :, first:], grads[first:]))
             grad_keys.append(dot(score_ref[head, slots, first:], queries[first:]))
-        dk_ref[slots, :] = jnp.where(lane_head == 0, grad_keys[0], grad_keys[1]).astype(BF16)
-        dv_ref[slots, :] = jnp.where(lane_head == 0, grad_values[0], grad_values[1]).astype(BF16)
+        grad_key = jnp.where(lane_head == 0, grad_keys[0], grad_keys[1]).astype(BF16)
+        grad_value = jnp.where(lane_head == 0, grad_values[0], grad_values[1]).astype(BF16)
+        dk_ref[slots, :] = grad_key
+        dk_half[slots, :] = grad_key
+        dv_ref[slots, :] = grad_value
+        dv_half[slots, :] = grad_value
     for block in range(row_count // QUERY_ROWS):
         rows = slice(block * QUERY_ROWS, (block + 1) * QUERY_ROWS)
         seen = (block + 1) * QUERY_ROWS if causal else key_count
@@ -164,22 +167,24 @@
             for head in range(2)
         ]
         grad_query = jnp.concatenate(parts, axis=0).T.astype(BF16)
-        dq_ref[rows, :] = (grad_query.astype(F32) * HEAD ** (-0.5)).astype(BF16)
+        grad_query = (grad_query.astype(F32) * HEAD ** (-0.5)).astype(BF16)
+        dq_ref[rows, :] = grad_query
+        dq_half[rows, :] = grad_query
 
 
 def head_pair(row_count, first):
     return pl.BlockSpec((row_count, LANES), lambda pair: (0, first + pair))
 
 
-def attention_forward(queries, keys, values, firsts, bias=None):
+def attention_forward(queries, keys, values, bias=None):
     causal = bias is None
     row_count = queries.shape[0]
     key_count = keys.shape[0]
     pairs = HEADS // 2
     in_specs = [
-        head_pair(row_count, firsts[0]),
-        head_pair(key_count, firsts[1]),
-        head_pair(key_count, firsts[2]),
+        head_pair(row_count, 0),
+        head_pair(key_count, 0),
+        head_pair(key_count, 0),
     ]
     operands = [queries, keys, values]
     if not causal:
@@ -206,49 +211,65 @@
     )(*operands)
 
 
-def attention_backward(queries, keys, values, firsts, grads, outs, log_total, bias=None):
+def attention_backward(half, width, queries, keys, values, grads, outs, log_total, bias, whole):
     causal = bias is None
-    row_count = queries.shape[0]
+    row_count, model = queries.shape
     key_count = keys.shape[0]
-    pairs = HEADS // 2
     key_rows = QUERY_ROWS if causal else LANES
+    per_unit = width // LANES
+    steps = HEADS // 4
+
+    def chosen(step, side):
+        return (2 * (step // per_unit) + side[0]) * per_unit + step % per_unit
+
+    def in_whole(count):
+        return pl.BlockSpec((count, LANES), lambda step, side: (0, chosen(step, side)))
+
+    def alone(count):
+        return pl.BlockSpec((count, LANES), lambda step, side: (0, step))
+
     in_specs = [
-        head_pair(row_count, firsts[0]),
-        head_pair(key_count, firsts[1]),
-        head_pair(key_count, firsts[2]),
-        head_pair(row_count, 0),
-        head_pair(row_count, 0),
-        pl.BlockSpec((1, 8, row_count), lambda pair: (pair, 0, 0)),
+        in_whole(row_count),
+        in_whole(key_count),
+        in_whole(key_count),
+        in_whole(row_count),
+        in_whole(row_count),
+        pl.BlockSpec((1, 8, row_count), lambda step, side: (chosen(step, side), 0, 0)),
     ]
     operands = [queries, keys, values, grads, outs, log_total]
     if not causal:
-        in_specs.append(pl.BlockSpec((key_count, LANES), lambda pair: (0, 0)))
+        in_specs.append(pl.BlockSpec((key_count, LANES), lambda step, side: (0, 0)))
         operands.append(bias)
-    return pl.pallas_call(
+    aliases = {}
+    if whole is not None:
+        for item, array in enumerate(whole):
+            aliases[1 + len(operands)] = item
+            in_specs.append(pl.BlockSpec(memory_space=pl.ANY))
+            operands.append(array)
+    counts = (row_count, key_count, key_count)
+    results = pl.pallas_call(
         functools.partial(attention_backward_kernel, causal=causal),
-        grid=(pairs,),
-        in_specs=in_specs,
-        out_specs=[
-            head_pair(row_count, 0),
-            head_pair(key_count, 0),
-            head_pair(key_count, 0),
-        ],
-        out_shape=[
-            jax.ShapeDtypeStruct((row_count, pairs * LANES), BF16),
-            jax.ShapeDtypeStruct((key_count, pairs * LANES), BF16),
-            jax.ShapeDtypeStruct((key_count, pairs * LANES), BF16),
-        ],
-        scratch_shapes=[
-            pltpu.VMEM((2, key_rows, row_count), BF16),
-            pltpu.VMEM((2, key_count, row_count), BF16),
-        ],
+        grid_spec=pltpu.PrefetchScalarGridSpec(
+            num_scalar_prefetch=1,
+            grid=(steps,),
+            in_specs=in_specs,
+            out_specs=[in_whole(count) for count in counts] + [alone(count) for count in counts],
+            scratch_shapes=[
+                pltpu.VMEM((2, key_rows, row_count), BF16),
+                pltpu.VMEM((2, key_count, row_count), BF16),
+            ],
+        ),
+        out_shape=[jax.ShapeDtypeStruct((count, model), BF16) for count in counts]
+        + [jax.ShapeDtypeStruct((count, model // 2), BF16) for count in counts],
+        input_output_aliases=aliases,
         compiler_params=pltpu.CompilerParams(vmem_limit_bytes=40 << 20),
         cost_estimate=pl.CostEstimate(
-            flops=20 * row_count * key_count * HEADS * HEAD,
-            bytes_accessed=16 << 20,
-            transcendentals=row_count * key_count * HEADS,
-        ),
-    )(*operands)
+            flops=10 * row_count * key_count * HEADS * HEAD,
+            bytes_accessed=12 << 20,
+            transcendentals=row_count * key_count * HEADS // 2,
+        ),
+    )(half, *operands)
+    return results[:3], results[3:]
 
 
 def gelu_parts(values):
@@ -373,100 +394,211 @@
     return result
 
 
-def halve(terms, own_bits, position, device, device_count):
-    bit = own_bits[position]
-    mine = (device // bit) % 2
-    sent = total_of(
-        [lax.dynamic_index_in_dim(term, 1 - mine, position, keepdims=False) for term in terms]
-    ).astype(BF16)
-    got = swap_bit(sent, device_count, bit)
-    kept = [lax.dynamic_index_in_dim(term, mine, position, keepdims=False) for term in terms]
-    return kept + [got], own_bits[:position] + own_bits[position + 1 :]
-
-
-def fold_planes(terms, group, plane_size):
-    near = []
-    for inner in range(plane_size):
-        for plane in range(GROUPS):
-            if (plane ^ group) & 1:
-                near.append((plane * plane_size + inner, (plane ^ 1) * plane_size + inner))
-    got = lax.ppermute(total_of(terms).astype(BF16), AXES, near)
-    terms = terms + [got]
-    other = group ^ 2
-    far = [
-        (other * plane_size + inner, group * plane_size + inner) for inner in range(plane_size)
-    ]
-    got = lax.ppermute(total_of(terms).astype(BF16), AXES, far)
-    return terms + [got]
-
-
-def sum_to_plane(sent, kept, group, device, device_count):
-    plane_size = device_count // GROUPS
-    got = swap_bit(sent, device_count, 1)
+def pinned(*values):
+    return lax.optimization_barrier(values)
+
+
+def begin_sum(kept, got, device_count):
     bits = []
-    bit = plane_size // 2
+    bit = device_count // GROUPS // 2
     while bit > 1:
         bits.append(bit)
         bit //= 2
-    rows = kept.shape[1]
+    rows = kept.shape[1] // 2
     parts = []
     for part in range(2):
-        first = part * (rows // 2)
         terms = [
-            term[:, first : first + rows // 2].reshape((2,) * len(bits) + (rows // 2, -1))
+            term[:, part * rows : (part + 1) * rows].reshape((2,) * len(bits) + (rows, -1))
             for term in (kept, got)
         ]
-        left = list(bits)
-        while left:
-            position = 0 if part == 0 else len(left) - 1
-            terms, left = halve(terms, left, position, device, device_count)
-        parts.append(total_of(fold_planes(terms, group, plane_size)))
-    return jnp.concatenate(parts, axis=0)
+        parts.append((terms, list(bits)))
+    return parts
+
+
+def halve_sends(parts, device):
+    sends = []
+    for part, (terms, bits) in enumerate(parts):
+        position = 0 if part == 0 else len(bits) - 1
+        other = 1 - (device // bits[position]) % 2
+        sends.append(
+            total_of(
+                [lax.dynamic_index_in_dim(term, other, position, keepdims=False) for term in terms]
+            ).astype(BF16)
+        )
+    return sends
+
+
+def halve_swaps(sends, parts, device_count):
+    swapped = []
+    for part, (_, bits) in enumerate(parts):
+        swapped.append(swap_bit(sends[part], device_count, bits[0 if part == 0 else -1]))
+    return swapped
+
+
+def halve_keeps(parts, swapped, device):
+    result = []
+    for part, (terms, bits) in enumerate(parts):
+        position = 0 if part == 0 else len(bits) - 1
+        mine = (device // bits[position]) % 2
+        kept = [lax.dynamic_index_in_dim(term, mine, position, keepdims=False) for term in terms]
+        result.append((kept + [swapped[part]], bits[:position] + bits[position + 1 :]))
+    return result
+
+
+def fold_sends(parts):
+    return [total_of(terms).astype(BF16) for terms, _ in parts]
+
+
+def fold_near(sends, group, plane_size):
+    pairs = []
+    for plane in range(GROUPS):
+        if (plane ^ group) & 1:
+            for inner in range(plane_size):
+                pairs.append((plane * plane_size + inner, (plane ^ 1) * plane_size + inner))
+    return [lax.ppermute(sent, AXES, pairs) for sent in sends]
+
+
+def fold_far(sends, group, plane_size):
+    other = group ^ 2
+    pairs = [
+        (other * plane_size + inner, group * plane_size + inner) for inner in range(plane_size)
+    ]
+    return [lax.ppermute(sent, AXES, pairs) for sent in sends]
+
+
+def fold_keeps(parts, got):
+    return [(terms + [item], bits) for (terms, bits), item in zip(parts, got, strict=True)]
+
+
+def end_sum(parts):
+    return jnp.concatenate([total_of(terms) for terms, _ in parts], axis=0)
 
 
 def column_half(values, half, width):
-    rows = values.shape[0]
+    rows, columns = values.shape
+    if columns == 2 * width:
+        return lax.dynamic_slice_in_dim(values, half * width, width, 1)
     pieces = values.reshape(rows, -1, 2, width)
     return lax.dynamic_index_in_dim(pieces, half, 2, keepdims=False).reshape(rows, -1)
 
 
-def weight_half(pairs, half, width):
+def weight_half(pairs, width):
     terms = []
     for left, right in pairs:
-        product = dot_rows(left, column_half(right, half, width)).astype(BF16)
-        terms.append(jnp.swapaxes(product.reshape(product.shape[0], -1, width), 0, 1))
+        product = dot_rows(left, right).astype(BF16)
+        if product.shape[1] == width:
+            terms.append(product[None])
+        else:
+            terms.append(jnp.swapaxes(product.reshape(product.shape[0], -1, width), 0, 1))
     return jnp.concatenate(terms, axis=0)
 
 
-def rotated_update(grad, weights, moment1, moment2, stats, bases):
-    block_count = stats.shape[0]
-    grads_three = grad.reshape(grad.shape[0], block_count, BLK)
-    turned = jnp.einsum("dnb,nbc->dnc", grads_three, bases, precision=HIGHEST)
-    first_moment = BETA_ONE * moment1.reshape(grads_three.shape) + (1.0 - BETA_ONE) * turned
-    second_moment = (
-        BETA_TWO * moment2.reshape(grads_three.shape) + (1.0 - BETA_TWO) * turned * turned
-    )
-    direction = (
-        first_moment
-        / (1.0 - BETA_ONE**STEP)
-        / (jnp.sqrt(second_moment / (1.0 - BETA_TWO**STEP)) + ADAM_EPS)
-    )
-    returned = jnp.einsum("dnc,nbc->dnb", direction, bases, precision=HIGHEST).reshape(grad.shape)
-    updated = weights - RATE * (returned + DECAY * weights)
-    renewed = BETA_TWO * stats + (1.0 - BETA_TWO) * jnp.einsum(
-        "dnb,dnc->nbc", grads_three, grads_three, precision=HIGHEST
-    )
-    product = jnp.einsum("nbc,ncd->nbd", renewed, bases, precision=HIGHEST)
-    gram_matrix = jnp.einsum("nbc,nbd->ncd", product, product, precision=HIGHEST)
-    factor = jnp.linalg.cholesky(gram_matrix)
-    solved = jax.scipy.linalg.solve_triangular(factor, jnp.swapaxes(product, 1, 2), lower=True)
-    return (
-        first_moment.reshape(grad.shape),
-        second_moment.reshape(grad.shape),
-        updated,
-        renewed,
-        jnp.swapaxes(solved, 1, 2),
-    )
+def dot_high(left, right, dims):
+    return lax.dot_general(
+        left, right, (dims, ((), ())), precision=HIGHEST, preferred_element_type=F32
+    )
+
+
+def update_kernel(
+    grad_ref,
+    weight_ref,
+    average_ref,
+    moment1_ref,
+    moment2_ref,
+    stats_ref,
+    bases_ref,
+    first_ref,
+    second_ref,
+    new_ref,
+    new_average_ref,
+    copy_ref,
+    new_stats_ref,
+    new_bases_ref,
+    square_ref,
+):
+    blocks = stats_ref.shape[0]
+
+    @pl.when(pl.program_id(0) == 0)
+    def _():
+        square_ref[...] = jnp.zeros_like(square_ref)
+
+    for block in range(blocks):
+        columns = slice(block * BLK, (block + 1) * BLK)
+        grad = grad_ref[:, columns]
+        basis = bases_ref[block]
+        turned = dot_high(grad, basis, ((1,), (0,)))
+        first = BETA_ONE * moment1_ref[:, columns] + (1.0 - BETA_ONE) * turned
+        second = BETA_TWO * moment2_ref[:, columns] + (1.0 - BETA_TWO) * turned * turned
+        first_ref[:, columns] = first
+        second_ref[:, columns] = second
+        direction = (
+            first
+            / (1.0 - BETA_ONE**STEP)
+            / (jnp.sqrt(second / (1.0 - BETA_TWO**STEP)) + ADAM_EPS)
+        )
+        returned = dot_high(direction, basis, ((1,), (1,)))
+        weight = weight_ref[:, columns]
+        updated = weight - RATE * (returned + DECAY * weight)
+        new_ref[:, columns] = updated
+        new_average_ref[:, columns] = AVERAGE * average_ref[:, columns] + (1.0 - AVERAGE) * updated
+        copy_ref[:, columns] = updated.astype(BF16)
+        square_ref[block] += dot_high(grad, grad, ((0,), (0,)))
+
+    @pl.when(pl.program_id(0) == pl.num_programs(0) - 1)
+    def _():
+        state = []
+        for block in range(blocks):
+            renewed = BETA_TWO * stats_ref[block] + (1.0 - BETA_TWO) * square_ref[block]
+            new_stats_ref[block] = renewed
+            product = dot_high(renewed, bases_ref[block], ((1,), (0,)))
+            gram = dot_high(product, product, ((0,), (0,)))
+            state.append(jnp.concatenate([gram, product.T], axis=1))
+        row_index = lax.broadcasted_iota(jnp.int32, (PANEL, 2 * BLK), 0)
+        solved = [[] for _ in range(blocks)]
+        for panel in range(BLK // PANEL):
+            tops = [item[:PANEL] for item in state]
+            for row in range(PANEL):
+                lane = panel * PANEL + row
+                for block in range(blocks):
+                    top = tops[block]
+                    pivot = top[row : row + 1, lane : lane + 1]
+                    inverse = lax.rsqrt(pivot)
+                    inverse = inverse * (1.5 - 0.5 * pivot * inverse * inverse)
+                    scaled = top[row : row + 1] * inverse
+                    reduced = top - (top[:, lane : lane + 1] * inverse) * scaled
+                    tops[block] = jnp.where(
+                        row_index == row, scaled, jnp.where(row_index > row, reduced, top)
+                    )
+            for block in range(blocks):
+                solved[block].append(tops[block][:, BLK:])
+                if panel + 1 < BLK // PANEL:
+                    left = tops[block][:, (panel + 1) * PANEL : BLK]
+                    state[block] = state[block][PANEL:] - dot_high(
+                        left, tops[block], ((0,), (0,))
+                    )
+        for block in range(blocks):
+            new_bases_ref[block] = jnp.concatenate(solved[block], axis=0).T
+
+
+def rotated_update(grad, weights, average, moment1, moment2, stats, bases):
+    rows, width = grad.shape
+    big = pl.BlockSpec((QUERY_ROWS, width), lambda step: (step, 0))
+    small = pl.BlockSpec(stats.shape, lambda step: (0, 0, 0))
+    wide = jax.ShapeDtypeStruct(grad.shape, F32)
+    return pl.pallas_call(
+        update_kernel,
+        grid=(rows // QUERY_ROWS,),
+        in_specs=[big] * 5 + [small] * 2,
+        out_specs=[big] * 5 + [small] * 2,
+        out_shape=[wide] * 4
+        + [jax.ShapeDtypeStruct(grad.shape, BF16)]
+        + [jax.ShapeDtypeStruct(stats.shape, F32)] * 2,
+        scratch_shapes=[pltpu.VMEM(stats.shape, F32)],
+        compiler_params=pltpu.CompilerParams(vmem_limit_bytes=40 << 20),
+        cost_estimate=pl.CostEstimate(
+            flops=36 * rows * width * BLK, bytes_accessed=42 * rows * width, transcendentals=0
+        ),
+    )(grad, weights, average, moment1, moment2, stats, bases)
 
 
 def adam_update(grad, values, moment1, moment2):
@@ -517,7 +649,7 @@
     core = device % 2
     quarter = memory.shape[1]
     scale_q = HEAD ** (-0.5)
-    pairs = HEADS // 2
+    plane_size = device_count // GROUPS
 
     memory_padded = jnp.pad(memory, ((0, 0), (0, SLOT_PAD - quarter), (0, 0)))
     memory_here = lax.all_to_all(memory_padded, "mem", split_axis=0, concat_axis=0, tiled=True)
@@ -540,16 +672,14 @@
     queries_self = ((dot(low_one, block_columns(0, 1)) + vector_rows[6]) * scale_q).astype(BF16)
     keys_self = dot(low_one, block_columns(1, 1)).astype(BF16)
     values_self = (dot(low_one, block_columns(2, 1)) + vector_rows[7]).astype(BF16)
-    attended, self_log = attention_forward(queries_self, keys_self, values_self, (0, 0, 0))
+    attended, self_log = attention_forward(queries_self, keys_self, values_self)
     after_self = inputs + dot(attended, block_columns(3, 1)) + vector_rows[8]
     normed_two, pull_two = jax.vjp(normalize, after_self, vector_rows[2], vector_rows[3])
     low_two = normed_two.astype(BF16)
     queries_cross = ((dot(low_two, block_columns(4, 1)) + vector_rows[9]) * scale_q).astype(BF16)
     keys_cross = dot(memory_here, block_columns(5, 1)).astype(BF16)
     values_cross = (dot(memory_here, block_columns(6, 1)) + vector_rows[10]).astype(BF16)
-    merged, cross_log = attention_forward(
-        queries_cross, keys_cross, values_cross, (0, 0, 0), slot_bias
-    )
+    merged, cross_log = attention_forward(queries_cross, keys_cross, values_cross, slot_bias)
     after_cross = after_self + dot(merged, block_columns(7, 1)) + vector_rows[11]
     normed_three, pull_three = jax.vjp(normalize, after_cross, vector_rows[4], vector_rows[5])
     low_three = normed_three.astype(BF16)
@@ -562,11 +692,23 @@
     out_a, back_a, up_sent, down_sent, bias_sent = feed_half(
         away, low_three, grad_low_three, full_weights, bias_up, width
     )
+    up_got = swap_bit(up_sent, device_count, 1)
+    down_got = swap_bit(down_sent, device_count, 1)
+    low_three, up_sent, down_sent = pinned(low_three, up_sent, down_sent)
     out_b, back_b, up_kept, down_kept, bias_kept = feed_half(
         here, low_three, grad_low_three, full_weights, bias_up, width
     )
-    group_two = sum_to_plane(up_sent, up_kept, 2, device, device_count)
-    group_three = sum_to_plane(down_sent, down_kept, 3, device, device_count)
+    out_b, back_b, up_kept, down_kept, up_got, down_got = pinned(
+        out_b, back_b, up_kept, down_kept, up_got, down_got
+    )
+    up_parts = begin_sum(up_kept, up_got, device_count)
+    down_parts = begin_sum(down_kept, down_got, device_count)
+    up_sends = halve_sends(up_parts, device)
+    down_sends = halve_sends(down_parts, device)
+    up_sends, down_sends, back_b = pinned(up_sends, down_sends, back_b)
+    up_swaps = halve_swaps(up_sends, up_parts, device_count)
+    down_swaps = halve_swaps(down_sends, down_parts, device_count)
+
     result = (after_cross + (out_a + out_b) + vector_rows[12]) * live_rows
     mixed = result.astype(BF16)
     bias_even = jnp.where(core == 0, bias_kept, bias_sent)
@@ -577,28 +719,48 @@
     grad_two = grad_result + back_three
     grad_low_two = grad_two.astype(BF16)
     grad_merged = dot_last(grad_low_two, block_columns(7, 1)).astype(BF16)
-    grad_queries_cross, grad_keys_cross, grad_values_cross = attention_backward(
+    cross_operands = (
         queries_cross,
         keys_cross,
         values_cross,
-        (0, 0, 0),
         grad_merged,
         merged,
         cross_log,
         slot_bias,
     )
-    cross_pairs = (
-        (low_two, grad_queries_cross),
-        (memory_here, grad_keys_cross),
-        (memory_here, grad_values_cross),
-        (merged, grad_low_two),
-    )
-    group_one = sum_to_plane(
-        weight_half(cross_pairs, 1 - core, width),
-        weight_half(cross_pairs, core, width),
-        1,
-        device,
-        device_count,
+    cross_whole, (queries_part, keys_part, values_part) = attention_backward(
+        away, width, *cross_operands, None
+    )
+    cross_whole, (queries_own, keys_own, values_own) = attention_backward(
+        here, width, *cross_operands, cross_whole
+    )
+    grad_queries_cross, grad_keys_cross, grad_values_cross = cross_whole
+    cross_sent = weight_half(
+        (
+            (low_two, queries_part),
+            (memory_here, keys_part),
+            (memory_here, values_part),
+            (merged, column_half(grad_low_two, 1 - core, width)),
+        ),
+        width,
+    )
+    up_swaps, down_swaps, cross_sent = pinned(up_swaps, down_swaps, cross_sent)
+    cross_got = swap_bit(cross_sent, device_count, 1)
+    up_parts = halve_keeps(up_parts, up_swaps, device)
+    down_parts = halve_keeps(down_parts, down_swaps, device)
+    up_sends = halve_sends(up_parts, device)
+    down_sends = halve_sends(down_parts, device)
+    up_sends, down_sends, queries_own = pinned(up_sends, down_sends, queries_own)
+    up_swaps = halve_swaps(up_sends, up_parts, device_count)
+    down_swaps = halve_swaps(down_sends, down_parts, device_count)
+    cross_kept = weight_half(
+        (
+            (low_two, queries_own),
+            (memory_here, keys_own),
+            (memory_here, values_own),
+            (merged, column_half(grad_low_two, core, width)),
+        ),
+        width,
     )
     grad_normed_two = dot_last(grad_queries_cross, block_columns(4, 1))
     back_two, gain_two, shift_two = pull_two(grad_normed_two)
@@ -606,28 +768,89 @@
     grad_one = grad_two + back_two
     grad_low_one = grad_one.astype(BF16)
     grad_attended = dot_last(grad_low_one, block_columns(3, 1)).astype(BF16)
-    grad_queries_self, grad_keys_self, grad_values_self = attention_backward(
+    up_swaps, down_swaps, cross_got, cross_kept, grad_attended = pinned(
+        up_swaps, down_swaps, cross_got, cross_kept, grad_attended
+    )
+    up_parts = halve_keeps(up_parts, up_swaps, device)
+    down_parts = halve_keeps(down_parts, down_swaps, device)
+    while up_parts[0][1]:
+        up_sends = halve_sends(up_parts, device)
+        down_sends = halve_sends(down_parts, device)
+        up_swaps = halve_swaps(up_sends, up_parts, device_count)
+        down_swaps = halve_swaps(down_sends, down_parts, device_count)
+        up_parts = halve_keeps(up_parts, up_swaps, device)
+        down_parts = halve_keeps(down_parts, down_swaps, device)
+    cross_parts = begin_sum(cross_kept, cross_got, device_count)
+    up_sends = fold_sends(up_parts)
+    down_sends = fold_sends(down_parts)
+    cross_sends = halve_sends(cross_parts, device)
+    up_sends, down_sends, cross_sends, grad_attended = pinned(
+        up_sends, down_sends, cross_sends, grad_attended
+    )
+    up_swaps = fold_near(up_sends, 2, plane_size)
+    down_swaps = fold_near(down_sends, 3, plane_size)
+    cross_swaps = halve_swaps(cross_sends, cross_parts, device_count)
+    self_operands = (
         queries_self,
         keys_self,
         values_self,
-        (0, 0, 0),
         grad_attended,
         attended,
         self_log,
-    )
-    self_pairs = (
-        (low_one, grad_queries_self),
-        (low_one, grad_keys_self),
-        (low_one, grad_values_self),
-        (attended, grad_low_one),
-    )
-    group_zero = sum_to_plane(
-        weight_half(self_pairs, 1 - core, width),
-        weight_half(self_pairs, core, width),
-        0,
-        device,
-        device_count,
-    )
+        None,
+    )
+    self_whole, (queries_part, keys_part, values_part) = attention_backward(
+        away, width, *self_operands, None
+    )
+    self_sent = weight_half(
+        (
+            (low_one, queries_part),
+            (low_one, keys_part),
+            (low_one, values_part),
+            (attended, column_half(grad_low_one, 1 - core, width)),
+        ),
+        width,
+    )
+    up_swaps, down_swaps, cross_swaps, self_sent = pinned(
+        up_swaps, down_swaps, cross_swaps, self_sent
+    )
+    up_parts = fold_keeps(up_parts, up_swaps)
+    down_parts = fold_keeps(down_parts, down_swaps)
+    cross_parts = halve_keeps(cross_parts, cross_swaps, device)
+    while cross_parts[0][1]:
+        cross_sends = halve_sends(cross_parts, device)
+        cross_swaps = halve_swaps(cross_sends, cross_parts, device_count)
+        cross_parts = halve_keeps(cross_parts, cross_swaps, device)
+    up_sends = fold_sends(up_parts)
+    down_sends = fold_sends(down_parts)
+    up_sends, down_sends, self_sent, self_whole = pinned(
+        up_sends, down_sends, self_sent, self_whole
+    )
+    self_got = swap_bit(self_sent, device_count, 1)
+    up_swaps = fold_far(up_sends, 2, plane_size)
+    down_swaps = fold_far(down_sends, 3, plane_size)
+    self_whole, (queries_own, keys_own, values_own) = attention_backward(
+        here, width, *self_operands, self_whole
+    )
+    grad_queries_self, grad_keys_self, grad_values_self = self_whole
+    self_kept = weight_half(
+        (
+            (low_one, queries_own),
+            (low_one, keys_own),
+            (low_one, values_own),
+            (attended, column_half(grad_low_one, core, width)),
+        ),
+        width,
+    )
+    up_swaps, down_swaps, self_got, self_kept = pinned(up_swaps, down_swaps, self_got, self_kept)
+    group_two = end_sum(fold_keeps(up_parts, up_swaps))
+    group_three = end_sum(fold_keeps(down_parts, down_swaps))
+    self_parts = begin_sum(self_kept, self_got, device_count)
+    self_sends = halve_sends(self_parts, device)
+    cross_sends = fold_sends(cross_parts)
+    self_sends, cross_sends, grad_queries_self = pinned(self_sends, cross_sends, grad_queries_self)
+    self_swaps = halve_swaps(self_sends, self_parts, device_count)
+    cross_swaps = fold_near(cross_sends, 1, plane_size)
     grad_normed_one = (
         dot_last(grad_queries_self, block_columns(0, 1))
         + dot_last(grad_keys_self, block_columns(1, 1))
@@ -635,6 +858,20 @@
     )
     back_one, gain_one, shift_one = pull_one(grad_normed_one)
     input_grad = grad_one + back_one
+    self_swaps, cross_swaps, back_one = pinned(self_swaps, cross_swaps, back_one)
+    self_parts = halve_keeps(self_parts, self_swaps, device)
+    cross_parts = fold_keeps(cross_parts, cross_swaps)
+    cross_sends = fold_sends(cross_parts)
+    cross_swaps = fold_far(cross_sends, 1, plane_size)
+    while self_parts[0][1]:
+        self_sends = halve_sends(self_parts, device)
+        self_swaps = halve_swaps(self_sends, self_parts, device_count)
+        self_parts = halve_keeps(self_parts, self_swaps, device)
+    group_one = end_sum(fold_keeps(cross_parts, cross_swaps))
+    self_swaps = fold_near(fold_sends(self_parts), 0, plane_size)
+    self_parts = fold_keeps(self_parts, self_swaps)
+    self_swaps = fold_far(fold_sends(self_parts), 0, plane_size)
+    group_zero = end_sum(fold_keeps(self_parts, self_swaps))
     memory_back = dot_last(grad_keys_cross, block_columns(5, 1)) + dot_last(
         grad_values_cross, block_columns(6, 1)
     )
@@ -668,16 +905,23 @@
     vector_terms = jnp.concatenate([vector_head, grad_bias_up], axis=0)
     vector_grad = lax.psum_scatter(vector_terms, AXES, scatter_dimension=1, tiled=True)
 
-    plane = device // (device_count // GROUPS)
+    plane = device // plane_size
     weight_grad = jnp.where(
         plane < 2,
         jnp.where(plane == 0, group_zero, group_one),
         jnp.where(plane == 2, group_two, group_three),
     )
-    weight_first, weight_second, new_weights, new_stats, new_bases = rotated_update(
-        weight_grad, weights, weight_moment1, weight_moment2, stats, bases
-    )
-    new_average = AVERAGE * weight_average + (1.0 - AVERAGE) * new_weights
+    (
+        weight_first,
+        weight_second,
+        new_weights,
+        new_average,
+        weights_copy,
+        new_stats,
+        new_bases,
+    ) = rotated_update(
+        weight_grad, weights, weight_average, weight_moment1, weight_moment2, stats, bases
+    )
     vector_first, vector_second, new_vectors = adam_update(
         vector_grad, vectors, vector_moment1, vector_moment2
     )
@@ -691,7 +935,7 @@
         weight_second,
         new_weights,
         new_average,
-        new_weights.astype(BF16),
+        weights_copy,
         new_stats,
         new_bases,
         vector_grad,

time: 1140 us -> 1010 us (0.89)
  local copies, waits for them, and re-layouts: 185 us -> 57 us
  other arithmetic: 199 us -> 94 us
  waiting for transfers between devices: 336 us -> 420 us
  Pallas kernels: 207 us -> 242 us
  matrix products: 115 us -> 100 us
    unnamed x3, waiting for transfers between devices: 4.91 us -> 131 us
    another operation x7 -> x0, other arithmetic: 88.7 us -> none  [the longest x4 48.7 us: rotated_update(): factor = jnp.linalg.cholesky(gram_matrix)]
    ppermute x20, waiting for transfers between devices: 103 us -> 25.8 us  [swap_bit(): lax.ppermute(values, AXES, [(item, item ^ bit) for item in range(device_c...]
    dynamic_slice x12 -> x0, local copies, waits for them, and re-layouts: 42.6 us -> none  [the longest x4 36.1 us: column_half(): lax.dynamic_index_in_dim(pieces, half, 2, keepdims=False).reshape(rows, -1)]
    reshape x9 -> x0, local copies, waits for them, and re-layouts: 31.6 us -> none  [the longest x8 29.8 us: column_half(): pieces = values.reshape(rows, -1, 2, width)]
    pallas_call x0 -> x1, Pallas kernels: none -> 28.7 us  [rotated_update(): pl.pallas_call(update_kernel, grid=(rows // QUERY_ROWS,), in_specs=[big]...]
    unnamed x286 -> x310, local copies, waits for them, and re-layouts: 55.4 us -> 28.6 us
    ppermute x16, waiting for transfers between devices: 19.7 us -> 43.4 us  [the longest x8 22.4 us: fold_far(): return [lax.ppermute(sent, AXES, pairs) for sent in sends]]
  transfers between devices with their start and end apart: 40 -> 40, of which waited for: 15 -> 12; matrix products, arithmetic and copies ran while one was open for 20% -> 17% of each run, Pallas kernels for 3% -> 14%
where the time goes in v2:
time: 1010 us; the launch traced here: 997 us
  waiting for transfers between devices  420 us (42%)
  Pallas kernels  242 us (24%)
  matrix products  100 us (10%)
  other arithmetic  94 us (9%)
  starting transfers between devices  67.2 us (7%)
  local copies, waits for them, and re-layouts  57 us (6%)
  between operations  17.4 us (2%)
    all_gather x1, waiting for transfers between devices, gather_parameters(): full = lax.all_gather(packed, AXES, axis=1, tiled=True)  219 us
    unnamed x3, waiting for transfers between devices  131 us
    pallas_call x2, Pallas kernels, feed_half(): pl.pallas_call(feed_kernel, grid_spec=pltpu.PrefetchScalarGridSpec(num_sc...  73.1 us
    pallas_call x4, Pallas kernels, attention_backward(): pl.pallas_call(functools.partial(attention_backward_kernel, causal=causal...  72.3 us
    pallas_call x2, Pallas kernels, attention_forward(): pl.pallas_call(functools.partial(attention_forward_kernel, causal=causal)...  67.9 us
    dot_general x8, matrix products, dot(): return jnp.dot(left, right, preferred_element_type=F32)  38.3 us
    dot_general x8, matrix products, dot_last(): lax.dot_general(left, right, CONTRACT_LAST, preferred_element_type=F32)  36.2 us
    ppermute x8, starting transfers between devices, fold_near(): return [lax.ppermute(sent, AXES, pairs) for sent in sends]  32.8 us
  transfers between devices with their start and end apart: 40, of which 12 were waited for; matrix products, arithmetic and copies ran while one was open for 17% of the time, Pallas kernels for 14%

profile of v2, /device:TPU:0, one launch (start us, length us, event | category | flops | bytes accessed | tf_op | source)
XLA Modules:
  0.0 997.4 jit_solution(1187179249248880727)
XLA Ops:
  13.0 4.2 all-to-all-start
  22.8 219.3 %all-gather.2.cloned.1.call-done.up_ref.down_ref = bf16[1040,16384]{1,0:T(8,128)(2,1)} async-done(((bf16[1040,512]{1,0:T(8,128)(2,1)}), bf16[1040,16384]{1,0:T(8,128)(2,1)}) %all-gather.2.cloned.1.call-update) | async-done | bytes 34078736 | tf_op jit(solution)/shard_map/all_gather | solution.py:619
  244.4 3.3 slice_reduce_fusion
  255.6 4.7 convolution_convert_fusion.2.refs_1_.refs_2_
  260.3 4.7 add_convert_fusion.2.refs_2_.refs_3_
  265.1 4.7 multiply_convert_fusion.2.refs_0_.refs_1_
  269.8 33.7 %shard_map.286 = (bf16[1024,1024]{1,0:T(8,128)(2,1)S(1)}, f32[8,8,1024]{2,1,0:T(8,128)S(1)}) custom-call(bf16[1024,1024]{1,0:T(8,128)(2,1)S(1)} %multiply_convert_fusion.2.refs_0_.refs_1_, bf16[1024,1024]{1,0:T(8,128)(2,1)S(1)} %convolution_convert_fusion.2.refs_1_.refs_2_, bf16[1024,1024]{1,0:T(8,128)(2,1)S(1)} %add_convert_fusion.2.refs_2_.refs_3_), custom_call_target="tpu_custom_call" | custom-call | flops 17179869184 | bytes 8388608 | tf_op jit(solution)/shard_map/pallas_call | solution.py:193
  303.6 6.9 fusion.141
  312.7 2.9 multiply_reduce_fusion.5
  317.0 4.4 fusion.38.refs_1_.refs_2_
  321.4 3.6 add_convert_fusion.4.refs_2_.refs_3_
  325.0 4.4 multiply_convert_fusion.1.refs_0_.refs_1_
  329.7 34.2 %shard_map.287 = (bf16[1024,1024]{1,0:T(8,128)(2,1)S(1)}, f32[8,8,1024]{2,1,0:T(8,128)S(1)}) custom-call(bf16[1024,1024]{1,0:T(8,128)(2,1)S(1)} %multiply_convert_fusion.1.refs_0_.refs_1_, bf16[640,1024]{1,0:T(8,128)(2,1)S(1)} %fusion.38.refs_1_.refs_2_, bf16[640,1024]{1,0:T(8,128)(2,1)S(1)} %add_convert_fusion.4.refs_2_.refs_3_, ...), custom_call_target="tpu_custom_call" | custom-call | flops 10737418240 | bytes 8388608 | tf_op jit(solution)/shard_map/pallas_call | solution.py:193
  363.9 4.9 fusion.142
  372.8 36.7 %shard_map.288 = (f32[1024,1024]{1,0:T(8,128)}, f32[1024,1024]{1,0:T(8,128)}, bf16[4,1024,512]{2,1,0:T(8,128)(2,1)}, bf16[4,1024,512]{2,1,0:T(8,128)(2,1)}, f32[4,1,512]{2,1,0:T(1,128)}) custom-call(s32[1]{0:T(128)} %bitcast.3.half_ref.refs_0_, bf16[1024,1024]{1,0:T(8,128)(2,1)} %add_convert_fusion.low_ref, bf16[1024,1024]{1,0:T(8,128)(2,1)} %get-tuple-element.286.grad_ref, ...), custom_call_target="tpu_custom_call" | custom-call | flops 25769803776 | bytes 41943040 | tf_op jit(solution)/shard_map/pallas_call | solution.py:342
  410.2 36.4 %shard_map.289 = (f32[1024,1024]{1,0:T(8,128)}, f32[1024,1024]{1,0:T(8,128)}, bf16[4,1024,512]{2,1,0:T(8,128)(2,1)}, bf16[4,1024,512]{2,1,0:T(8,128)(2,1)}, f32[4,1,512]{2,1,0:T(1,128)}) custom-call(s32[1]{0:T(128)} %bitcast.5.half_ref.refs_0_, bf16[1024,1024]{1,0:T(8,128)(2,1)} %add_convert_fusion.low_ref, bf16[1024,1024]{1,0:T(8,128)(2,1)} %get-tuple-element.286.grad_ref, ...), custom_call_target="tpu_custom_call" | custom-call | flops 25769803776 | bytes 41943040 | tf_op jit(solution)/shard_map/pallas_call | solution.py:342
  448.0 3.9 fusion.139
  465.3 4.7 multiply_reduce_fusion
  470.0 3.5 fusion.132
  481.4 4.1 convolution_convert_fusion.1.refs_4_
  485.5 18.1 %shard_map.290 = (bf16[1024,1024]{1,0:T(8,128)(2,1)S(1)}, bf16[640,1024]{1,0:T(8,128)(2,1)S(1)}, bf16[640,1024]{1,0:T(8,128)(2,1)S(1)}, bf16[1024,512]{1,0:T(8,1...) custom-call(s32[1]{0:T(128)} %bitcast.3.half_ref.refs_0_, bf16[1024,1024]{1,0:T(8,128)(2,1)S(1)} %copy-done.37, ...), custom_call_target="tpu_custom_call" | custom-call | flops 6710886400 | bytes 12582912 | tf_op jit(solution)/shard_map/pallas_call | solution.py:250
  510.0 18.3 %shard_map.291 = (bf16[1024,1024]{1,0:T(8,128)(2,1)S(1)}, bf16[640,1024]{1,0:T(8,128)(2,1)S(1)}, bf16[640,1024]{1,0:T(8,128)(2,1)S(1)}, bf16[1024,512]{1,0:T(8,1...) custom-call(s32[1]{0:T(128)} %bitcast.5.half_ref.refs_0_, ...), custom_call_target="tpu_custom_call", output_to_operand_aliasing={{0}: (8, {}), {1}: (9, {}), {2}: (10, {})} | custom-call | flops 6710886400 | bytes 12582912 | tf_op jit(solution)/shard_map/pallas_call | solution.py:250
  528.3 4.0 fusion.17
  532.3 4.2 add_convert_fusion.3
  536.5 4.3 all-to-all-start.1
  540.9 5.8 multiply_reduce_fusion.1
  566.6 5.4 convolution_convert_fusion.refs_4_
  583.6 8.8 collective-permute-done.6
  594.1 8.9 collective-permute-done.8
  619.0 4.6 collective-permute-start.13
  625.5 17.9 %shard_map.292 = (bf16[1024,1024]{1,0:T(8,128)(2,1)S(1)}, bf16[1024,1024]{1,0:T(8,128)(2,1)S(1)}, bf16[1024,1024]{1,0:T(8,128)(2,1)S(1)}, bf16[1024,512]{1,0:T(8...) custom-call(s32[1]{0:T(128)} %bitcast.3.half_ref.refs_0_, ...), custom_call_target="tpu_custom_call" | custom-call | flops 10737418240 | bytes 12582912 | tf_op jit(solution)/shard_map/pallas_call | solution.py:250
  651.7 6.3 collective-permute-done.14
  663.7 3.0 copy.53
  671.8 3.4 collective-permute-start.17
  676.6 17.9 %shard_map.293 = (bf16[1024,1024]{1,0:T(8,128)(2,1)S(1)}, bf16[1024,1024]{1,0:T(8,128)(2,1)S(1)}, bf16[1024,1024]{1,0:T(8,128)(2,1)S(1)}, bf16[1024,512]{1,0:T(8...) custom-call(s32[1]{0:T(128)} %bitcast.5.half_ref.refs_0_, ...), custom_call_target="tpu_custom_call", output_to_operand_aliasing={{0}: (7, {}), {1}: (8, {}), {2}: (9, {})} | custom-call | flops 10737418240 | bytes 12582912 | tf_op jit(solution)/shard_map/pallas_call | solution.py:250
  700.7 4.0 fusion.32
  717.1 4.0 fusion.134
  723.9 20.0 %collective-permute-start.26 = (bf16[512,512]{1,0:T(8,128)(2,1)}, bf16[512,512]{1,0:T(8,128)(2,1)}, u32[]{:S(2)}, u32[]{:S(2)}) collective-permute-start(bf16[512,512]{1,0:T(8,128)(2,1)} %get-tuple-element.221), channel_id=1, source_target_pairs={{0,8},{1,9},{2,10},{3,11},{4,12},{5,13},{6,14},{7,15},{16,24},{17,... | collective-permute-start | bytes 1572872 | tf_op jit(solution)/shard_map/ppermute | solution.py:458
  746.0 4.0 fusion.35
  750.0 4.6 fusion.109
  757.1 3.1 fusion.118
  765.1 131.2 %reduce-scatter.4.cloned.1.call-done = f32[32,17]{1,0:T(8,128)} async-done(((f32[1024,17]{1,0:T(8,128)}), f32[32,17]{1,0:T(8,128)}) %reduce-scatter.4.cloned.1.call-update) | async-done | bytes 2192
  905.0 4.9 collective-permute-done.31
  916.0 10.6 %collective-permute-done.32 = bf16[512,512]{1,0:T(8,128)(2,1)S(1)} collective-permute-done((bf16[512,512]{1,0:T(8,128)(2,1)S(1)}, bf16[512,512]{1,0:T(8,128)(2,1)S(1)}, u32[]{:S(2)}, u32[]{:S(2)}) %collective-permute-start.32) | collective-permute-done | bytes 524320 | tf_op jit(solution)/shard_map/ppermute | solution.py:458
  928.1 4.1 collective-permute-done.29
  935.0 11.4 %collective-permute-done.33 = bf16[512,512]{1,0:T(8,128)(2,1)S(1)} collective-permute-done((bf16[512,512]{1,0:T(8,128)(2,1)S(1)}, bf16[512,512]{1,0:T(8,128)(2,1)S(1)}, u32[]{:S(2)}, u32[]{:S(2)}) %collective-permute-start.33) | collective-permute-done | bytes 524320 | tf_op jit(solution)/shard_map/ppermute | solution.py:466
  946.7 10.9 %collective-permute-done.30 = bf16[512,512]{1,0:T(8,128)(2,1)S(1)} collective-permute-done((bf16[512,512]{1,0:T(8,128)(2,1)S(1)}, bf16[512,512]{1,0:T(8,128)(2,1)S(1)}, u32[]{:S(2)}, u32[]{:S(2)}) %collective-permute-start.30) | collective-permute-done | bytes 524320 | tf_op jit(solution)/shard_map/ppermute | solution.py:466
  961.4 28.7 %shard_map.294 = (f32[1024,512]{1,0:T(8,128)}, f32[1024,512]{1,0:T(8,128)}, f32[1024,512]{1,0:T(8,128)}, f32[1024,512]{1,0:T(8,128)}, bf16[1024,512]{1,0:T(8,128...) custom-call(f32[1024,512]{1,0:T(8,128)S(1)} %fusion.14.grad_ref, f32[1024,512]{1,0:T(8,128)S(1)} %copy-done.2, ...), custom_call_target="tpu_custom_call" | custom-call | flops 2415919104 | bytes 22020096 | tf_op jit(solution)/shard_map/pallas_call | solution.py:588
  (508 shorter events, 181.9 us)
Async XLA Ops:
  7.2 234.8 %all-gather.2.cloned.1.call-start = ((), (), s32[]{:S(2)}) async-start(), calls=%async_computation.3 | async-start | bytes 35143680 | tf_op jit(solution)/shard_map/all_gather | solution.py:619
  13.0 303.9 %all-to-all-start = ((bf16[4,160,1024]{2,1,0:T(8,128)(2,1)}), bf16[4,160,1024]{2,1,0:T(8,128)(2,1)S(1)}, u32[]{:S(2)}, u32[]{:S(2)}) async-start(bf16[4,160,1024]{2,1,0:T(8,128)(2,1)} %pad.13), calls=%async_computation | async-start | bytes 2621440 | tf_op jit(solution)/shard_map/all_to_all | solution.py:655
  19.1 235.0 %copy-start.126 = (f32[1024]{0:T(1024)}, f32[1024]{0:T(1024)S(1)}, u32[]{:S(2)}) copy-start(f32[1024]{0:T(1024)S(1)} %broadcast_multiply_fusion.2) | copy-start | bytes 12292
  20.3 233.7 %copy-start.131 = (f32[1024]{0:T(1024)}, f32[1024]{0:T(1024)S(1)}, u32[]{:S(2)}) copy-start(f32[1024]{0:T(1024)S(1)} %fusion.104) | copy-start | bytes 12292
  363.9 115.2 %copy-start.15 = (bf16[1024,1024]{1,0:T(8,128)(2,1)}, bf16[1024,1024]{1,0:T(8,128)(2,1)S(1)}, u32[]{:S(2)}) copy-start(bf16[1024,1024]{1,0:T(8,128)(2,1)S(1)} %get-tuple-element.130.refs_5_) | copy-start | bytes 6291460
  409.5 38.4 %collective-permute-start = (bf16[4,1024,512]{2,1,0:T(8,128)(2,1)}, bf16[4,1024,512]{2,1,0:T(8,128)(2,1)}, u32[]{:S(2)}, u32[]{:S(2)}) collective-permute-start(bf16[4,1024,512]{2,1,0:T(8,128)(2,1)} %get-tuple-element.132), channel_id=1, source_target_pairs={{0,1},{1,0},{2,3},{3,2},{4,5},{5,4},{6,7},{7,6},{8,9},{9,8},{10,11... | collective-permute-start | bytes 12582920 | tf_op jit(solution)/shard_map/ppermute | solution.py:387
  409.9 38.1 %collective-permute-start.1 = (bf16[4,1024,512]{2,1,0:T(8,128)(2,1)}, bf16[4,1024,512]{2,1,0:T(8,128)(2,1)}, u32[]{:S(2)}, u32[]{:S(2)}) collective-permute-start(bf16[4,1024,512]{2,1,0:T(8,128)(2,1)} %get-tuple-element.133), channel_id=1, source_target_pairs={{0,1},{1,0},{2,3},{3,2},{4,5},{5,4},{6,7},{7,6},{8,9},{9,8},{10,11... | collective-permute-start | bytes 12582920 | tf_op jit(solution)/shard_map/ppermute | solution.py:387
  473.6 78.7 %collective-permute-start.2 = (bf16[2,512,512]{2,1,0:T(8,128)(2,1)}, bf16[2,512,512]{2,1,0:T(8,128)(2,1)}, u32[]{:S(2)}, u32[]{:S(2)}) collective-permute-start(bf16[2,512,512]{2,1,0:T(8,128)(2,1)} %fusion.61), channel_id=1, source_target_pairs={{0,4},{1,5},{2,6},{3,7},{4,0},{5,1},{6,2},{7,3},{8,12},{9,13},{10,... | collective-permute-start | bytes 3145736 | tf_op jit(solution)/shard_map/ppermute | solution.py:387
  475.1 77.2 %collective-permute-start.3 = (bf16[2,512,512]{2,1,0:T(8,128)(2,1)}, bf16[2,512,512]{2,1,0:T(8,128)(2,1)}, u32[]{:S(2)}, u32[]{:S(2)}) collective-permute-start(bf16[2,512,512]{2,1,0:T(8,128)(2,1)} %fusion.62), channel_id=1, source_target_pairs={{0,2},{1,3},{2,0},{3,1},{4,6},{5,7},{6,4},{7,5},{8,10},{9,11},{10,... | collective-permute-start | bytes 3145736 | tf_op jit(solution)/shard_map/ppermute | solution.py:387
  476.4 75.9 %collective-permute-start.4 = (bf16[2,512,512]{2,1,0:T(8,128)(2,1)}, bf16[2,512,512]{2,1,0:T(8,128)(2,1)}, u32[]{:S(2)}, u32[]{:S(2)}) collective-permute-start(bf16[2,512,512]{2,1,0:T(8,128)(2,1)} %fusion.63), channel_id=1, source_target_pairs={{0,4},{1,5},{2,6},{3,7},{4,0},{5,1},{6,2},{7,3},{8,12},{9,13},{10,... | collective-permute-start | bytes 3145736 | tf_op jit(solution)/shard_map/ppermute | solution.py:387
  476.9 75.3 %collective-permute-start.5 = (bf16[2,512,512]{2,1,0:T(8,128)(2,1)}, bf16[2,512,512]{2,1,0:T(8,128)(2,1)}, u32[]{:S(2)}, u32[]{:S(2)}) collective-permute-start(bf16[2,512,512]{2,1,0:T(8,128)(2,1)} %fusion.64), channel_id=1, source_target_pairs={{0,2},{1,3},{2,0},{3,1},{4,6},{5,7},{6,4},{7,5},{8,10},{9,11},{10,... | collective-permute-start | bytes 3145736 | tf_op jit(solution)/shard_map/ppermute | solution.py:387
  536.5 125.4 %all-to-all-start.1 = ((bf16[4,160,1024]{2,1,0:T(8,128)(2,1)}), bf16[4,160,1024]{2,1,0:T(8,128)(2,1)}, u32[]{:S(2)}, u32[]{:S(2)}) async-start(bf16[4,160,1024]{2,1,0:T(8,128)(2,1)} %bitcast.295), calls=%async_computation.1 | async-start | bytes 2621440 | tf_op jit(solution)/shard_map/all_to_all | solution.py:878
  540.8 355.5 %reduce-scatter.4.cloned.1.call-start = ((), (), s32[]{:S(2)}) async-start(), calls=%async_computation.4 | async-start | bytes 540672
  552.3 52.2 %collective-permute-start.10 = (bf16[4,1024,512]{2,1,0:T(8,128)(2,1)S(1)}, bf16[4,1024,512]{2,1,0:T(8,128)(2,1)S(1)}, u32[]{:S(2)}, u32[]{:S(2)}) collective-permute-start(bf16[4,1024,512]{2,1,0:T(8,128)(2,1)S(1)} %pad_maximum_fusion), channel_id=1, source_target_pairs={{0,1},{1,0},{2,3},{3,2},{4,5},{5,4},{6,7},{7,6},{8,9},{9,8},{10,11... | collective-permute-start | bytes 12582920 | tf_op jit(solution)/shard_map/ppermute | solution.py:387
  577.6 14.8 %collective-permute-start.6 = (bf16[512,512]{1,0:T(8,128)(2,1)S(1)}, bf16[512,512]{1,0:T(8,128)(2,1)S(1)}, u32[]{:S(2)}, u32[]{:S(2)}) collective-permute-start(bf16[512,512]{1,0:T(8,128)(2,1)S(1)} %fusion.83), channel_id=1, source_target_pairs={{0,2},{1,3},{2,0},{3,1},{4,6},{5,7},{6,4},{7,5},{8,10},{9,11},{10,... | collective-permute-start | bytes 1572872 | tf_op jit(solution)/shard_map/ppermute | solution.py:387
  579.3 14.8 %collective-permute-start.7 = (bf16[512,512]{1,0:T(8,128)(2,1)S(1)}, bf16[512,512]{1,0:T(8,128)(2,1)S(1)}, u32[]{:S(2)}, u32[]{:S(2)}) collective-permute-start(bf16[512,512]{1,0:T(8,128)(2,1)S(1)} %fusion.82), channel_id=1, source_target_pairs={{0,4},{1,5},{2,6},{3,7},{4,0},{5,1},{6,2},{7,3},{8,12},{9,13},{10,... | collective-permute-start | bytes 1572872 | tf_op jit(solution)/shard_map/ppermute | solution.py:387
  580.8 22.2 %collective-permute-start.8 = (bf16[512,512]{1,0:T(8,128)(2,1)S(1)}, bf16[512,512]{1,0:T(8,128)(2,1)S(1)}, u32[]{:S(2)}, u32[]{:S(2)}) collective-permute-start(bf16[512,512]{1,0:T(8,128)(2,1)S(1)} %fusion.81), channel_id=1, source_target_pairs={{0,2},{1,3},{2,0},{3,1},{4,6},{5,7},{6,4},{7,5},{8,10},{9,11},{10,... | collective-permute-start | bytes 1572872 | tf_op jit(solution)/shard_map/ppermute | solution.py:387
  581.1 23.3 %collective-permute-start.9 = (bf16[512,512]{1,0:T(8,128)(2,1)S(1)}, bf16[512,512]{1,0:T(8,128)(2,1)S(1)}, u32[]{:S(2)}, u32[]{:S(2)}) collective-permute-start(bf16[512,512]{1,0:T(8,128)(2,1)S(1)} %fusion.80), channel_id=1, source_target_pairs={{0,4},{1,5},{2,6},{3,7},{4,0},{5,1},{6,2},{7,3},{8,12},{9,13},{10,... | collective-permute-start | bytes 1572872 | tf_op jit(solution)/shard_map/ppermute | solution.py:387
  616.3 30.5 %collective-permute-start.11 = (bf16[512,512]{1,0:T(8,128)(2,1)S(1)}, bf16[512,512]{1,0:T(8,128)(2,1)S(1)}, u32[]{:S(2)}, u32[]{:S(2)}) collective-permute-start(bf16[512,512]{1,0:T(8,128)(2,1)S(1)} %get-tuple-element.179), channel_id=1, source_target_pairs={{8,0},{9,1},{10,2},{11,3},{12,4},{13,5},{14,6},{15,7},{24,16},{25,... | collective-permute-start | bytes 1572872 | tf_op jit(solution)/shard_map/ppermute | solution.py:458
  617.7 34.0 %collective-permute-start.12 = (bf16[512,512]{1,0:T(8,128)(2,1)}, bf16[512,512]{1,0:T(8,128)(2,1)S(1)}, u32[]{:S(2)}, u32[]{:S(2)}) collective-permute-start(bf16[512,512]{1,0:T(8,128)(2,1)} %get-tuple-element.180), channel_id=1, source_target_pairs={{8,0},{9,1},{10,2},{11,3},{12,4},{13,5},{14,6},{15,7},{24,16},{25,... | collective-permute-start | bytes 1572872 | tf_op jit(solution)/shard_map/ppermute | solution.py:458
  619.0 32.7 %collective-permute-start.13 = (bf16[512,512]{1,0:T(8,128)(2,1)}, bf16[512,512]{1,0:T(8,128)(2,1)S(1)}, u32[]{:S(2)}, u32[]{:S(2)}) collective-permute-start(bf16[512,512]{1,0:T(8,128)(2,1)} %get-tuple-element.181), channel_id=1, source_target_pairs={{0,8},{1,9},{2,10},{3,11},{4,12},{5,13},{6,14},{7,15},{16,24},{17,... | collective-permute-start | bytes 1572872 | tf_op jit(solution)/shard_map/ppermute | solution.py:458
  623.6 34.4 %collective-permute-start.15 = (bf16[2,512,512]{2,1,0:T(8,128)(2,1)S(1)}, bf16[2,512,512]{2,1,0:T(8,128)(2,1)}, u32[]{:S(2)}, u32[]{:S(2)}) collective-permute-start(bf16[2,512,512]{2,1,0:T(8,128)(2,1)S(1)} %fusion.65), channel_id=1, source_target_pairs={{0,4},{1,5},{2,6},{3,7},{4,0},{5,1},{6,2},{7,3},{8,12},{9,13},{10,... | collective-permute-start | bytes 3145736 | tf_op jit(solution)/shard_map/ppermute | solution.py:387
  625.2 32.9 %collective-permute-start.16 = (bf16[2,512,512]{2,1,0:T(8,128)(2,1)S(1)}, bf16[2,512,512]{2,1,0:T(8,128)(2,1)}, u32[]{:S(2)}, u32[]{:S(2)}) collective-permute-start(bf16[2,512,512]{2,1,0:T(8,128)(2,1)S(1)} %fusion.66), channel_id=1, source_target_pairs={{0,2},{1,3},{2,0},{3,1},{4,6},{5,7},{6,4},{7,5},{8,10},{9,11},{10,... | collective-permute-start | bytes 3145736 | tf_op jit(solution)/shard_map/ppermute | solution.py:387
  646.8 11.3 %collective-permute-start.14 = (bf16[512,512]{1,0:T(8,128)(2,1)S(1)}, bf16[512,512]{1,0:T(8,128)(2,1)S(1)}, u32[]{:S(2)}, u32[]{:S(2)}) collective-permute-start(bf16[512,512]{1,0:T(8,128)(2,1)S(1)} %get-tuple-element.182), channel_id=1, source_target_pairs={{0,8},{1,9},{2,10},{3,11},{4,12},{5,13},{6,14},{7,15},{16,24},{17,... | collective-permute-start | bytes 1572872 | tf_op jit(solution)/shard_map/ppermute | solution.py:458
  662.0 50.0 %collective-permute-start.21 = (bf16[4,1024,512]{2,1,0:T(8,128)(2,1)}, bf16[4,1024,512]{2,1,0:T(8,128)(2,1)}, u32[]{:S(2)}, u32[]{:S(2)}) collective-permute-start(bf16[4,1024,512]{2,1,0:T(8,128)(2,1)} %pad_maximum_fusion.2), channel_id=1, source_target_pairs={{0,1},{1,0},{2,3},{3,2},{4,5},{5,4},{6,7},{7,6},{8,9},{9,8},{10,11... | collective-permute-start | bytes 12582920 | tf_op jit(solution)/shard_map/ppermute | solution.py:387
  668.4 36.3 %collective-permute-start.23 = (bf16[512,512]{1,0:T(8,128)(2,1)S(1)}, bf16[512,512]{1,0:T(8,128)(2,1)S(1)}, u32[]{:S(2)}, u32[]{:S(2)}) collective-permute-start(bf16[512,512]{1,0:T(8,128)(2,1)S(1)} %fusion.73), channel_id=1, source_target_pairs={{0,4},{1,5},{2,6},{3,7},{4,0},{5,1},{6,2},{7,3},{8,12},{9,13},{10,... | collective-permute-start | bytes 1572872 | tf_op jit(solution)/shard_map/ppermute | solution.py:387
  670.4 35.1 %collective-permute-start.22 = (bf16[512,512]{1,0:T(8,128)(2,1)S(1)}, bf16[512,512]{1,0:T(8,128)(2,1)S(1)}, u32[]{:S(2)}, u32[]{:S(2)}) collective-permute-start(bf16[512,512]{1,0:T(8,128)(2,1)S(1)} %fusion.75), channel_id=1, source_target_pairs={{0,2},{1,3},{2,0},{3,1},{4,6},{5,7},{6,4},{7,5},{8,10},{9,11},{10,... | collective-permute-start | bytes 1572872 | tf_op jit(solution)/shard_map/ppermute | solution.py:387
  671.8 40.0 %collective-permute-start.17 = (bf16[512,512]{1,0:T(8,128)(2,1)}, bf16[512,512]{1,0:T(8,128)(2,1)S(1)}, u32[]{:S(2)}, u32[]{:S(2)}) collective-permute-start(bf16[512,512]{1,0:T(8,128)(2,1)} %fusion.89), channel_id=1, source_target_pairs={{0,16},{1,17},{2,18},{3,19},{4,20},{5,21},{6,22},{7,23}} | collective-permute-start | bytes 1572872 | tf_op jit(solution)/shard_map/ppermute | solution.py:466
  675.3 36.6 %collective-permute-start.18 = (bf16[512,512]{1,0:T(8,128)(2,1)}, bf16[512,512]{1,0:T(8,128)(2,1)S(1)}, u32[]{:S(2)}, u32[]{:S(2)}) collective-permute-start(bf16[512,512]{1,0:T(8,128)(2,1)} %fusion.90), channel_id=1, source_target_pairs={{0,16},{1,17},{2,18},{3,19},{4,20},{5,21},{6,22},{7,23}} | collective-permute-start | bytes 1572872 | tf_op jit(solution)/shard_map/ppermute | solution.py:466
  704.7 7.1 collective-permute-start.19
  705.5 6.4 collective-permute-start.20
  723.9 175.0 %collective-permute-start.26 = (bf16[512,512]{1,0:T(8,128)(2,1)}, bf16[512,512]{1,0:T(8,128)(2,1)}, u32[]{:S(2)}, u32[]{:S(2)}) collective-permute-start(bf16[512,512]{1,0:T(8,128)(2,1)} %get-tuple-element.221), channel_id=1, source_target_pairs={{0,8},{1,9},{2,10},{3,11},{4,12},{5,13},{6,14},{7,15},{16,24},{17,... | collective-permute-start | bytes 1572872 | tf_op jit(solution)/shard_map/ppermute | solution.py:458
  743.9 155.0 %collective-permute-start.24 = (bf16[2,512,512]{2,1,0:T(8,128)(2,1)}, bf16[2,512,512]{2,1,0:T(8,128)(2,1)}, u32[]{:S(2)}, u32[]{:S(2)}) collective-permute-start(bf16[2,512,512]{2,1,0:T(8,128)(2,1)} %fusion.67), channel_id=1, source_target_pairs={{0,4},{1,5},{2,6},{3,7},{4,0},{5,1},{6,2},{7,3},{8,12},{9,13},{10,... | collective-permute-start | bytes 3145736 | tf_op jit(solution)/shard_map/ppermute | solution.py:387
  745.4 153.6 %collective-permute-start.25 = (bf16[2,512,512]{2,1,0:T(8,128)(2,1)}, bf16[2,512,512]{2,1,0:T(8,128)(2,1)}, u32[]{:S(2)}, u32[]{:S(2)}) collective-permute-start(bf16[2,512,512]{2,1,0:T(8,128)(2,1)} %fusion.68), channel_id=1, source_target_pairs={{0,2},{1,3},{2,0},{3,1},{4,6},{5,7},{6,4},{7,5},{8,10},{9,11},{10,... | collective-permute-start | bytes 3145736 | tf_op jit(solution)/shard_map/ppermute | solution.py:387
  761.2 136.5 %copy-start.134 = (f32[17,32]{1,0:T(8,128)S(1)}, f32[17,32]{1,0:T(8,128)}, u32[]{:S(2)}) copy-start(f32[17,32]{1,0:T(8,128)} %param.26) | copy-start | bytes 6532
  761.2 136.5 %copy-start.146 = (f32[17,32]{1,0:T(8,128)S(1)}, f32[17,32]{1,0:T(8,128)}, u32[]{:S(2)}) copy-start(f32[17,32]{1,0:T(8,128)} %param.29) | copy-start | bytes 6532
  761.2 136.5 %copy-start.147 = (f32[17,32]{1,0:T(8,128)S(1)}, f32[17,32]{1,0:T(8,128)}, u32[]{:S(2)}) copy-start(f32[17,32]{1,0:T(8,128)} %param.28) | copy-start | bytes 6532
  761.2 137.1 %copy-start.145 = (f32[17,32]{1,0:T(8,128)S(1)}, f32[17,32]{1,0:T(8,128)}, u32[]{:S(2)}) copy-start(f32[17,32]{1,0:T(8,128)} %param.27) | copy-start | bytes 6532
  762.2 138.5 %copy-start.56 = (f32[512,512]{1,0:T(8,128)S(1)}, f32[512,512]{1,0:T(8,128)}, u32[]{:S(2)}) copy-start(f32[512,512]{1,0:T(8,128)} %get-tuple-element.299) | copy-start | bytes 3145732
  763.8 135.1 %collective-permute-start.27 = (bf16[512,512]{1,0:T(8,128)(2,1)}, bf16[512,512]{1,0:T(8,128)(2,1)S(1)}, u32[]{:S(2)}, u32[]{:S(2)}) collective-permute-start(bf16[512,512]{1,0:T(8,128)(2,1)} %get-tuple-element.222), channel_id=1, source_target_pairs={{0,8},{1,9},{2,10},{3,11},{4,12},{5,13},{6,14},{7,15},{16,24},{17,... | collective-permute-start | bytes 1572872 | tf_op jit(solution)/shard_map/ppermute | solution.py:458
  900.7 9.2 collective-permute-start.31
  900.9 14.8 %collective-permute-start.35 = (bf16[512,512]{1,0:T(8,128)(2,1)S(1)}, bf16[512,512]{1,0:T(8,128)(2,1)S(1)}, u32[]{:S(2)}, u32[]{:S(2)}) collective-permute-start(bf16[512,512]{1,0:T(8,128)(2,1)S(1)} %fusion.96), channel_id=1, source_target_pairs={{24,8},{25,9},{26,10},{27,11},{28,12},{29,13},{30,14},{31,15}} | collective-permute-start | bytes 1572872 | tf_op jit(solution)/shard_map/ppermute | solution.py:466
  903.0 10.1 %collective-permute-start.28 = (bf16[512,512]{1,0:T(8,128)(2,1)S(1)}, bf16[512,512]{1,0:T(8,128)(2,1)S(1)}, u32[]{:S(2)}, u32[]{:S(2)}) collective-permute-start(bf16[512,512]{1,0:T(8,128)(2,1)S(1)} %fusion.71), channel_id=1, source_target_pairs={{0,2},{1,3},{2,0},{3,1},{4,6},{5,7},{6,4},{7,5},{8,10},{9,11},{10,... | collective-permute-start | bytes 1572872 | tf_op jit(solution)/shard_map/ppermute | solution.py:387
  904.3 29.4 %collective-permute-start.34 = (bf16[512,512]{1,0:T(8,128)(2,1)S(1)}, bf16[512,512]{1,0:T(8,128)(2,1)S(1)}, u32[]{:S(2)}, u32[]{:S(2)}) collective-permute-start(bf16[512,512]{1,0:T(8,128)(2,1)S(1)} %fusion.95), channel_id=1, source_target_pairs={{24,8},{25,9},{26,10},{27,11},{28,12},{29,13},{30,14},{31,15}} | collective-permute-start | bytes 1572872 | tf_op jit(solution)/shard_map/ppermute | solution.py:466
  911.6 15.0 %collective-permute-start.32 = (bf16[512,512]{1,0:T(8,128)(2,1)S(1)}, bf16[512,512]{1,0:T(8,128)(2,1)S(1)}, u32[]{:S(2)}, u32[]{:S(2)}) collective-permute-start(bf16[512,512]{1,0:T(8,128)(2,1)S(1)} %get-tuple-element.294), channel_id=1, source_target_pairs={{8,0},{9,1},{10,2},{11,3},{12,4},{13,5},{14,6},{15,7},{24,16},{25,... | collective-permute-start | bytes 1572872 | tf_op jit(solution)/shard_map/ppermute | solution.py:458
  914.4 17.7 %collective-permute-start.29 = (bf16[512,512]{1,0:T(8,128)(2,1)S(1)}, bf16[512,512]{1,0:T(8,128)(2,1)S(1)}, u32[]{:S(2)}, u32[]{:S(2)}) collective-permute-start(bf16[512,512]{1,0:T(8,128)(2,1)S(1)} %get-tuple-element.292), channel_id=1, source_target_pairs={{8,0},{9,1},{10,2},{11,3},{12,4},{13,5},{14,6},{15,7},{24,16},{25,... | collective-permute-start | bytes 1572872 | tf_op jit(solution)/shard_map/ppermute | solution.py:458
  926.8 19.6 %collective-permute-start.33 = (bf16[512,512]{1,0:T(8,128)(2,1)S(1)}, bf16[512,512]{1,0:T(8,128)(2,1)S(1)}, u32[]{:S(2)}, u32[]{:S(2)}) collective-permute-start(bf16[512,512]{1,0:T(8,128)(2,1)S(1)} %fusion.94), channel_id=1, source_target_pairs={{16,0},{17,1},{18,2},{19,3},{20,4},{21,5},{22,6},{23,7}} | collective-permute-start | bytes 1572872 | tf_op jit(solution)/shard_map/ppermute | solution.py:466
  932.4 25.2 %collective-permute-start.30 = (bf16[512,512]{1,0:T(8,128)(2,1)S(1)}, bf16[512,512]{1,0:T(8,128)(2,1)S(1)}, u32[]{:S(2)}, u32[]{:S(2)}) collective-permute-start(bf16[512,512]{1,0:T(8,128)(2,1)S(1)} %fusion.93), channel_id=1, source_target_pairs={{16,0},{17,1},{18,2},{19,3},{20,4},{21,5},{22,6},{23,7}} | collective-permute-start | bytes 1572872 | tf_op jit(solution)/shard_map/ppermute | solution.py:466
  (144 other events, 1130.3 us)
Sparse Core Ops, SparseCore 0:
  11.5 230.5 all-gather.1
  762.4 133.9 reduce-scatter.3

commit v3 on v2

v3 whole, which is shorter than its diff:
```python
import functools

import jax
import jax.numpy as jnp
from jax import lax
from jax.experimental import pallas as pl
from jax.experimental.pallas import tpu as pltpu
from jax.sharding import PartitionSpec as P

HEADS = 16
HEAD = 64
BLK = 128
STEP = 10
LANES = 128
QUERY_ROWS = 256
FORWARD_ROWS = 512
SLOT_PAD = 160
PANEL = 8
GROUPS = 4
AXES = ("seq", "mem")
SMALL = pl.CostEstimate(flops=1 << 20, bytes_accessed=1 << 16, transcendentals=0)

F32 = jnp.float32
BF16 = jnp.bfloat16
HIGHEST = lax.Precision.HIGHEST
NORM_EPS = 1e-05
ADAM_EPS = 1e-08
BETA_ONE = 0.9
BETA_TWO = 0.95
RATE = 0.04
VECTOR_RATE = 0.4
DECAY = 0.01
AVERAGE = 0.999
MASKED = -1e30
CONTRACT_ROWS = (((0,), (0,)), ((), ()))
CONTRACT_LAST = (((1,), (1,)), ((), ()))


def dot(left, right):
    return jnp.dot(left, right, preferred_element_type=F32)


def dot_last(left, right):
    return lax.dot_general(left, right, CONTRACT_LAST, preferred_element_type=F32)


def dot_rows(left, right):
    return lax.dot_general(left, right, CONTRACT_ROWS, preferred_element_type=F32)


def normalize(values, scale_gain, offset):
    centre = jnp.mean(values, axis=-1, keepdims=True)
    centred = values - centre
    variance = jnp.mean(centred * centred, axis=-1, keepdims=True)
    return centred * lax.rsqrt(variance + NORM_EPS) * scale_gain + offset


def column_total(values):
    return jnp.sum(values.astype(F32), axis=0)


def causal_mask(scores, first_key, first_query):
    key_pos = lax.broadcasted_iota(jnp.int32, scores.shape, 0) + first_key
    query_pos = lax.broadcasted_iota(jnp.int32, scores.shape, 1) + first_query
    return jnp.where(key_pos <= query_pos, scores, MASKED)


def head_of_lane(shape):
    return lax.broadcasted_iota(jnp.int32, shape, 1) // HEAD


def one_head(values, lane_head, head):
    return jnp.where(lane_head == head, values, jnp.zeros_like(values))


def widen(bias, columns):
    return jnp.concatenate([bias] * (columns // LANES), axis=1)


def attention_forward_kernel(*refs, causal):
    if causal:
        q_ref, k_ref, v_ref, out_ref, log_ref = refs
    else:
        q_ref, k_ref, v_ref, bias_ref, out_ref, log_ref = refs
    keys = k_ref[...]
    key_count = keys.shape[0]
    values_turned = v_ref[...].T
    lane_head = head_of_lane(keys.shape)
    key_heads = [one_head(keys, lane_head, head) for head in range(2)]
    units = [
        (block, head) for block in range(q_ref.shape[0] // FORWARD_ROWS) for head in range(2)
    ]

    def scores_of(unit):
        block, head = unit
        seen = (block + 1) * FORWARD_ROWS if causal else key_count
        queries = q_ref[block * FORWARD_ROWS : (block + 1) * FORWARD_ROWS, :]
        scores = dot_last(key_heads[head][:seen], queries)
        if not causal:
            return scores + widen(bias_ref[...], FORWARD_ROWS)
        last = causal_mask(scores[seen - FORWARD_ROWS :], 0, 0)
        if seen == FORWARD_ROWS:
            return last
        return jnp.concatenate([scores[: seen - FORWARD_ROWS], last], axis=0)

    scores = scores_of(units[0])
    outs = []
    for item, (block, head) in enumerate(units):
        later = scores_of(units[item + 1]) if item + 1 < len(units) else None
        rows = slice(block * FORWARD_ROWS, (block + 1) * FORWARD_ROWS)
        largest = jnp.max(scores, axis=0, keepdims=True)
        raised = jnp.exp(scores - largest)
        summed = jnp.sum(raised, axis=0, keepdims=True)
        turned = values_turned[head * HEAD : (head + 1) * HEAD, : scores.shape[0]]
        outs.append(dot(turned, raised.astype(BF16)) / summed)
        log_ref[0, head : head + 1, rows] = largest + jnp.log(summed)
        if head == 1:
            out_ref[rows, :] = jnp.concatenate(outs, axis=0).T.astype(BF16)
            outs = []
        scores = later


def attention_backward_kernel(*refs, causal):
    _, q_ref, k_ref, v_ref, grad_ref, out_ref, log_ref = refs[:7]
    bias_ref = None if causal else refs[7]
    dq_ref, dk_ref, dv_ref, dq_half, dk_half, dv_half, chance_ref, score_ref = refs[-8:]
    keys = k_ref[...]
    values = v_ref[...]
    key_count = keys.shape[0]
    row_count = q_ref.shape[0]
    keys_turned = keys.T
    product = (grad_ref[...].astype(F32) * out_ref[...].astype(F32)).T
    inner = [
        jnp.sum(product[head * HEAD : (head + 1) * HEAD], axis=0, keepdims=True)
        for head in range(2)
    ]
    slots_of = chance_ref.shape[0]
    key_rows = chance_ref.shape[1]
    lane_head = head_of_lane((key_rows, LANES))
    blocks = row_count // QUERY_ROWS
    units = [
        (piece, head, block)
        for piece in range(key_count // key_rows)
        for head in range(2)
        for block in range(piece * key_rows // QUERY_ROWS if causal else 0, blocks)
    ]

    def products_of(unit):
        piece, head, block = unit
        slots = slice(piece * key_rows, (piece + 1) * key_rows)
        rows = slice(block * QUERY_ROWS, (block + 1) * QUERY_ROWS)
        return (
            dot_last(one_head(keys[slots], lane_head, head), q_ref[rows, :]),
            dot_last(one_head(values[slots], lane_head, head), grad_ref[rows, :]),
        )

    even_heads = {}

    def finish(piece, head):
        slots = slice(piece * key_rows, (piece + 1) * key_rows)
        first = piece * key_rows if causal else 0
        kept = chance_ref[(2 * piece + head) % slots_of, :, first:]
        grad_value = dot(kept, grad_ref[first:, :])
        grad_key = dot(score_ref[head, slots, first:], q_ref[first:, :])
        if head == 0:
            even_heads[piece] = (grad_key, grad_value)
            return
        even_key, even_value = even_heads.pop(piece)
        grad_key = jnp.where(lane_head == 0, even_key, grad_key).astype(BF16)
        grad_value = jnp.where(lane_head == 0, even_value, grad_value).astype(BF16)
        dk_ref[slots, :] = grad_key
        dk_half[slots, :] = grad_key
        dv_ref[slots, :] = grad_value
        dv_half[slots, :] = grad_value

    current = products_of(units[0])
    ended = None
    for item, (piece, head, block) in enumerate(units):
        later = products_of(units[item + 1]) if item + 1 < len(units) else None
        if ended is not None:
            finish(*ended)
            ended = None
        scores, grad_chance = current
        slots = slice(piece * key_rows, (piece + 1) * key_rows)
        rows = slice(block * QUERY_ROWS, (block + 1) * QUERY_ROWS)
        if not causal:
            scores = scores + widen(bias_ref[slots, :], QUERY_ROWS)
        elif (piece + 1) * key_rows > block * QUERY_ROWS:
            scores = causal_mask(scores, piece * key_rows, block * QUERY_ROWS)
        chance = jnp.exp(scores - log_ref[0, head : head + 1, rows])
        chance_ref[(2 * piece + head) % slots_of, :, rows] = chance.astype(BF16)
        score_ref[head, slots, rows] = (chance * (grad_chance - inner[head][:, rows])).astype(BF16)
        if block == blocks - 1:
            ended = (piece, head)
        current = later
    finish(*ended)
    for block in range(blocks):
        rows = slice(block * QUERY_ROWS, (block + 1) * QUERY_ROWS)
        seen = (block + 1) * QUERY_ROWS if causal else key_count
        parts = [
            dot(
                keys_turned[head * HEAD : (head + 1) * HEAD, :seen],
                score_ref[head, :seen, rows],
            )
            for head in range(2)
        ]
        grad_query = jnp.concatenate(parts, axis=0).T.astype(BF16)
        grad_query = (grad_query.astype(F32) * HEAD ** (-0.5)).astype(BF16)
        dq_ref[rows, :] = grad_query
        dq_half[rows, :] = grad_query


def head_pair(row_count, first):
    return pl.BlockSpec((row_count, LANES), lambda pair: (0, first + pair))


def attention_forward(queries, keys, values, firsts, bias=None):
    causal = bias is None
    row_count = queries.shape[0]
    key_count = keys.shape[0]
    pairs = HEADS // 2
    in_specs = [
        head_pair(row_count, firsts[0]),
        head_pair(key_count, firsts[1]),
        head_pair(key_count, firsts[2]),
    ]
    operands = [queries, keys, values]
    if not causal:
        in_specs.append(pl.BlockSpec((key_count, LANES), lambda pair: (0, 0)))
        operands.append(bias)
    return pl.pallas_call(
        functools.partial(attention_forward_kernel, causal=causal),
        grid=(pairs,),
        in_specs=in_specs,
        out_specs=[
            head_pair(row_count, 0),
            pl.BlockSpec((1, 8, row_count), lambda pair: (pair, 0, 0)),
        ],
        out_shape=[
            jax.ShapeDtypeStruct((row_count, pairs * LANES), BF16),
            jax.ShapeDtypeStruct((pairs, 8, row_count), F32),
        ],
        compiler_params=pltpu.CompilerParams(vmem_limit_bytes=40 << 20),
        cost_estimate=SMALL,
    )(*operands)


def attention_backward(
    half, width, queries, keys, values, firsts, grads, outs, log_total, bias, whole
):
    causal = bias is None
    row_count, model = grads.shape
    key_count = keys.shape[0]
    key_rows = QUERY_ROWS if causal else key_count // 2
    per_unit = width // LANES
    steps = HEADS // 4

    def chosen(step, side):
        return (2 * (step // per_unit) + side[0]) * per_unit + step % per_unit

    def in_whole(count, first=0):
        return pl.BlockSpec((count, LANES), lambda step, side: (0, first + chosen(step, side)))

    def alone(count):
        return pl.BlockSpec((count, LANES), lambda step, side: (0, step))

    in_specs = [
        in_whole(row_count, firsts[0]),
        in_whole(key_count, firsts[1]),
        in_whole(key_count, firsts[2]),
        in_whole(row_count),
        in_whole(row_count),
        pl.BlockSpec((1, 8, row_count), lambda step, side: (chosen(step, side), 0, 0)),
    ]
    operands = [queries, keys, values, grads, outs, log_total]
    if not causal:
        in_specs.append(pl.BlockSpec((key_count, LANES), lambda step, side: (0, 0)))
        operands.append(bias)
    aliases = {}
    if whole is not None:
        for item, array in enumerate(whole):
            aliases[1 + len(operands)] = item
            in_specs.append(pl.BlockSpec(memory_space=pl.ANY))
            operands.append(array)
    counts = (row_count, key_count, key_count)
    results = pl.pallas_call(
        functools.partial(attention_backward_kernel, causal=causal),
        grid_spec=pltpu.PrefetchScalarGridSpec(
            num_scalar_prefetch=1,
            grid=(steps,),
            in_specs=in_specs,
            out_specs=[in_whole(count) for count in counts] + [alone(count) for count in counts],
            scratch_shapes=[
                pltpu.VMEM((4, key_rows, row_count), BF16),
                pltpu.VMEM((2, key_count, row_count), BF16),
            ],
        ),
        out_shape=[jax.ShapeDtypeStruct((count, model), BF16) for count in counts]
        + [jax.ShapeDtypeStruct((count, model // 2), BF16) for count in counts],
        input_output_aliases=aliases,
        compiler_params=pltpu.CompilerParams(vmem_limit_bytes=40 << 20),
        cost_estimate=SMALL,
    )(half, *operands)
    return results[:3], results[3:]


def gelu_parts(values):
    slope = 0.7978845608028654
    square = values * values
    turned = jnp.tanh(slope * values * (1.0 + 0.044715 * square))
    weight = 0.5 * (1.0 + turned)
    derivative = weight + 0.5 * values * (1.0 - turned * turned) * (
        slope + (3.0 * 0.044715 * slope) * square
    )
    return values * weight, derivative


def feed_kernel(*refs, norm):
    refs = list(refs[1:])
    values_ref = refs.pop(0)
    if norm:
        gain_ref = refs.pop(0)
        shift_ref = refs.pop(0)
    grad_ref, up_ref, down_ref, bias_ref = refs[:4]
    out_ref, back_ref, grad_up_ref, grad_down_ref, grad_bias_ref = refs[4:9]
    low_ref = refs[9] if norm else values_ref
    low_turned, grad_turned, active_ref, hidden_ref = refs[-4:]

    @pl.when(pl.program_id(0) == 0)
    def _():
        if norm:
            for first in range(0, values_ref.shape[0], QUERY_ROWS):
                rows = slice(first, first + QUERY_ROWS)
                low_ref[rows, :] = normalize(
                    values_ref[rows, :], gain_ref[...], shift_ref[...]
                ).astype(BF16)
        low_turned[...] = low_ref[...].T
        grad_turned[...] = grad_ref[...].T
        out_ref[...] = jnp.zeros_like(out_ref)
        back_ref[...] = jnp.zeros_like(back_ref)

    up = up_ref[0]
    down = down_ref[0]
    total = jnp.zeros((1, up.shape[1]), F32)
    pieces = low_ref.shape[0] // QUERY_ROWS
    for piece in range(pieces):
        rows = slice(piece * QUERY_ROWS, (piece + 1) * QUERY_ROWS)
        active, derivative = gelu_parts(dot(low_ref[rows, :], up) + bias_ref[0])
        active_low = active.astype(BF16)
        hidden_low = (derivative * dot(grad_ref[rows, :], down)).astype(BF16)
        active_ref[rows, :] = active_low
        hidden_ref[rows, :] = hidden_low
        total = total + jnp.sum(hidden_low.astype(F32), axis=0, keepdims=True)
        out_ref[rows, :] += dot_last(active_low, down)
        back_ref[rows, :] += dot_last(hidden_low, up)
    grad_bias_ref[0] = total
    for piece in range(low_turned.shape[0] // QUERY_ROWS):
        rows = slice(piece * QUERY_ROWS, (piece + 1) * QUERY_ROWS)
        grad_down_ref[0, rows, :] = dot(grad_turned[rows, :], active_ref[...]).astype(BF16)
        grad_up_ref[0, rows, :] = dot(low_turned[rows, :], hidden_ref[...]).astype(BF16)


def feed_half(place, values, grad, ups, downs, bias, norm=None):
    row_count, model = values.shape
    steps, _, width = ups.shape

    def whole(shape):
        return pl.BlockSpec(shape, lambda step, place: (0, 0), pipeline_mode=pl.Buffered(1))

    total = pl.BlockSpec((row_count, model), lambda step, place: (0, 0))
    chunk = pl.BlockSpec((1, model, width), lambda step, place: (step, 0, 0))
    in_specs = [whole((row_count, model))]
    operands = [values]
    out_specs = [
        total,
        total,
        chunk,
        chunk,
        pl.BlockSpec((1, 1, width), lambda step, place: (step ^ place[1], 0, 0)),
    ]
    out_shape = [
        jax.ShapeDtypeStruct((row_count, model), F32),
        jax.ShapeDtypeStruct((row_count, model), F32),
        jax.ShapeDtypeStruct((steps, model, width), BF16),
        jax.ShapeDtypeStruct((steps, model, width), BF16),
        jax.ShapeDtypeStruct((steps, 1, width), F32),
    ]
    if norm is not None:
        in_specs += [whole((1, model))] * 2
        operands += [norm[0].reshape(1, model), norm[1].reshape(1, model)]
        out_specs.append(total)
        out_shape.append(jax.ShapeDtypeStruct((row_count, model), BF16))
    in_specs += [
        whole((row_count, model)),
        chunk,
        chunk,
        pl.BlockSpec((1, 1, width), lambda step, place: (2 * (step ^ place[1]) + place[0], 0, 0)),
    ]
    operands += [grad, ups, downs, bias.reshape(-1, 1, width)]
    return pl.pallas_call(
        functools.partial(feed_kernel, norm=norm is not None),
        grid_spec=pltpu.PrefetchScalarGridSpec(
            num_scalar_prefetch=1,
            grid=(steps,),
            in_specs=in_specs,
            out_specs=out_specs,
            scratch_shapes=[
                pltpu.VMEM((model, row_count), BF16),
                pltpu.VMEM((model, row_count), BF16),
                pltpu.VMEM((row_count, width), BF16),
                pltpu.VMEM((row_count, width), BF16),
            ],
        ),
        out_shape=out_shape,
        compiler_params=pltpu.CompilerParams(vmem_limit_bytes=58 << 20),
        cost_estimate=SMALL,
    )(place, *operands)


def norm_back_kernel(*refs, count):
    values_ref, gain_ref, stream_ref = refs[:3]
    grad_refs = refs[3 : 3 + count]
    out_ref, low_ref, sums_ref = refs[3 + count :]
    values = values_ref[...].astype(F32)
    grad = grad_refs[0][...]
    for grad_ref in grad_refs[1:]:
        grad = grad + grad_ref[...]
    centred = values - jnp.mean(values, axis=-1, keepdims=True)
    inverse = lax.rsqrt(jnp.mean(centred * centred, axis=-1, keepdims=True) + NORM_EPS)
    normal = centred * inverse
    scaled = grad * gain_ref[...]
    product = scaled * normal
    back = inverse * (
        scaled
        - jnp.mean(scaled, axis=-1, keepdims=True)
        - normal * jnp.mean(product, axis=-1, keepdims=True)
    )
    result = stream_ref[...].astype(F32) + back
    low = result.astype(BF16)
    out_ref[...] = result
    low_ref[...] = low

    @pl.when(pl.program_id(0) == 0)
    def _():
        sums_ref[...] = jnp.zeros_like(sums_ref)

    sums_ref[0:1, :] += jnp.sum(grad * normal, axis=0, keepdims=True)
    sums_ref[1:2, :] += jnp.sum(grad, axis=0, keepdims=True)
    sums_ref[2:3, :] += jnp.sum(low.astype(F32), axis=0, keepdims=True)
    sums_ref[3:4, :] += jnp.sum(stream_ref[...].astype(F32), axis=0, keepdims=True)


def norm_back(values, gain, stream, grads):
    row_count, model = values.shape
    panel = pl.BlockSpec((QUERY_ROWS, model), lambda step: (step, 0))
    return pl.pallas_call(
        functools.partial(norm_back_kernel, count=len(grads)),
        grid=(row_count // QUERY_ROWS,),
        in_specs=[panel, pl.BlockSpec((1, model), lambda step: (0, 0)), panel]
        + [panel] * len(grads),
        out_specs=[panel, panel, pl.BlockSpec((8, model), lambda step: (0, 0))],
        out_shape=[
            jax.ShapeDtypeStruct((row_count, model), F32),
            jax.ShapeDtypeStruct((row_count, model), BF16),
            jax.ShapeDtypeStruct((8, model), F32),
        ],
        compiler_params=pltpu.CompilerParams(vmem_limit_bytes=40 << 20),
        cost_estimate=SMALL,
    )(values, gain.reshape(1, model), stream, *grads)


def project_kernel(*refs, norm, residual):
    refs = list(refs[1:])
    values_ref = refs.pop(0)
    if norm:
        gain_ref = refs.pop(0)
        shift_ref = refs.pop(0)
    here_ref, away_ref, bias_ref, scale_ref = refs[:4]
    refs = refs[4:]
    if residual:
        residual_ref = refs.pop(0)
    out_ref = refs.pop(0)
    source = values_ref
    if norm:
        low_ref = refs.pop(0)
        source = low_ref

        @pl.when((pl.program_id(0) == 0) & (pl.program_id(1) == 0))
        def _():
            for first in range(0, values_ref.shape[0], QUERY_ROWS):
                rows = slice(first, first + QUERY_ROWS)
                low_ref[rows, :] = normalize(
                    values_ref[rows, :].astype(F32), gain_ref[...], shift_ref[...]
                ).astype(BF16)

    def product(columns_ref):
        columns = columns_ref[0]
        row_count = values_ref.shape[0]
        step = min(QUERY_ROWS, row_count // 2)
        for first in range(0, row_count, step):
            rows = slice(first, first + step)
            made = (dot(source[rows, :], columns) + bias_ref[0]) * scale_ref[0]
            if residual:
                made = residual_ref[rows, :].astype(F32) + made
            out_ref[rows, :] = made.astype(out_ref.dtype)

    @pl.when(pl.program_id(1) == 0)
    def _():
        product(here_ref)

    @pl.when(pl.program_id(1) == 1)
    def _():
        product(away_ref)


def project(
    place, values, here, away, block, bias, scale=None, norm=None, residual=None, out_type=BF16
):
    row_count, model = values.shape
    width = here.shape[2]
    parts = model // (2 * width)
    count = bias.shape[0]
    if scale is None:
        scale = jnp.ones_like(bias)

    def whole(shape):
        return pl.BlockSpec(shape, lambda *_: (0, 0), pipeline_mode=pl.Buffered(1))

    def column(step, side, place):
        return 2 * step + (side ^ place[0])

    chunk = pl.BlockSpec(
        (1, model, width),
        lambda step, side, place: ((block * parts + step) ^ place[1], 0, 0),
    )
    line = pl.BlockSpec(
        (1, 1, width), lambda step, side, place: (column(step, side, place), 0, 0)
    )
    panel = pl.BlockSpec(
        (row_count, width), lambda step, side, place: (0, column(step, side, place))
    )
    in_specs = [whole((row_count, model))]
    operands = [values]
    if norm is not None:
        in_specs += [whole((1, model))] * 2
        operands += [norm[0].reshape(1, model), norm[1].reshape(1, model)]
    in_specs += [chunk, chunk, line, line]
    operands += [here, away, bias.reshape(-1, 1, width), scale.reshape(-1, 1, width)]
    if residual is not None:
        in_specs.append(panel)
        operands.append(residual)
    out_specs = [panel]
    out_shape = [jax.ShapeDtypeStruct((row_count, count * model), out_type)]
    if norm is not None:
        out_specs.append(pl.BlockSpec((row_count, model), lambda *_: (0, 0)))
        out_shape.append(jax.ShapeDtypeStruct((row_count, model), BF16))
    results = pl.pallas_call(
        functools.partial(
            project_kernel, norm=norm is not None, residual=residual is not None
        ),
        grid_spec=pltpu.PrefetchScalarGridSpec(
            num_scalar_prefetch=1,
            grid=(count * parts, 2),
            in_specs=in_specs,
            out_specs=out_specs,
        ),
        out_shape=out_shape,
        compiler_params=pltpu.CompilerParams(vmem_limit_bytes=40 << 20),
        cost_estimate=SMALL,
    )(place, *operands)
    return results if norm is not None else results[0]


def project_back_kernel(*refs, parts):
    count = len(refs) - 5
    grad_refs = refs[1 : 1 + count]
    here_ref, away_ref, out_ref, total_ref = refs[1 + count :]
    step = pl.program_id(0)
    side = pl.program_id(1)

    @pl.when((step == 0) & (side == 0))
    def _():
        total_ref[...] = jnp.zeros_like(total_ref)

    for item, grad_ref in enumerate(grad_refs):
        for which, columns_ref in enumerate((here_ref, away_ref)):

            @pl.when((step // parts == item) & (side == which))
            def _(grad_ref=grad_ref, columns_ref=columns_ref):
                columns = columns_ref[0]
                row_count = grad_ref.shape[0]
                size = min(QUERY_ROWS, row_count // 2)
                for first in range(0, row_count, size):
                    rows = slice(first, first + size)
                    total_ref[rows, :] += dot_last(grad_ref[rows, :], columns)

    @pl.when((step == pl.num_programs(0) - 1) & (side == 1))
    def _():
        out_ref[...] = total_ref[...].astype(out_ref.dtype)


def project_back(place, grads, here, away, block, out_type):
    row_count, model = grads[0].shape
    width = here.shape[2]
    parts = model // (2 * width)

    def grad_panel(item):
        def index(step, side, place):
            inside = (step // parts) == item
            column = 2 * (step % parts) + (side ^ place[0])
            return 0, jnp.where(inside, column, 0)

        return pl.BlockSpec((row_count, width), index)

    chunk = pl.BlockSpec(
        (1, model, width),
        lambda step, side, place: ((block * parts + step) ^ place[1], 0, 0),
    )
    return pl.pallas_call(
        functools.partial(project_back_kernel, parts=parts),
        grid_spec=pltpu.PrefetchScalarGridSpec(
            num_scalar_prefetch=1,
            grid=(len(grads) * parts, 2),
            in_specs=[grad_panel(item) for item in range(len(grads))] + [chunk, chunk],
            out_specs=pl.BlockSpec((row_count, model), lambda *_: (0, 0)),
            scratch_shapes=[pltpu.VMEM((row_count, model), F32)],
        ),
        out_shape=jax.ShapeDtypeStruct((row_count, model), out_type),
        compiler_params=pltpu.CompilerParams(vmem_limit_bytes=40 << 20),
        cost_estimate=SMALL,
    )(place, *grads, here, away)


NEAR = ((0, 1), (1, 0), (2, 3), (3, 2))


def pinned(*values):
    return lax.optimization_barrier(values)


def swap_bit(values, device_count, bit):
    return lax.ppermute(values, AXES, [(item, item ^ bit) for item in range(device_count)])


def move_planes(values, moves, plane_size):
    pairs = [
        (source * plane_size + inner, target * plane_size + inner)
        for source, target in moves
        for inner in range(plane_size)
    ]
    return lax.ppermute(values, AXES, pairs)


def inner_bits(device_count):
    bits = []
    bit = device_count // GROUPS // 2
    while bit > 1:
        bits.append(bit)
        bit //= 2
    return bits


def spread_far(own, plane_size, outer):
    return move_planes(own, ((0, 2), (3, 1)) if outer else ((1, 3), (2, 0)), plane_size)


def spread_held(own, got, plane, outer):
    sources = (0, 3) if outer else (1, 2)
    return jnp.where((plane == sources[0]) | (plane == sources[1]), own, got)


def spread_sorted(held, near, plane, outer):
    even = plane % 2 == 0
    low_held = even if outer else ~even
    return jnp.where(low_held, held, near), jnp.where(low_held, near, held)


def spread_begin(own):
    rows = own.shape[-2] // 2
    return [own[..., :rows, :], own[..., rows:, :]]


def spread_swaps(parts, stage, device_count):
    bits = inner_bits(device_count)
    return [
        swap_bit(parts[0], device_count, bits[len(bits) - 1 - stage]),
        swap_bit(parts[1], device_count, bits[stage]),
    ]


def spread_joins(parts, got):
    return [jnp.stack([part, item]) for part, item in zip(parts, got, strict=True)]


def spread_end(parts, device_count):
    levels = len(inner_bits(device_count))
    turned = jnp.transpose(
        parts[1], tuple(reversed(range(levels))) + tuple(range(levels, parts[1].ndim))
    )
    joined = jnp.concatenate([parts[0], turned], axis=-2)
    return joined.reshape((-1,) + joined.shape[levels:])


def total_of(terms):
    result = terms[0].astype(F32)
    for term in terms[1:]:
        result = result + term.astype(F32)
    return result


class Part:
    def __init__(self, members, bits, from_end):
        self.members = members
        self.bits = bits
        self.from_end = from_end

    def position(self):
        return len(self.bits) - 1 if self.from_end else 0


def begin_sum(members, device_count):
    bits = inner_bits(device_count)
    rows = members[0][0].shape[1] // 2
    parts = []
    for part in range(2):
        cut = [
            [
                term[:, part * rows : (part + 1) * rows].reshape((2,) * len(bits) + (rows, -1))
                for term in terms
            ]
            for terms in members
        ]
        parts.append(Part(cut, list(bits), part == 1))
    return parts


def pick(terms, index, position):
    return [lax.dynamic_index_in_dim(term, index, position, keepdims=False) for term in terms]


def own_place(device, bit):
    return 0 if device is None else (device // bit) % 2


def halve_sends(parts, device):
    sends = []
    for part in parts:
        position = part.position()
        other = 1 - own_place(device, part.bits[position])
        sends.append(
            jnp.stack(
                [total_of(pick(terms, other, position)).astype(BF16) for terms in part.members]
            )
        )
    return sends


def halve_swaps(sends, parts, device_count):
    return [
        swap_bit(sent, device_count, part.bits[part.position()])
        for sent, part in zip(sends, parts, strict=True)
    ]


def halve_keeps(parts, got, device):
    result = []
    every, got = pinned([part.members for part in parts], got)
    for part, terms_of, items in zip(parts, every, got, strict=True):
        part = Part(terms_of, part.bits, part.from_end)
        position = part.position()
        mine = own_place(device, part.bits[position])
        members = [
            [total_of(pick(terms, mine, position) + [items[member]])]
            for member, terms in enumerate(part.members)
        ]
        bits = part.bits[:position] + part.bits[position + 1 :]
        result.append(Part(members, bits, part.from_end))
    return result


def finish_halving(parts, device, device_count):
    while parts[0].bits:
        swapped = halve_swaps(halve_sends(parts, device), parts, device_count)
        parts = halve_keeps(parts, swapped, device)
    return parts


def member_total(parts, member=0):
    return jnp.concatenate([total_of(part.members[member]) for part in parts], axis=0)


def column_half(values, half, width):
    rows, columns = values.shape
    if columns == 2 * width:
        return lax.dynamic_slice_in_dim(values, half * width, width, 1)
    pieces = values.reshape(rows, -1, 2, width)
    return lax.dynamic_index_in_dim(pieces, half, 2, keepdims=False).reshape(rows, -1)


def weight_half(pairs, width):
    terms = []
    for left, right in pairs:
        product = dot_rows(left, right).astype(BF16)
        if product.shape[1] == width:
            terms.append(product[None])
        else:
            terms.append(jnp.swapaxes(product.reshape(product.shape[0], -1, width), 0, 1))
    return jnp.concatenate(terms, axis=0)


def dot_high(left, right, dims):
    return lax.dot_general(
        left, right, (dims, ((), ())), precision=HIGHEST, preferred_element_type=F32
    )


def update_kernel(
    grad_ref,
    weight_ref,
    average_ref,
    moment1_ref,
    moment2_ref,
    stats_ref,
    bases_ref,
    first_ref,
    second_ref,
    new_ref,
    new_average_ref,
    copy_ref,
    new_stats_ref,
    new_bases_ref,
    square_ref,
):
    blocks = stats_ref.shape[0]

    @pl.when(pl.program_id(0) == 0)
    def _():
        square_ref[...] = jnp.zeros_like(square_ref)

    for block in range(blocks):
        columns = slice(block * BLK, (block + 1) * BLK)
        grad = grad_ref[:, columns]
        basis = bases_ref[block]
        turned = dot_high(grad, basis, ((1,), (0,)))
        first = BETA_ONE * moment1_ref[:, columns] + (1.0 - BETA_ONE) * turned
        second = BETA_TWO * moment2_ref[:, columns] + (1.0 - BETA_TWO) * turned * turned
        first_ref[:, columns] = first
        second_ref[:, columns] = second
        direction = (
            first
            / (1.0 - BETA_ONE**STEP)
            / (jnp.sqrt(second / (1.0 - BETA_TWO**STEP)) + ADAM_EPS)
        )
        returned = dot_high(direction, basis, ((1,), (1,)))
        weight = weight_ref[:, columns]
        updated = weight - RATE * (returned + DECAY * weight)
        new_ref[:, columns] = updated
        new_average_ref[:, columns] = AVERAGE * average_ref[:, columns] + (1.0 - AVERAGE) * updated
        copy_ref[:, columns] = updated.astype(BF16)
        square_ref[block] += dot_high(grad, grad, ((0,), (0,)))

    @pl.when(pl.program_id(0) == pl.num_programs(0) - 1)
    def _():
        state = []
        for block in range(blocks):
            renewed = BETA_TWO * stats_ref[block] + (1.0 - BETA_TWO) * square_ref[block]
            new_stats_ref[block] = renewed
            product = dot_high(renewed, bases_ref[block], ((1,), (0,)))
            gram = dot_high(product, product, ((0,), (0,)))
            state.append(jnp.concatenate([gram, product.T], axis=1))
        row_index = lax.broadcasted_iota(jnp.int32, (PANEL, 2 * BLK), 0)
        solved = [[] for _ in range(blocks)]
        for panel in range(BLK // PANEL):
            tops = [item[:PANEL] for item in state]
            for row in range(PANEL):
                lane = panel * PANEL + row
                for block in range(blocks):
                    top = tops[block]
                    pivot = top[row : row + 1, lane : lane + 1]
                    inverse = lax.rsqrt(pivot)
                    inverse = inverse * (1.5 - 0.5 * pivot * inverse * inverse)
                    scaled = top[row : row + 1] * inverse
                    reduced = top - (top[:, lane : lane + 1] * inverse) * scaled
                    tops[block] = jnp.where(
                        row_index == row, scaled, jnp.where(row_index > row, reduced, top)
                    )
            for block in range(blocks):
                solved[block].append(tops[block][:, BLK:])
                if panel + 1 < BLK // PANEL:
                    left = tops[block][:, (panel + 1) * PANEL : BLK]
                    state[block] = state[block][PANEL:] - dot_high(
                        left, tops[block], ((0,), (0,))
                    )
        for block in range(blocks):
            new_bases_ref[block] = jnp.concatenate(solved[block], axis=0).T


def rotated_update(grad, weights, average, moment1, moment2, stats, bases):
    rows, width = grad.shape
    big = pl.BlockSpec((QUERY_ROWS, width), lambda step: (step, 0))
    small = pl.BlockSpec(stats.shape, lambda step: (0, 0, 0))
    wide = jax.ShapeDtypeStruct(grad.shape, F32)
    return pl.pallas_call(
        update_kernel,
        grid=(rows // QUERY_ROWS,),
        in_specs=[big] * 5 + [small] * 2,
        out_specs=[big] * 5 + [small] * 2,
        out_shape=[wide] * 4
        + [jax.ShapeDtypeStruct(grad.shape, BF16)]
        + [jax.ShapeDtypeStruct(stats.shape, F32)] * 2,
        scratch_shapes=[pltpu.VMEM(stats.shape, F32)],
        compiler_params=pltpu.CompilerParams(vmem_limit_bytes=40 << 20),
        cost_estimate=SMALL,
    )(grad, weights, average, moment1, moment2, stats, bases)


def adam_update(grad, values, moment1, moment2):
    first_moment = BETA_ONE * moment1 + (1.0 - BETA_ONE) * grad
    second_moment = BETA_TWO * moment2 + (1.0 - BETA_TWO) * grad * grad
    updated = values - VECTOR_RATE * (first_moment / (1.0 - BETA_ONE**STEP)) / (
        jnp.sqrt(second_moment / (1.0 - BETA_TWO**STEP)) + ADAM_EPS
    )
    return (first_moment, second_moment, updated)


def exchange_vectors(pieces, rows, width):
    device_count = pieces.shape[0]
    sublanes = 8 if pieces.dtype == F32 else 16
    room = sublanes * LANES
    size = rows * width
    tiles = -(-size // room)
    padded = jnp.pad(pieces, ((0, 0), (0, tiles * room - size)))
    padded = padded.reshape(device_count, tiles * sublanes, LANES)
    got = lax.all_to_all(padded, AXES, split_axis=0, concat_axis=0, tiled=True)
    return got.reshape(device_count, -1)[:, :size].reshape(device_count, rows, width)


def local(
    tokens,
    memory,
    page_lengths,
    slot_masks,
    upstream,
    weights,
    weight_average,
    weight_moment1,
    weight_moment2,
    stats,
    bases,
    vectors,
    vector_average,
    vector_moment1,
    vector_moment2,
):
    row_count, model = tokens.shape
    width = weights.shape[1]
    group_size = lax.axis_size("mem")
    device_count = lax.axis_size("seq") * group_size
    device = lax.axis_index(AXES)
    member = lax.axis_index("mem")
    core = device % 2
    quarter = memory.shape[1]
    scale_q = HEAD ** (-0.5)
    plane_size = device_count // GROUPS
    plane = device // plane_size
    inner = (device % plane_size) // 2
    levels = len(inner_bits(device_count))
    here = jnp.stack([core, inner]).astype(jnp.int32)
    away = jnp.stack([1 - core, inner]).astype(jnp.int32)

    vector_shape = vectors.shape
    own = weights.astype(BF16)
    outer_far = spread_far(own, plane_size, True)
    pieces = jnp.broadcast_to(
        vectors.astype(BF16).reshape(1, -1), (device_count, vectors.size)
    )
    vector_pieces = exchange_vectors(pieces, *vector_shape)
    memory_padded = jnp.pad(memory, ((0, 0), (0, SLOT_PAD - quarter), (0, 0)))
    memory_here = lax.all_to_all(memory_padded, "mem", split_axis=0, concat_axis=0, tiled=True)
    outer_held = spread_held(own, outer_far, plane, True)
    outer_near = move_planes(outer_held, NEAR, plane_size)
    outer_near, vector_pieces, own = pinned(outer_near, vector_pieces, own)
    self_own, down_own = spread_sorted(outer_held, outer_near, plane, True)
    self_stack = spread_begin(self_own)
    self_swaps = spread_swaps(self_stack, 0, device_count)
    inner_far = spread_far(own, plane_size, False)
    self_swaps, memory_here = pinned(self_swaps, memory_here)
    self_stack = spread_joins(self_stack, self_swaps)
    for stage in range(1, levels):
        self_swaps = spread_swaps(self_stack, stage, device_count)
        if stage < levels - 1:
            self_stack = spread_joins(self_stack, self_swaps)
    inner_held = spread_held(own, inner_far, plane, False)
    inner_held, self_swaps, down_own = pinned(inner_held, self_swaps, down_own)
    inner_near = move_planes(inner_held, NEAR, plane_size)
    down_stack = spread_begin(down_own)
    down_swaps = spread_swaps(down_stack, 0, device_count)
    self_here = spread_end(spread_joins(self_stack, self_swaps), device_count)
    self_away = swap_bit(self_here, device_count, 1)
    inner_near, self_away, down_swaps = pinned(inner_near, self_away, down_swaps)
    down_stack = spread_joins(down_stack, down_swaps)
    cross_own, up_own = spread_sorted(inner_held, inner_near, plane, False)
    cross_stack = spread_begin(cross_own)
    cross_stack, self_away = pinned(cross_stack, self_away)
    cross_swaps = spread_swaps(cross_stack, 0, device_count)
    memory_here = memory_here.reshape(group_size * SLOT_PAD, model)
    vector_rows = jnp.swapaxes(vector_pieces, 0, 1).reshape(vector_shape[0], model).astype(F32)

    live_rows = (jnp.arange(row_count) < page_lengths[0]).astype(F32)[:, None]
    slots_here = lax.dynamic_slice_in_dim(slot_masks, member, 1, 0).reshape(group_size, quarter)
    slots_here = jnp.pad(slots_here, ((0, 0), (0, SLOT_PAD - quarter))).reshape(-1, 1)
    slot_bias = jnp.broadcast_to(
        jnp.where(slots_here > 0, 0.0, MASKED).astype(F32), (group_size * SLOT_PAD, LANES)
    )
    nothing = jnp.zeros((model,), F32)
    ones = jnp.ones((model,), F32)
    scales = jnp.stack([scale_q * ones, ones, ones])
    pairs = HEADS // 2
    self_firsts = (0, pairs, 2 * pairs)
    cross_firsts = (0, 0, pairs)

    self_low, low_one = project(
        here,
        tokens,
        self_here,
        self_away,
        0,
        jnp.stack([vector_rows[6], nothing, vector_rows[7]]),
        scales,
        norm=(vector_rows[0], vector_rows[1]),
    )
    cross_swaps, self_low = pinned(cross_swaps, self_low)
    cross_stack = spread_joins(cross_stack, cross_swaps)
    for stage in range(1, levels):
        cross_swaps = spread_swaps(cross_stack, stage, device_count)
        if stage < levels - 1:
            cross_stack = spread_joins(cross_stack, cross_swaps)
    attended, self_log = attention_forward(self_low, self_low, self_low, self_firsts)
    cross_swaps, attended, up_own = pinned(cross_swaps, attended, up_own)
    cross_here = spread_end(spread_joins(cross_stack, cross_swaps), device_count)
    cross_away = swap_bit(cross_here, device_count, 1)
    for stage in range(1, levels):
        down_swaps = spread_swaps(down_stack, stage, device_count)
        if stage < levels - 1:
            down_stack = spread_joins(down_stack, down_swaps)
    after_self = project(
        here,
        attended,
        self_here,
        self_away,
        3,
        vector_rows[8:9],
        residual=tokens,
        out_type=F32,
    )
    cross_away, after_self = pinned(cross_away, after_self)
    queries_cross, low_two = project(
        here,
        after_self,
        cross_here,
        cross_away,
        0,
        vector_rows[9:10],
        scales[:1],
        norm=(vector_rows[2], vector_rows[3]),
    )
    cross_low = project(
        here,
        memory_here,
        cross_here,
        cross_away,
        1,
        jnp.stack([nothing, vector_rows[10]]),
    )
    down_swaps, queries_cross, cross_low, up_own = pinned(
        down_swaps, queries_cross, cross_low, up_own
    )
    up_stack = spread_begin(up_own)
    up_swaps = spread_swaps(up_stack, 0, device_count)
    down_here = spread_end(spread_joins(down_stack, down_swaps), device_count)
    down_away = swap_bit(down_here, device_count, 1)
    merged, cross_log = attention_forward(
        queries_cross, cross_low, cross_low, cross_firsts, slot_bias
    )
    up_swaps, down_away, merged = pinned(up_swaps, down_away, merged)
    up_stack = spread_joins(up_stack, up_swaps)
    for stage in range(1, levels):
        up_swaps = spread_swaps(up_stack, stage, device_count)
        if stage < levels - 1:
            up_stack = spread_joins(up_stack, up_swaps)
    after_cross = project(
        here,
        merged,
        cross_here,
        cross_away,
        3,
        vector_rows[11:12],
        residual=after_self,
        out_type=F32,
    )
    grad_low_three = (upstream.astype(F32) * live_rows).astype(BF16)
    up_swaps, after_cross, grad_low_three = pinned(up_swaps, after_cross, grad_low_three)
    up_here = spread_end(spread_joins(up_stack, up_swaps), device_count)
    up_away = swap_bit(up_here, device_count, 1)
    bias_up = vector_rows[13:17].reshape(-1)

    out_a, back_a, up_sent, down_sent, bias_sent, low_three = feed_half(
        away,
        after_cross,
        grad_low_three,
        up_away,
        down_away,
        bias_up,
        (vector_rows[4], vector_rows[5]),
    )
    up_got = swap_bit(up_sent, device_count, 1)
    down_got = swap_bit(down_sent, device_count, 1)
    low_three, up_sent, down_sent = pinned(low_three, up_sent, down_sent)
    out_b, back_b, up_kept, down_kept, bias_kept = feed_half(
        here, low_three, grad_low_three, up_here, down_here, bias_up
    )
    up_got, down_got, out_b, back_b, up_kept, down_kept = pinned(
        up_got, down_got, out_b, back_b, up_kept, down_kept
    )
    feed_parts = begin_sum(((up_kept, up_got), (down_kept, down_got)), device_count)
    feed_sends = halve_sends(feed_parts, None)
    feed_sends, back_b = pinned(feed_sends, back_b)
    feed_swaps = halve_swaps(feed_sends, feed_parts, device_count)

    result = (after_cross + (out_a + out_b) + vector_rows[12]) * live_rows
    mixed = result.astype(BF16)
    bias_even = jnp.where(core == 0, bias_kept, bias_sent)
    bias_odd = jnp.where(core == 0, bias_sent, bias_kept)
    grad_bias_up = jnp.concatenate([bias_even, bias_odd], axis=1).reshape(4, model)

    grad_two, grad_low_two, sums_three = norm_back(
        after_cross, vector_rows[4], grad_low_three, (back_a, back_b)
    )
    grad_merged = project_back(here, (grad_low_two,), cross_here, cross_away, 3, BF16)
    cross_operands = (
        queries_cross,
        cross_low,
        cross_low,
        cross_firsts,
        grad_merged,
        merged,
        cross_log,
        slot_bias,
    )
    cross_whole, (queries_part, keys_part, values_part) = attention_backward(
        away, width, *cross_operands, None
    )
    cross_whole, (queries_own, keys_own, values_own) = attention_backward(
        here, width, *cross_operands, cross_whole
    )
    grad_queries_cross, grad_keys_cross, grad_values_cross = cross_whole
    feed_swaps, queries_part, queries_own, grad_queries_cross = pinned(
        feed_swaps, queries_part, queries_own, grad_queries_cross
    )
    feed_parts = halve_keeps(feed_parts, feed_swaps, None)
    feed_sends = halve_sends(feed_parts, None)
    feed_sends, queries_part, queries_own, grad_queries_cross = pinned(
        feed_sends, queries_part, queries_own, grad_queries_cross
    )
    feed_swaps = halve_swaps(feed_sends, feed_parts, device_count)
    cross_sent = weight_half(
        (
            (low_two, queries_part),
            (memory_here, keys_part),
            (memory_here, values_part),
            (merged, column_half(grad_low_two, 1 - core, width)),
        ),
        width,
    )
    cross_sent, queries_own, grad_queries_cross = pinned(
        cross_sent, queries_own, grad_queries_cross
    )
    cross_got = swap_bit(cross_sent, device_count, 1)
    cross_kept = weight_half(
        (
            (low_two, queries_own),
            (memory_here, keys_own),
            (memory_here, values_own),
            (merged, column_half(grad_low_two, core, width)),
        ),
        width,
    )
    grad_normed_two = project_back(here, (grad_queries_cross,), cross_here, cross_away, 0, F32)

    grad_one, grad_low_one, sums_two = norm_back(
        after_self, vector_rows[2], grad_two, (grad_normed_two,)
    )
    grad_attended = project_back(here, (grad_low_one,), self_here, self_away, 3, BF16)
    feed_swaps, cross_got, cross_kept, grad_attended = pinned(
        feed_swaps, cross_got, cross_kept, grad_attended
    )
    feed_parts = finish_halving(
        halve_keeps(feed_parts, feed_swaps, None), None, device_count
    )
    even = plane % 2 == 0
    up_total = member_total(feed_parts, 0)
    down_total = member_total(feed_parts, 1)
    feed_sent = jnp.where(even, down_total, up_total).astype(BF16)
    feed_kept = jnp.where(even, up_total, down_total)
    cross_parts = begin_sum(((cross_kept, cross_got),), device_count)
    cross_sends = halve_sends(cross_parts, device)
    feed_sent, cross_sends, grad_attended = pinned(feed_sent, cross_sends, grad_attended)
    feed_got = move_planes(feed_sent, NEAR, plane_size)
    cross_swaps = halve_swaps(cross_sends, cross_parts, device_count)
    self_operands = (
        self_low,
        self_low,
        self_low,
        self_firsts,
        grad_attended,
        attended,
        self_log,
        None,
    )
    self_whole, (queries_part, keys_part, values_part) = attention_backward(
        away, width, *self_operands, None
    )
    self_sent = weight_half(
        (
            (low_one, queries_part),
            (low_one, keys_part),
            (low_one, values_part),
            (attended, column_half(grad_low_one, 1 - core, width)),
        ),
        width,
    )
    feed_got, cross_swaps, self_sent, self_whole = pinned(
        feed_got, cross_swaps, self_sent, self_whole
    )
    feed_kept = feed_kept + feed_got.astype(F32)
    cross_parts = halve_keeps(cross_parts, cross_swaps, device)
    cross_sends = halve_sends(cross_parts, device)
    feed_sent, cross_sends, self_sent, self_whole = pinned(
        feed_kept.astype(BF16), cross_sends, self_sent, self_whole
    )
    self_got = swap_bit(self_sent, device_count, 1)
    cross_swaps = halve_swaps(cross_sends, cross_parts, device_count)
    feed_got = move_planes(feed_sent, ((0, 2), (1, 3)), plane_size)
    self_whole, (queries_own, keys_own, values_own) = attention_backward(
        here, width, *self_operands, self_whole
    )
    grad_queries_self, grad_keys_self, grad_values_self = self_whole
    self_kept = weight_half(
        (
            (low_one, queries_own),
            (low_one, keys_own),
            (low_one, values_own),
            (attended, column_half(grad_low_one, core, width)),
        ),
        width,
    )
    self_got, cross_swaps, self_kept = pinned(self_got, cross_swaps, self_kept)
    self_parts = begin_sum(((self_kept, self_got),), device_count)
    self_sends = halve_sends(self_parts, device)
    cross_parts = finish_halving(
        halve_keeps(cross_parts, cross_swaps, device), device, device_count
    )
    cross_total = member_total(cross_parts)
    cross_sent = cross_total.astype(BF16)
    self_sends, cross_sent, grad_queries_self = pinned(self_sends, cross_sent, grad_queries_self)
    self_swaps = halve_swaps(self_sends, self_parts, device_count)
    cross_got = move_planes(cross_sent, ((0, 1), (2, 3)), plane_size)
    grad_normed_one = project_back(
        here,
        (grad_queries_self, grad_keys_self, grad_values_self),
        self_here,
        self_away,
        0,
        F32,
    )
    feed_got, self_swaps, cross_got, grad_normed_one = pinned(
        feed_got, self_swaps, cross_got, grad_normed_one
    )
    self_parts = halve_keeps(self_parts, self_swaps, device)
    self_sends = halve_sends(self_parts, device)
    cross_total = cross_total + cross_got.astype(F32)
    cross_sent = cross_total.astype(BF16)
    self_sends, cross_sent, grad_normed_one = pinned(self_sends, cross_sent, grad_normed_one)
    self_swaps = halve_swaps(self_sends, self_parts, device_count)
    cross_got = move_planes(cross_sent, ((3, 1),), plane_size)
    input_grad, _, sums_one = norm_back(tokens, vector_rows[0], grad_one, (grad_normed_one,))
    self_swaps, sums_one = pinned(self_swaps, sums_one)
    self_parts = finish_halving(
        halve_keeps(self_parts, self_swaps, device), device, device_count
    )
    self_total = member_total(self_parts)
    self_sent, grad_keys_cross = pinned(self_total.astype(BF16), grad_keys_cross)
    self_got = move_planes(self_sent, ((1, 0), (3, 2)), plane_size)
    vector_head = jnp.stack(
        [
            sums_one[0],
            sums_one[1],
            sums_two[0],
            sums_two[1],
            sums_three[0],
            sums_three[1],
            column_total(grad_queries_self),
            column_total(grad_values_self),
            sums_two[2],
            column_total(grad_queries_cross),
            column_total(grad_values_cross),
            sums_three[2],
            sums_three[3],
        ],
        axis=0,
    )
    vector_terms = jnp.concatenate([vector_head, grad_bias_up], axis=0)
    vector_terms = jnp.swapaxes(
        vector_terms.reshape(vector_shape[0], device_count, vector_shape[1]), 0, 1
    )
    vector_parts = exchange_vectors(vector_terms.reshape(device_count, -1), *vector_shape)
    vector_grad = jnp.sum(vector_parts, axis=0)

    memory_back = project_back(
        here, (grad_keys_cross, grad_values_cross), cross_here, cross_away, 1, BF16
    )
    memory_back = lax.all_to_all(
        memory_back.reshape(group_size, SLOT_PAD, model),
        "mem",
        split_axis=0,
        concat_axis=0,
        tiled=True,
    )
    memory_back = memory_back[:, :quarter].astype(F32)
    self_got, cross_got, memory_back = pinned(self_got, cross_got, memory_back)
    self_total = self_total + self_got.astype(F32)
    self_got = move_planes(self_total.astype(BF16), ((2, 0),), plane_size)
    group_zero = self_total + self_got.astype(F32)
    group_one = cross_total + cross_got.astype(F32)
    group_feed = feed_kept + feed_got.astype(F32)

    weight_grad = jnp.where(plane < 2, jnp.where(plane == 0, group_zero, group_one), group_feed)
    (
        weight_first,
        weight_second,
        new_weights,
        new_average,
        weights_copy,
        new_stats,
        new_bases,
    ) = rotated_update(
        weight_grad, weights, weight_average, weight_moment1, weight_moment2, stats, bases
    )
    vector_first, vector_second, new_vectors = adam_update(
        vector_grad, vectors, vector_moment1, vector_moment2
    )
    new_vector_average = AVERAGE * vector_average + (1.0 - AVERAGE) * new_vectors
    return (
        mixed,
        input_grad,
        memory_back,
        weight_grad,
        weight_first,
        weight_second,
        new_weights,
        new_average,
        weights_copy,
        new_stats,
        new_bases,
        vector_grad,
        vector_first,
        vector_second,
        new_vectors,
        new_vector_average,
        new_vectors.astype(BF16),
        vector_grad[12],
    )


def solution(mesh):
    return jax.shard_map(
        local,
        mesh=mesh,
        in_specs=(
            P(("seq", "mem"), None),
            P("seq", "mem", None),
            P(("seq", "mem")),
            P("seq", None),
            P(("seq", "mem"), None),
            P(None, ("seq", "mem")),
            P(None, ("seq", "mem")),
            P(None, ("seq", "mem")),
            P(None, ("seq", "mem")),
            P(("seq", "mem"), None, None),
            P(("seq", "mem"), None, None),
            P(None, ("seq", "mem")),
            P(None, ("seq", "mem")),
            P(None, ("seq", "mem")),
            P(None, ("seq", "mem")),
        ),
        out_specs=(
            P(("seq", "mem"), None),
            P(("seq", "mem"), None),
            P("seq", "mem", None),
            P(None, ("seq", "mem")),
            P(None, ("seq", "mem")),
            P(None, ("seq", "mem")),
            P(None, ("seq", "mem")),
            P(None, ("seq", "mem")),
            P(None, ("seq", "mem")),
            P(("seq", "mem"), None, None),
            P(("seq", "mem"), None, None),
            P(None, ("seq", "mem")),
            P(None, ("seq", "mem")),
            P(None, ("seq", "mem")),
            P(None, ("seq", "mem")),
            P(None, ("seq", "mem")),
            P(None, ("seq", "mem")),
            P(("seq", "mem")),
        ),
        check_vma=False,
    )
```

time: 1010 us -> 818 us (0.81)
  waiting for transfers between devices: 420 us -> 195 us
  matrix products: 100 us -> 25.1 us
  Pallas kernels: 242 us -> 306 us
  local copies, waits for them, and re-layouts: 57 us -> 98.2 us
  starting transfers between devices: 67.2 us -> 81.9 us
  between operations: 17.4 us -> 3.99 us
    all_gather x1 -> x0, waiting for transfers between devices: 219 us -> none  [gather_parameters(): full = lax.all_gather(packed, AXES, axis=1, tiled=True)]
    unnamed x3 -> x0, waiting for transfers between devices: 131 us -> none
    pallas_call x2 -> x15, Pallas kernels: 73.1 us -> 168 us  [the longest x2 75.6 us: feed_half(): pl.pallas_call(functools.partial(feed_kernel, norm=norm is not None), gri...]
    dot_general x16 -> x0, matrix products: 74.6 us -> none  [the longest x8 38.3 us: dot(): return jnp.dot(left, right, preferred_element_type=F32)]
    ppermute x20 -> x36, waiting for transfers between devices: 25.8 us -> 79.3 us  [swap_bit(): lax.ppermute(values, AXES, [(item, item ^ bit) for item in range(device_c...]
    all_to_all x1 -> x3, waiting for transfers between devices: 0.01 us -> 49 us  [the longest x2 39.8 us: exchange_vectors(): got = lax.all_to_all(padded, AXES, split_axis=0, concat_axis=0, tiled=True)]
    pallas_call x2, Pallas kernels: 67.9 us -> 37.5 us  [attention_forward(): pl.pallas_call(functools.partial(attention_forward_kernel, causal=causal)...]
    another operation x0 -> x15, other arithmetic: none -> 23.2 us  [the longest x8 17.1 us: spread_joins(): jnp.stack([part, item])]
  transfers between devices with their start and end apart: 40 -> 50, of which waited for: 12 -> 23; matrix products, arithmetic and copies ran while one was open for 17% -> 11% of each run, Pallas kernels for 14% -> 28%
where the time goes in v3:
time: 818 us; the launch traced here: 813 us
  Pallas kernels  306 us (37%)
  waiting for transfers between devices  195 us (24%)
  other arithmetic  103 us (13%)
  local copies, waits for them, and re-layouts  98.2 us (12%)
  starting transfers between devices  81.9 us (10%)
  matrix products  25.1 us (3%)
    ppermute x36, waiting for transfers between devices, swap_bit(): lax.ppermute(values, AXES, [(item, item ^ bit) for item in range(device_c...  79.3 us
    pallas_call x2, Pallas kernels, feed_half(): pl.pallas_call(functools.partial(feed_kernel, norm=norm is not None), gri...  75.6 us
    pallas_call x4, Pallas kernels, attention_backward(): pl.pallas_call(functools.partial(attention_backward_kernel, causal=causal...  71.5 us
    ppermute x10, waiting for transfers between devices, move_planes(): return lax.ppermute(values, AXES, pairs)  56.5 us
    unnamed x368, local copies, waits for them, and re-layouts  51.5 us
    all_to_all x2, waiting for transfers between devices, exchange_vectors(): got = lax.all_to_all(padded, AXES, split_axis=0, concat_axis=0, tiled=True)  39.8 us
    pallas_call x5, Pallas kernels, project(): pl.pallas_call(functools.partial(project_kernel, norm=norm is not None, r...  39.2 us
    pallas_call x2, Pallas kernels, attention_forward(): pl.pallas_call(functools.partial(attention_forward_kernel, causal=causal)...  37.5 us
  transfers between devices with their start and end apart: 50, of which 23 were waited for; matrix products, arithmetic and copies ran while one was open for 11% of the time, Pallas kernels for 28%

profile of v3, /device:TPU:0, one launch (start us, length us, event | category | flops | bytes accessed | tf_op | source)
XLA Modules:
  0.0 812.9 jit_solution(8320732855195189929)
XLA Ops:
  2.6 6.9 collective-permute-start
  9.5 21.4 %collective-permute-done = bf16[1024,512]{1,0:T(8,128)(2,1)} collective-permute-done((bf16[1024,512]{1,0:T(8,128)(2,1)S(1)}, bf16[1024,512]{1,0:T(8,128)(2,1)}, u32[]{:S(2)}, u32[]{:S(2)}) %collective-permute-start) | collective-permute-done | bytes 1048608 | tf_op jit(solution)/shard_map/ppermute | solution.py:651
  31.1 3.8 collective-permute-start.1
  35.7 4.7 all-to-all-start
  43.3 19.7 %all-to-all-done = bf16[32,16,128]{2,1,0:T(8,128)(2,1)S(1)} async-done(((bf16[32,16,128]{2,1,0:T(8,128)(2,1)}), bf16[32,16,128]{2,1,0:T(8,128)(2,1)S(1)}, u32[]{:S(2)}, u32[]{:S(2)}) %all-to-all-start) | async-done | bytes 131104 | tf_op jit(solution)/shard_map/all_to_all | solution.py:934
  74.1 10.1 %all-to-all-done.1 = bf16[4,160,1024]{2,1,0:T(8,128)(2,1)S(1)} async-done(((bf16[4,160,1024]{2,1,0:T(8,128)(2,1)}), bf16[4,160,1024]{2,1,0:T(8,128)(2,1)S(1)}, u32[]{:S(2)}, u32[]{:S(2)}) %all-to-all-start.1) | async-done | bytes 1310752 | tf_op jit(solution)/shard_map/all_to_all | solution.py:979
  84.8 10.3 %collective-permute-done.3 = bf16[512,512]{1,0:T(8,128)(2,1)} collective-permute-done((bf16[512,512]{1,0:T(8,128)(2,1)}, bf16[512,512]{1,0:T(8,128)(2,1)}, u32[]{:S(2)}, u32[]{:S(2)}) %collective-permute-start.3) | collective-permute-done | bytes 524320 | tf_op jit(solution)/shard_map/ppermute | solution.py:642
  102.7 20.0 %collective-permute-done.5 = bf16[2,512,512]{2,1,0:T(8,128)(2,1)} collective-permute-done((bf16[2,512,512]{2,1,0:T(8,128)(2,1)}, bf16[2,512,512]{2,1,0:T(8,128)(2,1)}, u32[]{:S(2)}, u32[]{:S(2)}) %collective-permute-start.5) | collective-permute-done | bytes 1048608 | tf_op jit(solution)/shard_map/ppermute | solution.py:642
  135.1 12.1 %collective-permute-done.10 = bf16[512,512]{1,0:T(8,128)(2,1)S(1)} collective-permute-done((bf16[512,512]{1,0:T(8,128)(2,1)}, bf16[512,512]{1,0:T(8,128)(2,1)S(1)}, u32[]{:S(2)}, u32[]{:S(2)}) %collective-permute-start.10) | collective-permute-done | bytes 524320 | tf_op jit(solution)/shard_map/ppermute | solution.py:642
  148.4 8.1 %collective-permute-done.7 = bf16[1024,512]{1,0:T(8,128)(2,1)S(1)} collective-permute-done((bf16[1024,512]{1,0:T(8,128)(2,1)S(1)}, bf16[1024,512]{1,0:T(8,128)(2,1)S(1)}, u32[]{:S(2)}, u32[]{:S(2)}) %collective-permute-start.7) | collective-permute-done | bytes 1048608 | tf_op jit(solution)/shard_map/ppermute | solution.py:651
  164.5 13.9 %shard_map.286 = (bf16[1024,3072]{1,0:T(8,128)(2,1)}, bf16[1024,1024]{1,0:T(8,128)(2,1)S(1)}) custom-call(s32[2]{0:T(128)S(1)} %pad_add_fusion.refs_0_, bf16[1024,1024]{1,0:T(8,128)(2,1)S(1)} %copy-done.12, f32[1,1024]{1,0:T(1,128)S(1)} %slice.255.refs_2_.refs_1_, f32[1,1024]{1,0:T(1,128)S(1)} %slice.257.refs_3_, ...), custom_call_target="tpu_custom_call" | custom-call | flops 1048576 | bytes 65536 | tf_op jit(solution)/shard_map/pallas_call | solution.py:557
  184.4 18.4 %shard_map.287 = (bf16[1024,1024]{1,0:T(8,128)(2,1)S(1)}, f32[8,8,1024]{2,1,0:T(8,128)S(1)}) custom-call(bf16[1024,3072]{1,0:T(8,128)(2,1)S(1)} %copy-done.2, bf16[1024,3072]{1,0:T(8,128)(2,1)S(1)} %copy-done.2, bf16[1024,3072]{1,0:T(8,128)(2,1)S(1)} %copy-done.2), custom_call_target="tpu_custom_call" | custom-call | flops 1048576 | bytes 65536 | tf_op jit(solution)/shard_map/pallas_call | solution.py:231
  217.6 5.2 shard_map.288.refs_1_.refs_6_.refs_0_
  222.8 7.4 shard_map.290.refs_1_.refs_2_.refs_3_
  230.3 6.9 shard_map.289
  250.6 19.1 %shard_map.291 = (bf16[1024,1024]{1,0:T(8,128)(2,1)S(1)}, f32[8,8,1024]{2,1,0:T(8,128)S(1)}) custom-call(bf16[1024,1024]{1,0:T(8,128)(2,1)S(1)} %copy-done.24, bf16[640,2048]{1,0:T(8,128)(2,1)S(1)} %shard_map.290.refs_1_.refs_2_.refs_3_, bf16[640,2048]{1,0:T(8,128)(2,1)S(1)} %shard_map.290.refs_1_.refs_2_.refs_3_, ...), custom_call_target="tpu_custom_call" | custom-call | flops 1048576 | bytes 65536 | tf_op jit(solution)/shard_map/pallas_call | solution.py:231
  279.6 5.7 shard_map.292.refs_1_.refs_0_
  285.4 12.6 %collective-permute-done.21 = bf16[2,512,512]{2,1,0:T(8,128)(2,1)} collective-permute-done((bf16[2,512,512]{2,1,0:T(8,128)(2,1)}, bf16[2,512,512]{2,1,0:T(8,128)(2,1)}, u32[]{:S(2)}, u32[]{:S(2)}) %collective-permute-start.21) | collective-permute-done | bytes 1048608 | tf_op jit(solution)/shard_map/ppermute | solution.py:642
  310.2 3.8 collective-permute-done.23.refs_5_
  314.1 38.5 %shard_map.293 = (f32[1024,1024]{1,0:T(8,128)}, f32[1024,1024]{1,0:T(8,128)}, bf16[4,1024,512]{2,1,0:T(8,128)(2,1)}, bf16[4,1024,512]{2,1,0:T(8,128)(2,1)}, f32[...) custom-call(s32[2]{0:T(128)} %pad_add_fusion.1.refs_0_, f32[1024,1024]{1,0:T(8,128)} %copy-done.6, ...), custom_call_target="tpu_custom_call" | custom-call | flops 1048576 | bytes 65536 | tf_op jit(solution)/shard_map/pallas_call | solution.py:400
  353.1 37.1 %shard_map.294 = (f32[1024,1024]{1,0:T(8,128)}, f32[1024,1024]{1,0:T(8,128)}, bf16[4,1024,512]{2,1,0:T(8,128)(2,1)}, bf16[4,1024,512]{2,1,0:T(8,128)(2,1)}, f32[4,1,512]{2,1,0:T(1,128)}) custom-call(s32[2]{0:T(128)} %copy-done.59, bf16[1024,1024]{1,0:T(8,128)(2,1)} %get-tuple-element.269.refs_1_, bf16[1024,1024]{1,0:T(8,128)(2,1)} %multiply_convert_fusion.1.refs_4_.refs_2_, ...), custom_call_target="tpu_custom_call" | custom-call | flops 1048576 | bytes 65536 | tf_op jit(solution)/shard_map/pallas_call | solution.py:400
  390.2 5.3 fusion.57
  411.1 6.6 shard_map.295
  419.7 6.0 shard_map.296.refs_4_
  425.7 17.8 %shard_map.297 = (bf16[1024,1024]{1,0:T(8,128)(2,1)S(1)}, bf16[640,1024]{1,0:T(8,128)(2,1)S(1)}, bf16[640,1024]{1,0:T(8,128)(2,1)S(1)}, bf16[1024,512]{1,0:T(8,1...) custom-call(s32[2]{0:T(128)S(1)} %copy-done.65, bf16[1024,1024]{1,0:T(8,128)(2,1)S(1)} %copy-done.25, ...), custom_call_target="tpu_custom_call" | custom-call | flops 1048576 | bytes 65536 | tf_op jit(solution)/shard_map/pallas_call | solution.py:286
  443.5 18.2 %shard_map.298 = (bf16[1024,1024]{1,0:T(8,128)(2,1)S(1)}, bf16[640,1024]{1,0:T(8,128)(2,1)S(1)}, bf16[640,1024]{1,0:T(8,128)(2,1)S(1)}, bf16[1024,512]{1,0:T(8,1...) custom-call(s32[2]{0:T(128)S(1)} %copy-done.60, ...), custom_call_target="tpu_custom_call", output_to_operand_aliasing={{0}: (8, {}), {1}: (9, {}), {2}: (10, {})} | custom-call | flops 1048576 | bytes 65536 | tf_op jit(solution)/shard_map/pallas_call | solution.py:286
  493.8 5.1 shard_map.299.refs_3_
  501.0 6.4 shard_map.300
  509.4 5.0 shard_map.301.refs_4_
  520.9 4.0 fusion.56
  537.2 18.0 %shard_map.302 = (bf16[1024,1024]{1,0:T(8,128)(2,1)S(1)}, bf16[1024,1024]{1,0:T(8,128)(2,1)S(1)}, bf16[1024,1024]{1,0:T(8,128)(2,1)S(1)}, bf16[1024,512]{1,0:T(8...) custom-call(s32[2]{0:T(128)S(1)} %copy-done.65, ...), custom_call_target="tpu_custom_call" | custom-call | flops 1048576 | bytes 65536 | tf_op jit(solution)/shard_map/pallas_call | solution.py:286
  575.5 17.5 %shard_map.303 = (bf16[1024,1024]{1,0:T(8,128)(2,1)S(1)}, bf16[1024,1024]{1,0:T(8,128)(2,1)S(1)}, bf16[1024,1024]{1,0:T(8,128)(2,1)S(1)}, bf16[1024,512]{1,0:T(8...) custom-call(s32[2]{0:T(128)S(1)} %copy-done.60, ...), custom_call_target="tpu_custom_call", output_to_operand_aliasing={{0}: (7, {}), {1}: (8, {}), {2}: (9, {})} | custom-call | flops 1048576 | bytes 65536 | tf_op jit(solution)/shard_map/pallas_call | solution.py:286
  597.6 4.4 collective-permute-start.37
  602.9 4.0 fusion.53
  620.3 11.4 %shard_map.304.refs_3_ = f32[1024,1024]{1,0:T(8,128)S(1)} custom-call(s32[2]{0:T(128)S(1)} %copy-done.60, bf16[1024,1024]{1,0:T(8,128)(2,1)S(1)} %get-tuple-element.381.refs_1_, bf16[1024,1024]{1,0:T(8,128)(2,1)S(1)} %copy-done.35, bf16[1024,1024]{1,0:T(8,128)(2,1)S(1)} %copy-done.29, bf16[4,1024,512]{2,1,0:T(8,128)(2,1)} %bitcast.12.refs_4_.refs_2_, ...), custom_call_target="tpu_custom_call" | custom-call | flops 1048576 | bytes 65536 | tf_op jit(solution)/shard_map/pallas_call | solution.py:619
  631.8 5.1 collective-permute-done.38
  637.6 8.8 %collective-permute-done.40 = bf16[1024,512]{1,0:T(8,128)(2,1)} collective-permute-done((bf16[1024,512]{1,0:T(8,128)(2,1)}, bf16[1024,512]{1,0:T(8,128)(2,1)}, u32[]{:S(2)}, u32[]{:S(2)}) %collective-permute-start.40) | collective-permute-done | bytes 1048608 | tf_op jit(solution)/shard_map/ppermute | solution.py:651
  665.1 5.5 shard_map.305
  676.0 7.3 shard_map.306
  684.3 4.4 all-to-all-start.2
  696.9 9.2 %all-to-all-done.2 = bf16[4,160,1024]{2,1,0:T(8,128)(2,1)} async-done(((bf16[4,160,1024]{2,1,0:T(8,128)(2,1)}), bf16[4,160,1024]{2,1,0:T(8,128)(2,1)}, u32[]{:S(2)}, u32[]{:S(2)}) %all-to-all-start.2) | async-done | bytes 1310752 | tf_op jit(solution)/shard_map/all_to_all | solution.py:1322
  706.1 15.5 %all-to-all-start.3 = ((f32[32,8,128]{2,1,0:T(8,128)}), f32[32,8,128]{2,1,0:T(8,128)S(1)}, u32[]{:S(2)}, u32[]{:S(2)}) async-start(f32[32,8,128]{2,1,0:T(8,128)} %bitcast.136), calls=%async_computation.3 | async-start | bytes 262144 | tf_op jit(solution)/shard_map/all_to_all | solution.py:934
  728.8 5.7 multiply_convert_fusion
  734.6 20.2 %all-to-all-done.3 = f32[32,8,128]{2,1,0:T(8,128)S(1)} async-done(((f32[32,8,128]{2,1,0:T(8,128)}), f32[32,8,128]{2,1,0:T(8,128)S(1)}, u32[]{:S(2)}, u32[]{:S(2)}) %all-to-all-start.3) | async-done | bytes 131104 | tf_op jit(solution)/shard_map/all_to_all | solution.py:934
  756.7 4.8 copy.110
  761.5 18.1 %collective-permute-done.45 = bf16[1024,512]{1,0:T(8,128)(2,1)} collective-permute-done((bf16[1024,512]{1,0:T(8,128)(2,1)}, bf16[1024,512]{1,0:T(8,128)(2,1)}, u32[]{:S(2)}, u32[]{:S(2)}) %collective-permute-start.45) | collective-permute-done | bytes 1048608 | tf_op jit(solution)/shard_map/ppermute | solution.py:651
  779.7 4.1 add_select_fusion.grad_ref
  783.9 28.7 %shard_map.307 = (f32[1024,512]{1,0:T(8,128)}, f32[1024,512]{1,0:T(8,128)}, f32[1024,512]{1,0:T(8,128)}, f32[1024,512]{1,0:T(8,128)}, bf16[1024,512]{1,0:T(8,128...) custom-call(f32[1024,512]{1,0:T(8,128)S(1)} %add_select_fusion.grad_ref, f32[1024,512]{1,0:T(8,128)S(1)} %copy-done.22, ...), custom_call_target="tpu_custom_call" | custom-call | flops 1048576 | bytes 65536 | tf_op jit(solution)/shard_map/pallas_call | solution.py:903
  (611 shorter events, 255.9 us)
Async XLA Ops:
  2.6 28.3 %collective-permute-start = (bf16[1024,512]{1,0:T(8,128)(2,1)S(1)}, bf16[1024,512]{1,0:T(8,128)(2,1)}, u32[]{:S(2)}, u32[]{:S(2)}) collective-permute-start(bf16[1024,512]{1,0:T(8,128)(2,1)S(1)} %convert_element_type.507), channel_id=1, source_target_pairs={{0,16},{1,17},{2,18},{3,19},{4,20},{5,21},{6,22},{7,23},{24,8},{25... | collective-permute-start | bytes 3145736 | tf_op jit(solution)/shard_map/ppermute | solution.py:651
  31.1 36.2 %collective-permute-start.1 = (bf16[1024,512]{1,0:T(8,128)(2,1)S(1)}, bf16[1024,512]{1,0:T(8,128)(2,1)}, u32[]{:S(2)}, u32[]{:S(2)}) collective-permute-start(bf16[1024,512]{1,0:T(8,128)(2,1)S(1)} %broadcast_select_fusion.4), channel_id=1, source_target_pairs={{0,8},{1,9},{2,10},{3,11},{4,12},{5,13},{6,14},{7,15},{8,0},{9,1},... | collective-permute-start | bytes 3145736 | tf_op jit(solution)/shard_map/ppermute | solution.py:651
  35.7 27.2 %all-to-all-start = ((bf16[32,16,128]{2,1,0:T(8,128)(2,1)}), bf16[32,16,128]{2,1,0:T(8,128)(2,1)S(1)}, u32[]{:S(2)}, u32[]{:S(2)}) async-start(bf16[32,16,128]{2,1,0:T(8,128)(2,1)} %pad.23), calls=%async_computation | async-start | bytes 262144 | tf_op jit(solution)/shard_map/all_to_all | solution.py:934
  62.9 21.3 %all-to-all-start.1 = ((bf16[4,160,1024]{2,1,0:T(8,128)(2,1)}), bf16[4,160,1024]{2,1,0:T(8,128)(2,1)S(1)}, u32[]{:S(2)}, u32[]{:S(2)}) async-start(bf16[4,160,1024]{2,1,0:T(8,128)(2,1)} %pad.24), calls=%async_computation.1 | async-start | bytes 2621440 | tf_op jit(solution)/shard_map/all_to_all | solution.py:979
  70.1 14.6 %collective-permute-start.4 = (bf16[512,512]{1,0:T(8,128)(2,1)}, bf16[512,512]{1,0:T(8,128)(2,1)}, u32[]{:S(2)}, u32[]{:S(2)}) collective-permute-start(bf16[512,512]{1,0:T(8,128)(2,1)} %get-tuple-element.517), channel_id=1, source_target_pairs={{0,4},{1,5},{2,6},{3,7},{4,0},{5,1},{6,2},{7,3},{8,12},{9,13},{10,... | collective-permute-start | bytes 1572872 | tf_op jit(solution)/shard_map/ppermute | solution.py:642
  70.8 24.3 %collective-permute-start.3 = (bf16[512,512]{1,0:T(8,128)(2,1)}, bf16[512,512]{1,0:T(8,128)(2,1)}, u32[]{:S(2)}, u32[]{:S(2)}) collective-permute-start(bf16[512,512]{1,0:T(8,128)(2,1)} %get-tuple-element.518), channel_id=1, source_target_pairs={{0,2},{1,3},{2,0},{3,1},{4,6},{5,7},{6,4},{7,5},{8,10},{9,11},{10,... | collective-permute-start | bytes 1572872 | tf_op jit(solution)/shard_map/ppermute | solution.py:642
  72.8 28.4 %collective-permute-start.2 = (bf16[1024,512]{1,0:T(8,128)(2,1)S(1)}, bf16[1024,512]{1,0:T(8,128)(2,1)}, u32[]{:S(2)}, u32[]{:S(2)}) collective-permute-start(bf16[1024,512]{1,0:T(8,128)(2,1)S(1)} %copy-done.139), channel_id=1, source_target_pairs={{8,24},{9,25},{10,26},{11,27},{12,28},{13,29},{14,30},{15,31},{16,... | collective-permute-start | bytes 3145736 | tf_op jit(solution)/shard_map/ppermute | solution.py:651
  97.7 25.0 %collective-permute-start.5 = (bf16[2,512,512]{2,1,0:T(8,128)(2,1)}, bf16[2,512,512]{2,1,0:T(8,128)(2,1)}, u32[]{:S(2)}, u32[]{:S(2)}) collective-permute-start(bf16[2,512,512]{2,1,0:T(8,128)(2,1)} %get-tuple-element.512), channel_id=1, source_target_pairs={{0,4},{1,5},{2,6},{3,7},{4,0},{5,1},{6,2},{7,3},{8,12},{9,13},{10,... | collective-permute-start | bytes 3145736 | tf_op jit(solution)/shard_map/ppermute | solution.py:642
  100.8 24.7 %collective-permute-start.6 = (bf16[2,512,512]{2,1,0:T(8,128)(2,1)}, bf16[2,512,512]{2,1,0:T(8,128)(2,1)}, u32[]{:S(2)}, u32[]{:S(2)}) collective-permute-start(bf16[2,512,512]{2,1,0:T(8,128)(2,1)} %get-tuple-element.514), channel_id=1, source_target_pairs={{0,2},{1,3},{2,0},{3,1},{4,6},{5,7},{6,4},{7,5},{8,10},{9,11},{10,... | collective-permute-start | bytes 3145736 | tf_op jit(solution)/shard_map/ppermute | solution.py:642
  130.9 26.5 %collective-permute-start.8 = (bf16[4,1024,512]{2,1,0:T(8,128)(2,1)}, bf16[4,1024,512]{2,1,0:T(8,128)(2,1)}, u32[]{:S(2)}, u32[]{:S(2)}) collective-permute-start(bf16[4,1024,512]{2,1,0:T(8,128)(2,1)} %bitcast.12.refs_4_.refs_2_), channel_id=1, source_target_pairs={{0,1},{1,0},{2,3},{3,2},{4,5},{5,4},{6,7},{7,6},{8,9},{9,8},{10,11... | collective-permute-start | bytes 12582920 | tf_op jit(solution)/shard_map/ppermute | solution.py:642
  130.9 25.6 %collective-permute-start.7 = (bf16[1024,512]{1,0:T(8,128)(2,1)S(1)}, bf16[1024,512]{1,0:T(8,128)(2,1)S(1)}, u32[]{:S(2)}, u32[]{:S(2)}) collective-permute-start(bf16[1024,512]{1,0:T(8,128)(2,1)S(1)} %broadcast_select_fusion.5), channel_id=1, source_target_pairs={{0,8},{1,9},{2,10},{3,11},{4,12},{5,13},{6,14},{7,15},{8,0},{9,1},... | collective-permute-start | bytes 3145736 | tf_op jit(solution)/shard_map/ppermute | solution.py:651
  133.0 14.3 %collective-permute-start.10 = (bf16[512,512]{1,0:T(8,128)(2,1)}, bf16[512,512]{1,0:T(8,128)(2,1)S(1)}, u32[]{:S(2)}, u32[]{:S(2)}) collective-permute-start(bf16[512,512]{1,0:T(8,128)(2,1)} %get-tuple-element.509), channel_id=1, source_target_pairs={{0,4},{1,5},{2,6},{3,7},{4,0},{5,1},{6,2},{7,3},{8,12},{9,13},{10,... | collective-permute-start | bytes 1572872 | tf_op jit(solution)/shard_map/ppermute | solution.py:642
  134.4 14.0 %collective-permute-start.9 = (bf16[512,512]{1,0:T(8,128)(2,1)}, bf16[512,512]{1,0:T(8,128)(2,1)S(1)}, u32[]{:S(2)}, u32[]{:S(2)}) collective-permute-start(bf16[512,512]{1,0:T(8,128)(2,1)} %get-tuple-element.510), channel_id=1, source_target_pairs={{0,2},{1,3},{2,0},{3,1},{4,6},{5,7},{6,4},{7,5},{8,10},{9,11},{10,... | collective-permute-start | bytes 1572872 | tf_op jit(solution)/shard_map/ppermute | solution.py:642
  160.9 17.5 %collective-permute-start.13 = (bf16[512,512]{1,0:T(8,128)(2,1)}, bf16[512,512]{1,0:T(8,128)(2,1)}, u32[]{:S(2)}, u32[]{:S(2)}) collective-permute-start(bf16[512,512]{1,0:T(8,128)(2,1)} %get-tuple-element.234), channel_id=1, source_target_pairs={{0,2},{1,3},{2,0},{3,1},{4,6},{5,7},{6,4},{7,5},{8,10},{9,11},{10,... | collective-permute-start | bytes 1572872 | tf_op jit(solution)/shard_map/ppermute | solution.py:642
  161.5 16.9 %collective-permute-start.14 = (bf16[512,512]{1,0:T(8,128)(2,1)}, bf16[512,512]{1,0:T(8,128)(2,1)S(1)}, u32[]{:S(2)}, u32[]{:S(2)}) collective-permute-start(bf16[512,512]{1,0:T(8,128)(2,1)} %get-tuple-element.235), channel_id=1, source_target_pairs={{0,4},{1,5},{2,6},{3,7},{4,0},{5,1},{6,2},{7,3},{8,12},{9,13},{10,... | collective-permute-start | bytes 1572872 | tf_op jit(solution)/shard_map/ppermute | solution.py:642
  180.8 24.3 %collective-permute-start.15 = (bf16[2,512,512]{2,1,0:T(8,128)(2,1)S(1)}, bf16[2,512,512]{2,1,0:T(8,128)(2,1)S(1)}, u32[]{:S(2)}, u32[]{:S(2)}) collective-permute-start(bf16[2,512,512]{2,1,0:T(8,128)(2,1)S(1)} %get-tuple-element.502), channel_id=1, source_target_pairs={{0,4},{1,5},{2,6},{3,7},{4,0},{5,1},{6,2},{7,3},{8,12},{9,13},{10,... | collective-permute-start | bytes 3145736 | tf_op jit(solution)/shard_map/ppermute | solution.py:642
  182.9 24.3 %collective-permute-start.16 = (bf16[2,512,512]{2,1,0:T(8,128)(2,1)S(1)}, bf16[2,512,512]{2,1,0:T(8,128)(2,1)S(1)}, u32[]{:S(2)}, u32[]{:S(2)}) collective-permute-start(bf16[2,512,512]{2,1,0:T(8,128)(2,1)S(1)} %get-tuple-element.504), channel_id=1, source_target_pairs={{0,2},{1,3},{2,0},{3,1},{4,6},{5,7},{6,4},{7,5},{8,10},{9,11},{10,... | collective-permute-start | bytes 3145736 | tf_op jit(solution)/shard_map/ppermute | solution.py:642
  211.6 25.9 %collective-permute-start.11 = (bf16[2,512,512]{2,1,0:T(8,128)(2,1)}, bf16[2,512,512]{2,1,0:T(8,128)(2,1)}, u32[]{:S(2)}, u32[]{:S(2)}) collective-permute-start(bf16[2,512,512]{2,1,0:T(8,128)(2,1)} %get-tuple-element.498), channel_id=1, source_target_pairs={{0,4},{1,5},{2,6},{3,7},{4,0},{5,1},{6,2},{7,3},{8,12},{9,13},{10,... | collective-permute-start | bytes 3145736 | tf_op jit(solution)/shard_map/ppermute | solution.py:642
  214.1 25.6 %collective-permute-start.12 = (bf16[2,512,512]{2,1,0:T(8,128)(2,1)}, bf16[2,512,512]{2,1,0:T(8,128)(2,1)}, u32[]{:S(2)}, u32[]{:S(2)}) collective-permute-start(bf16[2,512,512]{2,1,0:T(8,128)(2,1)} %get-tuple-element.500), channel_id=1, source_target_pairs={{0,2},{1,3},{2,0},{3,1},{4,6},{5,7},{6,4},{7,5},{8,10},{9,11},{10,... | collective-permute-start | bytes 3145736 | tf_op jit(solution)/shard_map/ppermute | solution.py:642
  245.0 24.8 %collective-permute-start.20 = (bf16[4,1024,512]{2,1,0:T(8,128)(2,1)}, bf16[4,1024,512]{2,1,0:T(8,128)(2,1)}, u32[]{:S(2)}, u32[]{:S(2)}) collective-permute-start(bf16[4,1024,512]{2,1,0:T(8,128)(2,1)} %bitcast.38.refs_4_), channel_id=1, source_target_pairs={{0,1},{1,0},{2,3},{3,2},{4,5},{5,4},{6,7},{7,6},{8,9},{9,8},{10,11... | collective-permute-start | bytes 12582920 | tf_op jit(solution)/shard_map/ppermute | solution.py:642
  246.2 23.5 %collective-permute-start.19 = (bf16[512,512]{1,0:T(8,128)(2,1)}, bf16[512,512]{1,0:T(8,128)(2,1)}, u32[]{:S(2)}, u32[]{:S(2)}) collective-permute-start(bf16[512,512]{1,0:T(8,128)(2,1)} %get-tuple-element.495), channel_id=1, source_target_pairs={{0,4},{1,5},{2,6},{3,7},{4,0},{5,1},{6,2},{7,3},{8,12},{9,13},{10,... | collective-permute-start | bytes 1572872 | tf_op jit(solution)/shard_map/ppermute | solution.py:642
  247.2 22.5 %collective-permute-start.18 = (bf16[512,512]{1,0:T(8,128)(2,1)}, bf16[512,512]{1,0:T(8,128)(2,1)}, u32[]{:S(2)}, u32[]{:S(2)}) collective-permute-start(bf16[512,512]{1,0:T(8,128)(2,1)} %get-tuple-element.496), channel_id=1, source_target_pairs={{0,2},{1,3},{2,0},{3,1},{4,6},{5,7},{6,4},{7,5},{8,10},{9,11},{10,... | collective-permute-start | bytes 1572872 | tf_op jit(solution)/shard_map/ppermute | solution.py:642
  272.7 25.3 %collective-permute-start.21 = (bf16[2,512,512]{2,1,0:T(8,128)(2,1)}, bf16[2,512,512]{2,1,0:T(8,128)(2,1)}, u32[]{:S(2)}, u32[]{:S(2)}) collective-permute-start(bf16[2,512,512]{2,1,0:T(8,128)(2,1)} %get-tuple-element.490), channel_id=1, source_target_pairs={{0,4},{1,5},{2,6},{3,7},{4,0},{5,1},{6,2},{7,3},{8,12},{9,13},{10,... | collective-permute-start | bytes 3145736 | tf_op jit(solution)/shard_map/ppermute | solution.py:642
  276.2 25.0 %collective-permute-start.22 = (bf16[2,512,512]{2,1,0:T(8,128)(2,1)}, bf16[2,512,512]{2,1,0:T(8,128)(2,1)}, u32[]{:S(2)}, u32[]{:S(2)}) collective-permute-start(bf16[2,512,512]{2,1,0:T(8,128)(2,1)} %get-tuple-element.492), channel_id=1, source_target_pairs={{0,2},{1,3},{2,0},{3,1},{4,6},{5,7},{6,4},{7,5},{8,10},{9,11},{10,... | collective-permute-start | bytes 3145736 | tf_op jit(solution)/shard_map/ppermute | solution.py:642
  352.6 37.6 %collective-permute-start.24 = (bf16[4,1024,512]{2,1,0:T(8,128)(2,1)}, bf16[4,1024,512]{2,1,0:T(8,128)(2,1)S(1)}, u32[]{:S(2)}, u32[]{:S(2)}) collective-permute-start(bf16[4,1024,512]{2,1,0:T(8,128)(2,1)} %get-tuple-element.266), channel_id=1, source_target_pairs={{0,1},{1,0},{2,3},{3,2},{4,5},{5,4},{6,7},{7,6},{8,9},{9,8},{10,11... | collective-permute-start | bytes 12582920 | tf_op jit(solution)/shard_map/ppermute | solution.py:642
  352.8 37.5 %collective-permute-start.25 = (bf16[4,1024,512]{2,1,0:T(8,128)(2,1)}, bf16[4,1024,512]{2,1,0:T(8,128)(2,1)}, u32[]{:S(2)}, u32[]{:S(2)}) collective-permute-start(bf16[4,1024,512]{2,1,0:T(8,128)(2,1)} %get-tuple-element.267), channel_id=1, source_target_pairs={{0,1},{1,0},{2,3},{3,2},{4,5},{5,4},{6,7},{7,6},{8,9},{9,8},{10,11... | collective-permute-start | bytes 12582920 | tf_op jit(solution)/shard_map/ppermute | solution.py:642
  407.3 59.1 %collective-permute-start.26 = (bf16[2,2,512,512]{3,2,1,0:T(8,128)(2,1)}, bf16[2,2,512,512]{3,2,1,0:T(8,128)(2,1)}, u32[]{:S(2)}, u32[]{:S(2)}) collective-permute-start(bf16[2,2,512,512]{3,2,1,0:T(8,128)(2,1)} %pad_maximum_fusion.8), channel_id=1, source_target_pairs={{0,4},{1,5},{2,6},{3,7},{4,0},{5,1},{6,2},{7,3},{8,12},{9,13},{10,... | collective-permute-start | bytes 6291464 | tf_op jit(solution)/shard_map/ppermute | solution.py:642
  408.3 58.2 %collective-permute-start.27 = (bf16[2,2,512,512]{3,2,1,0:T(8,128)(2,1)}, bf16[2,2,512,512]{3,2,1,0:T(8,128)(2,1)}, u32[]{:S(2)}, u32[]{:S(2)}) collective-permute-start(bf16[2,2,512,512]{3,2,1,0:T(8,128)(2,1)} %pad_maximum_fusion.9), channel_id=1, source_target_pairs={{0,2},{1,3},{2,0},{3,1},{4,6},{5,7},{6,4},{7,5},{8,10},{9,11},{10,... | collective-permute-start | bytes 6291464 | tf_op jit(solution)/shard_map/ppermute | solution.py:642
  483.4 35.8 %collective-permute-start.30 = (bf16[4,1024,512]{2,1,0:T(8,128)(2,1)}, bf16[4,1024,512]{2,1,0:T(8,128)(2,1)}, u32[]{:S(2)}, u32[]{:S(2)}) collective-permute-start(bf16[4,1024,512]{2,1,0:T(8,128)(2,1)} %pad_maximum_fusion.4), channel_id=1, source_target_pairs={{0,1},{1,0},{2,3},{3,2},{4,5},{5,4},{6,7},{7,6},{8,9},{9,8},{10,11... | collective-permute-start | bytes 12582920 | tf_op jit(solution)/shard_map/ppermute | solution.py:642
  491.4 27.8 %collective-permute-start.28 = (bf16[2,512,512]{2,1,0:T(8,128)(2,1)}, bf16[2,512,512]{2,1,0:T(8,128)(2,1)S(1)}, u32[]{:S(2)}, u32[]{:S(2)}) collective-permute-start(bf16[2,512,512]{2,1,0:T(8,128)(2,1)} %pad_maximum_fusion.22), channel_id=1, source_target_pairs={{0,2},{1,3},{2,0},{3,1},{4,6},{5,7},{6,4},{7,5},{8,10},{9,11},{10,... | collective-permute-start | bytes 3145736 | tf_op jit(solution)/shard_map/ppermute | solution.py:642
  492.7 26.4 %collective-permute-start.29 = (bf16[2,512,512]{2,1,0:T(8,128)(2,1)}, bf16[2,512,512]{2,1,0:T(8,128)(2,1)S(1)}, u32[]{:S(2)}, u32[]{:S(2)}) collective-permute-start(bf16[2,512,512]{2,1,0:T(8,128)(2,1)} %pad_maximum_fusion.23), channel_id=1, source_target_pairs={{0,4},{1,5},{2,6},{3,7},{4,0},{5,1},{6,2},{7,3},{8,12},{9,13},{10,... | collective-permute-start | bytes 3145736 | tf_op jit(solution)/shard_map/ppermute | solution.py:642
  534.9 26.6 %collective-permute-start.31 = (bf16[1024,512]{1,0:T(8,128)(2,1)}, bf16[1024,512]{1,0:T(8,128)(2,1)}, u32[]{:S(2)}, u32[]{:S(2)}) collective-permute-start(bf16[1024,512]{1,0:T(8,128)(2,1)} %select_convert_fusion), channel_id=1, source_target_pairs={{0,8},{1,9},{2,10},{3,11},{4,12},{5,13},{6,14},{7,15},{8,0},{9,1},... | collective-permute-start | bytes 3145736 | tf_op jit(solution)/shard_map/ppermute | solution.py:651
  535.6 26.0 %collective-permute-start.32 = (bf16[1,2,512,512]{3,2,1,0:T(8,128)(2,1)}, bf16[1,2,512,512]{3,2,1,0:T(8,128)(2,1)}, u32[]{:S(2)}, u32[]{:S(2)}) collective-permute-start(bf16[1,2,512,512]{3,2,1,0:T(8,128)(2,1)} %add_convert_fusion.3), channel_id=1, source_target_pairs={{0,4},{1,5},{2,6},{3,7},{4,0},{5,1},{6,2},{7,3},{8,12},{9,13},{10,... | collective-permute-start | bytes 3145736 | tf_op jit(solution)/shard_map/ppermute | solution.py:642
  536.6 25.0 %collective-permute-start.33 = (bf16[1,2,512,512]{3,2,1,0:T(8,128)(2,1)}, bf16[1,2,512,512]{3,2,1,0:T(8,128)(2,1)}, u32[]{:S(2)}, u32[]{:S(2)}) collective-permute-start(bf16[1,2,512,512]{3,2,1,0:T(8,128)(2,1)} %fusion.24), channel_id=1, source_target_pairs={{0,2},{1,3},{2,0},{3,1},{4,6},{5,7},{6,4},{7,5},{8,10},{9,11},{10,... | collective-permute-start | bytes 3145736 | tf_op jit(solution)/shard_map/ppermute | solution.py:642
  571.7 30.9 %collective-permute-start.34 = (bf16[4,1024,512]{2,1,0:T(8,128)(2,1)}, bf16[4,1024,512]{2,1,0:T(8,128)(2,1)}, u32[]{:S(2)}, u32[]{:S(2)}) collective-permute-start(bf16[4,1024,512]{2,1,0:T(8,128)(2,1)} %pad_maximum_fusion.6), channel_id=1, source_target_pairs={{0,1},{1,0},{2,3},{3,2},{4,5},{5,4},{6,7},{7,6},{8,9},{9,8},{10,11... | collective-permute-start | bytes 12582920 | tf_op jit(solution)/shard_map/ppermute | solution.py:642
  573.0 29.6 %collective-permute-start.35 = (bf16[1,512,512]{2,1,0:T(8,128)(2,1)S(1)}, bf16[1,512,512]{2,1,0:T(8,128)(2,1)S(1)}, u32[]{:S(2)}, u32[]{:S(2)}) collective-permute-start(bf16[1,512,512]{2,1,0:T(8,128)(2,1)S(1)} %fusion.30), channel_id=1, source_target_pairs={{0,2},{1,3},{2,0},{3,1},{4,6},{5,7},{6,4},{7,5},{8,10},{9,11},{10,... | collective-permute-start | bytes 1572872 | tf_op jit(solution)/shard_map/ppermute | solution.py:642
  574.4 28.2 %collective-permute-start.36 = (bf16[1,512,512]{2,1,0:T(8,128)(2,1)}, bf16[1,512,512]{2,1,0:T(8,128)(2,1)S(1)}, u32[]{:S(2)}, u32[]{:S(2)}) collective-permute-start(bf16[1,512,512]{2,1,0:T(8,128)(2,1)} %dynamic-slice_convert_fusion.2), channel_id=1, source_target_pairs={{0,4},{1,5},{2,6},{3,7},{4,0},{5,1},{6,2},{7,3},{8,12},{9,13},{10,... | collective-permute-start | bytes 1572872 | tf_op jit(solution)/shard_map/ppermute | solution.py:642
  597.6 34.2 %collective-permute-start.37 = (bf16[1024,512]{1,0:T(8,128)(2,1)}, bf16[1024,512]{1,0:T(8,128)(2,1)}, u32[]{:S(2)}, u32[]{:S(2)}) collective-permute-start(bf16[1024,512]{1,0:T(8,128)(2,1)} %fusion.50), channel_id=1, source_target_pairs={{0,16},{1,17},{2,18},{3,19},{4,20},{5,21},{6,22},{7,23},{8,24},{9,... | collective-permute-start | bytes 3145736 | tf_op jit(solution)/shard_map/ppermute | solution.py:651
  611.8 25.1 %collective-permute-start.38 = (bf16[1,2,512,512]{3,2,1,0:T(8,128)(2,1)}, bf16[1,2,512,512]{3,2,1,0:T(8,128)(2,1)}, u32[]{:S(2)}, u32[]{:S(2)}) collective-permute-start(bf16[1,2,512,512]{3,2,1,0:T(8,128)(2,1)} %add_convert_fusion.1), channel_id=1, source_target_pairs={{0,4},{1,5},{2,6},{3,7},{4,0},{5,1},{6,2},{7,3},{8,12},{9,13},{10,... | collective-permute-start | bytes 3145736 | tf_op jit(solution)/shard_map/ppermute | solution.py:642
  612.8 24.8 %collective-permute-start.39 = (bf16[1,2,512,512]{3,2,1,0:T(8,128)(2,1)}, bf16[1,2,512,512]{3,2,1,0:T(8,128)(2,1)}, u32[]{:S(2)}, u32[]{:S(2)}) collective-permute-start(bf16[1,2,512,512]{3,2,1,0:T(8,128)(2,1)} %fusion.25), channel_id=1, source_target_pairs={{0,2},{1,3},{2,0},{3,1},{4,6},{5,7},{6,4},{7,5},{8,10},{9,11},{10,... | collective-permute-start | bytes 3145736 | tf_op jit(solution)/shard_map/ppermute | solution.py:642
  613.4 32.9 %collective-permute-start.40 = (bf16[1024,512]{1,0:T(8,128)(2,1)}, bf16[1024,512]{1,0:T(8,128)(2,1)}, u32[]{:S(2)}, u32[]{:S(2)}) collective-permute-start(bf16[1024,512]{1,0:T(8,128)(2,1)} %fusion.1), channel_id=1, source_target_pairs={{0,8},{1,9},{2,10},{3,11},{4,12},{5,13},{6,14},{7,15},{16,24},{17,... | collective-permute-start | bytes 3145736 | tf_op jit(solution)/shard_map/ppermute | solution.py:651
  656.0 14.6 %collective-permute-start.41 = (bf16[1,512,512]{2,1,0:T(8,128)(2,1)}, bf16[1,512,512]{2,1,0:T(8,128)(2,1)}, u32[]{:S(2)}, u32[]{:S(2)}) collective-permute-start(bf16[1,512,512]{2,1,0:T(8,128)(2,1)} %fusion.31), channel_id=1, source_target_pairs={{0,2},{1,3},{2,0},{3,1},{4,6},{5,7},{6,4},{7,5},{8,10},{9,11},{10,... | collective-permute-start | bytes 1572872 | tf_op jit(solution)/shard_map/ppermute | solution.py:642
  656.6 14.0 %collective-permute-start.42 = (bf16[1,512,512]{2,1,0:T(8,128)(2,1)}, bf16[1,512,512]{2,1,0:T(8,128)(2,1)}, u32[]{:S(2)}, u32[]{:S(2)}) collective-permute-start(bf16[1,512,512]{2,1,0:T(8,128)(2,1)} %dynamic-slice_convert_fusion), channel_id=1, source_target_pairs={{0,4},{1,5},{2,6},{3,7},{4,0},{5,1},{6,2},{7,3},{8,12},{9,13},{10,... | collective-permute-start | bytes 1572872 | tf_op jit(solution)/shard_map/ppermute | solution.py:642
  684.3 21.8 %all-to-all-start.2 = ((bf16[4,160,1024]{2,1,0:T(8,128)(2,1)}), bf16[4,160,1024]{2,1,0:T(8,128)(2,1)}, u32[]{:S(2)}, u32[]{:S(2)}) async-start(bf16[4,160,1024]{2,1,0:T(8,128)(2,1)} %bitcast.256), calls=%async_computation.2 | async-start | bytes 2621440 | tf_op jit(solution)/shard_map/all_to_all | solution.py:1322
  689.1 35.6 %collective-permute-start.44 = (bf16[1024,512]{1,0:T(8,128)(2,1)}, bf16[1024,512]{1,0:T(8,128)(2,1)}, u32[]{:S(2)}, u32[]{:S(2)}) collective-permute-start(bf16[1024,512]{1,0:T(8,128)(2,1)} %fusion.18), channel_id=1, source_target_pairs={{24,8},{25,9},{26,10},{27,11},{28,12},{29,13},{30,14},{31,15}} | collective-permute-start | bytes 3145736 | tf_op jit(solution)/shard_map/ppermute | solution.py:651
  690.7 33.9 %collective-permute-start.43 = (bf16[1024,512]{1,0:T(8,128)(2,1)}, bf16[1024,512]{1,0:T(8,128)(2,1)}, u32[]{:S(2)}, u32[]{:S(2)}) collective-permute-start(bf16[1024,512]{1,0:T(8,128)(2,1)} %fusion), channel_id=1, source_target_pairs={{8,0},{9,1},{10,2},{11,3},{12,4},{13,5},{14,6},{15,7},{24,16},{25,... | collective-permute-start | bytes 3145736 | tf_op jit(solution)/shard_map/ppermute | solution.py:651
  706.1 48.6 %all-to-all-start.3 = ((f32[32,8,128]{2,1,0:T(8,128)}), f32[32,8,128]{2,1,0:T(8,128)S(1)}, u32[]{:S(2)}, u32[]{:S(2)}) async-start(f32[32,8,128]{2,1,0:T(8,128)} %bitcast.136), calls=%async_computation.3 | async-start | bytes 262144 | tf_op jit(solution)/shard_map/all_to_all | solution.py:934
  727.5 52.2 %collective-permute-start.45 = (bf16[1024,512]{1,0:T(8,128)(2,1)}, bf16[1024,512]{1,0:T(8,128)(2,1)}, u32[]{:S(2)}, u32[]{:S(2)}) collective-permute-start(bf16[1024,512]{1,0:T(8,128)(2,1)} %fusion.19), channel_id=1, source_target_pairs={{16,0},{17,1},{18,2},{19,3},{20,4},{21,5},{22,6},{23,7}} | collective-permute-start | bytes 3145736 | tf_op jit(solution)/shard_map/ppermute | solution.py:651
  (183 other events, 2057.9 us)

commit v4 on v3

--- a/solution.py
+++ b/solution.py
@@ -660,19 +660,30 @@
     return bits
 
 
-def spread_far(own, plane_size, outer):
-    return move_planes(own, ((0, 2), (3, 1)) if outer else ((1, 3), (2, 0)), plane_size)
-
-
-def spread_held(own, got, plane, outer):
-    sources = (0, 3) if outer else (1, 2)
-    return jnp.where((plane == sources[0]) | (plane == sources[1]), own, got)
-
-
-def spread_sorted(held, near, plane, outer):
+def spread_first(own, plane_size):
+    return move_planes(own, ((0, 2), (1, 0), (2, 3), (3, 1)), plane_size)
+
+
+def spread_second(own, first, plane, plane_size):
+    held = jnp.where((plane == 0) | (plane == 3), own, first)
+    near = move_planes(held, NEAR, plane_size)
+    middle = move_planes(own, ((1, 2), (2, 1)), plane_size)
+    return held, near, middle
+
+
+def spread_outer(held, near, plane):
     even = plane % 2 == 0
-    low_held = even if outer else ~even
-    return jnp.where(low_held, held, near), jnp.where(low_held, near, held)
+    return jnp.where(even, held, near), jnp.where(even, near, held)
+
+
+def spread_inner(own, first, middle, last, plane):
+    chunk_one = jnp.where(
+        plane < 2, jnp.where(plane == 0, first, own), jnp.where(plane == 2, middle, last)
+    )
+    chunk_two = jnp.where(
+        plane < 2, jnp.where(plane == 0, last, middle), jnp.where(plane == 2, own, first)
+    )
+    return chunk_one, chunk_two
 
 
 def spread_begin(own):
@@ -692,101 +703,214 @@
     return [jnp.stack([part, item]) for part, item in zip(parts, got, strict=True)]
 
 
-def spread_end(parts, device_count):
+def assemble_kernel(upper_ref, upper_got, lower_ref, lower_got, out_ref, *, top):
+    chunk = pl.program_id(0)
+    part = pl.program_id(1)
+    sources = (
+        ((part == 0) & (chunk < top), upper_ref),
+        ((part == 0) & (chunk >= top), upper_got),
+        ((part == 1) & (chunk % 2 == 0), lower_ref),
+        ((part == 1) & (chunk % 2 == 1), lower_got),
+    )
+    for chosen, source in sources:
+
+        @pl.when(chosen)
+        def _(source=source):
+            out_ref[0] = source[0]
+
+
+def assemble(parts, got):
+    half, width = parts[0].shape[-2:]
+    flat = [item.reshape(-1, half, width) for item in (parts[0], got[0], parts[1], got[1])]
+    top = flat[0].shape[0]
+
+    def upper(chunk, part):
+        return chunk % top, 0, 0
+
+    def lower(chunk, part):
+        place = 0
+        rest = chunk // 2
+        size = top
+        while size > 1:
+            place = place * 2 + rest % 2
+            rest = rest // 2
+            size //= 2
+        return place, 0, 0
+
+    def block(index):
+        return pl.BlockSpec((1, half, width), index)
+
+    return pl.pallas_call(
+        functools.partial(assemble_kernel, top=top),
+        grid=(2 * top, 2),
+        in_specs=[block(upper), block(upper), block(lower), block(lower)],
+        out_specs=pl.BlockSpec((1, half, width), lambda chunk, part: (chunk, part, 0)),
+        out_shape=jax.ShapeDtypeStruct((2 * top, 2 * half, width), BF16),
+        compiler_params=pltpu.CompilerParams(vmem_limit_bytes=32 << 20),
+        cost_estimate=SMALL,
+    )(*flat)
+
+
+class Sum:
+    def __init__(self, kept, got, absolute, swaps=()):
+        self.kept = kept
+        self.got = got
+        self.absolute = absolute
+        self.swaps = list(swaps)
+
+    def joined(self, got):
+        return Sum(self.kept, self.got, self.absolute, self.swaps + [got])
+
+
+def stage_kernel(*refs, members, terms, parts):
+    ins = refs[1:-parts]
+    outs = refs[-parts:]
+    per_part = 2 * members + terms
+    for part, out_ref in enumerate(outs):
+        mine = ins[part * per_part : (part + 1) * per_part]
+        for member in range(members):
+            total = mine[2 * member][0].astype(F32) + mine[2 * member + 1][0].astype(F32)
+            for swap_ref in mine[2 * members :]:
+                total = total + swap_ref[member, 0].astype(F32)
+            out_ref[member, 0] = total.astype(BF16)
+
+
+def stage_sends(place, pending, device_count):
     levels = len(inner_bits(device_count))
-    turned = jnp.transpose(
-        parts[1], tuple(reversed(range(levels))) + tuple(range(levels, parts[1].ndim))
-    )
-    joined = jnp.concatenate([parts[0], turned], axis=-2)
-    return joined.reshape((-1,) + joined.shape[levels:])
-
-
-def total_of(terms):
-    result = terms[0].astype(F32)
-    for term in terms[1:]:
-        result = result + term.astype(F32)
-    return result
-
-
-class Part:
-    def __init__(self, members, bits, from_end):
-        self.members = members
-        self.bits = bits
-        self.from_end = from_end
-
-    def position(self):
-        return len(self.bits) - 1 if self.from_end else 0
-
-
-def begin_sum(members, device_count):
+    stage = len(pending.swaps)
+    chunks, rows, width = pending.kept[0].shape
+    half = rows // 2
+    count = chunks >> (stage + 1)
+    members = len(pending.kept)
+
+    def relative(part, step):
+        if part == 0:
+            return count + step
+        return (step << (stage + 1)) + (1 << stage)
+
+    def stored(part):
+        def index(step, place):
+            chunk = relative(part, step)
+            return (chunk ^ place[1] if pending.absolute else chunk), part, 0
+
+        return pl.BlockSpec((1, half, width), index)
+
+    def swapped(part, earlier):
+        def index(step, place):
+            chunk = relative(part, step)
+            return 0, (chunk if part == 0 else chunk >> (earlier + 1)), 0, 0
+
+        return pl.BlockSpec((members, 1, half, width), index)
+
+    in_specs = []
+    operands = []
+    for part in range(2):
+        for kept, got in zip(pending.kept, pending.got, strict=True):
+            in_specs += [stored(part)] * 2
+            operands += [kept, got]
+        for earlier, items in enumerate(pending.swaps):
+            in_specs.append(swapped(part, earlier))
+            operands.append(items[part])
+    assert stage < levels
+    return pl.pallas_call(
+        functools.partial(stage_kernel, members=members, terms=stage, parts=2),
+        grid_spec=pltpu.PrefetchScalarGridSpec(
+            num_scalar_prefetch=1,
+            grid=(count,),
+            in_specs=in_specs,
+            out_specs=[pl.BlockSpec((members, 1, half, width), lambda step, place: (0, step, 0, 0))]
+            * 2,
+        ),
+        out_shape=[jax.ShapeDtypeStruct((members, count, half, width), BF16)] * 2,
+        compiler_params=pltpu.CompilerParams(vmem_limit_bytes=32 << 20),
+        cost_estimate=SMALL,
+    )(place, *operands)
+
+
+def stage_swaps(sends, pending, device_count):
     bits = inner_bits(device_count)
-    rows = members[0][0].shape[1] // 2
-    parts = []
+    stage = len(pending.swaps)
+    return [
+        swap_bit(sends[0], device_count, bits[stage]),
+        swap_bit(sends[1], device_count, bits[len(bits) - 1 - stage]),
+    ]
+
+
+def finish_stages(place, pending, device_count):
+    while len(pending.swaps) < len(inner_bits(device_count)):
+        sends = stage_sends(place, pending, device_count)
+        pending = pending.joined(stage_swaps(sends, pending, device_count))
+    return pending
+
+
+def total_kernel(*refs, members, stages):
+    place_ref = refs[0]
+    stored = refs[1 : 1 + 2 * members]
+    swaps = refs[1 + 2 * members : 1 + 2 * members + 2 * stages]
+    kept_ref, sent_ref = refs[1 + 2 * members + 2 * stages :]
+
+    def total(part, member):
+        result = stored[2 * member][0].astype(F32) + stored[2 * member + 1][0].astype(F32)
+        for stage in range(stages):
+            result = result + swaps[2 * stage + part][member, 0].astype(F32)
+        return result
+
     for part in range(2):
-        cut = [
-            [
-                term[:, part * rows : (part + 1) * rows].reshape((2,) * len(bits) + (rows, -1))
-                for term in terms
-            ]
-            for terms in members
-        ]
-        parts.append(Part(cut, list(bits), part == 1))
-    return parts
-
-
-def pick(terms, index, position):
-    return [lax.dynamic_index_in_dim(term, index, position, keepdims=False) for term in terms]
-
-
-def own_place(device, bit):
-    return 0 if device is None else (device // bit) % 2
-
-
-def halve_sends(parts, device):
-    sends = []
-    for part in parts:
-        position = part.position()
-        other = 1 - own_place(device, part.bits[position])
-        sends.append(
-            jnp.stack(
-                [total_of(pick(terms, other, position)).astype(BF16) for terms in part.members]
+
+        @pl.when(pl.program_id(0) // 2 == part)
+        def _(part=part):
+            if members == 1:
+                made = total(part, 0)
+                kept_ref[...] = made
+                sent_ref[...] = made.astype(BF16)
+            else:
+                low = total(part, 0)
+                high = total(part, 1)
+                even = place_ref[2] == 0
+                kept_ref[...] = jnp.where(even, low, high)
+                sent_ref[...] = jnp.where(even, high, low).astype(BF16)
+
+
+def plane_totals(place, pending):
+    chunks, rows, width = pending.kept[0].shape
+    quarter = rows // 4
+    members = len(pending.kept)
+
+    def stored(step, place):
+        return (place[1] if pending.absolute else 0), step, 0
+
+    in_specs = []
+    operands = []
+    for kept, got in zip(pending.kept, pending.got, strict=True):
+        in_specs += [pl.BlockSpec((1, quarter, width), stored)] * 2
+        operands += [kept, got]
+    for items in pending.swaps:
+        for part in range(2):
+            in_specs.append(
+                pl.BlockSpec(
+                    (members, 1, quarter, width),
+                    (lambda step, place: (0, 0, jnp.minimum(step, 1), 0))
+                    if part == 0
+                    else (lambda step, place: (0, 0, jnp.maximum(step - 2, 0), 0)),
+                )
             )
-        )
-    return sends
-
-
-def halve_swaps(sends, parts, device_count):
-    return [
-        swap_bit(sent, device_count, part.bits[part.position()])
-        for sent, part in zip(sends, parts, strict=True)
-    ]
-
-
-def halve_keeps(parts, got, device):
-    result = []
-    every, got = pinned([part.members for part in parts], got)
-    for part, terms_of, items in zip(parts, every, got, strict=True):
-        part = Part(terms_of, part.bits, part.from_end)
-        position = part.position()
-        mine = own_place(device, part.bits[position])
-        members = [
-            [total_of(pick(terms, mine, position) + [items[member]])]
-            for member, terms in enumerate(part.members)
-        ]
-        bits = part.bits[:position] + part.bits[position + 1 :]
-        result.append(Part(members, bits, part.from_end))
-    return result
-
-
-def finish_halving(parts, device, device_count):
-    while parts[0].bits:
-        swapped = halve_swaps(halve_sends(parts, device), parts, device_count)
-        parts = halve_keeps(parts, swapped, device)
-    return parts
-
-
-def member_total(parts, member=0):
-    return jnp.concatenate([total_of(part.members[member]) for part in parts], axis=0)
+            operands.append(items[part])
+    panel = pl.BlockSpec((quarter, width), lambda step, place: (step, 0))
+    return pl.pallas_call(
+        functools.partial(total_kernel, members=members, stages=len(pending.swaps)),
+        grid_spec=pltpu.PrefetchScalarGridSpec(
+            num_scalar_prefetch=1,
+            grid=(4,),
+            in_specs=in_specs,
+            out_specs=[panel, panel],
+        ),
+        out_shape=[
+            jax.ShapeDtypeStruct((rows, width), F32),
+            jax.ShapeDtypeStruct((rows, width), BF16),
+        ],
+        compiler_params=pltpu.CompilerParams(vmem_limit_bytes=32 << 20),
+        cost_estimate=SMALL,
+    )(place, *operands)
 
 
 def column_half(values, half, width):
@@ -965,45 +1089,48 @@
     plane = device // plane_size
     inner = (device % plane_size) // 2
     levels = len(inner_bits(device_count))
-    here = jnp.stack([core, inner]).astype(jnp.int32)
-    away = jnp.stack([1 - core, inner]).astype(jnp.int32)
+    here = jnp.stack([core, inner, plane % 2]).astype(jnp.int32)
+    away = jnp.stack([1 - core, inner, plane % 2]).astype(jnp.int32)
 
     vector_shape = vectors.shape
     own = weights.astype(BF16)
-    outer_far = spread_far(own, plane_size, True)
+    first = spread_first(own, plane_size)
     pieces = jnp.broadcast_to(
         vectors.astype(BF16).reshape(1, -1), (device_count, vectors.size)
     )
     vector_pieces = exchange_vectors(pieces, *vector_shape)
+    first, vector_pieces, own = pinned(first, vector_pieces, own)
+    held, near, middle = spread_second(own, first, plane, plane_size)
     memory_padded = jnp.pad(memory, ((0, 0), (0, SLOT_PAD - quarter), (0, 0)))
     memory_here = lax.all_to_all(memory_padded, "mem", split_axis=0, concat_axis=0, tiled=True)
-    outer_held = spread_held(own, outer_far, plane, True)
-    outer_near = move_planes(outer_held, NEAR, plane_size)
-    outer_near, vector_pieces, own = pinned(outer_near, vector_pieces, own)
-    self_own, down_own = spread_sorted(outer_held, outer_near, plane, True)
+    near, middle, memory_here = pinned(near, middle, memory_here)
+    memory_here = memory_here.reshape(group_size * SLOT_PAD, model)
+    self_own, down_own = spread_outer(held, near, plane)
     self_stack = spread_begin(self_own)
     self_swaps = spread_swaps(self_stack, 0, device_count)
-    inner_far = spread_far(own, plane_size, False)
-    self_swaps, memory_here = pinned(self_swaps, memory_here)
+    last = move_planes(middle, ((1, 0), (2, 3)), plane_size)
     self_stack = spread_joins(self_stack, self_swaps)
     for stage in range(1, levels):
         self_swaps = spread_swaps(self_stack, stage, device_count)
         if stage < levels - 1:
             self_stack = spread_joins(self_stack, self_swaps)
-    inner_held = spread_held(own, inner_far, plane, False)
-    inner_held, self_swaps, down_own = pinned(inner_held, self_swaps, down_own)
-    inner_near = move_planes(inner_held, NEAR, plane_size)
+    self_swaps, last, down_own = pinned(self_swaps, last, down_own)
+    cross_own, up_own = spread_inner(own, first, middle, last, plane)
+    cross_stack = spread_begin(cross_own)
+    cross_stack, self_swaps = pinned(cross_stack, self_swaps)
+    cross_swaps = spread_swaps(cross_stack, 0, device_count)
+    self_here = assemble(self_stack, self_swaps)
+    self_away = swap_bit(self_here, device_count, 1)
+    cross_stack = spread_joins(cross_stack, cross_swaps)
+    cross_stack, self_away, down_own, up_own = pinned(cross_stack, self_away, down_own, up_own)
+    for stage in range(1, levels):
+        cross_swaps = spread_swaps(cross_stack, stage, device_count)
+        if stage < levels - 1:
+            cross_stack = spread_joins(cross_stack, cross_swaps)
     down_stack = spread_begin(down_own)
     down_swaps = spread_swaps(down_stack, 0, device_count)
-    self_here = spread_end(spread_joins(self_stack, self_swaps), device_count)
-    self_away = swap_bit(self_here, device_count, 1)
-    inner_near, self_away, down_swaps = pinned(inner_near, self_away, down_swaps)
-    down_stack = spread_joins(down_stack, down_swaps)
-    cross_own, up_own = spread_sorted(inner_held, inner_near, plane, False)
-    cross_stack = spread_begin(cross_own)
-    cross_stack, self_away = pinned(cross_stack, self_away)
-    cross_swaps = spread_swaps(cross_stack, 0, device_count)
-    memory_here = memory_here.reshape(group_size * SLOT_PAD, model)
+    up_stack = spread_begin(up_own)
+    up_swaps = spread_swaps(up_stack, 0, device_count)
     vector_rows = jnp.swapaxes(vector_pieces, 0, 1).reshape(vector_shape[0], model).astype(F32)
 
     live_rows = (jnp.arange(row_count) < page_lengths[0]).astype(F32)[:, None]
@@ -1029,20 +1156,18 @@
         scales,
         norm=(vector_rows[0], vector_rows[1]),
     )
-    cross_swaps, self_low = pinned(cross_swaps, self_low)
-    cross_stack = spread_joins(cross_stack, cross_swaps)
-    for stage in range(1, levels):
-        cross_swaps = spread_swaps(cross_stack, stage, device_count)
-        if stage < levels - 1:
-            cross_stack = spread_joins(cross_stack, cross_swaps)
     attended, self_log = attention_forward(self_low, self_low, self_low, self_firsts)
-    cross_swaps, attended, up_own = pinned(cross_swaps, attended, up_own)
-    cross_here = spread_end(spread_joins(cross_stack, cross_swaps), device_count)
-    cross_away = swap_bit(cross_here, device_count, 1)
+    cross_swaps, down_swaps, up_swaps, attended = pinned(
+        cross_swaps, down_swaps, up_swaps, attended
+    )
+    down_stack = spread_joins(down_stack, down_swaps)
+    up_stack = spread_joins(up_stack, up_swaps)
     for stage in range(1, levels):
         down_swaps = spread_swaps(down_stack, stage, device_count)
         if stage < levels - 1:
             down_stack = spread_joins(down_stack, down_swaps)
+    cross_here = assemble(cross_stack, cross_swaps)
+    cross_away = swap_bit(cross_here, device_count, 1)
     after_self = project(
         here,
         attended,
@@ -1053,7 +1178,11 @@
         residual=tokens,
         out_type=F32,
     )
-    cross_away, after_self = pinned(cross_away, after_self)
+    cross_away, after_self, up_stack = pinned(cross_away, after_self, up_stack)
+    for stage in range(1, levels):
+        up_swaps = spread_swaps(up_stack, stage, device_count)
+        if stage < levels - 1:
+            up_stack = spread_joins(up_stack, up_swaps)
     queries_cross, low_two = project(
         here,
         after_self,
@@ -1072,22 +1201,15 @@
         1,
         jnp.stack([nothing, vector_rows[10]]),
     )
-    down_swaps, queries_cross, cross_low, up_own = pinned(
-        down_swaps, queries_cross, cross_low, up_own
-    )
-    up_stack = spread_begin(up_own)
-    up_swaps = spread_swaps(up_stack, 0, device_count)
-    down_here = spread_end(spread_joins(down_stack, down_swaps), device_count)
+    down_swaps, queries_cross, cross_low = pinned(down_swaps, queries_cross, cross_low)
+    down_here = assemble(down_stack, down_swaps)
     down_away = swap_bit(down_here, device_count, 1)
     merged, cross_log = attention_forward(
         queries_cross, cross_low, cross_low, cross_firsts, slot_bias
     )
     up_swaps, down_away, merged = pinned(up_swaps, down_away, merged)
-    up_stack = spread_joins(up_stack, up_swaps)
-    for stage in range(1, levels):
-        up_swaps = spread_swaps(up_stack, stage, device_count)
-        if stage < levels - 1:
-            up_stack = spread_joins(up_stack, up_swaps)
+    up_here = assemble(up_stack, up_swaps)
+    up_away = swap_bit(up_here, device_count, 1)
     after_cross = project(
         here,
         merged,
@@ -1099,9 +1221,7 @@
         out_type=F32,
     )
     grad_low_three = (upstream.astype(F32) * live_rows).astype(BF16)
-    up_swaps, after_cross, grad_low_three = pinned(up_swaps, after_cross, grad_low_three)
-    up_here = spread_end(spread_joins(up_stack, up_swaps), device_count)
-    up_away = swap_bit(up_here, device_count, 1)
+    up_away, after_cross, grad_low_three = pinned(up_away, after_cross, grad_low_three)
     bias_up = vector_rows[13:17].reshape(-1)
 
     out_a, back_a, up_sent, down_sent, bias_sent, low_three = feed_half(
@@ -1122,10 +1242,10 @@
     up_got, down_got, out_b, back_b, up_kept, down_kept = pinned(
         up_got, down_got, out_b, back_b, up_kept, down_kept
     )
-    feed_parts = begin_sum(((up_kept, up_got), (down_kept, down_got)), device_count)
-    feed_sends = halve_sends(feed_parts, None)
+    feed_sum = Sum((up_kept, down_kept), (up_got, down_got), False)
+    feed_sends = stage_sends(here, feed_sum, device_count)
     feed_sends, back_b = pinned(feed_sends, back_b)
-    feed_swaps = halve_swaps(feed_sends, feed_parts, device_count)
+    feed_swaps = stage_swaps(feed_sends, feed_sum, device_count)
 
     result = (after_cross + (out_a + out_b) + vector_rows[12]) * live_rows
     mixed = result.astype(BF16)
@@ -1157,12 +1277,12 @@
     feed_swaps, queries_part, queries_own, grad_queries_cross = pinned(
         feed_swaps, queries_part, queries_own, grad_queries_cross
     )
-    feed_parts = halve_keeps(feed_parts, feed_swaps, None)
-    feed_sends = halve_sends(feed_parts, None)
+    feed_sum = feed_sum.joined(feed_swaps)
+    feed_sends = stage_sends(here, feed_sum, device_count)
     feed_sends, queries_part, queries_own, grad_queries_cross = pinned(
         feed_sends, queries_part, queries_own, grad_queries_cross
     )
-    feed_swaps = halve_swaps(feed_sends, feed_parts, device_count)
+    feed_swaps = stage_swaps(feed_sends, feed_sum, device_count)
     cross_sent = weight_half(
         (
             (low_two, queries_part),
@@ -1194,19 +1314,13 @@
     feed_swaps, cross_got, cross_kept, grad_attended = pinned(
         feed_swaps, cross_got, cross_kept, grad_attended
     )
-    feed_parts = finish_halving(
-        halve_keeps(feed_parts, feed_swaps, None), None, device_count
-    )
-    even = plane % 2 == 0
-    up_total = member_total(feed_parts, 0)
-    down_total = member_total(feed_parts, 1)
-    feed_sent = jnp.where(even, down_total, up_total).astype(BF16)
-    feed_kept = jnp.where(even, up_total, down_total)
-    cross_parts = begin_sum(((cross_kept, cross_got),), device_count)
-    cross_sends = halve_sends(cross_parts, device)
+    feed_sum = finish_stages(here, feed_sum.joined(feed_swaps), device_count)
+    feed_kept, feed_sent = plane_totals(here, feed_sum)
+    cross_sum = Sum((cross_kept,), (cross_got,), True)
+    cross_sends = stage_sends(here, cross_sum, device_count)
     feed_sent, cross_sends, grad_attended = pinned(feed_sent, cross_sends, grad_attended)
     feed_got = move_planes(feed_sent, NEAR, plane_size)
-    cross_swaps = halve_swaps(cross_sends, cross_parts, device_count)
+    cross_swaps = stage_swaps(cross_sends, cross_sum, device_count)
     self_operands = (
         self_low,
         self_low,
@@ -1232,15 +1346,15 @@
     feed_got, cross_swaps, self_sent, self_whole = pinned(
         feed_got, cross_swaps, self_sent, self_whole
     )
+    self_got = swap_bit(self_sent, device_count, 1)
     feed_kept = feed_kept + feed_got.astype(F32)
-    cross_parts = halve_keeps(cross_parts, cross_swaps, device)
-    cross_sends = halve_sends(cross_parts, device)
-    feed_sent, cross_sends, self_sent, self_whole = pinned(
-        feed_kept.astype(BF16), cross_sends, self_sent, self_whole
-    )
-    self_got = swap_bit(self_sent, device_count, 1)
-    cross_swaps = halve_swaps(cross_sends, cross_parts, device_count)
+    cross_sum = cross_sum.joined(cross_swaps)
+    cross_sends = stage_sends(here, cross_sum, device_count)
+    feed_sent, cross_sends, self_whole = pinned(
+        feed_kept.astype(BF16), cross_sends, self_whole
+    )
     feed_got = move_planes(feed_sent, ((0, 2), (1, 3)), plane_size)
+    cross_swaps = stage_swaps(cross_sends, cross_sum, device_count)
     self_whole, (queries_own, keys_own, values_own) = attention_backward(
         here, width, *self_operands, self_whole
     )
@@ -1255,16 +1369,15 @@
         width,
     )
     self_got, cross_swaps, self_kept = pinned(self_got, cross_swaps, self_kept)
-    self_parts = begin_sum(((self_kept, self_got),), device_count)
-    self_sends = halve_sends(self_parts, device)
-    cross_parts = finish_halving(
-        halve_keeps(cross_parts, cross_swaps, device), device, device_count
-    )
-    cross_total = member_total(cross_parts)
-    cross_sent = cross_total.astype(BF16)
-    self_sends, cross_sent, grad_queries_self = pinned(self_sends, cross_sent, grad_queries_self)
-    self_swaps = halve_swaps(self_sends, self_parts, device_count)
-    cross_got = move_planes(cross_sent, ((0, 1), (2, 3)), plane_size)
+    self_sum = Sum((self_kept,), (self_got,), True)
+    self_sends = stage_sends(here, self_sum, device_count)
+    self_sends, grad_queries_self, cross_swaps, grad_keys_cross = pinned(
+        self_sends, grad_queries_self, cross_swaps, grad_keys_cross
+    )
+    self_swaps = stage_swaps(self_sends, self_sum, device_count)
+    cross_sum = finish_stages(here, cross_sum.joined(cross_swaps), device_count)
+    cross_total, cross_sent = plane_totals(here, cross_sum)
+    cross_got = move_planes(cross_sent, ((0, 1), (3, 2)), plane_size)
     grad_normed_one = project_back(
         here,
         (grad_queries_self, grad_keys_self, grad_values_self),
@@ -1273,24 +1386,22 @@
         0,
         F32,
     )
-    feed_got, self_swaps, cross_got, grad_normed_one = pinned(
-        feed_got, self_swaps, cross_got, grad_normed_one
-    )
-    self_parts = halve_keeps(self_parts, self_swaps, device)
-    self_sends = halve_sends(self_parts, device)
-    cross_total = cross_total + cross_got.astype(F32)
-    cross_sent = cross_total.astype(BF16)
-    self_sends, cross_sent, grad_normed_one = pinned(self_sends, cross_sent, grad_normed_one)
-    self_swaps = halve_swaps(self_sends, self_parts, device_count)
-    cross_got = move_planes(cross_sent, ((3, 1),), plane_size)
+    memory_back = project_back(
+        here, (grad_keys_cross, grad_values_cross), cross_here, cross_away, 1, BF16
+    )
+    self_swaps, grad_normed_one, memory_back = pinned(self_swaps, grad_normed_one, memory_back)
+    self_sum = self_sum.joined(self_swaps)
+    self_sends = stage_sends(here, self_sum, device_count)
+    self_sends, grad_normed_one, memory_back = pinned(self_sends, grad_normed_one, memory_back)
+    self_swaps = stage_swaps(self_sends, self_sum, device_count)
     input_grad, _, sums_one = norm_back(tokens, vector_rows[0], grad_one, (grad_normed_one,))
     self_swaps, sums_one = pinned(self_swaps, sums_one)
-    self_parts = finish_halving(
-        halve_keeps(self_parts, self_swaps, device), device, device_count
-    )
-    self_total = member_total(self_parts)
-    self_sent, grad_keys_cross = pinned(self_total.astype(BF16), grad_keys_cross)
+    self_sum = finish_stages(here, self_sum.joined(self_swaps), device_count)
+    self_total, self_sent = plane_totals(here, self_sum)
+    self_sent, memory_back, sums_one = pinned(self_sent, memory_back, sums_one)
     self_got = move_planes(self_sent, ((1, 0), (3, 2)), plane_size)
+    cross_total = cross_total + cross_got.astype(F32)
+    cross_got = move_planes(cross_total.astype(BF16), ((2, 1),), plane_size)
     vector_head = jnp.stack(
         [
             sums_one[0],
@@ -1316,9 +1427,10 @@
     vector_parts = exchange_vectors(vector_terms.reshape(device_count, -1), *vector_shape)
     vector_grad = jnp.sum(vector_parts, axis=0)
 
-    memory_back = project_back(
-        here, (grad_keys_cross, grad_values_cross), cross_here, cross_away, 1, BF16
-    )
+    self_got, vector_grad = pinned(self_got, vector_grad)
+    self_total = self_total + self_got.astype(F32)
+    self_sent, memory_back = pinned(self_total.astype(BF16), memory_back)
+    self_got = move_planes(self_sent, ((2, 0),), plane_size)
     memory_back = lax.all_to_all(
         memory_back.reshape(group_size, SLOT_PAD, model),
         "mem",
@@ -1327,14 +1439,13 @@
         tiled=True,
     )
     memory_back = memory_back[:, :quarter].astype(F32)
-    self_got, cross_got, memory_back = pinned(self_got, cross_got, memory_back)
-    self_total = self_total + self_got.astype(F32)
-    self_got = move_planes(self_total.astype(BF16), ((2, 0),), plane_size)
-    group_zero = self_total + self_got.astype(F32)
-    group_one = cross_total + cross_got.astype(F32)
-    group_feed = feed_kept + feed_got.astype(F32)
-
-    weight_grad = jnp.where(plane < 2, jnp.where(plane == 0, group_zero, group_one), group_feed)
+    group_other = jnp.where(
+        plane < 2,
+        cross_total + cross_got.astype(F32),
+        feed_kept + feed_got.astype(F32),
+    )
+    group_other, self_got, memory_back = pinned(group_other, self_got, memory_back)
+    weight_grad = jnp.where(plane == 0, self_total + self_got.astype(F32), group_other)
     (
         weight_first,
         weight_second,

time: 818 us -> 751 us (0.918)
  waiting for transfers between devices: 195 us -> 128 us
  Pallas kernels: 306 us -> 364 us
  other arithmetic: 103 us -> 53.7 us
  starting transfers between devices: 81.9 us -> 67.5 us
    pallas_call x0 -> x13, Pallas kernels: none -> 61.7 us  [the longest x4 27.9 us: assemble(): pl.pallas_call(functools.partial(assemble_kernel, top=top), grid=(2 * top...]
    ppermute x36, waiting for transfers between devices: 79.3 us -> 43.5 us  [swap_bit(): lax.ppermute(values, AXES, [(item, item ^ bit) for item in range(device_c...]
    ppermute x10, waiting for transfers between devices: 56.5 us -> 24.4 us  [move_planes(): return lax.ppermute(values, AXES, pairs)]
    unnamed x368 -> x306, local copies, waits for them, and re-layouts: 51.5 us -> 71 us
    slice x7 -> x0, local copies, waits for them, and re-layouts: 16.9 us -> none  [the longest x6 16.4 us: begin_sum(): term[:, part * rows:(part + 1) * rows]]
    add x12 -> x0, other arithmetic: 15.8 us -> none  [total_of(): result = result + term.astype(F32)]
    convert_element_type x12 -> x2, other arithmetic: 19.2 us -> 3.98 us  [the longest x1 2.63 us: local(): cross_got = move_planes(cross_total.astype(BF16), ((2, 1),), plane_size)]
    all_to_all x2, starting transfers between devices: 20.2 us -> 10.8 us  [exchange_vectors(): got = lax.all_to_all(padded, AXES, split_axis=0, concat_axis=0, tiled=True)]
  transfers between devices with their start and end apart: 50 -> 50, of which waited for: 23 -> 15; matrix products, arithmetic and copies ran while one was open for 11% -> 12% of each run, Pallas kernels for 28% -> 34%
where the time goes in v4:
time: 751 us; the launch traced here: 738 us
  Pallas kernels  364 us (48%)
  waiting for transfers between devices  128 us (17%)
  local copies, waits for them, and re-layouts  94.8 us (13%)
  starting transfers between devices  67.5 us (9%)
  other arithmetic  53.7 us (7%)
  matrix products  26.1 us (3%)
    pallas_call x2, Pallas kernels, feed_half(): pl.pallas_call(functools.partial(feed_kernel, norm=norm is not None), gri...  75.5 us
    pallas_call x4, Pallas kernels, attention_backward(): pl.pallas_call(functools.partial(attention_backward_kernel, causal=causal...  71.7 us
    unnamed x306, local copies, waits for them, and re-layouts  71 us
    ppermute x36, waiting for transfers between devices, swap_bit(): lax.ppermute(values, AXES, [(item, item ^ bit) for item in range(device_c...  43.5 us
    pallas_call x2, Pallas kernels, attention_forward(): pl.pallas_call(functools.partial(attention_forward_kernel, causal=causal)...  37.5 us
    pallas_call x5, Pallas kernels, project(): pl.pallas_call(functools.partial(project_kernel, norm=norm is not None, r...  35 us
    pallas_call x5, Pallas kernels, project_back(): pl.pallas_call(functools.partial(project_back_kernel, parts=parts), grid_...  34.5 us
    all_to_all x2, waiting for transfers between devices, exchange_vectors(): got = lax.all_to_all(padded, AXES, split_axis=0, concat_axis=0, tiled=True)  34 us
  transfers between devices with their start and end apart: 50, of which 15 were waited for; matrix products, arithmetic and copies ran while one was open for 12% of the time, Pallas kernels for 34%

profile of v4, /device:TPU:0, one launch (start us, length us, event | category | flops | bytes accessed | tf_op | source)
XLA Modules:
  0.0 737.9 jit_solution(16337947720158350186)
XLA Ops:
  2.4 4.1 collective-permute-start
  7.3 3.8 all-to-all-start
  11.2 23.9 %all-to-all-done = bf16[32,16,128]{2,1,0:T(8,128)(2,1)S(1)} async-done(((bf16[32,16,128]{2,1,0:T(8,128)(2,1)}), bf16[32,16,128]{2,1,0:T(8,128)(2,1)S(1)}, u32[]{:S(2)}, u32[]{:S(2)}) %all-to-all-start) | async-done | bytes 131104 | tf_op jit(solution)/shard_map/all_to_all | solution.py:1058
  44.9 17.2 %all-to-all-done.1 = bf16[4,160,1024]{2,1,0:T(8,128)(2,1)S(1)} async-done(((bf16[4,160,1024]{2,1,0:T(8,128)(2,1)}), bf16[4,160,1024]{2,1,0:T(8,128)(2,1)S(1)}, u32[]{:S(2)}, u32[]{:S(2)}) %all-to-all-start.1) | async-done | bytes 1310752 | tf_op jit(solution)/shard_map/all_to_all | solution.py:1105
  67.4 11.2 %collective-permute-done.3 = bf16[512,512]{1,0:T(8,128)(2,1)S(1)} collective-permute-done((bf16[512,512]{1,0:T(8,128)(2,1)S(1)}, bf16[512,512]{1,0:T(8,128)(2,1)S(1)}, u32[]{:S(2)}, u32[]{:S(2)}) %collective-permute-start.3) | collective-permute-done | bytes 524320 | tf_op jit(solution)/shard_map/ppermute | solution.py:642
  80.5 13.1 %collective-permute-done.7 = bf16[1024,512]{1,0:T(8,128)(2,1)} collective-permute-done((bf16[1024,512]{1,0:T(8,128)(2,1)}, bf16[1024,512]{1,0:T(8,128)(2,1)}, u32[]{:S(2)}, u32[]{:S(2)}) %collective-permute-start.7) | collective-permute-done | bytes 1048608 | tf_op jit(solution)/shard_map/ppermute | solution.py:651
  93.6 9.0 %collective-permute-done.4.upper_got = bf16[2,512,512]{2,1,0:T(8,128)(2,1)S(1)} collective-permute-done((bf16[2,512,512]{2,1,0:T(8,128)(2,1)S(1)}, bf16[2,512,512]{2,1,0:T(8,128)(2,1)S(1)}, u32[]{:S(2)}, u32[]{:S(2)}) %collective-permute-start.4) | collective-permute-done | bytes 1048608 | tf_op jit(solution)/shard_map/ppermute | solution.py:642
  111.9 12.0 %collective-permute-done.8 = bf16[512,512]{1,0:T(8,128)(2,1)S(1)} collective-permute-done((bf16[512,512]{1,0:T(8,128)(2,1)S(1)}, bf16[512,512]{1,0:T(8,128)(2,1)S(1)}, u32[]{:S(2)}, u32[]{:S(2)}) %collective-permute-start.8) | collective-permute-done | bytes 524320 | tf_op jit(solution)/shard_map/ppermute | solution.py:642
  137.8 6.5 collective-permute-done.14
  151.4 10.8 %shard_map.287 = (bf16[1024,3072]{1,0:T(8,128)(2,1)}, bf16[1024,1024]{1,0:T(8,128)(2,1)S(1)}) custom-call(s32[3]{0:T(128)S(1)} %get-tuple-element.461.refs_0_, bf16[1024,1024]{1,0:T(8,128)(2,1)S(1)} %copy-done.35, f32[1,1024]{1,0:T(1,128)S(1)} %slice.146.refs_2_.refs_1_, f32[1,1024]{1,0:T(1,128)S(1)} %slice.148.refs_3_, ...), custom_call_target="tpu_custom_call" | custom-call | flops 1048576 | bytes 65536 | tf_op jit(solution)/shard_map/pallas_call | solution.py:557
  165.8 18.4 %shard_map.288 = (bf16[1024,1024]{1,0:T(8,128)(2,1)S(1)}, f32[8,8,1024]{2,1,0:T(8,128)S(1)}) custom-call(bf16[1024,3072]{1,0:T(8,128)(2,1)S(1)} %copy-done.2, bf16[1024,3072]{1,0:T(8,128)(2,1)S(1)} %copy-done.2, bf16[1024,3072]{1,0:T(8,128)(2,1)S(1)} %copy-done.2), custom_call_target="tpu_custom_call" | custom-call | flops 1048576 | bytes 65536 | tf_op jit(solution)/shard_map/pallas_call | solution.py:231
  184.2 8.0 %shard_map.289.refs_4_.refs_2_.refs_3_ = bf16[4,1024,512]{2,1,0:T(8,128)(2,1)} custom-call(bf16[2,512,512]{2,1,0:T(8,128)(2,1)S(1)} %pad_maximum_fusion.6.upper_ref, bf16[2,512,512]{2,1,0:T(8,128)(2,1)} %collective-permute-done.11.upper_got, bf16[2,512,512]{2,1,0:T(8,128)(2,1)} %pad_maximum_fusion.7.lower_ref, ...), custom_call_target="tpu_custom_call" | custom-call | flops 1048576 | bytes 65536 | tf_op jit(solution)/shard_map/pallas_call | solution.py:743
  203.1 4.8 shard_map.290.refs_1_.refs_6_.refs_0_
  212.7 7.0 shard_map.292.refs_1_.refs_2_.refs_3_
  219.8 6.5 shard_map.291
  226.4 9.3 %shard_map.293.refs_4_ = bf16[4,1024,512]{2,1,0:T(8,128)(2,1)} custom-call(bf16[2,512,512]{2,1,0:T(8,128)(2,1)} %pad_maximum_fusion.10.upper_ref, bf16[2,512,512]{2,1,0:T(8,128)(2,1)} %collective-permute-done.20.upper_got, bf16[2,512,512]{2,1,0:T(8,128)(2,1)} %pad_maximum_fusion.11.lower_ref, bf16[2,512,512]{2,1,0:T(8,128)(2,1)} %collective-permute-done.21.lower_got), custom_call_target="tpu_custom_call" | custom-call | flops 1048576 | bytes 65536 | tf_op jit(solution)/shard_map/pallas_call | solution.py:743
  239.5 19.1 %shard_map.294 = (bf16[1024,1024]{1,0:T(8,128)(2,1)S(1)}, f32[8,8,1024]{2,1,0:T(8,128)S(1)}) custom-call(bf16[1024,1024]{1,0:T(8,128)(2,1)S(1)} %copy-done.45, bf16[640,2048]{1,0:T(8,128)(2,1)S(1)} %shard_map.292.refs_1_.refs_2_.refs_3_, bf16[640,2048]{1,0:T(8,128)(2,1)S(1)} %shard_map.292.refs_1_.refs_2_.refs_3_, ...), custom_call_target="tpu_custom_call" | custom-call | flops 1048576 | bytes 65536 | tf_op jit(solution)/shard_map/pallas_call | solution.py:231
  262.0 7.9 %shard_map.295.refs_3_ = bf16[4,1024,512]{2,1,0:T(8,128)(2,1)} custom-call(bf16[2,512,512]{2,1,0:T(8,128)(2,1)} %pad_maximum_fusion.8.upper_ref, bf16[2,512,512]{2,1,0:T(8,128)(2,1)} %collective-permute-done.18.upper_got, bf16[2,512,512]{2,1,0:T(8,128)(2,1)} %pad_maximum_fusion.9.lower_ref, bf16[2,512,512]{2,1,0:T(8,128)(2,1)} %collective-permute-done.19.lower_got), custom_call_target="tpu_custom_call" | custom-call | flops 1048576 | bytes 65536 | tf_op jit(solution)/shard_map/pallas_call | solution.py:743
  275.6 5.7 shard_map.296.refs_1_.refs_0_
  283.4 38.3 %shard_map.297 = (f32[1024,1024]{1,0:T(8,128)}, f32[1024,1024]{1,0:T(8,128)}, bf16[4,1024,512]{2,1,0:T(8,128)(2,1)}, bf16[4,1024,512]{2,1,0:T(8,128)(2,1)}, f32[...) custom-call(s32[3]{0:T(128)} %get-tuple-element.462.refs_0_, f32[1024,1024]{1,0:T(8,128)} %copy-done.27, ...), custom_call_target="tpu_custom_call" | custom-call | flops 1048576 | bytes 65536 | tf_op jit(solution)/shard_map/pallas_call | solution.py:400
  322.4 37.2 %shard_map.298 = (f32[1024,1024]{1,0:T(8,128)}, f32[1024,1024]{1,0:T(8,128)}, bf16[4,1024,512]{2,1,0:T(8,128)(2,1)}, bf16[4,1024,512]{2,1,0:T(8,128)(2,1)}, f32[4,1,512]{2,1,0:T(1,128)}) custom-call(s32[3]{0:T(128)} %copy-done.100, bf16[1024,1024]{1,0:T(8,128)(2,1)} %get-tuple-element.260.refs_1_, bf16[1024,1024]{1,0:T(8,128)(2,1)} %multiply_convert_fusion.1.refs_4_.refs_2_, ...), custom_call_target="tpu_custom_call" | custom-call | flops 1048576 | bytes 65536 | tf_op jit(solution)/shard_map/pallas_call | solution.py:400
  359.6 3.7 copy-done.12
  365.5 4.3 shard_map.299
  376.1 6.6 shard_map.300
  384.7 5.9 shard_map.301.refs_4_
  390.7 18.2 %shard_map.302 = (bf16[1024,1024]{1,0:T(8,128)(2,1)S(1)}, bf16[640,1024]{1,0:T(8,128)(2,1)S(1)}, bf16[640,1024]{1,0:T(8,128)(2,1)S(1)}, bf16[1024,512]{1,0:T(8,1...) custom-call(s32[3]{0:T(128)S(1)} %copy-done.108, bf16[1024,1024]{1,0:T(8,128)(2,1)S(1)} %copy-done.46, ...), custom_call_target="tpu_custom_call" | custom-call | flops 1048576 | bytes 65536 | tf_op jit(solution)/shard_map/pallas_call | solution.py:286
  408.9 17.8 %shard_map.303 = (bf16[1024,1024]{1,0:T(8,128)(2,1)S(1)}, bf16[640,1024]{1,0:T(8,128)(2,1)S(1)}, bf16[640,1024]{1,0:T(8,128)(2,1)S(1)}, bf16[1024,512]{1,0:T(8,1...) custom-call(s32[3]{0:T(128)S(1)} %copy-done.101, ...), custom_call_target="tpu_custom_call", output_to_operand_aliasing={{0}: (8, {}), {1}: (9, {}), {2}: (10, {})} | custom-call | flops 1048576 | bytes 65536 | tf_op jit(solution)/shard_map/pallas_call | solution.py:286
  434.1 4.3 shard_map.304
  442.4 3.6 fusion.8
  451.8 5.1 shard_map.305.refs_3_
  458.9 7.2 shard_map.306
  482.7 4.1 shard_map.308
  496.0 17.8 %shard_map.310 = (bf16[1024,1024]{1,0:T(8,128)(2,1)S(1)}, bf16[1024,1024]{1,0:T(8,128)(2,1)S(1)}, bf16[1024,1024]{1,0:T(8,128)(2,1)S(1)}, bf16[1024,512]{1,0:T(8...) custom-call(s32[3]{0:T(128)S(1)} %copy-done.108, ...), custom_call_target="tpu_custom_call" | custom-call | flops 1048576 | bytes 65536 | tf_op jit(solution)/shard_map/pallas_call | solution.py:286
  531.9 17.9 %shard_map.312 = (bf16[1024,1024]{1,0:T(8,128)(2,1)S(1)}, bf16[1024,1024]{1,0:T(8,128)(2,1)S(1)}, bf16[1024,1024]{1,0:T(8,128)(2,1)S(1)}, bf16[1024,512]{1,0:T(8...) custom-call(s32[3]{0:T(128)S(1)} %copy-done.101, ...), custom_call_target="tpu_custom_call", output_to_operand_aliasing={{0}: (7, {}), {1}: (8, {}), {2}: (9, {})} | custom-call | flops 1048576 | bytes 65536 | tf_op jit(solution)/shard_map/pallas_call | solution.py:286
  569.8 4.3 shard_map.318
  583.1 8.6 %shard_map.315 = bf16[640,1024]{1,0:T(8,128)(2,1)} custom-call(s32[3]{0:T(128)S(1)} %copy-done.101, bf16[640,1024]{1,0:T(8,128)(2,1)S(1)} %copy-done.66, bf16[640,1024]{1,0:T(8,128)(2,1)S(1)} %get-tuple-element.360.refs_2_, bf16[4,1024,512]{2,1,0:T(8,128)(2,1)} %shard_map.289.refs_4_.refs_2_.refs_3_, ...), custom_call_target="tpu_custom_call" | custom-call | flops 1048576 | bytes 65536 | tf_op jit(solution)/shard_map/pallas_call | solution.py:619
  591.8 11.4 %shard_map.314.refs_3_ = f32[1024,1024]{1,0:T(8,128)S(1)} custom-call(s32[3]{0:T(128)S(1)} %copy-done.101, bf16[1024,1024]{1,0:T(8,128)(2,1)S(1)} %copy-done.48, bf16[1024,1024]{1,0:T(8,128)(2,1)S(1)} %copy-done.63, bf16[1024,1024]{1,0:T(8,128)(2,1)S(1)} %copy-done.50, bf16[4,1024,512]{2,1,0:T(8,128)(2,1)} %copy-done.18, bf16[4,1024,512]{2,1,0:T(8,128)(2,1)} %copy-done.29), custom_call_target="tpu_custom_call" | custom-call | flops 1048576 | bytes 65536 | tf_op jit(solution)/shard_map/pallas_call | solution.py:619
  603.2 3.8 shard_map.316
  622.4 5.7 shard_map.317
  628.1 4.3 shard_map.319
  644.0 7.0 all-to-all-start.2
  650.9 6.7 multiply_convert_fusion
  657.6 10.1 %all-to-all-done.2 = f32[32,8,128]{2,1,0:T(8,128)S(1)} async-done(((f32[32,8,128]{2,1,0:T(8,128)}), f32[32,8,128]{2,1,0:T(8,128)S(1)}, u32[]{:S(2)}, u32[]{:S(2)}) %all-to-all-start.2) | async-done | bytes 131104 | tf_op jit(solution)/shard_map/all_to_all | solution.py:1058
  669.2 3.7 all-to-all-start.3
  674.4 5.1 add_select_fusion.1
  681.3 8.8 %all-to-all-done.3 = bf16[4,160,1024]{2,1,0:T(8,128)(2,1)S(1)} async-done(((bf16[4,160,1024]{2,1,0:T(8,128)(2,1)}), bf16[4,160,1024]{2,1,0:T(8,128)(2,1)S(1)}, u32[]{:S(2)}, u32[]{:S(2)}) %all-to-all-start.3) | async-done | bytes 1310752 | tf_op jit(solution)/shard_map/all_to_all | solution.py:1434
  690.5 11.2 %collective-permute-done.45 = bf16[1024,512]{1,0:T(8,128)(2,1)} collective-permute-done((bf16[1024,512]{1,0:T(8,128)(2,1)}, bf16[1024,512]{1,0:T(8,128)(2,1)}, u32[]{:S(2)}, u32[]{:S(2)}) %collective-permute-start.45) | collective-permute-done | bytes 1048608 | tf_op jit(solution)/shard_map/ppermute | solution.py:651
  708.5 29.0 %shard_map.320 = (f32[1024,512]{1,0:T(8,128)}, f32[1024,512]{1,0:T(8,128)}, f32[1024,512]{1,0:T(8,128)}, f32[1024,512]{1,0:T(8,128)}, bf16[1024,512]{1,0:T(8,128...) custom-call(f32[1024,512]{1,0:T(8,128)S(1)} %add_select_fusion.grad_ref, f32[1024,512]{1,0:T(8,128)S(1)} %copy-done.54, ...), custom_call_target="tpu_custom_call" | custom-call | flops 1048576 | bytes 65536 | tf_op jit(solution)/shard_map/pallas_call | solution.py:1027
  (509 shorter events, 224.1 us)
Async XLA Ops:
  2.4 33.5 %collective-permute-start = (bf16[1024,512]{1,0:T(8,128)(2,1)S(1)}, bf16[1024,512]{1,0:T(8,128)(2,1)S(1)}, u32[]{:S(2)}, u32[]{:S(2)}) collective-permute-start(bf16[1024,512]{1,0:T(8,128)(2,1)S(1)} %convert_element_type.128), channel_id=1, source_target_pairs={{0,16},{1,17},{2,18},{3,19},{4,20},{5,21},{6,22},{7,23},{8,0},{9,1... | collective-permute-start | bytes 3145736 | tf_op jit(solution)/shard_map/ppermute | solution.py:651
  7.3 27.7 %all-to-all-start = ((bf16[32,16,128]{2,1,0:T(8,128)(2,1)}), bf16[32,16,128]{2,1,0:T(8,128)(2,1)S(1)}, u32[]{:S(2)}, u32[]{:S(2)}) async-start(bf16[32,16,128]{2,1,0:T(8,128)(2,1)} %pad.23), calls=%async_computation | async-start | bytes 262144 | tf_op jit(solution)/shard_map/all_to_all | solution.py:1058
  36.0 26.1 %collective-permute-start.1 = (bf16[1024,512]{1,0:T(8,128)(2,1)S(1)}, bf16[1024,512]{1,0:T(8,128)(2,1)}, u32[]{:S(2)}, u32[]{:S(2)}) collective-permute-start(bf16[1024,512]{1,0:T(8,128)(2,1)S(1)} %broadcast_select_fusion.2), channel_id=1, source_target_pairs={{0,8},{1,9},{2,10},{3,11},{4,12},{5,13},{6,14},{7,15},{8,0},{9,1},... | collective-permute-start | bytes 3145736 | tf_op jit(solution)/shard_map/ppermute | solution.py:651
  36.9 25.3 %collective-permute-start.2 = (bf16[1024,512]{1,0:T(8,128)(2,1)S(1)}, bf16[1024,512]{1,0:T(8,128)(2,1)}, u32[]{:S(2)}, u32[]{:S(2)}) collective-permute-start(bf16[1024,512]{1,0:T(8,128)(2,1)S(1)} %convert_element_type.128), channel_id=1, source_target_pairs={{8,16},{9,17},{10,18},{11,19},{12,20},{13,21},{14,22},{15,23},{16,... | collective-permute-start | bytes 3145736 | tf_op jit(solution)/shard_map/ppermute | solution.py:651
  41.3 20.8 %all-to-all-start.1 = ((bf16[4,160,1024]{2,1,0:T(8,128)(2,1)}), bf16[4,160,1024]{2,1,0:T(8,128)(2,1)S(1)}, u32[]{:S(2)}, u32[]{:S(2)}) async-start(bf16[4,160,1024]{2,1,0:T(8,128)(2,1)} %pad.24), calls=%async_computation.1 | async-start | bytes 2621440 | tf_op jit(solution)/shard_map/all_to_all | solution.py:1105
  65.5 13.9 %collective-permute-start.5 = (bf16[512,512]{1,0:T(8,128)(2,1)S(1)}, bf16[512,512]{1,0:T(8,128)(2,1)S(1)}, u32[]{:S(2)}, u32[]{:S(2)}) collective-permute-start(bf16[512,512]{1,0:T(8,128)(2,1)S(1)} %get-tuple-element.455), channel_id=1, source_target_pairs={{0,4},{1,5},{2,6},{3,7},{4,0},{5,1},{6,2},{7,3},{8,12},{9,13},{10,... | collective-permute-start | bytes 1572872 | tf_op jit(solution)/shard_map/ppermute | solution.py:642
  66.1 27.5 %collective-permute-start.7 = (bf16[1024,512]{1,0:T(8,128)(2,1)}, bf16[1024,512]{1,0:T(8,128)(2,1)}, u32[]{:S(2)}, u32[]{:S(2)}) collective-permute-start(bf16[1024,512]{1,0:T(8,128)(2,1)} %collective-permute-done.2), channel_id=1, source_target_pairs={{8,0},{9,1},{10,2},{11,3},{12,4},{13,5},{14,6},{15,7},{16,24},{17,... | collective-permute-start | bytes 3145736 | tf_op jit(solution)/shard_map/ppermute | solution.py:651
  78.7 24.0 %collective-permute-start.4 = (bf16[2,512,512]{2,1,0:T(8,128)(2,1)S(1)}, bf16[2,512,512]{2,1,0:T(8,128)(2,1)S(1)}, u32[]{:S(2)}, u32[]{:S(2)}) collective-permute-start(bf16[2,512,512]{2,1,0:T(8,128)(2,1)S(1)} %pad_maximum_fusion.4.upper_ref), channel_id=1, source_target_pairs={{0,4},{1,5},{2,6},{3,7},{4,0},{5,1},{6,2},{7,3},{8,12},{9,13},{10,... | collective-permute-start | bytes 3145736 | tf_op jit(solution)/shard_map/ppermute | solution.py:642
  79.5 23.8 %collective-permute-start.6 = (bf16[2,512,512]{2,1,0:T(8,128)(2,1)S(1)}, bf16[2,512,512]{2,1,0:T(8,128)(2,1)}, u32[]{:S(2)}, u32[]{:S(2)}) collective-permute-start(bf16[2,512,512]{2,1,0:T(8,128)(2,1)S(1)} %pad_maximum_fusion.5.lower_ref), channel_id=1, source_target_pairs={{0,2},{1,3},{2,0},{3,1},{4,6},{5,7},{6,4},{7,5},{8,10},{9,11},{10,... | collective-permute-start | bytes 3145736 | tf_op jit(solution)/shard_map/ppermute | solution.py:642
  109.5 16.1 %collective-permute-start.10 = (bf16[4,1024,512]{2,1,0:T(8,128)(2,1)S(1)}, bf16[4,1024,512]{2,1,0:T(8,128)(2,1)S(1)}, u32[]{:S(2)}, u32[]{:S(2)}) collective-permute-start(bf16[4,1024,512]{2,1,0:T(8,128)(2,1)S(1)} %shard_map.286.refs_4_.refs_2_), channel_id=1, source_target_pairs={{0,1},{1,0},{2,3},{3,2},{4,5},{5,4},{6,7},{7,6},{8,9},{9,8},{10,11... | collective-permute-start | bytes 12582920 | tf_op jit(solution)/shard_map/ppermute | solution.py:642
  109.6 14.3 %collective-permute-start.8 = (bf16[512,512]{1,0:T(8,128)(2,1)S(1)}, bf16[512,512]{1,0:T(8,128)(2,1)S(1)}, u32[]{:S(2)}, u32[]{:S(2)}) collective-permute-start(bf16[512,512]{1,0:T(8,128)(2,1)S(1)} %get-tuple-element.218), channel_id=1, source_target_pairs={{0,2},{1,3},{2,0},{3,1},{4,6},{5,7},{6,4},{7,5},{8,10},{9,11},{10,... | collective-permute-start | bytes 1572872 | tf_op jit(solution)/shard_map/ppermute | solution.py:642
  110.6 14.0 %collective-permute-start.9 = (bf16[512,512]{1,0:T(8,128)(2,1)S(1)}, bf16[512,512]{1,0:T(8,128)(2,1)S(1)}, u32[]{:S(2)}, u32[]{:S(2)}) collective-permute-start(bf16[512,512]{1,0:T(8,128)(2,1)S(1)} %get-tuple-element.219), channel_id=1, source_target_pairs={{0,4},{1,5},{2,6},{3,7},{4,0},{5,1},{6,2},{7,3},{8,12},{9,13},{10,... | collective-permute-start | bytes 1572872 | tf_op jit(solution)/shard_map/ppermute | solution.py:642
  129.1 15.2 %collective-permute-start.14 = (bf16[512,512]{1,0:T(8,128)(2,1)}, bf16[512,512]{1,0:T(8,128)(2,1)}, u32[]{:S(2)}, u32[]{:S(2)}) collective-permute-start(bf16[512,512]{1,0:T(8,128)(2,1)} %get-tuple-element.445), channel_id=1, source_target_pairs={{0,4},{1,5},{2,6},{3,7},{4,0},{5,1},{6,2},{7,3},{8,12},{9,13},{10,... | collective-permute-start | bytes 1572872 | tf_op jit(solution)/shard_map/ppermute | solution.py:642
  130.5 53.7 %collective-permute-start.11 = (bf16[2,512,512]{2,1,0:T(8,128)(2,1)S(1)}, bf16[2,512,512]{2,1,0:T(8,128)(2,1)}, u32[]{:S(2)}, u32[]{:S(2)}) collective-permute-start(bf16[2,512,512]{2,1,0:T(8,128)(2,1)S(1)} %pad_maximum_fusion.6.upper_ref), channel_id=1, source_target_pairs={{0,4},{1,5},{2,6},{3,7},{4,0},{5,1},{6,2},{7,3},{8,12},{9,13},{10,... | collective-permute-start | bytes 3145736 | tf_op jit(solution)/shard_map/ppermute | solution.py:642
  131.1 53.1 %collective-permute-start.12 = (bf16[2,512,512]{2,1,0:T(8,128)(2,1)}, bf16[2,512,512]{2,1,0:T(8,128)(2,1)}, u32[]{:S(2)}, u32[]{:S(2)}) collective-permute-start(bf16[2,512,512]{2,1,0:T(8,128)(2,1)} %pad_maximum_fusion.7.lower_ref), channel_id=1, source_target_pairs={{0,2},{1,3},{2,0},{3,1},{4,6},{5,7},{6,4},{7,5},{8,10},{9,11},{10,... | collective-permute-start | bytes 3145736 | tf_op jit(solution)/shard_map/ppermute | solution.py:642
  132.9 51.3 %collective-permute-start.13 = (bf16[512,512]{1,0:T(8,128)(2,1)}, bf16[512,512]{1,0:T(8,128)(2,1)}, u32[]{:S(2)}, u32[]{:S(2)}) collective-permute-start(bf16[512,512]{1,0:T(8,128)(2,1)} %get-tuple-element.446), channel_id=1, source_target_pairs={{0,2},{1,3},{2,0},{3,1},{4,6},{5,7},{6,4},{7,5},{8,10},{9,11},{10,... | collective-permute-start | bytes 1572872 | tf_op jit(solution)/shard_map/ppermute | solution.py:642
  136.4 47.7 %collective-permute-start.16 = (bf16[512,512]{1,0:T(8,128)(2,1)}, bf16[512,512]{1,0:T(8,128)(2,1)}, u32[]{:S(2)}, u32[]{:S(2)}) collective-permute-start(bf16[512,512]{1,0:T(8,128)(2,1)} %get-tuple-element.449), channel_id=1, source_target_pairs={{0,4},{1,5},{2,6},{3,7},{4,0},{5,1},{6,2},{7,3},{8,12},{9,13},{10,... | collective-permute-start | bytes 1572872 | tf_op jit(solution)/shard_map/ppermute | solution.py:642
  144.3 39.9 %collective-permute-start.15 = (bf16[512,512]{1,0:T(8,128)(2,1)}, bf16[512,512]{1,0:T(8,128)(2,1)}, u32[]{:S(2)}, u32[]{:S(2)}) collective-permute-start(bf16[512,512]{1,0:T(8,128)(2,1)} %get-tuple-element.450), channel_id=1, source_target_pairs={{0,2},{1,3},{2,0},{3,1},{4,6},{5,7},{6,4},{7,5},{8,10},{9,11},{10,... | collective-permute-start | bytes 1572872 | tf_op jit(solution)/shard_map/ppermute | solution.py:642
  192.2 20.5 %collective-permute-start.17 = (bf16[4,1024,512]{2,1,0:T(8,128)(2,1)}, bf16[4,1024,512]{2,1,0:T(8,128)(2,1)}, u32[]{:S(2)}, u32[]{:S(2)}) collective-permute-start(bf16[4,1024,512]{2,1,0:T(8,128)(2,1)} %shard_map.289.refs_4_.refs_2_.refs_3_), channel_id=1, source_target_pairs={{0,1},{1,0},{2,3},{3,2},{4,5},{5,4},{6,7},{7,6},{8,9},{9,8},{10,11... | collective-permute-start | bytes 12582920 | tf_op jit(solution)/shard_map/ppermute | solution.py:642
  194.4 32.0 %collective-permute-start.21 = (bf16[2,512,512]{2,1,0:T(8,128)(2,1)}, bf16[2,512,512]{2,1,0:T(8,128)(2,1)}, u32[]{:S(2)}, u32[]{:S(2)}) collective-permute-start(bf16[2,512,512]{2,1,0:T(8,128)(2,1)} %pad_maximum_fusion.11.lower_ref), channel_id=1, source_target_pairs={{0,2},{1,3},{2,0},{3,1},{4,6},{5,7},{6,4},{7,5},{8,10},{9,11},{10,... | collective-permute-start | bytes 3145736 | tf_op jit(solution)/shard_map/ppermute | solution.py:642
  197.5 28.9 %collective-permute-start.20 = (bf16[2,512,512]{2,1,0:T(8,128)(2,1)}, bf16[2,512,512]{2,1,0:T(8,128)(2,1)}, u32[]{:S(2)}, u32[]{:S(2)}) collective-permute-start(bf16[2,512,512]{2,1,0:T(8,128)(2,1)} %pad_maximum_fusion.10.upper_ref), channel_id=1, source_target_pairs={{0,4},{1,5},{2,6},{3,7},{4,0},{5,1},{6,2},{7,3},{8,12},{9,13},{10,... | collective-permute-start | bytes 3145736 | tf_op jit(solution)/shard_map/ppermute | solution.py:642
  235.7 26.3 %collective-permute-start.22 = (bf16[4,1024,512]{2,1,0:T(8,128)(2,1)}, bf16[4,1024,512]{2,1,0:T(8,128)(2,1)}, u32[]{:S(2)}, u32[]{:S(2)}) collective-permute-start(bf16[4,1024,512]{2,1,0:T(8,128)(2,1)} %shard_map.293.refs_4_), channel_id=1, source_target_pairs={{0,1},{1,0},{2,3},{3,2},{4,5},{5,4},{6,7},{7,6},{8,9},{9,8},{10,11... | collective-permute-start | bytes 12582920 | tf_op jit(solution)/shard_map/ppermute | solution.py:642
  235.8 25.9 %collective-permute-start.18 = (bf16[2,512,512]{2,1,0:T(8,128)(2,1)}, bf16[2,512,512]{2,1,0:T(8,128)(2,1)}, u32[]{:S(2)}, u32[]{:S(2)}) collective-permute-start(bf16[2,512,512]{2,1,0:T(8,128)(2,1)} %pad_maximum_fusion.8.upper_ref), channel_id=1, source_target_pairs={{0,4},{1,5},{2,6},{3,7},{4,0},{5,1},{6,2},{7,3},{8,12},{9,13},{10,... | collective-permute-start | bytes 3145736 | tf_op jit(solution)/shard_map/ppermute | solution.py:642
  236.5 25.5 %collective-permute-start.19 = (bf16[2,512,512]{2,1,0:T(8,128)(2,1)}, bf16[2,512,512]{2,1,0:T(8,128)(2,1)}, u32[]{:S(2)}, u32[]{:S(2)}) collective-permute-start(bf16[2,512,512]{2,1,0:T(8,128)(2,1)} %pad_maximum_fusion.9.lower_ref), channel_id=1, source_target_pairs={{0,2},{1,3},{2,0},{3,1},{4,6},{5,7},{6,4},{7,5},{8,10},{9,11},{10,... | collective-permute-start | bytes 3145736 | tf_op jit(solution)/shard_map/ppermute | solution.py:642
  321.8 37.8 %collective-permute-start.24 = (bf16[4,1024,512]{2,1,0:T(8,128)(2,1)}, bf16[4,1024,512]{2,1,0:T(8,128)(2,1)S(1)}, u32[]{:S(2)}, u32[]{:S(2)}) collective-permute-start(bf16[4,1024,512]{2,1,0:T(8,128)(2,1)} %get-tuple-element.257), channel_id=1, source_target_pairs={{0,1},{1,0},{2,3},{3,2},{4,5},{5,4},{6,7},{7,6},{8,9},{9,8},{10,11... | collective-permute-start | bytes 12582920 | tf_op jit(solution)/shard_map/ppermute | solution.py:642
  322.3 37.3 %collective-permute-start.25 = (bf16[4,1024,512]{2,1,0:T(8,128)(2,1)}, bf16[4,1024,512]{2,1,0:T(8,128)(2,1)}, u32[]{:S(2)}, u32[]{:S(2)}) collective-permute-start(bf16[4,1024,512]{2,1,0:T(8,128)(2,1)} %get-tuple-element.258), channel_id=1, source_target_pairs={{0,1},{1,0},{2,3},{3,2},{4,5},{5,4},{6,7},{7,6},{8,9},{9,8},{10,11... | collective-permute-start | bytes 12582920 | tf_op jit(solution)/shard_map/ppermute | solution.py:642
  369.8 61.7 %collective-permute-start.26 = (bf16[2,2,512,512]{3,2,1,0:T(8,128)(2,1)}, bf16[2,2,512,512]{3,2,1,0:T(8,128)(2,1)}, u32[]{:S(2)}, u32[]{:S(2)}) collective-permute-start(bf16[2,2,512,512]{3,2,1,0:T(8,128)(2,1)} %get-tuple-element.277), channel_id=1, source_target_pairs={{0,4},{1,5},{2,6},{3,7},{4,0},{5,1},{6,2},{7,3},{8,12},{9,13},{10,... | collective-permute-start | bytes 6291464 | tf_op jit(solution)/shard_map/ppermute | solution.py:642
  371.2 60.4 %collective-permute-start.27 = (bf16[2,2,512,512]{3,2,1,0:T(8,128)(2,1)}, bf16[2,2,512,512]{3,2,1,0:T(8,128)(2,1)}, u32[]{:S(2)}, u32[]{:S(2)}) collective-permute-start(bf16[2,2,512,512]{3,2,1,0:T(8,128)(2,1)} %get-tuple-element.278), channel_id=1, source_target_pairs={{0,2},{1,3},{2,0},{3,1},{4,6},{5,7},{6,4},{7,5},{8,10},{9,11},{10,... | collective-permute-start | bytes 6291464 | tf_op jit(solution)/shard_map/ppermute | solution.py:642
  442.2 35.4 %collective-permute-start.30 = (bf16[4,1024,512]{2,1,0:T(8,128)(2,1)}, bf16[4,1024,512]{2,1,0:T(8,128)(2,1)}, u32[]{:S(2)}, u32[]{:S(2)}) collective-permute-start(bf16[4,1024,512]{2,1,0:T(8,128)(2,1)} %pad_maximum_fusion), channel_id=1, source_target_pairs={{0,1},{1,0},{2,3},{3,2},{4,5},{5,4},{6,7},{7,6},{8,9},{9,8},{10,11... | collective-permute-start | bytes 12582920 | tf_op jit(solution)/shard_map/ppermute | solution.py:642
  450.2 26.1 %collective-permute-start.28 = (bf16[2,1,512,512]{3,2,1,0:T(8,128)(2,1)}, bf16[2,1,512,512]{3,2,1,0:T(8,128)(2,1)S(1)}, u32[]{:S(2)}, u32[]{:S(2)}) collective-permute-start(bf16[2,1,512,512]{3,2,1,0:T(8,128)(2,1)} %get-tuple-element.301), channel_id=1, source_target_pairs={{0,2},{1,3},{2,0},{3,1},{4,6},{5,7},{6,4},{7,5},{8,10},{9,11},{10,... | collective-permute-start | bytes 3145736 | tf_op jit(solution)/shard_map/ppermute | solution.py:642
  451.2 25.5 %collective-permute-start.29 = (bf16[2,1,512,512]{3,2,1,0:T(8,128)(2,1)}, bf16[2,1,512,512]{3,2,1,0:T(8,128)(2,1)S(1)}, u32[]{:S(2)}, u32[]{:S(2)}) collective-permute-start(bf16[2,1,512,512]{3,2,1,0:T(8,128)(2,1)} %get-tuple-element.302), channel_id=1, source_target_pairs={{0,4},{1,5},{2,6},{3,7},{4,0},{5,1},{6,2},{7,3},{8,12},{9,13},{10,... | collective-permute-start | bytes 3145736 | tf_op jit(solution)/shard_map/ppermute | solution.py:642
  490.5 29.5 %collective-permute-start.31 = (bf16[1024,512]{1,0:T(8,128)(2,1)S(1)}, bf16[1024,512]{1,0:T(8,128)(2,1)}, u32[]{:S(2)}, u32[]{:S(2)}) collective-permute-start(bf16[1024,512]{1,0:T(8,128)(2,1)S(1)} %get-tuple-element.316), channel_id=1, source_target_pairs={{0,8},{1,9},{2,10},{3,11},{4,12},{5,13},{6,14},{7,15},{8,0},{9,1},... | collective-permute-start | bytes 3145736 | tf_op jit(solution)/shard_map/ppermute | solution.py:651
  493.8 26.3 %collective-permute-start.32 = (bf16[1,2,512,512]{3,2,1,0:T(8,128)(2,1)}, bf16[1,2,512,512]{3,2,1,0:T(8,128)(2,1)S(1)}, u32[]{:S(2)}, u32[]{:S(2)}) collective-permute-start(bf16[1,2,512,512]{3,2,1,0:T(8,128)(2,1)} %get-tuple-element.317), channel_id=1, source_target_pairs={{0,4},{1,5},{2,6},{3,7},{4,0},{5,1},{6,2},{7,3},{8,12},{9,13},{10,... | collective-permute-start | bytes 3145736 | tf_op jit(solution)/shard_map/ppermute | solution.py:642
  495.1 25.9 %collective-permute-start.33 = (bf16[1,2,512,512]{3,2,1,0:T(8,128)(2,1)}, bf16[1,2,512,512]{3,2,1,0:T(8,128)(2,1)S(1)}, u32[]{:S(2)}, u32[]{:S(2)}) collective-permute-start(bf16[1,2,512,512]{3,2,1,0:T(8,128)(2,1)} %get-tuple-element.318), channel_id=1, source_target_pairs={{0,2},{1,3},{2,0},{3,1},{4,6},{5,7},{6,4},{7,5},{8,10},{9,11},{10,... | collective-permute-start | bytes 3145736 | tf_op jit(solution)/shard_map/ppermute | solution.py:642
  522.0 33.8 %collective-permute-start.34 = (bf16[4,1024,512]{2,1,0:T(8,128)(2,1)}, bf16[4,1024,512]{2,1,0:T(8,128)(2,1)S(1)}, u32[]{:S(2)}, u32[]{:S(2)}) collective-permute-start(bf16[4,1024,512]{2,1,0:T(8,128)(2,1)} %pad_maximum_fusion.2), channel_id=1, source_target_pairs={{0,1},{1,0},{2,3},{3,2},{4,5},{5,4},{6,7},{7,6},{8,9},{9,8},{10,11... | collective-permute-start | bytes 12582920 | tf_op jit(solution)/shard_map/ppermute | solution.py:642
  530.1 25.7 %collective-permute-start.35 = (bf16[1,1,512,512]{3,2,1,0:T(8,128)(2,1)}, bf16[1,1,512,512]{3,2,1,0:T(8,128)(2,1)S(1)}, u32[]{:S(2)}, u32[]{:S(2)}) collective-permute-start(bf16[1,1,512,512]{3,2,1,0:T(8,128)(2,1)} %get-tuple-element.338), channel_id=1, source_target_pairs={{0,2},{1,3},{2,0},{3,1},{4,6},{5,7},{6,4},{7,5},{8,10},{9,11},{10,... | collective-permute-start | bytes 1572872 | tf_op jit(solution)/shard_map/ppermute | solution.py:642
  531.2 24.5 %collective-permute-start.36 = (bf16[1,1,512,512]{3,2,1,0:T(8,128)(2,1)}, bf16[1,1,512,512]{3,2,1,0:T(8,128)(2,1)S(1)}, u32[]{:S(2)}, u32[]{:S(2)}) collective-permute-start(bf16[1,1,512,512]{3,2,1,0:T(8,128)(2,1)} %get-tuple-element.339), channel_id=1, source_target_pairs={{0,4},{1,5},{2,6},{3,7},{4,0},{5,1},{6,2},{7,3},{8,12},{9,13},{10,... | collective-permute-start | bytes 1572872 | tf_op jit(solution)/shard_map/ppermute | solution.py:642
  560.0 43.3 %collective-permute-start.37 = (bf16[1,2,512,512]{3,2,1,0:T(8,128)(2,1)}, bf16[1,2,512,512]{3,2,1,0:T(8,128)(2,1)}, u32[]{:S(2)}, u32[]{:S(2)}) collective-permute-start(bf16[1,2,512,512]{3,2,1,0:T(8,128)(2,1)} %get-tuple-element.354), channel_id=1, source_target_pairs={{0,4},{1,5},{2,6},{3,7},{4,0},{5,1},{6,2},{7,3},{8,12},{9,13},{10,... | collective-permute-start | bytes 3145736 | tf_op jit(solution)/shard_map/ppermute | solution.py:642
  561.3 41.9 %collective-permute-start.38 = (bf16[1,2,512,512]{3,2,1,0:T(8,128)(2,1)}, bf16[1,2,512,512]{3,2,1,0:T(8,128)(2,1)}, u32[]{:S(2)}, u32[]{:S(2)}) collective-permute-start(bf16[1,2,512,512]{3,2,1,0:T(8,128)(2,1)} %get-tuple-element.355), channel_id=1, source_target_pairs={{0,2},{1,3},{2,0},{3,1},{4,6},{5,7},{6,4},{7,5},{8,10},{9,11},{10,... | collective-permute-start | bytes 3145736 | tf_op jit(solution)/shard_map/ppermute | solution.py:642
  575.4 58.3 %collective-permute-start.39 = (bf16[1024,512]{1,0:T(8,128)(2,1)}, bf16[1024,512]{1,0:T(8,128)(2,1)}, u32[]{:S(2)}, u32[]{:S(2)}) collective-permute-start(bf16[1024,512]{1,0:T(8,128)(2,1)} %get-tuple-element.372), channel_id=1, source_target_pairs={{0,8},{1,9},{2,10},{3,11},{4,12},{5,13},{6,14},{7,15},{24,16},{25,... | collective-permute-start | bytes 3145736 | tf_op jit(solution)/shard_map/ppermute | solution.py:651
  607.0 21.1 %collective-permute-start.42 = (bf16[1,1,512,512]{3,2,1,0:T(8,128)(2,1)}, bf16[1,1,512,512]{3,2,1,0:T(8,128)(2,1)S(1)}, u32[]{:S(2)}, u32[]{:S(2)}) collective-permute-start(bf16[1,1,512,512]{3,2,1,0:T(8,128)(2,1)} %get-tuple-element.374), channel_id=1, source_target_pairs={{0,2},{1,3},{2,0},{3,1},{4,6},{5,7},{6,4},{7,5},{8,10},{9,11},{10,... | collective-permute-start | bytes 1572872 | tf_op jit(solution)/shard_map/ppermute | solution.py:642
  608.1 19.9 %collective-permute-start.43 = (bf16[1,1,512,512]{3,2,1,0:T(8,128)(2,1)}, bf16[1,1,512,512]{3,2,1,0:T(8,128)(2,1)S(1)}, u32[]{:S(2)}, u32[]{:S(2)}) collective-permute-start(bf16[1,1,512,512]{3,2,1,0:T(8,128)(2,1)} %get-tuple-element.375), channel_id=1, source_target_pairs={{0,4},{1,5},{2,6},{3,7},{4,0},{5,1},{6,2},{7,3},{8,12},{9,13},{10,... | collective-permute-start | bytes 1572872 | tf_op jit(solution)/shard_map/ppermute | solution.py:642
  613.0 61.4 %collective-permute-start.41 = (bf16[1024,512]{1,0:T(8,128)(2,1)}, bf16[1024,512]{1,0:T(8,128)(2,1)}, u32[]{:S(2)}, u32[]{:S(2)}) collective-permute-start(bf16[1024,512]{1,0:T(8,128)(2,1)} %fusion), channel_id=1, source_target_pairs={{0,16},{1,17},{2,18},{3,19},{4,20},{5,21},{6,22},{7,23},{8,24},{9,... | collective-permute-start | bytes 3145736 | tf_op jit(solution)/shard_map/ppermute | solution.py:651
  632.4 35.4 %collective-permute-start.44 = (bf16[1024,512]{1,0:T(8,128)(2,1)}, bf16[1024,512]{1,0:T(8,128)(2,1)S(1)}, u32[]{:S(2)}, u32[]{:S(2)}) collective-permute-start(bf16[1024,512]{1,0:T(8,128)(2,1)} %get-tuple-element.383), channel_id=1, source_target_pairs={{8,0},{9,1},{10,2},{11,3},{12,4},{13,5},{14,6},{15,7},{24,16},{25,... | collective-permute-start | bytes 3145736 | tf_op jit(solution)/shard_map/ppermute | solution.py:651
  636.4 38.0 %collective-permute-start.40 = (bf16[1024,512]{1,0:T(8,128)(2,1)}, bf16[1024,512]{1,0:T(8,128)(2,1)}, u32[]{:S(2)}, u32[]{:S(2)}) collective-permute-start(bf16[1024,512]{1,0:T(8,128)(2,1)} %fusion.1), channel_id=1, source_target_pairs={{16,8},{17,9},{18,10},{19,11},{20,12},{21,13},{22,14},{23,15}} | collective-permute-start | bytes 3145736 | tf_op jit(solution)/shard_map/ppermute | solution.py:651
  644.0 23.8 %all-to-all-start.2 = ((f32[32,8,128]{2,1,0:T(8,128)}), f32[32,8,128]{2,1,0:T(8,128)S(1)}, u32[]{:S(2)}, u32[]{:S(2)}) async-start(f32[32,8,128]{2,1,0:T(8,128)} %bitcast.48), calls=%async_computation.2 | async-start | bytes 262144 | tf_op jit(solution)/shard_map/all_to_all | solution.py:1058
  669.2 20.9 %all-to-all-start.3 = ((bf16[4,160,1024]{2,1,0:T(8,128)(2,1)}), bf16[4,160,1024]{2,1,0:T(8,128)(2,1)S(1)}, u32[]{:S(2)}, u32[]{:S(2)}) async-start(bf16[4,160,1024]{2,1,0:T(8,128)(2,1)} %bitcast.42), calls=%async_computation.3 | async-start | bytes 2621440 | tf_op jit(solution)/shard_map/all_to_all | solution.py:1434
  673.0 28.7 %collective-permute-start.45 = (bf16[1024,512]{1,0:T(8,128)(2,1)}, bf16[1024,512]{1,0:T(8,128)(2,1)}, u32[]{:S(2)}, u32[]{:S(2)}) collective-permute-start(bf16[1024,512]{1,0:T(8,128)(2,1)} %fusion.2), channel_id=1, source_target_pairs={{16,0},{17,1},{18,2},{19,3},{20,4},{21,5},{22,6},{23,7}} | collective-permute-start | bytes 3145736 | tf_op jit(solution)/shard_map/ppermute | solution.py:651
  (152 other events, 1499.5 us)

commit v5 on v4

--- a/solution.py
+++ b/solution.py
@@ -14,6 +14,7 @@
 LANES = 128
 QUERY_ROWS = 256
 FORWARD_ROWS = 512
+FEED_ROWS = 1024
 SLOT_PAD = 160
 PANEL = 8
 GROUPS = 4
@@ -240,7 +241,7 @@
             jax.ShapeDtypeStruct((row_count, pairs * LANES), BF16),
             jax.ShapeDtypeStruct((pairs, 8, row_count), F32),
         ],
-        compiler_params=pltpu.CompilerParams(vmem_limit_bytes=40 << 20),
+        compiler_params=pltpu.CompilerParams(vmem_limit_bytes=60 << 20),
         cost_estimate=SMALL,
     )(*operands)
 
@@ -298,10 +299,111 @@
         out_shape=[jax.ShapeDtypeStruct((count, model), BF16) for count in counts]
         + [jax.ShapeDtypeStruct((count, model // 2), BF16) for count in counts],
         input_output_aliases=aliases,
-        compiler_params=pltpu.CompilerParams(vmem_limit_bytes=40 << 20),
+        compiler_params=pltpu.CompilerParams(vmem_limit_bytes=60 << 20),
         cost_estimate=SMALL,
     )(half, *operands)
     return results[:3], results[3:]
+
+
+PLACE_PLANE = 3
+VECTOR_ROWS = 24
+
+
+def holders(group, plane):
+    if group == 0:
+        return ((1, plane != 0), (0, plane == 0))
+    if group == 1:
+        return ((2, plane > 1), (0, plane == 1), (1, plane == 0))
+    if group == 2:
+        return ((2, plane < 2), (0, plane == 2), (3, plane == 3))
+    return ((3, plane != 3), (0, plane == 3))
+
+
+class Source:
+    def __init__(self, slots, group, sides):
+        self.group = group
+        self.sides = sides
+        self.which = [slot for slot, _ in holders(group, 0)]
+        self.operands = [
+            array for slot in self.which for side in sides for array in slots[slot][side]
+        ]
+        self.shape = self.operands[0].shape
+        self.dtype = self.operands[0].dtype
+
+    def chunks(self):
+        return 2 * self.shape[0]
+
+    def specs(self):
+        return [pl.BlockSpec(memory_space=pl.ANY)] * len(self.operands)
+
+    def scratch(self):
+        return [
+            pltpu.VMEM((2, 2 * self.shape[1], self.shape[2]), self.dtype),
+            pltpu.SemaphoreType.DMA((2, 2)),
+        ]
+
+
+def start_fetch(source, refs, buffer, semaphores, plane, side, chunk, turn):
+    top, half = source.shape[:2]
+    lower_place = 0
+    rest = chunk // 2
+    size = top
+    while size > 1:
+        lower_place = lower_place * 2 + rest % 2
+        rest = rest // 2
+        size //= 2
+    item = 0
+    for _, chosen in holders(source.group, plane):
+        for number in range(len(source.sides)):
+            wanted = chosen & (side == number)
+            lows, highs, evens, odds = refs[item : item + 4]
+            item += 4
+            copies = (
+                (chunk < top, lows, chunk, 0),
+                (chunk >= top, highs, chunk - top, 0),
+                (chunk % 2 == 0, evens, lower_place, 1),
+                (chunk % 2 == 1, odds, lower_place, 1),
+            )
+            for condition, array, index, part in copies:
+
+                @pl.when(wanted & condition)
+                def _(array=array, index=index, part=part):
+                    pltpu.make_async_copy(
+                        array.at[index],
+                        buffer.at[turn, pl.ds(part * half, half), :],
+                        semaphores.at[turn, part],
+                    ).start()
+
+
+def wait_fetch(source, refs, buffer, semaphores, turn):
+    half = source.shape[1]
+    for part in range(2):
+        pltpu.make_async_copy(
+            refs[0].at[0],
+            buffer.at[turn, pl.ds(part * half, half), :],
+            semaphores.at[turn, part],
+        ).wait()
+
+
+def fetched(source, refs, buffer, semaphores, plane, order, item, count):
+    turn = item % 2
+
+    @pl.when(item == 0)
+    def _():
+        side, chunk = order(0)
+        start_fetch(source, refs, buffer, semaphores, plane, side, chunk, 0)
+
+    @pl.when(item + 1 < count)
+    def _():
+        side, chunk = order(item + 1)
+        start_fetch(source, refs, buffer, semaphores, plane, side, chunk, (item + 1) % 2)
+
+    wait_fetch(source, refs, buffer, semaphores, turn)
+    return buffer.at[turn]
+
+
+def vector_part(vectors_ref, row, first, width):
+    return vectors_ref[row : row + 1, pl.ds(pl.multiple_of(first, width), width)]
 
 
 def gelu_parts(values):
@@ -315,36 +417,52 @@
     return values * weight, derivative
 
 
-def feed_kernel(*refs, norm):
-    refs = list(refs[1:])
+def feed_kernel(*refs, norm, up_source, down_source):
+    refs = list(refs)
+    place_ref = refs.pop(0)
     values_ref = refs.pop(0)
-    if norm:
-        gain_ref = refs.pop(0)
-        shift_ref = refs.pop(0)
-    grad_ref, up_ref, down_ref, bias_ref = refs[:4]
-    out_ref, back_ref, grad_up_ref, grad_down_ref, grad_bias_ref = refs[4:9]
-    low_ref = refs[9] if norm else values_ref
-    low_turned, grad_turned, active_ref, hidden_ref = refs[-4:]
-
-    @pl.when(pl.program_id(0) == 0)
+    grad_ref = refs.pop(0)
+    vectors_ref = refs.pop(0)
+    bias_ref = refs.pop(0)
+    up_refs = refs[: len(up_source.operands)]
+    refs = refs[len(up_refs) :]
+    down_refs = refs[: len(down_source.operands)]
+    refs = refs[len(down_refs) :]
+    out_ref, back_ref, grad_up_ref, grad_down_ref, grad_bias_ref = refs[:5]
+    low_ref = refs[5] if norm else values_ref
+    low_turned, grad_turned, active_ref, hidden_ref = refs[-8:-4]
+    up_buffer, up_semaphores, down_buffer, down_semaphores = refs[-4:]
+    plane = place_ref[PLACE_PLANE]
+    step = pl.program_id(0)
+    count = up_source.chunks()
+
+    def order(item):
+        return 0, item
+
+    up_chunk = fetched(up_source, up_refs, up_buffer, up_semaphores, plane, order, step, count)
+    down_chunk = fetched(
+        down_source, down_refs, down_buffer, down_semaphores, plane, order, step, count
+    )
+
+    @pl.when(step == 0)
     def _():
         if norm:
             for first in range(0, values_ref.shape[0], QUERY_ROWS):
                 rows = slice(first, first + QUERY_ROWS)
                 low_ref[rows, :] = normalize(
-                    values_ref[rows, :], gain_ref[...], shift_ref[...]
+                    values_ref[rows, :], vectors_ref[4:5, :], vectors_ref[5:6, :]
                 ).astype(BF16)
         low_turned[...] = low_ref[...].T
         grad_turned[...] = grad_ref[...].T
         out_ref[...] = jnp.zeros_like(out_ref)
         back_ref[...] = jnp.zeros_like(back_ref)
 
-    up = up_ref[0]
-    down = down_ref[0]
+    up = up_chunk[...]
+    down = down_chunk[...]
     total = jnp.zeros((1, up.shape[1]), F32)
-    pieces = low_ref.shape[0] // QUERY_ROWS
+    pieces = low_ref.shape[0] // FEED_ROWS
     for piece in range(pieces):
-        rows = slice(piece * QUERY_ROWS, (piece + 1) * QUERY_ROWS)
+        rows = slice(piece * FEED_ROWS, (piece + 1) * FEED_ROWS)
         active, derivative = gelu_parts(dot(low_ref[rows, :], up) + bias_ref[0])
         active_low = active.astype(BF16)
         hidden_low = (derivative * dot(grad_ref[rows, :], down)).astype(BF16)
@@ -354,23 +472,24 @@
         out_ref[rows, :] += dot_last(active_low, down)
         back_ref[rows, :] += dot_last(hidden_low, up)
     grad_bias_ref[0] = total
-    for piece in range(low_turned.shape[0] // QUERY_ROWS):
-        rows = slice(piece * QUERY_ROWS, (piece + 1) * QUERY_ROWS)
+    for piece in range(low_turned.shape[0] // FEED_ROWS):
+        rows = slice(piece * FEED_ROWS, (piece + 1) * FEED_ROWS)
         grad_down_ref[0, rows, :] = dot(grad_turned[rows, :], active_ref[...]).astype(BF16)
         grad_up_ref[0, rows, :] = dot(low_turned[rows, :], hidden_ref[...]).astype(BF16)
 
 
-def feed_half(place, values, grad, ups, downs, bias, norm=None):
+def feed_half(place, values, grad, vectors, bias, slots, side, norm):
     row_count, model = values.shape
-    steps, _, width = ups.shape
+    up_source = Source(slots, 2, (side,))
+    down_source = Source(slots, 3, (side,))
+    steps = up_source.chunks()
+    width = up_source.shape[2]
 
     def whole(shape):
         return pl.BlockSpec(shape, lambda step, place: (0, 0), pipeline_mode=pl.Buffered(1))
 
     total = pl.BlockSpec((row_count, model), lambda step, place: (0, 0))
     chunk = pl.BlockSpec((1, model, width), lambda step, place: (step, 0, 0))
-    in_specs = [whole((row_count, model))]
-    operands = [values]
     out_specs = [
         total,
         total,
@@ -385,40 +504,44 @@
         jax.ShapeDtypeStruct((steps, model, width), BF16),
         jax.ShapeDtypeStruct((steps, 1, width), F32),
     ]
-    if norm is not None:
-        in_specs += [whole((1, model))] * 2
-        operands += [norm[0].reshape(1, model), norm[1].reshape(1, model)]
+    if norm:
         out_specs.append(total)
         out_shape.append(jax.ShapeDtypeStruct((row_count, model), BF16))
-    in_specs += [
-        whole((row_count, model)),
-        chunk,
-        chunk,
-        pl.BlockSpec((1, 1, width), lambda step, place: (2 * (step ^ place[1]) + place[0], 0, 0)),
-    ]
-    operands += [grad, ups, downs, bias.reshape(-1, 1, width)]
     return pl.pallas_call(
-        functools.partial(feed_kernel, norm=norm is not None),
+        functools.partial(
+            feed_kernel, norm=norm, up_source=up_source, down_source=down_source
+        ),
         grid_spec=pltpu.PrefetchScalarGridSpec(
             num_scalar_prefetch=1,
             grid=(steps,),
-            in_specs=in_specs,
+            in_specs=[
+                whole((row_count, model)),
+                whole((row_count, model)),
+                whole((VECTOR_ROWS, model)),
+                pl.BlockSpec(
+                    (1, 1, width), lambda step, place: (2 * (step ^ place[1]) + place[0], 0, 0)
+                ),
+            ]
+            + up_source.specs()
+            + down_source.specs(),
             out_specs=out_specs,
             scratch_shapes=[
                 pltpu.VMEM((model, row_count), BF16),
                 pltpu.VMEM((model, row_count), BF16),
                 pltpu.VMEM((row_count, width), BF16),
                 pltpu.VMEM((row_count, width), BF16),
-            ],
+            ]
+            + up_source.scratch()
+            + down_source.scratch(),
         ),
         out_shape=out_shape,
-        compiler_params=pltpu.CompilerParams(vmem_limit_bytes=58 << 20),
+        compiler_params=pltpu.CompilerParams(vmem_limit_bytes=60 << 20),
         cost_estimate=SMALL,
-    )(place, *operands)
-
-
-def norm_back_kernel(*refs, count):
-    values_ref, gain_ref, stream_ref = refs[:3]
+    )(place, values, grad, vectors, bias, *up_source.operands, *down_source.operands)
+
+
+def norm_back_kernel(*refs, count, row):
+    values_ref, vectors_ref, stream_ref = refs[:3]
     grad_refs = refs[3 : 3 + count]
     out_ref, low_ref, sums_ref = refs[3 + count :]
     values = values_ref[...].astype(F32)
@@ -428,7 +551,7 @@
     centred = values - jnp.mean(values, axis=-1, keepdims=True)
     inverse = lax.rsqrt(jnp.mean(centred * centred, axis=-1, keepdims=True) + NORM_EPS)
     normal = centred * inverse
-    scaled = grad * gain_ref[...]
+    scaled = grad * vectors_ref[row : row + 1, :]
     product = scaled * normal
     back = inverse * (
         scaled
@@ -450,13 +573,13 @@
     sums_ref[3:4, :] += jnp.sum(stream_ref[...].astype(F32), axis=0, keepdims=True)
 
 
-def norm_back(values, gain, stream, grads):
+def norm_back(values, vectors, row, stream, grads):
     row_count, model = values.shape
     panel = pl.BlockSpec((QUERY_ROWS, model), lambda step: (step, 0))
     return pl.pallas_call(
-        functools.partial(norm_back_kernel, count=len(grads)),
+        functools.partial(norm_back_kernel, count=len(grads), row=row),
         grid=(row_count // QUERY_ROWS,),
-        in_specs=[panel, pl.BlockSpec((1, model), lambda step: (0, 0)), panel]
+        in_specs=[panel, pl.BlockSpec((VECTOR_ROWS, model), lambda step: (0, 0)), panel]
         + [panel] * len(grads),
         out_specs=[panel, panel, pl.BlockSpec((8, model), lambda step: (0, 0))],
         out_shape=[
@@ -464,171 +587,182 @@
             jax.ShapeDtypeStruct((row_count, model), BF16),
             jax.ShapeDtypeStruct((8, model), F32),
         ],
-        compiler_params=pltpu.CompilerParams(vmem_limit_bytes=40 << 20),
+        compiler_params=pltpu.CompilerParams(vmem_limit_bytes=60 << 20),
         cost_estimate=SMALL,
-    )(values, gain.reshape(1, model), stream, *grads)
-
-
-def project_kernel(*refs, norm, residual):
-    refs = list(refs[1:])
+    )(values, vectors, stream, *grads)
+
+
+def project_kernel(*refs, source, block, lines, norm, residual):
+    refs = list(refs)
+    place_ref = refs.pop(0)
     values_ref = refs.pop(0)
-    if norm:
-        gain_ref = refs.pop(0)
-        shift_ref = refs.pop(0)
-    here_ref, away_ref, bias_ref, scale_ref = refs[:4]
-    refs = refs[4:]
-    if residual:
-        residual_ref = refs.pop(0)
+    vectors_ref = refs.pop(0)
+    residual_ref = refs.pop(0) if residual else None
+    source_refs = refs[: len(source.operands)]
+    refs = refs[len(source_refs) :]
     out_ref = refs.pop(0)
-    source = values_ref
-    if norm:
-        low_ref = refs.pop(0)
-        source = low_ref
-
-        @pl.when((pl.program_id(0) == 0) & (pl.program_id(1) == 0))
+    low_ref = refs.pop(0) if norm is not None else values_ref
+    buffer, semaphores = refs
+    model = values_ref.shape[1]
+    width = out_ref.shape[1]
+    parts = model // (2 * width)
+    item = pl.program_id(0)
+    count = 2 * parts * len(lines)
+
+    def order(item):
+        return item % 2, (block * parts + item // 2) ^ place_ref[1]
+
+    columns_ref = fetched(
+        source, source_refs, buffer, semaphores, place_ref[PLACE_PLANE], order, item, count
+    )
+    if norm is not None:
+
+        @pl.when(item == 0)
         def _():
             for first in range(0, values_ref.shape[0], QUERY_ROWS):
                 rows = slice(first, first + QUERY_ROWS)
                 low_ref[rows, :] = normalize(
-                    values_ref[rows, :].astype(F32), gain_ref[...], shift_ref[...]
+                    values_ref[rows, :].astype(F32),
+                    vectors_ref[norm : norm + 1, :],
+                    vectors_ref[norm + 1 : norm + 2, :],
                 ).astype(BF16)
 
-    def product(columns_ref):
-        columns = columns_ref[0]
-        row_count = values_ref.shape[0]
-        step = min(QUERY_ROWS, row_count // 2)
-        for first in range(0, row_count, step):
-            rows = slice(first, first + step)
-            made = (dot(source[rows, :], columns) + bias_ref[0]) * scale_ref[0]
-            if residual:
-                made = residual_ref[rows, :].astype(F32) + made
-            out_ref[rows, :] = made.astype(out_ref.dtype)
-
-    @pl.when(pl.program_id(1) == 0)
-    def _():
-        product(here_ref)
-
-    @pl.when(pl.program_id(1) == 1)
-    def _():
-        product(away_ref)
+    inside = item // 2 % parts
+    column = (2 * inside + (item % 2 ^ place_ref[0])) * width
+    row_count = values_ref.shape[0]
+    step = row_count // 2
+    for number, (line, scale) in enumerate(lines):
+
+        @pl.when(item // (2 * parts) == number)
+        def _(line=line, scale=scale):
+            columns = columns_ref[...]
+            for first in range(0, row_count, step):
+                rows = slice(first, first + step)
+                made = dot(low_ref[rows, :], columns)
+                if line is not None:
+                    made = made + vector_part(vectors_ref, line, column, width)
+                if scale != 1.0:
+                    made = made * scale
+                if residual:
+                    made = residual_ref[rows, :].astype(F32) + made
+                out_ref[rows, :] = made.astype(out_ref.dtype)
 
 
 def project(
-    place, values, here, away, block, bias, scale=None, norm=None, residual=None, out_type=BF16
+    place, values, vectors, slots, group, block, lines, norm=None, residual=None, out_type=BF16
 ):
     row_count, model = values.shape
-    width = here.shape[2]
+    source = Source(slots, group, (0, 1))
+    width = source.shape[2]
     parts = model // (2 * width)
-    count = bias.shape[0]
-    if scale is None:
-        scale = jnp.ones_like(bias)
 
     def whole(shape):
         return pl.BlockSpec(shape, lambda *_: (0, 0), pipeline_mode=pl.Buffered(1))
 
-    def column(step, side, place):
-        return 2 * step + (side ^ place[0])
-
-    chunk = pl.BlockSpec(
-        (1, model, width),
-        lambda step, side, place: ((block * parts + step) ^ place[1], 0, 0),
-    )
-    line = pl.BlockSpec(
-        (1, 1, width), lambda step, side, place: (column(step, side, place), 0, 0)
-    )
     panel = pl.BlockSpec(
-        (row_count, width), lambda step, side, place: (0, column(step, side, place))
-    )
-    in_specs = [whole((row_count, model))]
-    operands = [values]
-    if norm is not None:
-        in_specs += [whole((1, model))] * 2
-        operands += [norm[0].reshape(1, model), norm[1].reshape(1, model)]
-    in_specs += [chunk, chunk, line, line]
-    operands += [here, away, bias.reshape(-1, 1, width), scale.reshape(-1, 1, width)]
+        (row_count, width),
+        lambda item, place: (0, 2 * (item // 2) + (item % 2 ^ place[0])),
+    )
+    in_specs = [whole((row_count, model)), whole((VECTOR_ROWS, model))]
+    operands = [values, vectors]
     if residual is not None:
         in_specs.append(panel)
         operands.append(residual)
     out_specs = [panel]
-    out_shape = [jax.ShapeDtypeStruct((row_count, count * model), out_type)]
+    out_shape = [jax.ShapeDtypeStruct((row_count, len(lines) * model), out_type)]
     if norm is not None:
         out_specs.append(pl.BlockSpec((row_count, model), lambda *_: (0, 0)))
         out_shape.append(jax.ShapeDtypeStruct((row_count, model), BF16))
     results = pl.pallas_call(
         functools.partial(
-            project_kernel, norm=norm is not None, residual=residual is not None
+            project_kernel,
+            source=source,
+            block=block,
+            lines=lines,
+            norm=norm,
+            residual=residual is not None,
         ),
         grid_spec=pltpu.PrefetchScalarGridSpec(
             num_scalar_prefetch=1,
-            grid=(count * parts, 2),
-            in_specs=in_specs,
+            grid=(2 * parts * len(lines),),
+            in_specs=in_specs + source.specs(),
             out_specs=out_specs,
+            scratch_shapes=source.scratch(),
         ),
         out_shape=out_shape,
-        compiler_params=pltpu.CompilerParams(vmem_limit_bytes=40 << 20),
+        compiler_params=pltpu.CompilerParams(vmem_limit_bytes=60 << 20),
         cost_estimate=SMALL,
-    )(place, *operands)
+    )(place, *operands, *source.operands)
     return results if norm is not None else results[0]
 
 
-def project_back_kernel(*refs, parts):
-    count = len(refs) - 5
-    grad_refs = refs[1 : 1 + count]
-    here_ref, away_ref, out_ref, total_ref = refs[1 + count :]
-    step = pl.program_id(0)
-    side = pl.program_id(1)
-
-    @pl.when((step == 0) & (side == 0))
+def project_back_kernel(*refs, source, block, count):
+    refs = list(refs)
+    place_ref = refs.pop(0)
+    grad_refs = refs[:count]
+    source_refs = refs[count : count + len(source.operands)]
+    out_ref, total_ref, buffer, semaphores = refs[count + len(source.operands) :]
+    model = out_ref.shape[1]
+    width = grad_refs[0].shape[1]
+    parts = model // (2 * width)
+    item = pl.program_id(0)
+    steps = 2 * parts * count
+
+    def order(item):
+        return item % 2, (block * parts + item // 2) ^ place_ref[1]
+
+    columns_ref = fetched(
+        source, source_refs, buffer, semaphores, place_ref[PLACE_PLANE], order, item, steps
+    )
+
+    @pl.when(item == 0)
     def _():
         total_ref[...] = jnp.zeros_like(total_ref)
 
-    for item, grad_ref in enumerate(grad_refs):
-        for which, columns_ref in enumerate((here_ref, away_ref)):
-
-            @pl.when((step // parts == item) & (side == which))
-            def _(grad_ref=grad_ref, columns_ref=columns_ref):
-                columns = columns_ref[0]
-                row_count = grad_ref.shape[0]
-                size = min(QUERY_ROWS, row_count // 2)
-                for first in range(0, row_count, size):
-                    rows = slice(first, first + size)
-                    total_ref[rows, :] += dot_last(grad_ref[rows, :], columns)
-
-    @pl.when((step == pl.num_programs(0) - 1) & (side == 1))
+    for number, grad_ref in enumerate(grad_refs):
+
+        @pl.when(item // (2 * parts) == number)
+        def _(grad_ref=grad_ref):
+            columns = columns_ref[...]
+            row_count = grad_ref.shape[0]
+            size = row_count // 2
+            for first in range(0, row_count, size):
+                rows = slice(first, first + size)
+                total_ref[rows, :] += dot_last(grad_ref[rows, :], columns)
+
+    @pl.when(item == steps - 1)
     def _():
         out_ref[...] = total_ref[...].astype(out_ref.dtype)
 
 
-def project_back(place, grads, here, away, block, out_type):
+def project_back(place, grads, slots, group, block, out_type):
     row_count, model = grads[0].shape
-    width = here.shape[2]
+    source = Source(slots, group, (0, 1))
+    width = source.shape[2]
     parts = model // (2 * width)
 
-    def grad_panel(item):
-        def index(step, side, place):
-            inside = (step // parts) == item
-            column = 2 * (step % parts) + (side ^ place[0])
-            return 0, jnp.where(inside, column, 0)
+    def grad_panel(number):
+        def index(item, place):
+            column = 2 * (item // 2 % parts) + (item % 2 ^ place[0])
+            last = 2 * (parts - 1) + (1 ^ place[0])
+            done = item // (2 * parts) > number
+            return 0, jnp.where(item // (2 * parts) == number, column, jnp.where(done, last, place[0]))
 
         return pl.BlockSpec((row_count, width), index)
 
-    chunk = pl.BlockSpec(
-        (1, model, width),
-        lambda step, side, place: ((block * parts + step) ^ place[1], 0, 0),
-    )
     return pl.pallas_call(
-        functools.partial(project_back_kernel, parts=parts),
+        functools.partial(project_back_kernel, source=source, block=block, count=len(grads)),
         grid_spec=pltpu.PrefetchScalarGridSpec(
             num_scalar_prefetch=1,
-            grid=(len(grads) * parts, 2),
-            in_specs=[grad_panel(item) for item in range(len(grads))] + [chunk, chunk],
+            grid=(2 * parts * len(grads),),
+            in_specs=[grad_panel(number) for number in range(len(grads))] + source.specs(),
             out_specs=pl.BlockSpec((row_count, model), lambda *_: (0, 0)),
-            scratch_shapes=[pltpu.VMEM((row_count, model), F32)],
+            scratch_shapes=[pltpu.VMEM((row_count, model), F32)] + source.scratch(),
         ),
         out_shape=jax.ShapeDtypeStruct((row_count, model), out_type),
-        compiler_params=pltpu.CompilerParams(vmem_limit_bytes=40 << 20),
+        compiler_params=pltpu.CompilerParams(vmem_limit_bytes=60 << 20),
         cost_estimate=SMALL,
-    )(place, *grads, here, away)
+    )(place, *grads, *source.operands)
 
 
 NEAR = ((0, 1), (1, 0), (2, 3), (3, 2))
@@ -660,32 +794,6 @@
     return bits
 
 
-def spread_first(own, plane_size):
-    return move_planes(own, ((0, 2), (1, 0), (2, 3), (3, 1)), plane_size)
-
-
-def spread_second(own, first, plane, plane_size):
-    held = jnp.where((plane == 0) | (plane == 3), own, first)
-    near = move_planes(held, NEAR, plane_size)
-    middle = move_planes(own, ((1, 2), (2, 1)), plane_size)
-    return held, near, middle
-
-
-def spread_outer(held, near, plane):
-    even = plane % 2 == 0
-    return jnp.where(even, held, near), jnp.where(even, near, held)
-
-
-def spread_inner(own, first, middle, last, plane):
-    chunk_one = jnp.where(
-        plane < 2, jnp.where(plane == 0, first, own), jnp.where(plane == 2, middle, last)
-    )
-    chunk_two = jnp.where(
-        plane < 2, jnp.where(plane == 0, last, middle), jnp.where(plane == 2, own, first)
-    )
-    return chunk_one, chunk_two
-
-
 def spread_begin(own):
     rows = own.shape[-2] // 2
     return [own[..., :rows, :], own[..., rows:, :]]
@@ -699,56 +807,20 @@
     ]
 
 
-def spread_joins(parts, got):
-    return [jnp.stack([part, item]) for part, item in zip(parts, got, strict=True)]
-
-
-def assemble_kernel(upper_ref, upper_got, lower_ref, lower_got, out_ref, *, top):
-    chunk = pl.program_id(0)
-    part = pl.program_id(1)
-    sources = (
-        ((part == 0) & (chunk < top), upper_ref),
-        ((part == 0) & (chunk >= top), upper_got),
-        ((part == 1) & (chunk % 2 == 0), lower_ref),
-        ((part == 1) & (chunk % 2 == 1), lower_got),
-    )
-    for chosen, source in sources:
-
-        @pl.when(chosen)
-        def _(source=source):
-            out_ref[0] = source[0]
-
-
-def assemble(parts, got):
-    half, width = parts[0].shape[-2:]
-    flat = [item.reshape(-1, half, width) for item in (parts[0], got[0], parts[1], got[1])]
-    top = flat[0].shape[0]
-
-    def upper(chunk, part):
-        return chunk % top, 0, 0
-
-    def lower(chunk, part):
-        place = 0
-        rest = chunk // 2
-        size = top
-        while size > 1:
-            place = place * 2 + rest % 2
-            rest = rest // 2
-            size //= 2
-        return place, 0, 0
-
-    def block(index):
-        return pl.BlockSpec((1, half, width), index)
-
-    return pl.pallas_call(
-        functools.partial(assemble_kernel, top=top),
-        grid=(2 * top, 2),
-        in_specs=[block(upper), block(upper), block(lower), block(lower)],
-        out_specs=pl.BlockSpec((1, half, width), lambda chunk, part: (chunk, part, 0)),
-        out_shape=jax.ShapeDtypeStruct((2 * top, 2 * half, width), BF16),
-        compiler_params=pltpu.CompilerParams(vmem_limit_bytes=32 << 20),
-        cost_estimate=SMALL,
-    )(*flat)
+def spread_on(parts, got, device_count):
+    for stage in range(1, len(inner_bits(device_count))):
+        parts = [jnp.stack([part, item]) for part, item in zip(parts, got, strict=True)]
+        got = spread_swaps(parts, stage, device_count)
+    return parts, got
+
+
+def swap_cores(items, device_count):
+    return [swap_bit(item, device_count, 1) for item in items]
+
+
+def flat_slot(parts, got):
+    shape = (-1,) + parts[0].shape[-2:]
+    return tuple(item.reshape(shape) for item in (parts[0], got[0], parts[1], got[1]))
 
 
 class Sum:
@@ -822,7 +894,7 @@
             * 2,
         ),
         out_shape=[jax.ShapeDtypeStruct((members, count, half, width), BF16)] * 2,
-        compiler_params=pltpu.CompilerParams(vmem_limit_bytes=32 << 20),
+        compiler_params=pltpu.CompilerParams(vmem_limit_bytes=60 << 20),
         cost_estimate=SMALL,
     )(place, *operands)
 
@@ -908,7 +980,7 @@
             jax.ShapeDtypeStruct((rows, width), F32),
             jax.ShapeDtypeStruct((rows, width), BF16),
         ],
-        compiler_params=pltpu.CompilerParams(vmem_limit_bytes=32 << 20),
+        compiler_params=pltpu.CompilerParams(vmem_limit_bytes=60 << 20),
         cost_estimate=SMALL,
     )(place, *operands)
 
@@ -939,13 +1011,18 @@
 
 
 def update_kernel(
-    grad_ref,
+    place_ref,
+    total_ref,
+    near_ref,
+    far_ref,
+    other_ref,
     weight_ref,
     average_ref,
     moment1_ref,
     moment2_ref,
     stats_ref,
     bases_ref,
+    grad_ref,
     first_ref,
     second_ref,
     new_ref,
@@ -953,89 +1030,128 @@
     copy_ref,
     new_stats_ref,
     new_bases_ref,
-    square_ref,
+    state_ref,
+    solved_ref,
+    *,
+    chunks,
 ):
     blocks = stats_ref.shape[0]
-
-    @pl.when(pl.program_id(0) == 0)
+    step = pl.program_id(0)
+    rows = weight_ref.shape[0]
+
+    @pl.when(step == 0)
     def _():
-        square_ref[...] = jnp.zeros_like(square_ref)
-
-    for block in range(blocks):
-        columns = slice(block * BLK, (block + 1) * BLK)
-        grad = grad_ref[:, columns]
-        basis = bases_ref[block]
-        turned = dot_high(grad, basis, ((1,), (0,)))
-        first = BETA_ONE * moment1_ref[:, columns] + (1.0 - BETA_ONE) * turned
-        second = BETA_TWO * moment2_ref[:, columns] + (1.0 - BETA_TWO) * turned * turned
-        first_ref[:, columns] = first
-        second_ref[:, columns] = second
-        direction = (
-            first
-            / (1.0 - BETA_ONE**STEP)
-            / (jnp.sqrt(second / (1.0 - BETA_TWO**STEP)) + ADAM_EPS)
-        )
-        returned = dot_high(direction, basis, ((1,), (1,)))
-        weight = weight_ref[:, columns]
-        updated = weight - RATE * (returned + DECAY * weight)
-        new_ref[:, columns] = updated
-        new_average_ref[:, columns] = AVERAGE * average_ref[:, columns] + (1.0 - AVERAGE) * updated
-        copy_ref[:, columns] = updated.astype(BF16)
-        square_ref[block] += dot_high(grad, grad, ((0,), (0,)))
-
-    @pl.when(pl.program_id(0) == pl.num_programs(0) - 1)
-    def _():
-        state = []
+        @pl.when(place_ref[PLACE_PLANE] == 0)
+        def _():
+            grad_ref[...] = total_ref[...] + near_ref[...].astype(F32) + far_ref[...].astype(F32)
+
+        @pl.when(place_ref[PLACE_PLANE] != 0)
+        def _():
+            grad_ref[...] = other_ref[...]
+
         for block in range(blocks):
-            renewed = BETA_TWO * stats_ref[block] + (1.0 - BETA_TWO) * square_ref[block]
+            grad = grad_ref[:, block * BLK : (block + 1) * BLK]
+            square = dot_high(grad, grad, ((0,), (0,)))
+            renewed = BETA_TWO * stats_ref[block] + (1.0 - BETA_TWO) * square
             new_stats_ref[block] = renewed
             product = dot_high(renewed, bases_ref[block], ((1,), (0,)))
             gram = dot_high(product, product, ((0,), (0,)))
-            state.append(jnp.concatenate([gram, product.T], axis=1))
-        row_index = lax.broadcasted_iota(jnp.int32, (PANEL, 2 * BLK), 0)
-        solved = [[] for _ in range(blocks)]
-        for panel in range(BLK // PANEL):
-            tops = [item[:PANEL] for item in state]
-            for row in range(PANEL):
-                lane = panel * PANEL + row
+            state_ref[block] = jnp.concatenate([gram, product.T], axis=1)
+
+    def rotate(chunk):
+        for block in range(blocks):
+            columns = slice(block * BLK, (block + 1) * BLK)
+            basis = bases_ref[block]
+            turned = dot_high(
+                grad_ref[chunk * rows : (chunk + 1) * rows, columns], basis, ((1,), (0,))
+            )
+            first = BETA_ONE * moment1_ref[:, columns] + (1.0 - BETA_ONE) * turned
+            second = BETA_TWO * moment2_ref[:, columns] + (1.0 - BETA_TWO) * turned * turned
+            first_ref[:, columns] = first
+            second_ref[:, columns] = second
+            direction = (
+                first
+                / (1.0 - BETA_ONE**STEP)
+                / (jnp.sqrt(second / (1.0 - BETA_TWO**STEP)) + ADAM_EPS)
+            )
+            returned = dot_high(direction, basis, ((1,), (1,)))
+            weight = weight_ref[:, columns]
+            updated = weight - RATE * (returned + DECAY * weight)
+            new_ref[:, columns] = updated
+            new_average_ref[:, columns] = (
+                AVERAGE * average_ref[:, columns] + (1.0 - AVERAGE) * updated
+            )
+            copy_ref[:, columns] = updated.astype(BF16)
+
+    row_index = lax.broadcasted_iota(jnp.int32, (PANEL, 2 * BLK), 0)
+    panels = BLK // PANEL
+
+    def eliminate(panel):
+        top_rows = slice(panel * PANEL, (panel + 1) * PANEL)
+        tops = [state_ref[block, top_rows, :] for block in range(blocks)]
+        for row in range(PANEL):
+            lane = panel * PANEL + row
+            for block in range(blocks):
+                top = tops[block]
+                pivot = top[row : row + 1, lane : lane + 1]
+                inverse = lax.rsqrt(pivot)
+                inverse = inverse * (1.5 - 0.5 * pivot * inverse * inverse)
+                scaled = top[row : row + 1] * inverse
+                reduced = top - (top[:, lane : lane + 1] * inverse) * scaled
+                tops[block] = jnp.where(
+                    row_index == row, scaled, jnp.where(row_index > row, reduced, top)
+                )
+        for block in range(blocks):
+            solved_ref[block, top_rows, :] = tops[block][:, BLK:]
+            if panel + 1 < panels:
+                rest = slice((panel + 1) * PANEL, BLK)
+                state_ref[block, rest, :] -= dot_high(
+                    tops[block][:, rest], tops[block], ((0,), (0,))
+                )
+
+    for chunk in range(chunks):
+
+        @pl.when(step == chunk)
+        def _(chunk=chunk):
+            rotate(chunk)
+            for panel in range(panels * chunk // chunks, panels * (chunk + 1) // chunks):
+                eliminate(panel)
+            if chunk == chunks - 1:
                 for block in range(blocks):
-                    top = tops[block]
-                    pivot = top[row : row + 1, lane : lane + 1]
-                    inverse = lax.rsqrt(pivot)
-                    inverse = inverse * (1.5 - 0.5 * pivot * inverse * inverse)
-                    scaled = top[row : row + 1] * inverse
-                    reduced = top - (top[:, lane : lane + 1] * inverse) * scaled
-                    tops[block] = jnp.where(
-                        row_index == row, scaled, jnp.where(row_index > row, reduced, top)
-                    )
-            for block in range(blocks):
-                solved[block].append(tops[block][:, BLK:])
-                if panel + 1 < BLK // PANEL:
-                    left = tops[block][:, (panel + 1) * PANEL : BLK]
-                    state[block] = state[block][PANEL:] - dot_high(
-                        left, tops[block], ((0,), (0,))
-                    )
-        for block in range(blocks):
-            new_bases_ref[block] = jnp.concatenate(solved[block], axis=0).T
-
-
-def rotated_update(grad, weights, average, moment1, moment2, stats, bases):
-    rows, width = grad.shape
-    big = pl.BlockSpec((QUERY_ROWS, width), lambda step: (step, 0))
-    small = pl.BlockSpec(stats.shape, lambda step: (0, 0, 0))
-    wide = jax.ShapeDtypeStruct(grad.shape, F32)
+                    new_bases_ref[block] = solved_ref[block].T
+
+
+def rotated_update(
+    place, total, near, far, other, weights, average, moment1, moment2, stats, bases
+):
+    rows, width = weights.shape
+    chunks = rows // QUERY_ROWS
+    whole = pl.BlockSpec(
+        (rows, width), lambda step, place: (0, 0), pipeline_mode=pl.Buffered(1)
+    )
+    big = pl.BlockSpec((QUERY_ROWS, width), lambda step, place: (step, 0))
+    small = pl.BlockSpec(stats.shape, lambda step, place: (0, 0, 0))
+    wide = jax.ShapeDtypeStruct(weights.shape, F32)
     return pl.pallas_call(
-        update_kernel,
-        grid=(rows // QUERY_ROWS,),
-        in_specs=[big] * 5 + [small] * 2,
-        out_specs=[big] * 5 + [small] * 2,
-        out_shape=[wide] * 4
-        + [jax.ShapeDtypeStruct(grad.shape, BF16)]
+        functools.partial(update_kernel, chunks=chunks),
+        grid_spec=pltpu.PrefetchScalarGridSpec(
+            num_scalar_prefetch=1,
+            grid=(chunks,),
+            in_specs=[whole] * 4 + [big] * 4 + [small] * 2,
+            out_specs=[pl.BlockSpec((rows, width), lambda step, place: (0, 0))]
+            + [big] * 5
+            + [small] * 2,
+            scratch_shapes=[
+                pltpu.VMEM(stats.shape[:2] + (2 * BLK,), F32),
+                pltpu.VMEM(stats.shape, F32),
+            ],
+        ),
+        out_shape=[wide] * 5
+        + [jax.ShapeDtypeStruct(weights.shape, BF16)]
         + [jax.ShapeDtypeStruct(stats.shape, F32)] * 2,
-        scratch_shapes=[pltpu.VMEM(stats.shape, F32)],
-        compiler_params=pltpu.CompilerParams(vmem_limit_bytes=40 << 20),
+        compiler_params=pltpu.CompilerParams(vmem_limit_bytes=60 << 20),
         cost_estimate=SMALL,
-    )(grad, weights, average, moment1, moment2, stats, bases)
+    )(place, total, near, far, other, weights, average, moment1, moment2, stats, bases)
 
 
 def adam_update(grad, values, moment1, moment2):
@@ -1088,50 +1204,46 @@
     plane_size = device_count // GROUPS
     plane = device // plane_size
     inner = (device % plane_size) // 2
-    levels = len(inner_bits(device_count))
-    here = jnp.stack([core, inner, plane % 2]).astype(jnp.int32)
-    away = jnp.stack([1 - core, inner, plane % 2]).astype(jnp.int32)
+    here = jnp.stack([core, inner, plane % 2, plane]).astype(jnp.int32)
+    away = jnp.stack([1 - core, inner, plane % 2, plane]).astype(jnp.int32)
 
     vector_shape = vectors.shape
     own = weights.astype(BF16)
-    first = spread_first(own, plane_size)
+    first = move_planes(own, ((0, 2), (1, 0), (2, 3), (3, 1)), plane_size)
+    memory_padded = jnp.pad(memory, ((0, 0), (0, SLOT_PAD - quarter), (0, 0)))
+    memory_here = lax.all_to_all(memory_padded, "mem", split_axis=0, concat_axis=0, tiled=True)
+    memory_here = memory_here.reshape(group_size * SLOT_PAD, model)
+    parts = spread_begin(own)
+    got = spread_swaps(parts, 0, device_count)
+    first, got, memory_here, own = pinned(first, got, memory_here, own)
+    held = jnp.where((plane == 0) | (plane == 3), own, first)
+    near = move_planes(held, NEAR, plane_size)
+    middle = move_planes(own, ((1, 2), (2, 1)), plane_size)
+    parts, got = spread_on(parts, got, device_count)
     pieces = jnp.broadcast_to(
         vectors.astype(BF16).reshape(1, -1), (device_count, vectors.size)
     )
     vector_pieces = exchange_vectors(pieces, *vector_shape)
-    first, vector_pieces, own = pinned(first, vector_pieces, own)
-    held, near, middle = spread_second(own, first, plane, plane_size)
-    memory_padded = jnp.pad(memory, ((0, 0), (0, SLOT_PAD - quarter), (0, 0)))
-    memory_here = lax.all_to_all(memory_padded, "mem", split_axis=0, concat_axis=0, tiled=True)
-    near, middle, memory_here = pinned(near, middle, memory_here)
-    memory_here = memory_here.reshape(group_size * SLOT_PAD, model)
-    self_own, down_own = spread_outer(held, near, plane)
-    self_stack = spread_begin(self_own)
-    self_swaps = spread_swaps(self_stack, 0, device_count)
+    near, middle, first, got, vector_pieces = pinned(near, middle, first, got, vector_pieces)
+    slot_zero = flat_slot(parts, got)
+    even = plane % 2 == 0
+    parts_one = spread_begin(jnp.where(even, first, near))
+    got_one = spread_swaps(parts_one, 0, device_count)
     last = move_planes(middle, ((1, 0), (2, 3)), plane_size)
-    self_stack = spread_joins(self_stack, self_swaps)
-    for stage in range(1, levels):
-        self_swaps = spread_swaps(self_stack, stage, device_count)
-        if stage < levels - 1:
-            self_stack = spread_joins(self_stack, self_swaps)
-    self_swaps, last, down_own = pinned(self_swaps, last, down_own)
-    cross_own, up_own = spread_inner(own, first, middle, last, plane)
-    cross_stack = spread_begin(cross_own)
-    cross_stack, self_swaps = pinned(cross_stack, self_swaps)
-    cross_swaps = spread_swaps(cross_stack, 0, device_count)
-    self_here = assemble(self_stack, self_swaps)
-    self_away = swap_bit(self_here, device_count, 1)
-    cross_stack = spread_joins(cross_stack, cross_swaps)
-    cross_stack, self_away, down_own, up_own = pinned(cross_stack, self_away, down_own, up_own)
-    for stage in range(1, levels):
-        cross_swaps = spread_swaps(cross_stack, stage, device_count)
-        if stage < levels - 1:
-            cross_stack = spread_joins(cross_stack, cross_swaps)
-    down_stack = spread_begin(down_own)
-    down_swaps = spread_swaps(down_stack, 0, device_count)
-    up_stack = spread_begin(up_own)
-    up_swaps = spread_swaps(up_stack, 0, device_count)
+    zero_away = swap_cores(slot_zero, device_count)
     vector_rows = jnp.swapaxes(vector_pieces, 0, 1).reshape(vector_shape[0], model).astype(F32)
+    table = jnp.pad(vector_rows, ((0, VECTOR_ROWS - vector_shape[0]), (0, 0)))
+    got_one, zero_away, vector_rows, table = pinned(got_one, zero_away, vector_rows, table)
+    parts_one, got_one = spread_on(parts_one, got_one, device_count)
+    one_away = swap_cores(parts_one, device_count)
+    got_one, one_away, last = pinned(got_one, one_away, last)
+    got_one_away = swap_cores(got_one, device_count)
+    parts_two = spread_begin(jnp.where((plane == 1) | (plane == 2), middle, last))
+    got_two = spread_swaps(parts_two, 0, device_count)
+    slots = [
+        (slot_zero, tuple(zero_away)),
+        (flat_slot(parts_one, got_one), flat_slot(one_away, got_one_away)),
+    ]
 
     live_rows = (jnp.arange(row_count) < page_lengths[0]).astype(F32)[:, None]
     slots_here = lax.dynamic_slice_in_dim(slot_masks, member, 1, 0).reshape(group_size, quarter)
@@ -1139,105 +1251,56 @@
     slot_bias = jnp.broadcast_to(
         jnp.where(slots_here > 0, 0.0, MASKED).astype(F32), (group_size * SLOT_PAD, LANES)
     )
-    nothing = jnp.zeros((model,), F32)
-    ones = jnp.ones((model,), F32)
-    scales = jnp.stack([scale_q * ones, ones, ones])
     pairs = HEADS // 2
     self_firsts = (0, pairs, 2 * pairs)
     cross_firsts = (0, 0, pairs)
 
     self_low, low_one = project(
-        here,
-        tokens,
-        self_here,
-        self_away,
-        0,
-        jnp.stack([vector_rows[6], nothing, vector_rows[7]]),
-        scales,
-        norm=(vector_rows[0], vector_rows[1]),
-    )
+        here, tokens, table, slots, 0, 0, ((6, scale_q), (None, 1.0), (7, 1.0)), norm=0
+    )
+    got_two, self_low = pinned(got_two, self_low)
+    parts_two, got_two = spread_on(parts_two, got_two, device_count)
+    two_away = swap_cores(parts_two, device_count)
     attended, self_log = attention_forward(self_low, self_low, self_low, self_firsts)
-    cross_swaps, down_swaps, up_swaps, attended = pinned(
-        cross_swaps, down_swaps, up_swaps, attended
-    )
-    down_stack = spread_joins(down_stack, down_swaps)
-    up_stack = spread_joins(up_stack, up_swaps)
-    for stage in range(1, levels):
-        down_swaps = spread_swaps(down_stack, stage, device_count)
-        if stage < levels - 1:
-            down_stack = spread_joins(down_stack, down_swaps)
-    cross_here = assemble(cross_stack, cross_swaps)
-    cross_away = swap_bit(cross_here, device_count, 1)
+    got_two, two_away, attended = pinned(got_two, two_away, attended)
+    got_two_away = swap_cores(got_two, device_count)
+    parts_three = spread_begin(jnp.where(even, near, first))
+    got_three = spread_swaps(parts_three, 0, device_count)
     after_self = project(
-        here,
-        attended,
-        self_here,
-        self_away,
-        3,
-        vector_rows[8:9],
-        residual=tokens,
-        out_type=F32,
-    )
-    cross_away, after_self, up_stack = pinned(cross_away, after_self, up_stack)
-    for stage in range(1, levels):
-        up_swaps = spread_swaps(up_stack, stage, device_count)
-        if stage < levels - 1:
-            up_stack = spread_joins(up_stack, up_swaps)
+        here, attended, table, slots, 0, 3, ((8, 1.0),), residual=tokens, out_type=F32
+    )
+    got_two_away, after_self = pinned(got_two_away, after_self)
+    slots.append((flat_slot(parts_two, got_two), flat_slot(two_away, got_two_away)))
     queries_cross, low_two = project(
-        here,
-        after_self,
-        cross_here,
-        cross_away,
-        0,
-        vector_rows[9:10],
-        scales[:1],
-        norm=(vector_rows[2], vector_rows[3]),
-    )
-    cross_low = project(
-        here,
-        memory_here,
-        cross_here,
-        cross_away,
-        1,
-        jnp.stack([nothing, vector_rows[10]]),
-    )
-    down_swaps, queries_cross, cross_low = pinned(down_swaps, queries_cross, cross_low)
-    down_here = assemble(down_stack, down_swaps)
-    down_away = swap_bit(down_here, device_count, 1)
+        here, after_self, table, slots, 1, 0, ((9, scale_q),), norm=2
+    )
+    got_three, queries_cross, memory_here = pinned(got_three, queries_cross, memory_here)
+    parts_three, got_three = spread_on(parts_three, got_three, device_count)
+    three_away = swap_cores(parts_three, device_count)
+    cross_low = project(here, memory_here, table, slots, 1, 1, ((None, 1.0), (10, 1.0)))
     merged, cross_log = attention_forward(
         queries_cross, cross_low, cross_low, cross_firsts, slot_bias
     )
-    up_swaps, down_away, merged = pinned(up_swaps, down_away, merged)
-    up_here = assemble(up_stack, up_swaps)
-    up_away = swap_bit(up_here, device_count, 1)
+    got_three, three_away, merged = pinned(got_three, three_away, merged)
+    got_three_away = swap_cores(got_three, device_count)
     after_cross = project(
-        here,
-        merged,
-        cross_here,
-        cross_away,
-        3,
-        vector_rows[11:12],
-        residual=after_self,
-        out_type=F32,
+        here, merged, table, slots, 1, 3, ((11, 1.0),), residual=after_self, out_type=F32
     )
     grad_low_three = (upstream.astype(F32) * live_rows).astype(BF16)
-    up_away, after_cross, grad_low_three = pinned(up_away, after_cross, grad_low_three)
-    bias_up = vector_rows[13:17].reshape(-1)
-
+    got_three_away, after_cross, grad_low_three = pinned(
+        got_three_away, after_cross, grad_low_three
+    )
+    slots.append((flat_slot(parts_three, got_three), flat_slot(three_away, got_three_away)))
+
+    bias_up = vector_rows[13:17].reshape(-1, 1, width)
     out_a, back_a, up_sent, down_sent, bias_sent, low_three = feed_half(
-        away,
-        after_cross,
-        grad_low_three,
-        up_away,
-        down_away,
-        bias_up,
-        (vector_rows[4], vector_rows[5]),
+        away, after_cross, grad_low_three, table, bias_up, slots, 1, True
     )
     up_got = swap_bit(up_sent, device_count, 1)
     down_got = swap_bit(down_sent, device_count, 1)
     low_three, up_sent, down_sent = pinned(low_three, up_sent, down_sent)
     out_b, back_b, up_kept, down_kept, bias_kept = feed_half(
-        here, low_three, grad_low_three, up_here, down_here, bias_up
+        here, low_three, grad_low_three, table, bias_up, slots, 0, False
     )
     up_got, down_got, out_b, back_b, up_kept, down_kept = pinned(
         up_got, down_got, out_b, back_b, up_kept, down_kept
@@ -1254,9 +1317,9 @@
     grad_bias_up = jnp.concatenate([bias_even, bias_odd], axis=1).reshape(4, model)
 
     grad_two, grad_low_two, sums_three = norm_back(
-        after_cross, vector_rows[4], grad_low_three, (back_a, back_b)
-    )
-    grad_merged = project_back(here, (grad_low_two,), cross_here, cross_away, 3, BF16)
+        after_cross, table, 4, grad_low_three, (back_a, back_b)
+    )
+    grad_merged = project_back(here, (grad_low_two,), slots, 1, 3, BF16)
     cross_operands = (
         queries_cross,
         cross_low,
@@ -1305,12 +1368,12 @@
         ),
         width,
     )
-    grad_normed_two = project_back(here, (grad_queries_cross,), cross_here, cross_away, 0, F32)
+    grad_normed_two = project_back(here, (grad_queries_cross,), slots, 1, 0, F32)
 
     grad_one, grad_low_one, sums_two = norm_back(
-        after_self, vector_rows[2], grad_two, (grad_normed_two,)
-    )
-    grad_attended = project_back(here, (grad_low_one,), self_here, self_away, 3, BF16)
+        after_self, table, 2, grad_two, (grad_normed_two,)
+    )
+    grad_attended = project_back(here, (grad_low_one,), slots, 0, 3, BF16)
     feed_swaps, cross_got, cross_kept, grad_attended = pinned(
         feed_swaps, cross_got, cross_kept, grad_attended
     )
@@ -1371,37 +1434,50 @@
     self_got, cross_swaps, self_kept = pinned(self_got, cross_swaps, self_kept)
     self_sum = Sum((self_kept,), (self_got,), True)
     self_sends = stage_sends(here, self_sum, device_count)
-    self_sends, grad_queries_self, cross_swaps, grad_keys_cross = pinned(
-        self_sends, grad_queries_self, cross_swaps, grad_keys_cross
+    self_sends, grad_queries_self, cross_swaps = pinned(
+        self_sends, grad_queries_self, cross_swaps
     )
     self_swaps = stage_swaps(self_sends, self_sum, device_count)
     cross_sum = finish_stages(here, cross_sum.joined(cross_swaps), device_count)
-    cross_total, cross_sent = plane_totals(here, cross_sum)
-    cross_got = move_planes(cross_sent, ((0, 1), (3, 2)), plane_size)
     grad_normed_one = project_back(
         here,
         (grad_queries_self, grad_keys_self, grad_values_self),
-        self_here,
-        self_away,
+        slots,
+        0,
         0,
         F32,
     )
-    memory_back = project_back(
-        here, (grad_keys_cross, grad_values_cross), cross_here, cross_away, 1, BF16
-    )
-    self_swaps, grad_normed_one, memory_back = pinned(self_swaps, grad_normed_one, memory_back)
+    grad_normed_one, cross_swaps = pinned(grad_normed_one, cross_sum.swaps)
+    cross_sum.swaps = list(cross_swaps)
+    cross_total, cross_sent = plane_totals(here, cross_sum)
+    self_swaps, cross_sent, grad_normed_one = pinned(self_swaps, cross_sent, grad_normed_one)
+    cross_got = move_planes(cross_sent, ((0, 1), (3, 2)), plane_size)
     self_sum = self_sum.joined(self_swaps)
     self_sends = stage_sends(here, self_sum, device_count)
-    self_sends, grad_normed_one, memory_back = pinned(self_sends, grad_normed_one, memory_back)
+    self_sends, grad_normed_one = pinned(self_sends, grad_normed_one)
     self_swaps = stage_swaps(self_sends, self_sum, device_count)
-    input_grad, _, sums_one = norm_back(tokens, vector_rows[0], grad_one, (grad_normed_one,))
-    self_swaps, sums_one = pinned(self_swaps, sums_one)
+    input_grad, _, sums_one = norm_back(tokens, table, 0, grad_one, (grad_normed_one,))
+    self_swaps, cross_got, sums_one, grad_keys_cross = pinned(
+        self_swaps, cross_got, sums_one, grad_keys_cross
+    )
     self_sum = finish_stages(here, self_sum.joined(self_swaps), device_count)
     self_total, self_sent = plane_totals(here, self_sum)
-    self_sent, memory_back, sums_one = pinned(self_sent, memory_back, sums_one)
+    self_sent, sums_one, grad_keys_cross = pinned(self_sent, sums_one, grad_keys_cross)
     self_got = move_planes(self_sent, ((1, 0), (3, 2)), plane_size)
     cross_total = cross_total + cross_got.astype(F32)
-    cross_got = move_planes(cross_total.astype(BF16), ((2, 1),), plane_size)
+    cross_sent, grad_keys_cross = pinned(cross_total.astype(BF16), grad_keys_cross)
+    cross_got = move_planes(cross_sent, ((2, 1),), plane_size)
+    memory_back = project_back(
+        here, (grad_keys_cross, grad_values_cross), slots, 1, 1, BF16
+    )
+    memory_back = lax.all_to_all(
+        memory_back.reshape(group_size, SLOT_PAD, model),
+        "mem",
+        split_axis=0,
+        concat_axis=0,
+        tiled=True,
+    )
+    memory_back = memory_back[:, :quarter].astype(F32)
     vector_head = jnp.stack(
         [
             sums_one[0],
@@ -1427,26 +1503,20 @@
     vector_parts = exchange_vectors(vector_terms.reshape(device_count, -1), *vector_shape)
     vector_grad = jnp.sum(vector_parts, axis=0)
 
-    self_got, vector_grad = pinned(self_got, vector_grad)
-    self_total = self_total + self_got.astype(F32)
-    self_sent, memory_back = pinned(self_total.astype(BF16), memory_back)
-    self_got = move_planes(self_sent, ((2, 0),), plane_size)
-    memory_back = lax.all_to_all(
-        memory_back.reshape(group_size, SLOT_PAD, model),
-        "mem",
-        split_axis=0,
-        concat_axis=0,
-        tiled=True,
-    )
-    memory_back = memory_back[:, :quarter].astype(F32)
+    self_got, cross_got, feed_got = pinned(self_got, cross_got, feed_got)
+    self_sent = (self_total + self_got.astype(F32)).astype(BF16)
+    self_sent, cross_got, feed_got = pinned(self_sent, cross_got, feed_got)
+    self_far = move_planes(self_sent, ((2, 0),), plane_size)
     group_other = jnp.where(
         plane < 2,
         cross_total + cross_got.astype(F32),
         feed_kept + feed_got.astype(F32),
     )
-    group_other, self_got, memory_back = pinned(group_other, self_got, memory_back)
-    weight_grad = jnp.where(plane == 0, self_total + self_got.astype(F32), group_other)
+    group_other, self_far, memory_back, vector_grad, mixed = pinned(
+        group_other, self_far, memory_back, vector_grad, mixed
+    )
     (
+        weight_grad,
         weight_first,
         weight_second,
         new_weights,
@@ -1455,7 +1525,17 @@
         new_stats,
         new_bases,
     ) = rotated_update(
-        weight_grad, weights, weight_average, weight_moment1, weight_moment2, stats, bases
+        here,
+        self_total,
+        self_got,
+        self_far,
+        group_other,
+        weights,
+        weight_average,
+        weight_moment1,
+        weight_moment2,
+        stats,
+        bases,
     )
     vector_first, vector_second, new_vectors = adam_update(
         vector_grad, vectors, vector_moment1, vector_moment2

time: 751 us -> 698 us (0.929)
  local copies, waits for them, and re-layouts: 94.8 us -> 31 us
  Pallas kernels: 364 us -> 385 us
  waiting for transfers between devices: 128 us -> 111 us
  matrix products: 26.1 us -> 35.4 us
  starting transfers between devices: 67.5 us -> 75.3 us
    unnamed x306 -> x186, local copies, waits for them, and re-layouts: 71 us -> 13.3 us
    all_to_all x1, waiting for transfers between devices: 17.2 us -> 0.01 us  [local(): lax.all_to_all(memory_padded, 'mem', split_axis=0, concat_axis=0, tiled=T...]
    ppermute x36 -> x48, waiting for transfers between devices: 43.5 us -> 56.6 us  [swap_bit(): lax.ppermute(values, AXES, [(item, item ^ bit) for item in range(device_c...]
    pallas_call x20 -> x16, Pallas kernels: 221 us -> 233 us  [the longest x2 76.2 us: feed_half(): pl.pallas_call(functools.partial(feed_kernel, norm=norm, up_source=up_sou...]
    all_to_all x2, waiting for transfers between devices: 34 us -> 23.2 us  [exchange_vectors(): got = lax.all_to_all(padded, AXES, split_axis=0, concat_axis=0, tiled=True)]
    dot_general x16, matrix products: 26.1 us -> 35.4 us  [dot_rows(): lax.dot_general(left, right, CONTRACT_ROWS, preferred_element_type=F32)]
    concatenate x16, local copies, waits for them, and re-layouts: 9.93 us -> 1.48 us  [local(): vector_terms = jnp.concatenate([vector_head, grad_bias_up], axis=0)]
    ppermute x36 -> x48, starting transfers between devices: 28.9 us -> 34.9 us  [swap_bit(): lax.ppermute(values, AXES, [(item, item ^ bit) for item in range(device_c...]
  transfers between devices with their start and end apart: 50 -> 62, of which waited for: 15 -> 15; matrix products, arithmetic and copies ran while one was open for 12% -> 13% of each run, Pallas kernels for 34% -> 42%
where the time goes in v5:
time: 698 us; the launch traced here: 691 us
  Pallas kernels  385 us (55%)
  waiting for transfers between devices  111 us (16%)
  starting transfers between devices  75.3 us (11%)
  other arithmetic  50.5 us (7%)
  matrix products  35.4 us (5%)
  local copies, waits for them, and re-layouts  31 us (4%)
    pallas_call x2, Pallas kernels, feed_half(): pl.pallas_call(functools.partial(feed_kernel, norm=norm, up_source=up_sou...  76.2 us
    pallas_call x4, Pallas kernels, attention_backward(): pl.pallas_call(functools.partial(attention_backward_kernel, causal=causal...  70.4 us
    ppermute x48, waiting for transfers between devices, swap_bit(): lax.ppermute(values, AXES, [(item, item ^ bit) for item in range(device_c...  56.6 us
    pallas_call x5, Pallas kernels, project(): pl.pallas_call(functools.partial(project_kernel, source=source, block=blo...  50 us
    pallas_call x5, Pallas kernels, project_back(): pl.pallas_call(functools.partial(project_back_kernel, source=source, bloc...  48.8 us
    pallas_call x2, Pallas kernels, attention_forward(): pl.pallas_call(functools.partial(attention_forward_kernel, causal=causal)...  36.8 us
    dot_general x16, matrix products, dot_rows(): lax.dot_general(left, right, CONTRACT_ROWS, preferred_element_type=F32)  35.4 us
    ppermute x48, starting transfers between devices, swap_bit(): lax.ppermute(values, AXES, [(item, item ^ bit) for item in range(device_c...  34.9 us
  transfers between devices with their start and end apart: 62, of which 15 were waited for; matrix products, arithmetic and copies ran while one was open for 13% of the time, Pallas kernels for 42%

profile of v5, /device:TPU:0, one launch (start us, length us, event | category | flops | bytes accessed | tf_op | source)
XLA Modules:
  0.0 691.2 jit_solution(17100080600252832491)
XLA Ops:
  3.5 4.0 collective-permute-start
  18.7 11.0 %collective-permute-done.2 = bf16[512,512]{1,0:T(8,128)(2,1)S(1)} collective-permute-done((bf16[512,512]{1,0:T(8,128)(2,1)}, bf16[512,512]{1,0:T(8,128)(2,1)S(1)}, u32[]{:S(2)}, u32[]{:S(2)}) %collective-permute-start.2) | collective-permute-done | bytes 524320 | tf_op jit(solution)/shard_map/ppermute | solution.py:776
  29.7 11.4 %collective-permute-done.1 = bf16[512,512]{1,0:T(8,128)(2,1)S(1)} collective-permute-done((bf16[512,512]{1,0:T(8,128)(2,1)}, bf16[512,512]{1,0:T(8,128)(2,1)S(1)}, u32[]{:S(2)}, u32[]{:S(2)}) %collective-permute-start.1) | collective-permute-done | bytes 524320 | tf_op jit(solution)/shard_map/ppermute | solution.py:776
  50.2 5.4 all-to-all-start.1
  55.7 23.2 %all-to-all-done.1 = bf16[32,16,128]{2,1,0:T(8,128)(2,1)S(1)} async-done(((bf16[32,16,128]{2,1,0:T(8,128)(2,1)}), bf16[32,16,128]{2,1,0:T(8,128)(2,1)S(1)}, u32[]{:S(2)}, u32[]{:S(2)}) %all-to-all-start.1) | async-done | bytes 131104 | tf_op jit(solution)/shard_map/all_to_all | solution.py:1174
  88.2 10.3 %collective-permute-done.10 = bf16[512,512]{1,0:T(8,128)(2,1)} collective-permute-done((bf16[512,512]{1,0:T(8,128)(2,1)}, bf16[512,512]{1,0:T(8,128)(2,1)}, u32[]{:S(2)}, u32[]{:S(2)}) %collective-permute-start.10) | collective-permute-done | bytes 524320 | tf_op jit(solution)/shard_map/ppermute | solution.py:776
  103.8 10.2 %collective-permute-done.19 = bf16[1024,512]{1,0:T(8,128)(2,1)} collective-permute-done((bf16[1024,512]{1,0:T(8,128)(2,1)}, bf16[1024,512]{1,0:T(8,128)(2,1)}, u32[]{:S(2)}, u32[]{:S(2)}) %collective-permute-start.19) | collective-permute-done | bytes 1048608 | tf_op jit(solution)/shard_map/ppermute | solution.py:785
  113.9 12.8 %collective-permute-done.16.refs_6_.refs_7_.refs_22_.refs_23_.refs_21_.refs_5_ = bf16[2,512,512]{2,1,0:T(8,128)(2,1)} collective-permute-done((bf16[2,512,512]{2,1,0:T(8,128)(2,1)S(1)}, bf16[2,512,512]{2,1,0:T(8,128)(2,1)}, u32[]{:S(2)}, u32[]{:S(2)}) %collective-permute-start.16) | collective-permute-done | bytes 1048608 | tf_op jit(solution)/shard_map/ppermute | solution.py:776
  134.3 15.5 %shard_map.286 = (bf16[1024,3072]{1,0:T(8,128)(2,1)}, bf16[1024,1024]{1,0:T(8,128)(2,1)}) custom-call(s32[4]{0:T(128)} %add_add_fusion.refs_0_.place_ref, bf16[1024,1024]{1,0:T(8,128)(2,1)} %refs_0_.1, f32[24,1024]{1,0:T(8,128)} %pad.28.refs_2_.refs_3_.refs_1_, bf16[2,512,512]{2,1,0:T(8,128)(2,1)} %copy-done.6, ...), custom_call_target="tpu_custom_call" | custom-call | flops 1048576 | bytes 65536 | tf_op jit(solution)/shard_map/pallas_call | solution.py:676
  152.8 17.7 %shard_map.287 = (bf16[1024,1024]{1,0:T(8,128)(2,1)}, f32[8,8,1024]{2,1,0:T(8,128)}) custom-call(bf16[1024,3072]{1,0:T(8,128)(2,1)} %get-tuple-element.255.refs_0_.refs_1_.refs_2_.refs_3_, bf16[1024,3072]{1,0:T(8,128)(2,1)} %get-tuple-element.255.refs_0_.refs_1_.refs_2_.refs_3_, bf16[1024,3072]{1,0:T(8,128)(2,1)} %get-tuple-element.255.refs_0_.refs_1_.refs_2_.refs_3_), custom_call_target="tpu_custom_call" | custom-call | flops 1048576 | bytes 65536 | tf_op jit(solution)/shard_map/pallas_call | solution.py:232
  170.5 5.1 collective-permute-done.25.refs_6_.refs_7_.refs_8_.refs_5_
  182.6 7.9 %shard_map.288.refs_1_.refs_3_.refs_0_ = f32[1024,1024]{1,0:T(8,128)} custom-call(s32[4]{0:T(128)} %add_add_fusion.refs_0_.place_ref, bf16[1024,1024]{1,0:T(8,128)(2,1)} %get-tuple-element.259.refs_1_.refs_5_, f32[24,1024]{1,0:T(8,128)} %pad.28.refs_2_.refs_3_.refs_1_, bf16[1024,1024]{1,0:T(8,128)(2,1)} %refs_0_.1, bf16[2,512,512]{2,1,0:T(8,128)(2,1)} %copy-done.6, ...), custom_call_target="tpu_custom_call" | custom-call | flops 1048576 | bytes 65536 | tf_op jit(solution)/shard_map/pallas_call | solution.py:676
  192.5 9.7 %shard_map.289 = (bf16[1024,1024]{1,0:T(8,128)(2,1)}, bf16[1024,1024]{1,0:T(8,128)(2,1)}) custom-call(s32[4]{0:T(128)} %add_add_fusion.refs_0_.place_ref, f32[1024,1024]{1,0:T(8,128)} %shard_map.288.refs_1_.refs_3_.refs_0_, f32[24,1024]{1,0:T(8,128)} %pad.28.refs_2_.refs_3_.refs_1_, bf16[2,512,512]{2,1,0:T(8,128)(2,1)} %copy-done.9, ...), custom_call_target="tpu_custom_call" | custom-call | flops 1048576 | bytes 65536 | tf_op jit(solution)/shard_map/pallas_call | solution.py:676
  206.5 8.5 %shard_map.290.refs_1_.refs_2_.refs_3_ = bf16[640,2048]{1,0:T(8,128)(2,1)} custom-call(s32[4]{0:T(128)} %add_add_fusion.refs_0_.place_ref, bf16[640,1024]{1,0:T(8,128)(2,1)} %bitcast.113, f32[24,1024]{1,0:T(8,128)} %pad.28.refs_2_.refs_3_.refs_1_, bf16[2,512,512]{2,1,0:T(8,128)(2,1)} %copy-done.9, ...), custom_call_target="tpu_custom_call" | custom-call | flops 1048576 | bytes 65536 | tf_op jit(solution)/shard_map/pallas_call | solution.py:676
  215.9 19.1 %shard_map.291 = (bf16[1024,1024]{1,0:T(8,128)(2,1)}, f32[8,8,1024]{2,1,0:T(8,128)}) custom-call(bf16[1024,1024]{1,0:T(8,128)(2,1)} %get-tuple-element.269.refs_0_.refs_1_, bf16[640,2048]{1,0:T(8,128)(2,1)} %shard_map.290.refs_1_.refs_2_.refs_3_, bf16[640,2048]{1,0:T(8,128)(2,1)} %shard_map.290.refs_1_.refs_2_.refs_3_, ...), custom_call_target="tpu_custom_call" | custom-call | flops 1048576 | bytes 65536 | tf_op jit(solution)/shard_map/pallas_call | solution.py:232
  240.8 8.4 %shard_map.292.refs_1_.refs_0_ = f32[1024,1024]{1,0:T(8,128)} custom-call(s32[4]{0:T(128)} %add_add_fusion.refs_0_.place_ref, bf16[1024,1024]{1,0:T(8,128)(2,1)} %get-tuple-element.274.refs_1_.refs_5_, f32[24,1024]{1,0:T(8,128)} %pad.28.refs_2_.refs_3_.refs_1_, f32[1024,1024]{1,0:T(8,128)} %shard_map.288.refs_1_.refs_3_.refs_0_, ...), custom_call_target="tpu_custom_call" | custom-call | flops 1048576 | bytes 65536 | tf_op jit(solution)/shard_map/pallas_call | solution.py:676
  251.1 38.8 %shard_map.293 = (f32[1024,1024]{1,0:T(8,128)}, f32[1024,1024]{1,0:T(8,128)}, bf16[4,1024,512]{2,1,0:T(8,128)(2,1)}, bf16[4,1024,512]{2,1,0:T(8,128)(2,1)}, f32[...) custom-call(s32[4]{0:T(128)} %add_add_fusion.1.refs_0_, f32[1024,1024]{1,0:T(8,128)} %shard_map.292.refs_1_.refs_0_, ...), custom_call_target="tpu_custom_call" | custom-call | flops 1048576 | bytes 65536 | tf_op jit(solution)/shard_map/pallas_call | solution.py:510
  290.5 37.3 %shard_map.294 = (f32[1024,1024]{1,0:T(8,128)}, f32[1024,1024]{1,0:T(8,128)}, bf16[4,1024,512]{2,1,0:T(8,128)(2,1)}, bf16[4,1024,512]{2,1,0:T(8,128)(2,1)}, f32[4,1,512]{2,1,0:T(1,128)}) custom-call(s32[4]{0:T(128)} %add_add_fusion.refs_0_.place_ref, bf16[1024,1024]{1,0:T(8,128)(2,1)} %get-tuple-element.285.refs_1_, ...), custom_call_target="tpu_custom_call" | custom-call | flops 1048576 | bytes 65536 | tf_op jit(solution)/shard_map/pallas_call | solution.py:510
  327.9 5.9 shard_map.295
  336.6 9.1 %shard_map.296 = (f32[1024,1024]{1,0:T(8,128)}, bf16[1024,1024]{1,0:T(8,128)(2,1)}, f32[8,1024]{1,0:T(8,128)}) custom-call(f32[1024,1024]{1,0:T(8,128)} %shard_map.292.refs_1_.refs_0_, f32[24,1024]{1,0:T(8,128)} %pad.28.refs_2_.refs_3_.refs_1_, bf16[1024,1024]{1,0:T(8,128)(2,1)} %multiply_convert_fusion.1.refs_2_, f32[1024,1024]{1,0:T(8,128)} %get-tuple-element.299.refs_3_, ...), custom_call_target="tpu_custom_call" | custom-call | flops 1048576 | bytes 65536 | tf_op jit(solution)/shard_map/pallas_call | solution.py:579
  345.7 7.8 %shard_map.297.refs_4_ = bf16[1024,1024]{1,0:T(8,128)(2,1)} custom-call(s32[4]{0:T(128)} %add_add_fusion.refs_0_.place_ref, bf16[1024,1024]{1,0:T(8,128)(2,1)} %get-tuple-element.301.refs_1_, bf16[2,512,512]{2,1,0:T(8,128)(2,1)} %copy-done.9, bf16[2,512,512]{2,1,0:T(8,128)(2,1)} %collective-permute-done.24.refs_4_.refs_5_.refs_6_.refs_3_, ...), custom_call_target="tpu_custom_call" | custom-call | flops 1048576 | bytes 65536 | tf_op jit(solution)/shard_map/pallas_call | solution.py:753
  353.5 17.8 %shard_map.298 = (bf16[1024,1024]{1,0:T(8,128)(2,1)}, bf16[640,1024]{1,0:T(8,128)(2,1)}, bf16[640,1024]{1,0:T(8,128)(2,1)}, bf16[1024,512]{1,0:T(8,128)(2,1)}, b...) custom-call(s32[4]{0:T(128)} %add_add_fusion.1.refs_0_, bf16[1024,1024]{1,0:T(8,128)(2,1)} %get-tuple-element.269.refs_0_.refs_1_, ...), custom_call_target="tpu_custom_call" | custom-call | flops 1048576 | bytes 65536 | tf_op jit(solution)/shard_map/pallas_call | solution.py:287
  371.3 17.7 %shard_map.299 = (bf16[1024,1024]{1,0:T(8,128)(2,1)}, bf16[640,1024]{1,0:T(8,128)(2,1)}, bf16[640,1024]{1,0:T(8,128)(2,1)}, bf16[1024,512]{1,0:T(8,128)(2,1)}, b...) custom-call(s32[4]{0:T(128)} %add_add_fusion.refs_0_.place_ref, ...), custom_call_target="tpu_custom_call", output_to_operand_aliasing={{0}: (8, {}), {1}: (9, {}), {2}: (10, {})} | custom-call | flops 1048576 | bytes 65536 | tf_op jit(solution)/shard_map/pallas_call | solution.py:287
  396.0 5.2 shard_map.300
  416.0 8.6 %shard_map.301.refs_3_ = f32[1024,1024]{1,0:T(8,128)} custom-call(s32[4]{0:T(128)} %add_add_fusion.refs_0_.place_ref, bf16[1024,1024]{1,0:T(8,128)(2,1)} %get-tuple-element.329.refs_1_, bf16[2,512,512]{2,1,0:T(8,128)(2,1)} %copy-done.9, bf16[2,512,512]{2,1,0:T(8,128)(2,1)} %collective-permute-done.24.refs_4_.refs_5_.refs_6_.refs_3_, ...), custom_call_target="tpu_custom_call" | custom-call | flops 1048576 | bytes 65536 | tf_op jit(solution)/shard_map/pallas_call | solution.py:753
  424.6 9.2 %shard_map.302 = (f32[1024,1024]{1,0:T(8,128)}, bf16[1024,1024]{1,0:T(8,128)(2,1)}, f32[8,1024]{1,0:T(8,128)}) custom-call(f32[1024,1024]{1,0:T(8,128)} %shard_map.288.refs_1_.refs_3_.refs_0_, f32[24,1024]{1,0:T(8,128)} %pad.28.refs_2_.refs_3_.refs_1_, f32[1024,1024]{1,0:T(8,128)} %get-tuple-element.328.refs_2_, f32[1024,1024]{1,0:T(8,128)} %shard_map.301.refs_3_), custom_call_target="tpu_custom_call" | custom-call | flops 1048576 | bytes 65536 | tf_op jit(solution)/shard_map/pallas_call | solution.py:579
  433.7 7.9 %shard_map.303.refs_4_ = bf16[1024,1024]{1,0:T(8,128)(2,1)} custom-call(s32[4]{0:T(128)} %add_add_fusion.refs_0_.place_ref, bf16[1024,1024]{1,0:T(8,128)(2,1)} %get-tuple-element.330.refs_1_, bf16[2,512,512]{2,1,0:T(8,128)(2,1)} %copy-done.6, bf16[2,512,512]{2,1,0:T(8,128)(2,1)} %collective-permute-done.15.refs_4_.refs_5_.refs_20_.refs_21_.refs_19_.refs_3_, ...), custom_call_target="tpu_custom_call" | custom-call | flops 1048576 | bytes 65536 | tf_op jit(solution)/shard_map/pallas_call | solution.py:753
  450.5 6.5 shard_map.304
  457.0 4.0 shard_map.305
  464.4 17.6 %shard_map.306 = (bf16[1024,1024]{1,0:T(8,128)(2,1)}, bf16[1024,1024]{1,0:T(8,128)(2,1)}, bf16[1024,1024]{1,0:T(8,128)(2,1)}, bf16[1024,512]{1,0:T(8,128)(2,1)},...) custom-call(s32[4]{0:T(128)} %add_add_fusion.1.refs_0_, ...), custom_call_target="tpu_custom_call" | custom-call | flops 1048576 | bytes 65536 | tf_op jit(solution)/shard_map/pallas_call | solution.py:287
  494.8 3.8 shard_map.307
  501.1 17.4 %shard_map.308 = (bf16[1024,1024]{1,0:T(8,128)(2,1)}, bf16[1024,1024]{1,0:T(8,128)(2,1)}, bf16[1024,1024]{1,0:T(8,128)(2,1)}, bf16[1024,512]{1,0:T(8,128)(2,1)},...) custom-call(s32[4]{0:T(128)} %add_add_fusion.refs_0_.place_ref, ...), custom_call_target="tpu_custom_call", output_to_operand_aliasing={{0}: (7, {}), {1}: (8, {}), {2}: (9, {})} | custom-call | flops 1048576 | bytes 65536 | tf_op jit(solution)/shard_map/pallas_call | solution.py:287
  526.1 4.0 shard_map.309
  533.0 15.3 %shard_map.310.refs_3_ = f32[1024,1024]{1,0:T(8,128)} custom-call(s32[4]{0:T(128)} %add_add_fusion.refs_0_.place_ref, bf16[1024,1024]{1,0:T(8,128)(2,1)} %get-tuple-element.376.refs_1_, bf16[1024,1024]{1,0:T(8,128)(2,1)} %get-tuple-element.377.refs_2_, bf16[1024,1024]{1,0:T(8,128)(2,1)} %get-tuple-element.378.refs_3_, bf16[2,512,512]{2,1,0:T(8,128)(2,1)} %copy-done.6, ...), custom_call_target="tpu_custom_call" | custom-call | flops 1048576 | bytes 65536 | tf_op jit(solution)/shard_map/pallas_call | solution.py:753
  548.3 5.3 shard_map.311
  555.3 3.8 collective-permute-start.53
  559.1 3.8 shard_map.312
  568.5 8.6 %shard_map.313 = (f32[1024,1024]{1,0:T(8,128)}, bf16[1024,1024]{1,0:T(8,128)(2,1)}, f32[8,1024]{1,0:T(8,128)}) custom-call(bf16[1024,1024]{1,0:T(8,128)(2,1)} %refs_0_.1, f32[24,1024]{1,0:T(8,128)} %pad.28.refs_2_.refs_3_.refs_1_, f32[1024,1024]{1,0:T(8,128)} %get-tuple-element.398.refs_2_, f32[1024,1024]{1,0:T(8,128)} %shard_map.310.refs_3_), custom_call_target="tpu_custom_call" | custom-call | flops 1048576 | bytes 65536 | tf_op jit(solution)/shard_map/pallas_call | solution.py:579
  577.1 5.4 collective-permute-done.53
  582.5 5.6 shard_map.314
  599.5 9.9 %all-to-all-start.3 = ((f32[32,8,128]{2,1,0:T(8,128)}), f32[32,8,128]{2,1,0:T(8,128)S(1)}, u32[]{:S(2)}, u32[]{:S(2)}) async-start(f32[32,8,128]{2,1,0:T(8,128)} %bitcast.49), calls=%async_computation.3 | async-start | bytes 262144 | tf_op jit(solution)/shard_map/all_to_all | solution.py:1174
  610.2 9.2 %shard_map.315 = bf16[640,1024]{1,0:T(8,128)(2,1)} custom-call(s32[4]{0:T(128)} %add_add_fusion.refs_0_.place_ref, bf16[640,1024]{1,0:T(8,128)(2,1)} %get-tuple-element.419.refs_1_, bf16[640,1024]{1,0:T(8,128)(2,1)} %get-tuple-element.420.refs_2_, bf16[2,512,512]{2,1,0:T(8,128)(2,1)} %copy-done.9, ...), custom_call_target="tpu_custom_call" | custom-call | flops 1048576 | bytes 65536 | tf_op jit(solution)/shard_map/pallas_call | solution.py:753
  619.4 3.7 all-to-all-start.2
  627.2 5.7 multiply_convert_fusion
  633.0 7.3 %all-to-all-done.2 = bf16[4,160,1024]{2,1,0:T(8,128)(2,1)S(1)} async-done(((bf16[4,160,1024]{2,1,0:T(8,128)(2,1)}), bf16[4,160,1024]{2,1,0:T(8,128)(2,1)S(1)}, u32[]{:S(2)}, u32[]{:S(2)}) %all-to-all-start.2) | async-done | bytes 1310752 | tf_op jit(solution)/shard_map/all_to_all | solution.py:1473
  641.6 4.7 add_select_fusion.other_ref
  646.2 8.3 %collective-permute-done.57.far_ref = bf16[1024,512]{1,0:T(8,128)(2,1)} collective-permute-done((bf16[1024,512]{1,0:T(8,128)(2,1)}, bf16[1024,512]{1,0:T(8,128)(2,1)}, u32[]{:S(2)}, u32[]{:S(2)}) %collective-permute-start.57) | collective-permute-done | bytes 1048608 | tf_op jit(solution)/shard_map/ppermute | solution.py:785
  659.3 31.7 %shard_map.316 = (f32[1024,512]{1,0:T(8,128)}, f32[1024,512]{1,0:T(8,128)}, f32[1024,512]{1,0:T(8,128)}, f32[1024,512]{1,0:T(8,128)}, f32[1024,512]{1,0:T(8,128)...) custom-call(s32[4]{0:T(128)} %add_add_fusion.refs_0_.place_ref, ...), custom_call_target="tpu_custom_call" | custom-call | flops 1048576 | bytes 65536 | tf_op jit(solution)/shard_map/pallas_call | solution.py:1135
  (390 shorter events, 161.2 us)
Async XLA Ops:
  3.5 37.6 %collective-permute-start = (bf16[1024,512]{1,0:T(8,128)(2,1)}, bf16[1024,512]{1,0:T(8,128)(2,1)S(1)}, u32[]{:S(2)}, u32[]{:S(2)}) collective-permute-start(bf16[1024,512]{1,0:T(8,128)(2,1)} %convert_element_type.129), channel_id=1, source_target_pairs={{0,16},{1,17},{2,18},{3,19},{4,20},{5,21},{6,22},{7,23},{8,0},{9,1... | collective-permute-start | bytes 3145736 | tf_op jit(solution)/shard_map/ppermute | solution.py:785
  9.1 32.0 %all-to-all-start = ((bf16[4,160,1024]{2,1,0:T(8,128)(2,1)}), bf16[4,160,1024]{2,1,0:T(8,128)(2,1)S(1)}, u32[]{:S(2)}, u32[]{:S(2)}) async-start(bf16[4,160,1024]{2,1,0:T(8,128)(2,1)} %pad.24), calls=%async_computation | async-start | bytes 2621440 | tf_op jit(solution)/shard_map/all_to_all | solution.py:1214
  16.7 24.4 %collective-permute-start.1 = (bf16[512,512]{1,0:T(8,128)(2,1)}, bf16[512,512]{1,0:T(8,128)(2,1)S(1)}, u32[]{:S(2)}, u32[]{:S(2)}) collective-permute-start(bf16[512,512]{1,0:T(8,128)(2,1)} %get-tuple-element.481), channel_id=1, source_target_pairs={{0,2},{1,3},{2,0},{3,1},{4,6},{5,7},{6,4},{7,5},{8,10},{9,11},{10,... | collective-permute-start | bytes 1572872 | tf_op jit(solution)/shard_map/ppermute | solution.py:776
  44.4 34.7 %collective-permute-start.3 = (bf16[1024,512]{1,0:T(8,128)(2,1)}, bf16[1024,512]{1,0:T(8,128)(2,1)}, u32[]{:S(2)}, u32[]{:S(2)}) collective-permute-start(bf16[1024,512]{1,0:T(8,128)(2,1)} %broadcast_select_fusion.1), channel_id=1, source_target_pairs={{0,8},{1,9},{2,10},{3,11},{4,12},{5,13},{6,14},{7,15},{8,0},{9,1},... | collective-permute-start | bytes 3145736 | tf_op jit(solution)/shard_map/ppermute | solution.py:785
  45.7 33.6 %collective-permute-start.6 = (bf16[2,512,512]{2,1,0:T(8,128)(2,1)S(1)}, bf16[2,512,512]{2,1,0:T(8,128)(2,1)S(1)}, u32[]{:S(2)}, u32[]{:S(2)}) collective-permute-start(bf16[2,512,512]{2,1,0:T(8,128)(2,1)S(1)} %pad_maximum_fusion.5.refs_13_.refs_14_.refs_11_.refs_23_.refs_12_), channel_id=1, source_target_pairs={{0,2},{1,3},{2,0},{3,1},{4,6},{5,7},{6,4},{7,5},{8,10},{9,11},{10,... | collective-permute-start | bytes 3145736 | tf_op jit(solution)/shard_map/ppermute | solution.py:776
  46.2 33.0 %collective-permute-start.5 = (bf16[2,512,512]{2,1,0:T(8,128)(2,1)S(1)}, bf16[2,512,512]{2,1,0:T(8,128)(2,1)}, u32[]{:S(2)}, u32[]{:S(2)}) collective-permute-start(bf16[2,512,512]{2,1,0:T(8,128)(2,1)S(1)} %pad_maximum_fusion.4.refs_11_.refs_12_.refs_9_.refs_21_.refs_10_), channel_id=1, source_target_pairs={{0,4},{1,5},{2,6},{3,7},{4,0},{5,1},{6,2},{7,3},{8,12},{9,13},{10,... | collective-permute-start | bytes 3145736 | tf_op jit(solution)/shard_map/ppermute | solution.py:776
  47.8 31.5 %collective-permute-start.4 = (bf16[1024,512]{1,0:T(8,128)(2,1)}, bf16[1024,512]{1,0:T(8,128)(2,1)}, u32[]{:S(2)}, u32[]{:S(2)}) collective-permute-start(bf16[1024,512]{1,0:T(8,128)(2,1)} %convert_element_type.129), channel_id=1, source_target_pairs={{8,16},{9,17},{10,18},{11,19},{12,20},{13,21},{14,22},{15,23},{16,... | collective-permute-start | bytes 3145736 | tf_op jit(solution)/shard_map/ppermute | solution.py:785
  49.5 36.0 %collective-permute-start.13 = (bf16[2,512,512]{2,1,0:T(8,128)(2,1)S(1)}, bf16[2,512,512]{2,1,0:T(8,128)(2,1)}, u32[]{:S(2)}, u32[]{:S(2)}) collective-permute-start(bf16[2,512,512]{2,1,0:T(8,128)(2,1)S(1)} %pad_maximum_fusion.5.refs_13_.refs_14_.refs_11_.refs_23_.refs_12_), channel_id=1, source_target_pairs={{0,1},{1,0},{2,3},{3,2},{4,5},{5,4},{6,7},{7,6},{8,9},{9,8},{10,11... | collective-permute-start | bytes 3145736 | tf_op jit(solution)/shard_map/ppermute | solution.py:776
  50.2 28.6 %all-to-all-start.1 = ((bf16[32,16,128]{2,1,0:T(8,128)(2,1)}), bf16[32,16,128]{2,1,0:T(8,128)(2,1)S(1)}, u32[]{:S(2)}, u32[]{:S(2)}) async-start(bf16[32,16,128]{2,1,0:T(8,128)(2,1)} %pad.27), calls=%async_computation.1 | async-start | bytes 262144 | tf_op jit(solution)/shard_map/all_to_all | solution.py:1174
  79.3 20.5 %collective-permute-start.12 = (bf16[2,512,512]{2,1,0:T(8,128)(2,1)}, bf16[2,512,512]{2,1,0:T(8,128)(2,1)}, u32[]{:S(2)}, u32[]{:S(2)}) collective-permute-start(bf16[2,512,512]{2,1,0:T(8,128)(2,1)} %collective-permute-done.5.refs_12_.refs_13_.refs_10_.refs_22_.refs_11_), channel_id=1, source_target_pairs={{0,1},{1,0},{2,3},{3,2},{4,5},{5,4},{6,7},{7,6},{8,9},{9,8},{10,11... | collective-permute-start | bytes 3145736 | tf_op jit(solution)/shard_map/ppermute | solution.py:776
  79.7 20.1 %collective-permute-start.14 = (bf16[2,512,512]{2,1,0:T(8,128)(2,1)S(1)}, bf16[2,512,512]{2,1,0:T(8,128)(2,1)}, u32[]{:S(2)}, u32[]{:S(2)}) collective-permute-start(bf16[2,512,512]{2,1,0:T(8,128)(2,1)S(1)} %collective-permute-done.6.refs_14_.refs_15_.refs_12_.refs_24_.refs_13_), channel_id=1, source_target_pairs={{0,1},{1,0},{2,3},{3,2},{4,5},{5,4},{6,7},{7,6},{8,9},{9,8},{10,11... | collective-permute-start | bytes 3145736 | tf_op jit(solution)/shard_map/ppermute | solution.py:776
  86.9 27.1 %collective-permute-start.19 = (bf16[1024,512]{1,0:T(8,128)(2,1)}, bf16[1024,512]{1,0:T(8,128)(2,1)}, u32[]{:S(2)}, u32[]{:S(2)}) collective-permute-start(bf16[1024,512]{1,0:T(8,128)(2,1)} %collective-permute-done.4), channel_id=1, source_target_pairs={{8,0},{9,1},{10,2},{11,3},{12,4},{13,5},{14,6},{15,7},{16,24},{17,... | collective-permute-start | bytes 3145736 | tf_op jit(solution)/shard_map/ppermute | solution.py:785
  101.1 25.7 %collective-permute-start.16 = (bf16[2,512,512]{2,1,0:T(8,128)(2,1)S(1)}, bf16[2,512,512]{2,1,0:T(8,128)(2,1)}, u32[]{:S(2)}, u32[]{:S(2)}) collective-permute-start(bf16[2,512,512]{2,1,0:T(8,128)(2,1)S(1)} %pad_maximum_fusion.7.refs_5_.refs_6_.refs_21_.refs_22_.refs_20_.refs_4_), channel_id=1, source_target_pairs={{0,2},{1,3},{2,0},{3,1},{4,6},{5,7},{6,4},{7,5},{8,10},{9,11},{10,... | collective-permute-start | bytes 3145736 | tf_op jit(solution)/shard_map/ppermute | solution.py:776
  102.6 24.1 %collective-permute-start.17 = (bf16[2,512,512]{2,1,0:T(8,128)(2,1)S(1)}, bf16[2,512,512]{2,1,0:T(8,128)(2,1)}, u32[]{:S(2)}, u32[]{:S(2)}) collective-permute-start(bf16[2,512,512]{2,1,0:T(8,128)(2,1)S(1)} %pad_maximum_fusion.6.refs_3_.refs_4_.refs_19_.refs_20_.refs_18_.refs_2_), channel_id=1, source_target_pairs={{0,1},{1,0},{2,3},{3,2},{4,5},{5,4},{6,7},{7,6},{8,9},{9,8},{10,11... | collective-permute-start | bytes 3145736 | tf_op jit(solution)/shard_map/ppermute | solution.py:776
  102.9 25.5 %collective-permute-start.15 = (bf16[2,512,512]{2,1,0:T(8,128)(2,1)S(1)}, bf16[2,512,512]{2,1,0:T(8,128)(2,1)}, u32[]{:S(2)}, u32[]{:S(2)}) collective-permute-start(bf16[2,512,512]{2,1,0:T(8,128)(2,1)S(1)} %pad_maximum_fusion.6.refs_3_.refs_4_.refs_19_.refs_20_.refs_18_.refs_2_), channel_id=1, source_target_pairs={{0,4},{1,5},{2,6},{3,7},{4,0},{5,1},{6,2},{7,3},{8,12},{9,13},{10,... | collective-permute-start | bytes 3145736 | tf_op jit(solution)/shard_map/ppermute | solution.py:776
  131.7 18.2 %collective-permute-start.21 = (bf16[512,512]{1,0:T(8,128)(2,1)}, bf16[512,512]{1,0:T(8,128)(2,1)S(1)}, u32[]{:S(2)}, u32[]{:S(2)}) collective-permute-start(bf16[512,512]{1,0:T(8,128)(2,1)} %get-tuple-element.472), channel_id=1, source_target_pairs={{0,4},{1,5},{2,6},{3,7},{4,0},{5,1},{6,2},{7,3},{8,12},{9,13},{10,... | collective-permute-start | bytes 1572872 | tf_op jit(solution)/shard_map/ppermute | solution.py:776
  150.0 20.5 %collective-permute-start.27 = (bf16[2,512,512]{2,1,0:T(8,128)(2,1)S(1)}, bf16[2,512,512]{2,1,0:T(8,128)(2,1)}, u32[]{:S(2)}, u32[]{:S(2)}) collective-permute-start(bf16[2,512,512]{2,1,0:T(8,128)(2,1)S(1)} %pad_maximum_fusion.9.refs_5_.refs_6_.refs_7_.refs_4_), channel_id=1, source_target_pairs={{0,1},{1,0},{2,3},{3,2},{4,5},{5,4},{6,7},{7,6},{8,9},{9,8},{10,11... | collective-permute-start | bytes 3145736 | tf_op jit(solution)/shard_map/ppermute | solution.py:776
  150.1 25.6 %collective-permute-start.25 = (bf16[2,512,512]{2,1,0:T(8,128)(2,1)S(1)}, bf16[2,512,512]{2,1,0:T(8,128)(2,1)S(1)}, u32[]{:S(2)}, u32[]{:S(2)}) collective-permute-start(bf16[2,512,512]{2,1,0:T(8,128)(2,1)S(1)} %pad_maximum_fusion.9.refs_5_.refs_6_.refs_7_.refs_4_), channel_id=1, source_target_pairs={{0,2},{1,3},{2,0},{3,1},{4,6},{5,7},{6,4},{7,5},{8,10},{9,11},{10,... | collective-permute-start | bytes 3145736 | tf_op jit(solution)/shard_map/ppermute | solution.py:776
  151.1 24.5 %collective-permute-start.26 = (bf16[2,512,512]{2,1,0:T(8,128)(2,1)S(1)}, bf16[2,512,512]{2,1,0:T(8,128)(2,1)}, u32[]{:S(2)}, u32[]{:S(2)}) collective-permute-start(bf16[2,512,512]{2,1,0:T(8,128)(2,1)S(1)} %pad_maximum_fusion.8.refs_3_.refs_4_.refs_5_.refs_2_), channel_id=1, source_target_pairs={{0,1},{1,0},{2,3},{3,2},{4,5},{5,4},{6,7},{7,6},{8,9},{9,8},{10,11... | collective-permute-start | bytes 3145736 | tf_op jit(solution)/shard_map/ppermute | solution.py:776
  151.3 25.5 %collective-permute-start.24 = (bf16[2,512,512]{2,1,0:T(8,128)(2,1)S(1)}, bf16[2,512,512]{2,1,0:T(8,128)(2,1)}, u32[]{:S(2)}, u32[]{:S(2)}) collective-permute-start(bf16[2,512,512]{2,1,0:T(8,128)(2,1)S(1)} %pad_maximum_fusion.8.refs_3_.refs_4_.refs_5_.refs_2_), channel_id=1, source_target_pairs={{0,4},{1,5},{2,6},{3,7},{4,0},{5,1},{6,2},{7,3},{8,12},{9,13},{10,... | collective-permute-start | bytes 3145736 | tf_op jit(solution)/shard_map/ppermute | solution.py:776
  179.8 22.5 %collective-permute-start.8 = (bf16[512,512]{1,0:T(8,128)(2,1)}, bf16[512,512]{1,0:T(8,128)(2,1)}, u32[]{:S(2)}, u32[]{:S(2)}) collective-permute-start(bf16[512,512]{1,0:T(8,128)(2,1)} %get-tuple-element.468), channel_id=1, source_target_pairs={{0,4},{1,5},{2,6},{3,7},{4,0},{5,1},{6,2},{7,3},{8,12},{9,13},{10,... | collective-permute-start | bytes 1572872 | tf_op jit(solution)/shard_map/ppermute | solution.py:776
  181.3 21.0 %collective-permute-start.7 = (bf16[512,512]{1,0:T(8,128)(2,1)}, bf16[512,512]{1,0:T(8,128)(2,1)}, u32[]{:S(2)}, u32[]{:S(2)}) collective-permute-start(bf16[512,512]{1,0:T(8,128)(2,1)} %get-tuple-element.469), channel_id=1, source_target_pairs={{0,2},{1,3},{2,0},{3,1},{4,6},{5,7},{6,4},{7,5},{8,10},{9,11},{10,... | collective-permute-start | bytes 1572872 | tf_op jit(solution)/shard_map/ppermute | solution.py:776
  203.5 31.5 %collective-permute-start.33 = (bf16[2,512,512]{2,1,0:T(8,128)(2,1)S(1)}, bf16[2,512,512]{2,1,0:T(8,128)(2,1)}, u32[]{:S(2)}, u32[]{:S(2)}) collective-permute-start(bf16[2,512,512]{2,1,0:T(8,128)(2,1)S(1)} %pad_maximum_fusion.11.refs_15_.refs_19_), channel_id=1, source_target_pairs={{0,1},{1,0},{2,3},{3,2},{4,5},{5,4},{6,7},{7,6},{8,9},{9,8},{10,11... | collective-permute-start | bytes 3145736 | tf_op jit(solution)/shard_map/ppermute | solution.py:776
  203.6 31.4 %collective-permute-start.31 = (bf16[2,512,512]{2,1,0:T(8,128)(2,1)S(1)}, bf16[2,512,512]{2,1,0:T(8,128)(2,1)S(1)}, u32[]{:S(2)}, u32[]{:S(2)}) collective-permute-start(bf16[2,512,512]{2,1,0:T(8,128)(2,1)S(1)} %pad_maximum_fusion.11.refs_15_.refs_19_), channel_id=1, source_target_pairs={{0,2},{1,3},{2,0},{3,1},{4,6},{5,7},{6,4},{7,5},{8,10},{9,11},{10,... | collective-permute-start | bytes 3145736 | tf_op jit(solution)/shard_map/ppermute | solution.py:776
  205.6 29.4 %collective-permute-start.32 = (bf16[2,512,512]{2,1,0:T(8,128)(2,1)S(1)}, bf16[2,512,512]{2,1,0:T(8,128)(2,1)}, u32[]{:S(2)}, u32[]{:S(2)}) collective-permute-start(bf16[2,512,512]{2,1,0:T(8,128)(2,1)S(1)} %pad_maximum_fusion.10.refs_13_.refs_17_), channel_id=1, source_target_pairs={{0,1},{1,0},{2,3},{3,2},{4,5},{5,4},{6,7},{7,6},{8,9},{9,8},{10,11... | collective-permute-start | bytes 3145736 | tf_op jit(solution)/shard_map/ppermute | solution.py:776
  205.8 29.2 %collective-permute-start.30 = (bf16[2,512,512]{2,1,0:T(8,128)(2,1)S(1)}, bf16[2,512,512]{2,1,0:T(8,128)(2,1)}, u32[]{:S(2)}, u32[]{:S(2)}) collective-permute-start(bf16[2,512,512]{2,1,0:T(8,128)(2,1)S(1)} %pad_maximum_fusion.10.refs_13_.refs_17_), channel_id=1, source_target_pairs={{0,4},{1,5},{2,6},{3,7},{4,0},{5,1},{6,2},{7,3},{8,12},{9,13},{10,... | collective-permute-start | bytes 3145736 | tf_op jit(solution)/shard_map/ppermute | solution.py:776
  290.0 37.9 %collective-permute-start.36 = (bf16[4,1024,512]{2,1,0:T(8,128)(2,1)}, bf16[4,1024,512]{2,1,0:T(8,128)(2,1)}, u32[]{:S(2)}, u32[]{:S(2)}) collective-permute-start(bf16[4,1024,512]{2,1,0:T(8,128)(2,1)} %get-tuple-element.282), channel_id=1, source_target_pairs={{0,1},{1,0},{2,3},{3,2},{4,5},{5,4},{6,7},{7,6},{8,9},{9,8},{10,11... | collective-permute-start | bytes 12582920 | tf_op jit(solution)/shard_map/ppermute | solution.py:776
  290.1 37.8 %collective-permute-start.37 = (bf16[4,1024,512]{2,1,0:T(8,128)(2,1)}, bf16[4,1024,512]{2,1,0:T(8,128)(2,1)}, u32[]{:S(2)}, u32[]{:S(2)}) collective-permute-start(bf16[4,1024,512]{2,1,0:T(8,128)(2,1)} %get-tuple-element.283), channel_id=1, source_target_pairs={{0,1},{1,0},{2,3},{3,2},{4,5},{5,4},{6,7},{7,6},{8,9},{9,8},{10,11... | collective-permute-start | bytes 12582920 | tf_op jit(solution)/shard_map/ppermute | solution.py:776
  333.8 62.2 %collective-permute-start.38 = (bf16[2,2,512,512]{3,2,1,0:T(8,128)(2,1)}, bf16[2,2,512,512]{3,2,1,0:T(8,128)(2,1)}, u32[]{:S(2)}, u32[]{:S(2)}) collective-permute-start(bf16[2,2,512,512]{3,2,1,0:T(8,128)(2,1)} %get-tuple-element.297), channel_id=1, source_target_pairs={{0,4},{1,5},{2,6},{3,7},{4,0},{5,1},{6,2},{7,3},{8,12},{9,13},{10,... | collective-permute-start | bytes 6291464 | tf_op jit(solution)/shard_map/ppermute | solution.py:776
  335.3 60.7 %collective-permute-start.39 = (bf16[2,2,512,512]{3,2,1,0:T(8,128)(2,1)}, bf16[2,2,512,512]{3,2,1,0:T(8,128)(2,1)}, u32[]{:S(2)}, u32[]{:S(2)}) collective-permute-start(bf16[2,2,512,512]{3,2,1,0:T(8,128)(2,1)} %get-tuple-element.298), channel_id=1, source_target_pairs={{0,2},{1,3},{2,0},{3,1},{4,6},{5,7},{6,4},{7,5},{8,10},{9,11},{10,... | collective-permute-start | bytes 6291464 | tf_op jit(solution)/shard_map/ppermute | solution.py:776
  407.1 42.4 %collective-permute-start.42 = (bf16[4,1024,512]{2,1,0:T(8,128)(2,1)}, bf16[4,1024,512]{2,1,0:T(8,128)(2,1)}, u32[]{:S(2)}, u32[]{:S(2)}) collective-permute-start(bf16[4,1024,512]{2,1,0:T(8,128)(2,1)} %pad_maximum_fusion), channel_id=1, source_target_pairs={{0,1},{1,0},{2,3},{3,2},{4,5},{5,4},{6,7},{7,6},{8,9},{9,8},{10,11... | collective-permute-start | bytes 12582920 | tf_op jit(solution)/shard_map/ppermute | solution.py:776
  414.7 34.8 %collective-permute-start.40 = (bf16[2,1,512,512]{3,2,1,0:T(8,128)(2,1)}, bf16[2,1,512,512]{3,2,1,0:T(8,128)(2,1)S(1)}, u32[]{:S(2)}, u32[]{:S(2)}) collective-permute-start(bf16[2,1,512,512]{3,2,1,0:T(8,128)(2,1)} %get-tuple-element.316), channel_id=1, source_target_pairs={{0,2},{1,3},{2,0},{3,1},{4,6},{5,7},{6,4},{7,5},{8,10},{9,11},{10,... | collective-permute-start | bytes 3145736 | tf_op jit(solution)/shard_map/ppermute | solution.py:776
  415.5 34.0 %collective-permute-start.41 = (bf16[2,1,512,512]{3,2,1,0:T(8,128)(2,1)}, bf16[2,1,512,512]{3,2,1,0:T(8,128)(2,1)}, u32[]{:S(2)}, u32[]{:S(2)}) collective-permute-start(bf16[2,1,512,512]{3,2,1,0:T(8,128)(2,1)} %get-tuple-element.317), channel_id=1, source_target_pairs={{0,4},{1,5},{2,6},{3,7},{4,0},{5,1},{6,2},{7,3},{8,12},{9,13},{10,... | collective-permute-start | bytes 3145736 | tf_op jit(solution)/shard_map/ppermute | solution.py:776
  461.0 29.4 %collective-permute-start.43 = (bf16[1024,512]{1,0:T(8,128)(2,1)}, bf16[1024,512]{1,0:T(8,128)(2,1)S(1)}, u32[]{:S(2)}, u32[]{:S(2)}) collective-permute-start(bf16[1024,512]{1,0:T(8,128)(2,1)} %get-tuple-element.339), channel_id=1, source_target_pairs={{0,8},{1,9},{2,10},{3,11},{4,12},{5,13},{6,14},{7,15},{8,0},{9,1},... | collective-permute-start | bytes 3145736 | tf_op jit(solution)/shard_map/ppermute | solution.py:785
  461.6 28.8 %collective-permute-start.44 = (bf16[1,2,512,512]{3,2,1,0:T(8,128)(2,1)}, bf16[1,2,512,512]{3,2,1,0:T(8,128)(2,1)S(1)}, u32[]{:S(2)}, u32[]{:S(2)}) collective-permute-start(bf16[1,2,512,512]{3,2,1,0:T(8,128)(2,1)} %get-tuple-element.340), channel_id=1, source_target_pairs={{0,4},{1,5},{2,6},{3,7},{4,0},{5,1},{6,2},{7,3},{8,12},{9,13},{10,... | collective-permute-start | bytes 3145736 | tf_op jit(solution)/shard_map/ppermute | solution.py:776
  463.2 27.3 %collective-permute-start.45 = (bf16[1,2,512,512]{3,2,1,0:T(8,128)(2,1)}, bf16[1,2,512,512]{3,2,1,0:T(8,128)(2,1)S(1)}, u32[]{:S(2)}, u32[]{:S(2)}) collective-permute-start(bf16[1,2,512,512]{3,2,1,0:T(8,128)(2,1)} %get-tuple-element.341), channel_id=1, source_target_pairs={{0,2},{1,3},{2,0},{3,1},{4,6},{5,7},{6,4},{7,5},{8,10},{9,11},{10,... | collective-permute-start | bytes 3145736 | tf_op jit(solution)/shard_map/ppermute | solution.py:776
  490.4 35.7 %collective-permute-start.46 = (bf16[4,1024,512]{2,1,0:T(8,128)(2,1)}, bf16[4,1024,512]{2,1,0:T(8,128)(2,1)}, u32[]{:S(2)}, u32[]{:S(2)}) collective-permute-start(bf16[4,1024,512]{2,1,0:T(8,128)(2,1)} %pad_maximum_fusion.2), channel_id=1, source_target_pairs={{0,1},{1,0},{2,3},{3,2},{4,5},{5,4},{6,7},{7,6},{8,9},{9,8},{10,11... | collective-permute-start | bytes 12582920 | tf_op jit(solution)/shard_map/ppermute | solution.py:776
  499.9 26.1 %collective-permute-start.47 = (bf16[1,1,512,512]{3,2,1,0:T(8,128)(2,1)}, bf16[1,1,512,512]{3,2,1,0:T(8,128)(2,1)S(1)}, u32[]{:S(2)}, u32[]{:S(2)}) collective-permute-start(bf16[1,1,512,512]{3,2,1,0:T(8,128)(2,1)} %get-tuple-element.361), channel_id=1, source_target_pairs={{0,2},{1,3},{2,0},{3,1},{4,6},{5,7},{6,4},{7,5},{8,10},{9,11},{10,... | collective-permute-start | bytes 1572872 | tf_op jit(solution)/shard_map/ppermute | solution.py:776
  500.7 25.4 %collective-permute-start.48 = (bf16[1,1,512,512]{3,2,1,0:T(8,128)(2,1)S(1)}, bf16[1,1,512,512]{3,2,1,0:T(8,128)(2,1)S(1)}, u32[]{:S(2)}, u32[]{:S(2)}) collective-permute-start(bf16[1,1,512,512]{3,2,1,0:T(8,128)(2,1)S(1)} %copy-done.89), channel_id=1, source_target_pairs={{0,4},{1,5},{2,6},{3,7},{4,0},{5,1},{6,2},{7,3},{8,12},{9,13},{10,... | collective-permute-start | bytes 1572872 | tf_op jit(solution)/shard_map/ppermute | solution.py:776
  530.1 23.9 %collective-permute-start.49 = (bf16[1,2,512,512]{3,2,1,0:T(8,128)(2,1)}, bf16[1,2,512,512]{3,2,1,0:T(8,128)(2,1)S(1)}, u32[]{:S(2)}, u32[]{:S(2)}) collective-permute-start(bf16[1,2,512,512]{3,2,1,0:T(8,128)(2,1)} %get-tuple-element.386), channel_id=1, source_target_pairs={{0,4},{1,5},{2,6},{3,7},{4,0},{5,1},{6,2},{7,3},{8,12},{9,13},{10,... | collective-permute-start | bytes 3145736 | tf_op jit(solution)/shard_map/ppermute | solution.py:776
  531.8 23.5 %collective-permute-start.50 = (bf16[1,2,512,512]{3,2,1,0:T(8,128)(2,1)}, bf16[1,2,512,512]{3,2,1,0:T(8,128)(2,1)S(1)}, u32[]{:S(2)}, u32[]{:S(2)}) collective-permute-start(bf16[1,2,512,512]{3,2,1,0:T(8,128)(2,1)} %get-tuple-element.387), channel_id=1, source_target_pairs={{0,2},{1,3},{2,0},{3,1},{4,6},{5,7},{6,4},{7,5},{8,10},{9,11},{10,... | collective-permute-start | bytes 3145736 | tf_op jit(solution)/shard_map/ppermute | solution.py:776
  555.3 27.2 %collective-permute-start.53 = (bf16[1024,512]{1,0:T(8,128)(2,1)}, bf16[1024,512]{1,0:T(8,128)(2,1)S(1)}, u32[]{:S(2)}, u32[]{:S(2)}) collective-permute-start(bf16[1024,512]{1,0:T(8,128)(2,1)} %get-tuple-element.397), channel_id=1, source_target_pairs={{0,8},{1,9},{2,10},{3,11},{4,12},{5,13},{6,14},{7,15},{24,16},{25,... | collective-permute-start | bytes 3145736 | tf_op jit(solution)/shard_map/ppermute | solution.py:785
  566.2 53.1 %collective-permute-start.56 = (bf16[1024,512]{1,0:T(8,128)(2,1)}, bf16[1024,512]{1,0:T(8,128)(2,1)}, u32[]{:S(2)}, u32[]{:S(2)}) collective-permute-start(bf16[1024,512]{1,0:T(8,128)(2,1)} %fusion), channel_id=1, source_target_pairs={{0,16},{1,17},{2,18},{3,19},{4,20},{5,21},{6,22},{7,23},{8,24},{9,... | collective-permute-start | bytes 3145736 | tf_op jit(solution)/shard_map/ppermute | solution.py:785
  589.5 29.9 %collective-permute-start.55 = (bf16[1024,512]{1,0:T(8,128)(2,1)}, bf16[1024,512]{1,0:T(8,128)(2,1)}, u32[]{:S(2)}, u32[]{:S(2)}) collective-permute-start(bf16[1024,512]{1,0:T(8,128)(2,1)} %fusion.1), channel_id=1, source_target_pairs={{16,8},{17,9},{18,10},{19,11},{20,12},{21,13},{22,14},{23,15}} | collective-permute-start | bytes 3145736 | tf_op jit(solution)/shard_map/ppermute | solution.py:785
  591.3 28.1 %collective-permute-start.54 = (bf16[1024,512]{1,0:T(8,128)(2,1)}, bf16[1024,512]{1,0:T(8,128)(2,1)}, u32[]{:S(2)}, u32[]{:S(2)}) collective-permute-start(bf16[1024,512]{1,0:T(8,128)(2,1)} %get-tuple-element.409), channel_id=1, source_target_pairs={{8,0},{9,1},{10,2},{11,3},{12,4},{13,5},{14,6},{15,7},{24,16},{25,... | collective-permute-start | bytes 3145736 | tf_op jit(solution)/shard_map/ppermute | solution.py:785
  599.5 19.9 %all-to-all-start.3 = ((f32[32,8,128]{2,1,0:T(8,128)}), f32[32,8,128]{2,1,0:T(8,128)S(1)}, u32[]{:S(2)}, u32[]{:S(2)}) async-start(f32[32,8,128]{2,1,0:T(8,128)} %bitcast.49), calls=%async_computation.3 | async-start | bytes 262144 | tf_op jit(solution)/shard_map/all_to_all | solution.py:1174
  619.4 20.9 %all-to-all-start.2 = ((bf16[4,160,1024]{2,1,0:T(8,128)(2,1)}), bf16[4,160,1024]{2,1,0:T(8,128)(2,1)S(1)}, u32[]{:S(2)}, u32[]{:S(2)}) async-start(bf16[4,160,1024]{2,1,0:T(8,128)(2,1)} %bitcast.118), calls=%async_computation.2 | async-start | bytes 2621440 | tf_op jit(solution)/shard_map/all_to_all | solution.py:1473
  625.9 28.6 %collective-permute-start.57 = (bf16[1024,512]{1,0:T(8,128)(2,1)}, bf16[1024,512]{1,0:T(8,128)(2,1)}, u32[]{:S(2)}, u32[]{:S(2)}) collective-permute-start(bf16[1024,512]{1,0:T(8,128)(2,1)} %add_convert_fusion), channel_id=1, source_target_pairs={{16,0},{17,1},{18,2},{19,3},{20,4},{21,5},{22,6},{23,7}} | collective-permute-start | bytes 3145736 | tf_op jit(solution)/shard_map/ppermute | solution.py:785
  (104 other events, 1210.3 us)

commit v6 on v5

--- a/solution.py
+++ b/solution.py
@@ -16,7 +16,7 @@
 FORWARD_ROWS = 512
 FEED_ROWS = 1024
 SLOT_PAD = 160
-PANEL = 8
+PANEL = 32
 GROUPS = 4
 AXES = ("seq", "mem")
 SMALL = pl.CostEstimate(flops=1 << 20, bytes_accessed=1 << 16, transcendentals=0)
@@ -54,10 +54,6 @@
     centred = values - centre
     variance = jnp.mean(centred * centred, axis=-1, keepdims=True)
     return centred * lax.rsqrt(variance + NORM_EPS) * scale_gain + offset
-
-
-def column_total(values):
-    return jnp.sum(values.astype(F32), axis=0)
 
 
 def causal_mask(scores, first_key, first_query):
@@ -124,7 +120,9 @@
 def attention_backward_kernel(*refs, causal):
     _, q_ref, k_ref, v_ref, grad_ref, out_ref, log_ref = refs[:7]
     bias_ref = None if causal else refs[7]
-    dq_ref, dk_ref, dv_ref, dq_half, dk_half, dv_half, chance_ref, score_ref = refs[-8:]
+    dq_ref, dk_ref, dv_ref, sums_ref, dq_half, dk_half, dv_half, chance_ref, score_ref = refs[-9:]
+    query_sum = jnp.zeros((1, LANES), F32)
+    value_sums = []
     keys = k_ref[...]
     values = v_ref[...]
     key_count = keys.shape[0]
@@ -173,6 +171,7 @@
         dk_half[slots, :] = grad_key
         dv_ref[slots, :] = grad_value
         dv_half[slots, :] = grad_value
+        value_sums.append(jnp.sum(grad_value.astype(F32), axis=0, keepdims=True))
 
     current = products_of(units[0])
     ended = None
@@ -209,6 +208,9 @@
         grad_query = (grad_query.astype(F32) * HEAD ** (-0.5)).astype(BF16)
         dq_ref[rows, :] = grad_query
         dq_half[rows, :] = grad_query
+        query_sum = query_sum + jnp.sum(grad_query.astype(F32), axis=0, keepdims=True)
+    sums_ref[0:1, :] = query_sum
+    sums_ref[1:2, :] = sum(value_sums[1:], value_sums[0])
 
 
 def head_pair(row_count, first):
@@ -290,19 +292,22 @@
             num_scalar_prefetch=1,
             grid=(steps,),
             in_specs=in_specs,
-            out_specs=[in_whole(count) for count in counts] + [alone(count) for count in counts],
+            out_specs=[in_whole(count) for count in counts]
+            + [in_whole(8)]
+            + [alone(count) for count in counts],
             scratch_shapes=[
                 pltpu.VMEM((4, key_rows, row_count), BF16),
                 pltpu.VMEM((2, key_count, row_count), BF16),
             ],
         ),
         out_shape=[jax.ShapeDtypeStruct((count, model), BF16) for count in counts]
+        + [jax.ShapeDtypeStruct((8, model), F32)]
         + [jax.ShapeDtypeStruct((count, model // 2), BF16) for count in counts],
         input_output_aliases=aliases,
         compiler_params=pltpu.CompilerParams(vmem_limit_bytes=60 << 20),
         cost_estimate=SMALL,
     )(half, *operands)
-    return results[:3], results[3:]
+    return results[:4], results[4:]
 
 
 PLACE_PLANE = 3
@@ -540,25 +545,36 @@
     )(place, values, grad, vectors, bias, *up_source.operands, *down_source.operands)
 
 
-def norm_back_kernel(*refs, count, row):
-    values_ref, vectors_ref, stream_ref = refs[:3]
-    grad_refs = refs[3 : 3 + count]
-    out_ref, low_ref, sums_ref = refs[3 + count :]
-    values = values_ref[...].astype(F32)
-    grad = grad_refs[0][...]
-    for grad_ref in grad_refs[1:]:
-        grad = grad + grad_ref[...]
+def norm_back_rows(values, grad, gain, stream):
+    values = values.astype(F32)
     centred = values - jnp.mean(values, axis=-1, keepdims=True)
     inverse = lax.rsqrt(jnp.mean(centred * centred, axis=-1, keepdims=True) + NORM_EPS)
     normal = centred * inverse
-    scaled = grad * vectors_ref[row : row + 1, :]
+    scaled = grad * gain
     product = scaled * normal
     back = inverse * (
         scaled
         - jnp.mean(scaled, axis=-1, keepdims=True)
         - normal * jnp.mean(product, axis=-1, keepdims=True)
     )
-    result = stream_ref[...].astype(F32) + back
+    return stream.astype(F32) + back, normal
+
+
+def row_sums(grad, normal, low, stream):
+    parts = (grad * normal, grad, low.astype(F32), stream.astype(F32))
+    return [jnp.sum(part, axis=0, keepdims=True) for part in parts]
+
+
+def norm_back_kernel(*refs, count, row):
+    values_ref, vectors_ref, stream_ref = refs[:3]
+    grad_refs = refs[3 : 3 + count]
+    out_ref, low_ref, sums_ref = refs[3 + count :]
+    grad = grad_refs[0][...]
+    for grad_ref in grad_refs[1:]:
+        grad = grad + grad_ref[...]
+    result, normal = norm_back_rows(
+        values_ref[...], grad, vectors_ref[row : row + 1, :], stream_ref[...]
+    )
     low = result.astype(BF16)
     out_ref[...] = result
     low_ref[...] = low
@@ -567,18 +583,16 @@
     def _():
         sums_ref[...] = jnp.zeros_like(sums_ref)
 
-    sums_ref[0:1, :] += jnp.sum(grad * normal, axis=0, keepdims=True)
-    sums_ref[1:2, :] += jnp.sum(grad, axis=0, keepdims=True)
-    sums_ref[2:3, :] += jnp.sum(low.astype(F32), axis=0, keepdims=True)
-    sums_ref[3:4, :] += jnp.sum(stream_ref[...].astype(F32), axis=0, keepdims=True)
+    for number, part in enumerate(row_sums(grad, normal, low, stream_ref[...])):
+        sums_ref[number : number + 1, :] += part
 
 
 def norm_back(values, vectors, row, stream, grads):
     row_count, model = values.shape
-    panel = pl.BlockSpec((QUERY_ROWS, model), lambda step: (step, 0))
+    panel = pl.BlockSpec((QUERY_ROWS // 2, model), lambda step: (step, 0))
     return pl.pallas_call(
         functools.partial(norm_back_kernel, count=len(grads), row=row),
-        grid=(row_count // QUERY_ROWS,),
+        grid=(2 * row_count // QUERY_ROWS,),
         in_specs=[panel, pl.BlockSpec((VECTOR_ROWS, model), lambda step: (0, 0)), panel]
         + [panel] * len(grads),
         out_specs=[panel, panel, pl.BlockSpec((8, model), lambda step: (0, 0))],
@@ -696,13 +710,22 @@
     return results if norm is not None else results[0]
 
 
-def project_back_kernel(*refs, source, block, count):
+def project_back_kernel(*refs, source, block, count, row):
     refs = list(refs)
     place_ref = refs.pop(0)
     grad_refs = refs[:count]
-    source_refs = refs[count : count + len(source.operands)]
-    out_ref, total_ref, buffer, semaphores = refs[count + len(source.operands) :]
-    model = out_ref.shape[1]
+    refs = refs[count:]
+    if row is not None:
+        values_hbm, stream_hbm, vectors_ref = refs[:3]
+        refs = refs[3:]
+    source_refs = refs[: len(source.operands)]
+    refs = refs[len(source.operands) :]
+    if row is None:
+        out_ref, total_ref, buffer, semaphores = refs
+    else:
+        out_hbm, low_hbm, sums_ref, total_ref, buffer, semaphores = refs[:6]
+        values_ref, stream_ref, low_ref, load_semaphores, store_semaphores = refs[6:]
+    row_count, model = total_ref.shape
     width = grad_refs[0].shape[1]
     parts = model // (2 * width)
     item = pl.program_id(0)
@@ -714,9 +737,17 @@
     columns_ref = fetched(
         source, source_refs, buffer, semaphores, place_ref[PLACE_PLANE], order, item, steps
     )
+    if row is not None:
+        loads = [
+            pltpu.make_async_copy(values_hbm, values_ref, load_semaphores.at[0]),
+            pltpu.make_async_copy(stream_hbm, stream_ref, load_semaphores.at[1]),
+        ]
 
     @pl.when(item == 0)
     def _():
+        if row is not None:
+            for load in loads:
+                load.start()
         total_ref[...] = jnp.zeros_like(total_ref)
 
     for number, grad_ref in enumerate(grad_refs):
@@ -724,7 +755,6 @@
         @pl.when(item // (2 * parts) == number)
         def _(grad_ref=grad_ref):
             columns = columns_ref[...]
-            row_count = grad_ref.shape[0]
             size = row_count // 2
             for first in range(0, row_count, size):
                 rows = slice(first, first + size)
@@ -732,10 +762,38 @@
 
     @pl.when(item == steps - 1)
     def _():
-        out_ref[...] = total_ref[...].astype(out_ref.dtype)
-
-
-def project_back(place, grads, slots, group, block, out_type):
+        if row is None:
+            out_ref[...] = total_ref[...].astype(out_ref.dtype)
+            return
+        for load in loads:
+            load.wait()
+        stores = []
+        sums = None
+        for number in range(row_count // QUERY_ROWS):
+            rows = slice(number * QUERY_ROWS, (number + 1) * QUERY_ROWS)
+            grad = total_ref[rows, :]
+            stream = stream_ref[rows, :]
+            result, normal = norm_back_rows(
+                values_ref[rows, :], grad, vectors_ref[row : row + 1, :], stream
+            )
+            low = result.astype(BF16)
+            made = row_sums(grad, normal, low, stream)
+            sums = made if sums is None else [a + b for a, b in zip(sums, made, strict=True)]
+            total_ref[rows, :] = result
+            low_ref[rows, :] = low
+            for kind, (held, target) in enumerate(((total_ref, out_hbm), (low_ref, low_hbm))):
+                store = pltpu.make_async_copy(
+                    held.at[rows, :], target.at[rows, :], store_semaphores.at[kind, number]
+                )
+                store.start()
+                stores.append(store)
+        for number, part in enumerate(sums):
+            sums_ref[number : number + 1, :] = part
+        for store in stores:
+            store.wait()
+
+
+def project_back(place, grads, slots, group, block, out_type, norm=None):
     row_count, model = grads[0].shape
     source = Source(slots, group, (0, 1))
     width = source.shape[2]
@@ -750,19 +808,49 @@
 
         return pl.BlockSpec((row_count, width), index)
 
-    return pl.pallas_call(
-        functools.partial(project_back_kernel, source=source, block=block, count=len(grads)),
+    anywhere = pl.BlockSpec(memory_space=pl.ANY)
+    in_specs = [grad_panel(number) for number in range(len(grads))]
+    operands = list(grads)
+    out_specs = [pl.BlockSpec((row_count, model), lambda *_: (0, 0))]
+    out_shape = [jax.ShapeDtypeStruct((row_count, model), out_type)]
+    scratch = [pltpu.VMEM((row_count, model), F32)] + source.scratch()
+    row = None
+    if norm is not None:
+        values, stream, vectors, row = norm
+        in_specs += [
+            anywhere,
+            anywhere,
+            pl.BlockSpec((VECTOR_ROWS, model), lambda *_: (0, 0)),
+        ]
+        operands += [values, stream, vectors]
+        out_specs = [anywhere, anywhere, pl.BlockSpec((8, model), lambda *_: (0, 0))]
+        out_shape += [
+            jax.ShapeDtypeStruct((row_count, model), BF16),
+            jax.ShapeDtypeStruct((8, model), F32),
+        ]
+        scratch += [
+            pltpu.VMEM(values.shape, values.dtype),
+            pltpu.VMEM(stream.shape, stream.dtype),
+            pltpu.VMEM((row_count, model), BF16),
+            pltpu.SemaphoreType.DMA((2,)),
+            pltpu.SemaphoreType.DMA((2, row_count // QUERY_ROWS)),
+        ]
+    results = pl.pallas_call(
+        functools.partial(
+            project_back_kernel, source=source, block=block, count=len(grads), row=row
+        ),
         grid_spec=pltpu.PrefetchScalarGridSpec(
             num_scalar_prefetch=1,
             grid=(2 * parts * len(grads),),
-            in_specs=[grad_panel(number) for number in range(len(grads))] + source.specs(),
-            out_specs=pl.BlockSpec((row_count, model), lambda *_: (0, 0)),
-            scratch_shapes=[pltpu.VMEM((row_count, model), F32)] + source.scratch(),
+            in_specs=in_specs + source.specs(),
+            out_specs=out_specs,
+            scratch_shapes=scratch,
         ),
-        out_shape=jax.ShapeDtypeStruct((row_count, model), out_type),
+        out_shape=out_shape,
         compiler_params=pltpu.CompilerParams(vmem_limit_bytes=60 << 20),
         cost_estimate=SMALL,
-    )(place, *grads, *source.operands)
+    )(place, *operands, *source.operands)
+    return results[0] if norm is None else results
 
 
 NEAR = ((0, 1), (1, 0), (2, 3), (3, 2))
@@ -783,6 +871,21 @@
         for inner in range(plane_size)
     ]
     return lax.ppermute(values, AXES, pairs)
+
+
+def by_member(values, member):
+    count = values.shape[0]
+    bit = 1
+    while bit < count:
+        pairs = values.reshape((count // (2 * bit), 2, bit) + values.shape[1:])
+        turned = jnp.where((member // bit) % 2 == 1, pairs[:, ::-1], pairs)
+        values = turned.reshape(values.shape)
+        bit *= 2
+    return values
+
+
+def exchange_members(items, device_count):
+    return [items[0]] + [swap_bit(item, device_count, k) for k, item in enumerate(items) if k > 0]
 
 
 def inner_bits(device_count):
@@ -1165,14 +1268,26 @@
 
 def exchange_vectors(pieces, rows, width):
     device_count = pieces.shape[0]
-    sublanes = 8 if pieces.dtype == F32 else 16
+    size = rows * width
+    padded = pad_vectors(pieces, 16)
+    got = lax.all_to_all(padded, AXES, split_axis=0, concat_axis=0, tiled=True)
+    return got.reshape(device_count, -1)[:, :size].reshape(device_count, rows, width)
+
+
+def pad_vectors(pieces, sublanes):
+    device_count, size = pieces.shape
     room = sublanes * LANES
-    size = rows * width
     tiles = -(-size // room)
     padded = jnp.pad(pieces, ((0, 0), (0, tiles * room - size)))
-    padded = padded.reshape(device_count, tiles * sublanes, LANES)
-    got = lax.all_to_all(padded, AXES, split_axis=0, concat_axis=0, tiled=True)
-    return got.reshape(device_count, -1)[:, :size].reshape(device_count, rows, width)
+    return padded.reshape(device_count, tiles * sublanes, LANES)
+
+
+def vector_send(pieces, device, bit):
+    halves = pieces.reshape((2, -1) + pieces.shape[1:])
+    mine = (device // bit) % 2
+    kept = lax.dynamic_index_in_dim(halves, mine, 0, keepdims=False)
+    sent = lax.dynamic_index_in_dim(halves, 1 - mine, 0, keepdims=False)
+    return kept, sent
 
 
 def local(
@@ -1210,33 +1325,40 @@
     vector_shape = vectors.shape
     own = weights.astype(BF16)
     first = move_planes(own, ((0, 2), (1, 0), (2, 3), (3, 1)), plane_size)
+    pieces = jnp.broadcast_to(
+        vectors.astype(BF16).reshape(1, -1), (device_count, vectors.size)
+    )
+    vector_pieces = exchange_vectors(pieces, *vector_shape)
     memory_padded = jnp.pad(memory, ((0, 0), (0, SLOT_PAD - quarter), (0, 0)))
-    memory_here = lax.all_to_all(memory_padded, "mem", split_axis=0, concat_axis=0, tiled=True)
-    memory_here = memory_here.reshape(group_size * SLOT_PAD, model)
+    memory_parts = exchange_members(
+        [
+            lax.dynamic_index_in_dim(memory_padded, member ^ item, 0, keepdims=False)
+            for item in range(group_size)
+        ],
+        device_count,
+    )
     parts = spread_begin(own)
     got = spread_swaps(parts, 0, device_count)
-    first, got, memory_here, own = pinned(first, got, memory_here, own)
+    first, got, vector_pieces, own = pinned(first, got, vector_pieces, own)
     held = jnp.where((plane == 0) | (plane == 3), own, first)
     near = move_planes(held, NEAR, plane_size)
     middle = move_planes(own, ((1, 2), (2, 1)), plane_size)
     parts, got = spread_on(parts, got, device_count)
-    pieces = jnp.broadcast_to(
-        vectors.astype(BF16).reshape(1, -1), (device_count, vectors.size)
-    )
-    vector_pieces = exchange_vectors(pieces, *vector_shape)
-    near, middle, first, got, vector_pieces = pinned(near, middle, first, got, vector_pieces)
+    near, middle, first, got, memory_parts = pinned(near, middle, first, got, memory_parts)
     slot_zero = flat_slot(parts, got)
     even = plane % 2 == 0
     parts_one = spread_begin(jnp.where(even, first, near))
     got_one = spread_swaps(parts_one, 0, device_count)
     last = move_planes(middle, ((1, 0), (2, 3)), plane_size)
     zero_away = swap_cores(slot_zero, device_count)
+    got_one, zero_away = pinned(got_one, zero_away)
     vector_rows = jnp.swapaxes(vector_pieces, 0, 1).reshape(vector_shape[0], model).astype(F32)
     table = jnp.pad(vector_rows, ((0, VECTOR_ROWS - vector_shape[0]), (0, 0)))
-    got_one, zero_away, vector_rows, table = pinned(got_one, zero_away, vector_rows, table)
     parts_one, got_one = spread_on(parts_one, got_one, device_count)
     one_away = swap_cores(parts_one, device_count)
-    got_one, one_away, last = pinned(got_one, one_away, last)
+    got_one, one_away, last, vector_rows, table = pinned(
+        got_one, one_away, last, vector_rows, table
+    )
     got_one_away = swap_cores(got_one, device_count)
     parts_two = spread_begin(jnp.where((plane == 1) | (plane == 2), middle, last))
     got_two = spread_swaps(parts_two, 0, device_count)
@@ -1245,8 +1367,10 @@
         (flat_slot(parts_one, got_one), flat_slot(one_away, got_one_away)),
     ]
 
+    memory_here = jnp.concatenate(memory_parts, axis=0)
     live_rows = (jnp.arange(row_count) < page_lengths[0]).astype(F32)[:, None]
     slots_here = lax.dynamic_slice_in_dim(slot_masks, member, 1, 0).reshape(group_size, quarter)
+    slots_here = by_member(slots_here, member)
     slots_here = jnp.pad(slots_here, ((0, 0), (0, SLOT_PAD - quarter))).reshape(-1, 1)
     slot_bias = jnp.broadcast_to(
         jnp.where(slots_here > 0, 0.0, MASKED).astype(F32), (group_size * SLOT_PAD, LANES)
@@ -1310,8 +1434,6 @@
     feed_sends, back_b = pinned(feed_sends, back_b)
     feed_swaps = stage_swaps(feed_sends, feed_sum, device_count)
 
-    result = (after_cross + (out_a + out_b) + vector_rows[12]) * live_rows
-    mixed = result.astype(BF16)
     bias_even = jnp.where(core == 0, bias_kept, bias_sent)
     bias_odd = jnp.where(core == 0, bias_sent, bias_kept)
     grad_bias_up = jnp.concatenate([bias_even, bias_odd], axis=1).reshape(4, model)
@@ -1336,7 +1458,7 @@
     cross_whole, (queries_own, keys_own, values_own) = attention_backward(
         here, width, *cross_operands, cross_whole
     )
-    grad_queries_cross, grad_keys_cross, grad_values_cross = cross_whole
+    grad_queries_cross, grad_keys_cross, grad_values_cross, cross_sums = cross_whole
     feed_swaps, queries_part, queries_own, grad_queries_cross = pinned(
         feed_swaps, queries_part, queries_own, grad_queries_cross
     )
@@ -1368,12 +1490,14 @@
         ),
         width,
     )
-    grad_normed_two = project_back(here, (grad_queries_cross,), slots, 1, 0, F32)
-
-    grad_one, grad_low_one, sums_two = norm_back(
-        after_self, table, 2, grad_two, (grad_normed_two,)
+
+    grad_one, grad_low_one, sums_two = project_back(
+        here, (grad_queries_cross,), slots, 1, 0, F32, (after_self, grad_two, table, 2)
     )
     grad_attended = project_back(here, (grad_low_one,), slots, 0, 3, BF16)
+    memory_back = project_back(here, (grad_keys_cross, grad_values_cross), slots, 1, 1, BF16)
+    memory_back = memory_back.reshape(group_size, SLOT_PAD, model)
+    memory_back = exchange_members([memory_back[item] for item in range(group_size)], device_count)
     feed_swaps, cross_got, cross_kept, grad_attended = pinned(
         feed_swaps, cross_got, cross_kept, grad_attended
     )
@@ -1406,8 +1530,8 @@
         ),
         width,
     )
-    feed_got, cross_swaps, self_sent, self_whole = pinned(
-        feed_got, cross_swaps, self_sent, self_whole
+    feed_got, cross_swaps, self_sent, self_whole, memory_back = pinned(
+        feed_got, cross_swaps, self_sent, self_whole, memory_back
     )
     self_got = swap_bit(self_sent, device_count, 1)
     feed_kept = feed_kept + feed_got.astype(F32)
@@ -1421,7 +1545,7 @@
     self_whole, (queries_own, keys_own, values_own) = attention_backward(
         here, width, *self_operands, self_whole
     )
-    grad_queries_self, grad_keys_self, grad_values_self = self_whole
+    grad_queries_self, grad_keys_self, grad_values_self, self_sums = self_whole
     self_kept = weight_half(
         (
             (low_one, queries_own),
@@ -1439,45 +1563,24 @@
     )
     self_swaps = stage_swaps(self_sends, self_sum, device_count)
     cross_sum = finish_stages(here, cross_sum.joined(cross_swaps), device_count)
-    grad_normed_one = project_back(
+    input_grad, _, sums_one = project_back(
         here,
         (grad_queries_self, grad_keys_self, grad_values_self),
         slots,
         0,
         0,
         F32,
-    )
-    grad_normed_one, cross_swaps = pinned(grad_normed_one, cross_sum.swaps)
+        (tokens, grad_one, table, 0),
+    )
+    sums_one, cross_swaps = pinned(sums_one, cross_sum.swaps)
     cross_sum.swaps = list(cross_swaps)
     cross_total, cross_sent = plane_totals(here, cross_sum)
-    self_swaps, cross_sent, grad_normed_one = pinned(self_swaps, cross_sent, grad_normed_one)
+    self_swaps, cross_sent, sums_one = pinned(self_swaps, cross_sent, sums_one)
     cross_got = move_planes(cross_sent, ((0, 1), (3, 2)), plane_size)
     self_sum = self_sum.joined(self_swaps)
     self_sends = stage_sends(here, self_sum, device_count)
-    self_sends, grad_normed_one = pinned(self_sends, grad_normed_one)
+    self_sends, sums_one = pinned(self_sends, sums_one)
     self_swaps = stage_swaps(self_sends, self_sum, device_count)
-    input_grad, _, sums_one = norm_back(tokens, table, 0, grad_one, (grad_normed_one,))
-    self_swaps, cross_got, sums_one, grad_keys_cross = pinned(
-        self_swaps, cross_got, sums_one, grad_keys_cross
-    )
-    self_sum = finish_stages(here, self_sum.joined(self_swaps), device_count)
-    self_total, self_sent = plane_totals(here, self_sum)
-    self_sent, sums_one, grad_keys_cross = pinned(self_sent, sums_one, grad_keys_cross)
-    self_got = move_planes(self_sent, ((1, 0), (3, 2)), plane_size)
-    cross_total = cross_total + cross_got.astype(F32)
-    cross_sent, grad_keys_cross = pinned(cross_total.astype(BF16), grad_keys_cross)
-    cross_got = move_planes(cross_sent, ((2, 1),), plane_size)
-    memory_back = project_back(
-        here, (grad_keys_cross, grad_values_cross), slots, 1, 1, BF16
-    )
-    memory_back = lax.all_to_all(
-        memory_back.reshape(group_size, SLOT_PAD, model),
-        "mem",
-        split_axis=0,
-        concat_axis=0,
-        tiled=True,
-    )
-    memory_back = memory_back[:, :quarter].astype(F32)
     vector_head = jnp.stack(
         [
             sums_one[0],
@@ -1486,11 +1589,11 @@
             sums_two[1],
             sums_three[0],
             sums_three[1],
-            column_total(grad_queries_self),
-            column_total(grad_values_self),
+            self_sums[0],
+            self_sums[1],
             sums_two[2],
-            column_total(grad_queries_cross),
-            column_total(grad_values_cross),
+            cross_sums[0],
+            cross_sums[1],
             sums_three[2],
             sums_three[3],
         ],
@@ -1500,21 +1603,49 @@
     vector_terms = jnp.swapaxes(
         vector_terms.reshape(vector_shape[0], device_count, vector_shape[1]), 0, 1
     )
-    vector_parts = exchange_vectors(vector_terms.reshape(device_count, -1), *vector_shape)
-    vector_grad = jnp.sum(vector_parts, axis=0)
-
-    self_got, cross_got, feed_got = pinned(self_got, cross_got, feed_got)
+    vector_bits = [1 << number for number in reversed(range(device_count.bit_length() - 1))]
+    vector_terms = pad_vectors(vector_terms.reshape(device_count, -1), 8)
+    vector_kept, vector_sent = vector_send(vector_terms, device, vector_bits[0])
+    vector_got = swap_bit(vector_sent, device_count, vector_bits[0])
+
+    def vector_next(kept, got, number):
+        kept, sent = vector_send(kept + got, device, vector_bits[number])
+        return kept, swap_bit(sent, device_count, vector_bits[number])
+
+    self_swaps, vector_got = pinned(self_swaps, vector_got)
+    self_sum = finish_stages(here, self_sum.joined(self_swaps), device_count)
+    self_total, self_sent = plane_totals(here, self_sum)
+    self_sent, vector_got = pinned(self_sent, vector_got)
+    self_got = move_planes(self_sent, ((1, 0), (3, 2)), plane_size)
+    vector_kept, vector_got = vector_next(vector_kept, vector_got, 1)
+    result = (after_cross + (out_a + out_b) + vector_rows[12]) * live_rows
+    mixed = result.astype(BF16)
+    mixed, vector_got = pinned(mixed, vector_got)
+    vector_kept, vector_got = vector_next(vector_kept, vector_got, 2)
+    cross_total = cross_total + cross_got.astype(F32)
+    cross_got = move_planes(cross_total.astype(BF16), ((2, 1),), plane_size)
+
+    self_got, cross_got, feed_got, vector_got = pinned(
+        self_got, cross_got, feed_got, vector_got
+    )
     self_sent = (self_total + self_got.astype(F32)).astype(BF16)
-    self_sent, cross_got, feed_got = pinned(self_sent, cross_got, feed_got)
+    self_sent, cross_got, feed_got, memory_back, vector_got = pinned(
+        self_sent, cross_got, feed_got, memory_back, vector_got
+    )
     self_far = move_planes(self_sent, ((2, 0),), plane_size)
     group_other = jnp.where(
         plane < 2,
         cross_total + cross_got.astype(F32),
         feed_kept + feed_got.astype(F32),
     )
-    group_other, self_far, memory_back, vector_grad, mixed = pinned(
-        group_other, self_far, memory_back, vector_grad, mixed
-    )
+    memory_back = jnp.stack([item[:quarter] for item in memory_back])
+    memory_back = by_member(memory_back, member).astype(F32)
+    vector_kept, vector_got = vector_next(vector_kept, vector_got, 3)
+    group_other, vector_got = pinned(group_other, vector_got)
+    for number in range(4, len(vector_bits)):
+        vector_kept, vector_got = vector_next(vector_kept, vector_got, number)
+    group_other, self_far, vector_got = pinned(group_other, self_far, vector_got)
+    vector_grad = (vector_kept + vector_got).reshape(-1)[: vectors.size].reshape(vector_shape)
     (
         weight_grad,
         weight_first,

time: 698 us -> 691 us (0.990)
  local copies, waits for them, and re-layouts: 31 us -> 49.1 us
  Pallas kernels: 385 us -> 371 us
  starting transfers between devices: 75.3 us -> 67.9 us
    pallas_call x3 -> x1, Pallas kernels: 26.8 us -> 10.8 us  [norm_back(): pl.pallas_call(functools.partial(norm_back_kernel, count=len(grads), row=...]
    ppermute x48 -> x59, waiting for transfers between devices: 56.6 us -> 71.2 us  [swap_bit(): lax.ppermute(values, AXES, [(item, item ^ bit) for item in range(device_c...]
    all_to_all x2 -> x1, starting transfers between devices: 15.3 us -> 2.58 us  [exchange_vectors(): got = lax.all_to_all(padded, AXES, split_axis=0, concat_axis=0, tiled=True)]
    ppermute x48 -> x59, starting transfers between devices: 34.9 us -> 43.5 us  [swap_bit(): lax.ppermute(values, AXES, [(item, item ^ bit) for item in range(device_c...]
    pallas_call x5, Pallas kernels: 48.8 us -> 56.8 us  [project_back(): pl.pallas_call(functools.partial(project_back_kernel, source=source, bloc...]
    all_to_all x2 -> x1, waiting for transfers between devices: 23.2 us -> 15.5 us  [exchange_vectors(): got = lax.all_to_all(padded, AXES, split_axis=0, concat_axis=0, tiled=True)]
    all_to_all x2 -> x0, waiting for transfers between devices: 7.34 us -> none  [the longest x1 7.33 us: local(): lax.all_to_all(memory_back.reshape(group_size, SLOT_PAD, model), 'mem', s...]
    all_to_all x2 -> x0, starting transfers between devices: 7.22 us -> none  [the longest x1 3.68 us: local(): lax.all_to_all(memory_back.reshape(group_size, SLOT_PAD, model), 'mem', s...]
  transfers between devices with their start and end apart: 62 -> 70, of which waited for: 15 -> 13; matrix products, arithmetic and copies ran while one was open for 13% -> 16% of each run, Pallas kernels for 42% -> 43%
where the time goes in v6:
time: 691 us; the launch traced here: 684 us
  Pallas kernels  371 us (54%)
  waiting for transfers between devices  105 us (15%)
  starting transfers between devices  67.9 us (10%)
  other arithmetic  52.2 us (8%)
  local copies, waits for them, and re-layouts  49.1 us (7%)
  matrix products  34.7 us (5%)
    pallas_call x2, Pallas kernels, feed_half(): pl.pallas_call(functools.partial(feed_kernel, norm=norm, up_source=up_sou...  76 us
    ppermute x59, waiting for transfers between devices, swap_bit(): lax.ppermute(values, AXES, [(item, item ^ bit) for item in range(device_c...  71.2 us
    pallas_call x4, Pallas kernels, attention_backward(): pl.pallas_call(functools.partial(attention_backward_kernel, causal=causal...  70.2 us
    pallas_call x5, Pallas kernels, project_back(): pl.pallas_call(functools.partial(project_back_kernel, source=source, bloc...  56.8 us
    pallas_call x5, Pallas kernels, project(): pl.pallas_call(functools.partial(project_kernel, source=source, block=blo...  50.3 us
    ppermute x59, starting transfers between devices, swap_bit(): lax.ppermute(values, AXES, [(item, item ^ bit) for item in range(device_c...  43.5 us
    pallas_call x2, Pallas kernels, attention_forward(): pl.pallas_call(functools.partial(attention_forward_kernel, causal=causal)...  36.8 us
    dot_general x16, matrix products, dot_rows(): lax.dot_general(left, right, CONTRACT_ROWS, preferred_element_type=F32)  34.7 us
  transfers between devices with their start and end apart: 70, of which 13 were waited for; matrix products, arithmetic and copies ran while one was open for 16% of the time, Pallas kernels for 43%

profile of v6, /device:TPU:0, one launch (start us, length us, event | category | flops | bytes accessed | tf_op | source)
XLA Modules:
  0.0 683.6 jit_solution(8711727041522778658)
XLA Ops:
  3.4 4.0 collective-permute-start
  20.6 15.5 %all-to-all-done = bf16[32,16,128]{2,1,0:T(8,128)(2,1)S(1)} async-done(((bf16[32,16,128]{2,1,0:T(8,128)(2,1)}), bf16[32,16,128]{2,1,0:T(8,128)(2,1)S(1)}, u32[]{:S(2)}, u32[]{:S(2)}) %all-to-all-start) | async-done | bytes 131104 | tf_op jit(solution)/shard_map/all_to_all | solution.py:1273
  46.7 26.3 %collective-permute-done.8 = bf16[160,1024]{1,0:T(8,128)(2,1)} collective-permute-done((bf16[160,1024]{1,0:T(8,128)(2,1)S(1)}, bf16[160,1024]{1,0:T(8,128)(2,1)}, u32[]{:S(2)}, u32[]{:S(2)}) %collective-permute-start.8) | collective-permute-done | bytes 327712 | tf_op jit(solution)/shard_map/ppermute | solution.py:864
  80.0 10.9 %collective-permute-done.13 = bf16[512,512]{1,0:T(8,128)(2,1)S(1)} collective-permute-done((bf16[512,512]{1,0:T(8,128)(2,1)S(1)}, bf16[512,512]{1,0:T(8,128)(2,1)S(1)}, u32[]{:S(2)}, u32[]{:S(2)}) %collective-permute-start.13) | collective-permute-done | bytes 524320 | tf_op jit(solution)/shard_map/ppermute | solution.py:864
  99.3 6.6 collective-permute-done.22
  105.9 11.5 %collective-permute-done.19.refs_6_.refs_7_.refs_22_.refs_23_.refs_21_.refs_24_.refs_5_.refs_10_ = bf16[2,512,512]{2,1,0:T(8,128)(2,1)} collective-permute-done((bf16[2,512,512]{2,1,0:T(8,128)(2,1)S(1)}, bf16[2,512,512]{2,1,0:T(8,128)(2,1)}, u32[]{:S(2)}, u32[]{:S(2)}) %collective-permute-start.19) | collective-permute-done | bytes 1048608 | tf_op jit(solution)/shard_map/ppermute | solution.py:864
  124.8 15.8 %shard_map.286 = (bf16[1024,3072]{1,0:T(8,128)(2,1)}, bf16[1024,1024]{1,0:T(8,128)(2,1)}) custom-call(s32[4]{0:T(128)} %add_add_fusion.refs_0_.place_ref, bf16[1024,1024]{1,0:T(8,128)(2,1)} %refs_4_.1, f32[24,1024]{1,0:T(8,128)} %pad.28.refs_2_.refs_3_.refs_1_.refs_4_.refs_6_, bf16[2,512,512]{2,1,0:T(8,128)(2,1)} %copy-done.9, ...), custom_call_target="tpu_custom_call" | custom-call | flops 1048576 | bytes 65536 | tf_op jit(solution)/shard_map/pallas_call | solution.py:690
  142.9 17.7 %shard_map.287 = (bf16[1024,1024]{1,0:T(8,128)(2,1)}, f32[8,8,1024]{2,1,0:T(8,128)}) custom-call(bf16[1024,3072]{1,0:T(8,128)(2,1)} %get-tuple-element.271.refs_0_.refs_1_.refs_2_.refs_3_, bf16[1024,3072]{1,0:T(8,128)(2,1)} %get-tuple-element.271.refs_0_.refs_1_.refs_2_.refs_3_, bf16[1024,3072]{1,0:T(8,128)(2,1)} %get-tuple-element.271.refs_0_.refs_1_.refs_2_.refs_3_), custom_call_target="tpu_custom_call" | custom-call | flops 1048576 | bytes 65536 | tf_op jit(solution)/shard_map/pallas_call | solution.py:234
  160.7 5.7 collective-permute-done.28.refs_6_.refs_7_.refs_8_.refs_5_
  174.9 7.9 %shard_map.288.refs_1_.refs_3_.refs_2_ = f32[1024,1024]{1,0:T(8,128)} custom-call(s32[4]{0:T(128)} %add_add_fusion.refs_0_.place_ref, bf16[1024,1024]{1,0:T(8,128)(2,1)} %get-tuple-element.275.refs_1_.refs_5_, f32[24,1024]{1,0:T(8,128)} %pad.28.refs_2_.refs_3_.refs_1_.refs_4_.refs_6_, bf16[1024,1024]{1,0:T(8,128)(2,1)} %refs_4_.1, ...), custom_call_target="tpu_custom_call" | custom-call | flops 1048576 | bytes 65536 | tf_op jit(solution)/shard_map/pallas_call | solution.py:690
  184.8 9.7 %shard_map.289 = (bf16[1024,1024]{1,0:T(8,128)(2,1)}, bf16[1024,1024]{1,0:T(8,128)(2,1)}) custom-call(s32[4]{0:T(128)} %add_add_fusion.refs_0_.place_ref, f32[1024,1024]{1,0:T(8,128)} %shard_map.288.refs_1_.refs_3_.refs_2_, f32[24,1024]{1,0:T(8,128)} %pad.28.refs_2_.refs_3_.refs_1_.refs_4_.refs_6_, bf16[2,512,512]{2,1,0:T(8,128)(2,1)} %copy-done.12, ...), custom_call_target="tpu_custom_call" | custom-call | flops 1048576 | bytes 65536 | tf_op jit(solution)/shard_map/pallas_call | solution.py:690
  199.8 8.5 %shard_map.290.refs_1_.refs_2_.refs_3_ = bf16[640,2048]{1,0:T(8,128)(2,1)} custom-call(s32[4]{0:T(128)} %add_add_fusion.refs_0_.place_ref, bf16[640,1024]{1,0:T(8,128)(2,1)} %pad_maximum_fusion.4.refs_1_, f32[24,1024]{1,0:T(8,128)} %pad.28.refs_2_.refs_3_.refs_1_.refs_4_.refs_6_, bf16[2,512,512]{2,1,0:T(8,128)(2,1)} %copy-done.12, ...), custom_call_target="tpu_custom_call" | custom-call | flops 1048576 | bytes 65536 | tf_op jit(solution)/shard_map/pallas_call | solution.py:690
  209.2 19.0 %shard_map.291 = (bf16[1024,1024]{1,0:T(8,128)(2,1)}, f32[8,8,1024]{2,1,0:T(8,128)}) custom-call(bf16[1024,1024]{1,0:T(8,128)(2,1)} %get-tuple-element.288.refs_0_.refs_1_, bf16[640,2048]{1,0:T(8,128)(2,1)} %shard_map.290.refs_1_.refs_2_.refs_3_, bf16[640,2048]{1,0:T(8,128)(2,1)} %shard_map.290.refs_1_.refs_2_.refs_3_, ...), custom_call_target="tpu_custom_call" | custom-call | flops 1048576 | bytes 65536 | tf_op jit(solution)/shard_map/pallas_call | solution.py:234
  230.1 3.3 multiply_convert_fusion.1.refs_2_
  234.9 8.4 %shard_map.292.refs_1_.refs_0_ = f32[1024,1024]{1,0:T(8,128)} custom-call(s32[4]{0:T(128)} %add_add_fusion.refs_0_.place_ref, bf16[1024,1024]{1,0:T(8,128)(2,1)} %get-tuple-element.293.refs_1_.refs_5_, f32[24,1024]{1,0:T(8,128)} %pad.28.refs_2_.refs_3_.refs_1_.refs_4_.refs_6_, f32[1024,1024]{1,0:T(8,128)} %shard_map.288.refs_1_.refs_3_.refs_2_, ...), custom_call_target="tpu_custom_call" | custom-call | flops 1048576 | bytes 65536 | tf_op jit(solution)/shard_map/pallas_call | solution.py:690
  245.3 38.9 %shard_map.293 = (f32[1024,1024]{1,0:T(8,128)}, f32[1024,1024]{1,0:T(8,128)}, bf16[4,1024,512]{2,1,0:T(8,128)(2,1)}, bf16[4,1024,512]{2,1,0:T(8,128)(2,1)}, f32[...) custom-call(s32[4]{0:T(128)} %add_add_fusion.1.refs_0_, f32[1024,1024]{1,0:T(8,128)} %shard_map.292.refs_1_.refs_0_, ...), custom_call_target="tpu_custom_call" | custom-call | flops 1048576 | bytes 65536 | tf_op jit(solution)/shard_map/pallas_call | solution.py:515
  284.7 37.1 %shard_map.294 = (f32[1024,1024]{1,0:T(8,128)}, f32[1024,1024]{1,0:T(8,128)}, bf16[4,1024,512]{2,1,0:T(8,128)(2,1)}, bf16[4,1024,512]{2,1,0:T(8,128)(2,1)}, f32[4,1,512]{2,1,0:T(1,128)}) custom-call(s32[4]{0:T(128)} %add_add_fusion.refs_0_.place_ref, bf16[1024,1024]{1,0:T(8,128)(2,1)} %get-tuple-element.305.refs_1_, ...), custom_call_target="tpu_custom_call" | custom-call | flops 1048576 | bytes 65536 | tf_op jit(solution)/shard_map/pallas_call | solution.py:515
  321.9 5.9 shard_map.295
  329.7 10.8 %shard_map.296 = (f32[1024,1024]{1,0:T(8,128)}, bf16[1024,1024]{1,0:T(8,128)(2,1)}, f32[8,1024]{1,0:T(8,128)}) custom-call(f32[1024,1024]{1,0:T(8,128)} %shard_map.292.refs_1_.refs_0_, f32[24,1024]{1,0:T(8,128)} %pad.28.refs_2_.refs_3_.refs_1_.refs_4_.refs_6_, bf16[1024,1024]{1,0:T(8,128)(2,1)} %multiply_convert_fusion.1.refs_2_, ...), custom_call_target="tpu_custom_call" | custom-call | flops 1048576 | bytes 65536 | tf_op jit(solution)/shard_map/pallas_call | solution.py:593
  340.5 7.8 %shard_map.297.refs_4_ = bf16[1024,1024]{1,0:T(8,128)(2,1)} custom-call(s32[4]{0:T(128)} %add_add_fusion.refs_0_.place_ref, bf16[1024,1024]{1,0:T(8,128)(2,1)} %get-tuple-element.322.refs_1_, bf16[2,512,512]{2,1,0:T(8,128)(2,1)} %copy-done.12, bf16[2,512,512]{2,1,0:T(8,128)(2,1)} %collective-permute-done.27.refs_4_.refs_5_.refs_6_.refs_3_, ...), custom_call_target="tpu_custom_call" | custom-call | flops 1048576 | bytes 65536 | tf_op jit(solution)/shard_map/pallas_call | solution.py:838
  348.4 18.1 %shard_map.298 = (bf16[1024,1024]{1,0:T(8,128)(2,1)}, bf16[640,1024]{1,0:T(8,128)(2,1)}, bf16[640,1024]{1,0:T(8,128)(2,1)}, f32[8,1024]{1,0:T(8,128)}, bf16[1024...) custom-call(s32[4]{0:T(128)} %add_add_fusion.1.refs_0_, ...), custom_call_target="tpu_custom_call" | custom-call | flops 1048576 | bytes 65536 | tf_op jit(solution)/shard_map/pallas_call | solution.py:289
  366.5 17.8 %shard_map.299 = (bf16[1024,1024]{1,0:T(8,128)(2,1)}, bf16[640,1024]{1,0:T(8,128)(2,1)}, bf16[640,1024]{1,0:T(8,128)(2,1)}, f32[8,1024]{1,0:T(8,128)}, bf16[1024...) custom-call(s32[4]{0:T(128)} %add_add_fusion.refs_0_.place_ref, ...), custom_call_target="tpu_custom_call", output_to_operand_aliasing={{0}: (8, {}), {1}: (9, {}), {2}: (10, {}), {3}: (11, {})} | custom-call | flops 1048576 | bytes 65536 | tf_op jit(solution)/shard_map/pallas_call | solution.py:289
  391.2 5.2 shard_map.300
  396.5 3.3 fusion.2
  402.0 9.2 %shard_map.306 = bf16[640,1024]{1,0:T(8,128)(2,1)} custom-call(s32[4]{0:T(128)} %add_add_fusion.refs_0_.place_ref, bf16[640,1024]{1,0:T(8,128)(2,1)} %get-tuple-element.374.refs_1_, bf16[640,1024]{1,0:T(8,128)(2,1)} %get-tuple-element.375.refs_2_, bf16[2,512,512]{2,1,0:T(8,128)(2,1)} %copy-done.12, ...), custom_call_target="tpu_custom_call" | custom-call | flops 1048576 | bytes 65536 | tf_op jit(solution)/shard_map/pallas_call | solution.py:838
  424.3 12.5 %shard_map.301 = (f32[1024,1024]{1,0:T(8,128)}, bf16[1024,1024]{1,0:T(8,128)(2,1)}, f32[8,1024]{1,0:T(8,128)}) custom-call(s32[4]{0:T(128)} %add_add_fusion.refs_0_.place_ref, bf16[1024,1024]{1,0:T(8,128)(2,1)} %get-tuple-element.350.refs_1_, f32[1024,1024]{1,0:T(8,128)} %shard_map.288.refs_1_.refs_3_.refs_2_, f32[1024,1024]{1,0:T(8,128)} %get-tuple-element.351.refs_3_, ...), custom_call_target="tpu_custom_call" | custom-call | flops 1048576 | bytes 65536 | tf_op jit(solution)/shard_map/pallas_call | solution.py:838
  436.8 8.1 %shard_map.302.refs_4_ = bf16[1024,1024]{1,0:T(8,128)(2,1)} custom-call(s32[4]{0:T(128)} %add_add_fusion.refs_0_.place_ref, bf16[1024,1024]{1,0:T(8,128)(2,1)} %get-tuple-element.352.refs_1_, bf16[2,512,512]{2,1,0:T(8,128)(2,1)} %copy-done.9, bf16[2,512,512]{2,1,0:T(8,128)(2,1)} %collective-permute-done.18.refs_4_.refs_5_.refs_20_.refs_21_.refs_19_.refs_22_.refs_3_.refs_8_, ...), custom_call_target="tpu_custom_call" | custom-call | flops 1048576 | bytes 65536 | tf_op jit(solution)/shard_map/pallas_call | solution.py:838
  445.0 3.7 fusion.13
  454.4 6.6 shard_map.303
  461.0 4.0 shard_map.304
  468.9 17.2 %shard_map.305 = (bf16[1024,1024]{1,0:T(8,128)(2,1)}, bf16[1024,1024]{1,0:T(8,128)(2,1)}, bf16[1024,1024]{1,0:T(8,128)(2,1)}, f32[8,1024]{1,0:T(8,128)}, bf16[10...) custom-call(s32[4]{0:T(128)} %add_add_fusion.1.refs_0_, ...), custom_call_target="tpu_custom_call" | custom-call | flops 1048576 | bytes 65536 | tf_op jit(solution)/shard_map/pallas_call | solution.py:289
  486.1 3.3 fusion.10
  498.7 3.8 shard_map.307
  505.8 17.2 %shard_map.308 = (bf16[1024,1024]{1,0:T(8,128)(2,1)}, bf16[1024,1024]{1,0:T(8,128)(2,1)}, bf16[1024,1024]{1,0:T(8,128)(2,1)}, f32[8,1024]{1,0:T(8,128)}, bf16[10...) custom-call(s32[4]{0:T(128)} %add_add_fusion.refs_0_.place_ref, ...), custom_call_target="tpu_custom_call", output_to_operand_aliasing={{0}: (7, {}), {1}: (8, {}), {2}: (9, {}), {3}: (10, {})} | custom-call | flops 1048576 | bytes 65536 | tf_op jit(solution)/shard_map/pallas_call | solution.py:289
  523.0 3.3 fusion.14
  531.2 4.0 shard_map.309
  537.5 19.1 %shard_map.310 = (f32[1024,1024]{1,0:T(8,128)}, bf16[1024,1024]{1,0:T(8,128)(2,1)}, f32[8,1024]{1,0:T(8,128)}) custom-call(s32[4]{0:T(128)} %add_add_fusion.refs_0_.place_ref, bf16[1024,1024]{1,0:T(8,128)(2,1)} %get-tuple-element.405.refs_1_, bf16[1024,1024]{1,0:T(8,128)(2,1)} %get-tuple-element.406.refs_2_, bf16[1024,1024]{1,0:T(8,128)(2,1)} %get-tuple-element.407.refs_3_, ...), custom_call_target="tpu_custom_call" | custom-call | flops 1048576 | bytes 65536 | tf_op jit(solution)/shard_map/pallas_call | solution.py:838
  556.6 5.4 shard_map.311
  562.0 3.1 collective-permute-start.62
  566.0 3.8 shard_map.312
  586.0 5.7 collective-permute-start.64
  593.3 5.3 shard_map.313
  600.9 3.3 fusion.1
  608.3 5.7 multiply_convert_fusion
  613.9 10.4 %collective-permute-done.60 = f32[8,8,128]{2,1,0:T(8,128)S(1)} collective-permute-done((f32[8,8,128]{2,1,0:T(8,128)S(1)}, f32[8,8,128]{2,1,0:T(8,128)S(1)}, u32[]{:S(2)}, u32[]{:S(2)}) %collective-permute-start.60) | collective-permute-done | bytes 32800 | tf_op jit(solution)/shard_map/ppermute | solution.py:864
  635.0 4.0 add_select_fusion.other_ref
  643.2 12.0 %collective-permute-done.67.far_ref = bf16[1024,512]{1,0:T(8,128)(2,1)S(1)} collective-permute-done((bf16[1024,512]{1,0:T(8,128)(2,1)S(1)}, bf16[1024,512]{1,0:T(8,128)(2,1)S(1)}, u32[]{:S(2)}, u32[]{:S(2)}) %collective-permute-start.67) | collective-permute-done | bytes 1048608 | tf_op jit(solution)/shard_map/ppermute | solution.py:873
  657.1 26.3 %shard_map.314 = (f32[1024,512]{1,0:T(8,128)}, f32[1024,512]{1,0:T(8,128)}, f32[1024,512]{1,0:T(8,128)}, f32[1024,512]{1,0:T(8,128)}, f32[1024,512]{1,0:T(8,128)...) custom-call(s32[4]{0:T(128)} %add_add_fusion.refs_0_.place_ref, ...), custom_call_target="tpu_custom_call" | custom-call | flops 1048576 | bytes 65536 | tf_op jit(solution)/shard_map/pallas_call | solution.py:1238
  (413 shorter events, 167.5 us)
Async XLA Ops:
  3.4 33.7 %collective-permute-start = (bf16[1024,512]{1,0:T(8,128)(2,1)}, bf16[1024,512]{1,0:T(8,128)(2,1)S(1)}, u32[]{:S(2)}, u32[]{:S(2)}) collective-permute-start(bf16[1024,512]{1,0:T(8,128)(2,1)} %convert_element_type.120), channel_id=1, source_target_pairs={{0,16},{1,17},{2,18},{3,19},{4,20},{5,21},{6,22},{7,23},{8,0},{9,1... | collective-permute-start | bytes 3145736 | tf_op jit(solution)/shard_map/ppermute | solution.py:873
  9.8 27.2 %collective-permute-start.2 = (bf16[512,512]{1,0:T(8,128)(2,1)}, bf16[512,512]{1,0:T(8,128)(2,1)}, u32[]{:S(2)}, u32[]{:S(2)}) collective-permute-start(bf16[512,512]{1,0:T(8,128)(2,1)} %get-tuple-element.503), channel_id=1, source_target_pairs={{0,4},{1,5},{2,6},{3,7},{4,0},{5,1},{6,2},{7,3},{8,12},{9,13},{10,... | collective-permute-start | bytes 1572872 | tf_op jit(solution)/shard_map/ppermute | solution.py:864
  11.4 25.7 %collective-permute-start.1 = (bf16[512,512]{1,0:T(8,128)(2,1)}, bf16[512,512]{1,0:T(8,128)(2,1)}, u32[]{:S(2)}, u32[]{:S(2)}) collective-permute-start(bf16[512,512]{1,0:T(8,128)(2,1)} %get-tuple-element.504), channel_id=1, source_target_pairs={{0,2},{1,3},{2,0},{3,1},{4,6},{5,7},{6,4},{7,5},{8,10},{9,11},{10,... | collective-permute-start | bytes 1572872 | tf_op jit(solution)/shard_map/ppermute | solution.py:864
  13.6 22.5 %all-to-all-start = ((bf16[32,16,128]{2,1,0:T(8,128)(2,1)}), bf16[32,16,128]{2,1,0:T(8,128)(2,1)S(1)}, u32[]{:S(2)}, u32[]{:S(2)}) async-start(bf16[32,16,128]{2,1,0:T(8,128)(2,1)} %pad.26), calls=%async_computation | async-start | bytes 262144 | tf_op jit(solution)/shard_map/all_to_all | solution.py:1273
  18.9 24.9 %collective-permute-start.9 = (bf16[160,1024]{1,0:T(8,128)(2,1)}, bf16[160,1024]{1,0:T(8,128)(2,1)}, u32[]{:S(2)}, u32[]{:S(2)}) collective-permute-start(bf16[160,1024]{1,0:T(8,128)(2,1)} %get-tuple-element.485), channel_id=1, source_target_pairs={{0,3},{1,2},{2,1},{3,0},{4,7},{5,6},{6,5},{7,4},{8,11},{9,10},{10,... | collective-permute-start | bytes 983048 | tf_op jit(solution)/shard_map/ppermute | solution.py:864
  20.3 25.2 %collective-permute-start.7 = (bf16[160,1024]{1,0:T(8,128)(2,1)}, bf16[160,1024]{1,0:T(8,128)(2,1)}, u32[]{:S(2)}, u32[]{:S(2)}) collective-permute-start(bf16[160,1024]{1,0:T(8,128)(2,1)} %get-tuple-element.486), channel_id=1, source_target_pairs={{0,1},{1,0},{2,3},{3,2},{4,5},{5,4},{6,7},{7,6},{8,9},{9,8},{10,11... | collective-permute-start | bytes 983048 | tf_op jit(solution)/shard_map/ppermute | solution.py:864
  39.8 33.2 %collective-permute-start.3 = (bf16[1024,512]{1,0:T(8,128)(2,1)}, bf16[1024,512]{1,0:T(8,128)(2,1)}, u32[]{:S(2)}, u32[]{:S(2)}) collective-permute-start(bf16[1024,512]{1,0:T(8,128)(2,1)} %broadcast_select_fusion.1), channel_id=1, source_target_pairs={{0,8},{1,9},{2,10},{3,11},{4,12},{5,13},{6,14},{7,15},{8,0},{9,1},... | collective-permute-start | bytes 3145736 | tf_op jit(solution)/shard_map/ppermute | solution.py:873
  41.0 32.5 %collective-permute-start.6 = (bf16[2,512,512]{2,1,0:T(8,128)(2,1)S(1)}, bf16[2,512,512]{2,1,0:T(8,128)(2,1)S(1)}, u32[]{:S(2)}, u32[]{:S(2)}) collective-permute-start(bf16[2,512,512]{2,1,0:T(8,128)(2,1)S(1)} %pad_maximum_fusion.7.refs_13_.refs_14_.refs_11_.refs_23_.refs_12_.refs_15_.refs_17_), channel_id=1, source_target_pairs={{0,2},{1,3},{2,0},{3,1},{4,6},{5,7},{6,4},{7,5},{8,10},{9,11},{10,... | collective-permute-start | bytes 3145736 | tf_op jit(solution)/shard_map/ppermute | solution.py:864
  42.8 30.7 %collective-permute-start.5 = (bf16[2,512,512]{2,1,0:T(8,128)(2,1)S(1)}, bf16[2,512,512]{2,1,0:T(8,128)(2,1)}, u32[]{:S(2)}, u32[]{:S(2)}) collective-permute-start(bf16[2,512,512]{2,1,0:T(8,128)(2,1)S(1)} %pad_maximum_fusion.6.refs_11_.refs_12_.refs_9_.refs_21_.refs_10_.refs_13_.refs_15_), channel_id=1, source_target_pairs={{0,4},{1,5},{2,6},{3,7},{4,0},{5,1},{6,2},{7,3},{8,12},{9,13},{10,... | collective-permute-start | bytes 3145736 | tf_op jit(solution)/shard_map/ppermute | solution.py:864
  43.8 29.7 %collective-permute-start.4 = (bf16[1024,512]{1,0:T(8,128)(2,1)}, bf16[1024,512]{1,0:T(8,128)(2,1)}, u32[]{:S(2)}, u32[]{:S(2)}) collective-permute-start(bf16[1024,512]{1,0:T(8,128)(2,1)} %convert_element_type.120), channel_id=1, source_target_pairs={{8,16},{9,17},{10,18},{11,19},{12,20},{13,21},{14,22},{15,23},{16,... | collective-permute-start | bytes 3145736 | tf_op jit(solution)/shard_map/ppermute | solution.py:873
  45.5 27.5 %collective-permute-start.8 = (bf16[160,1024]{1,0:T(8,128)(2,1)S(1)}, bf16[160,1024]{1,0:T(8,128)(2,1)}, u32[]{:S(2)}, u32[]{:S(2)}) collective-permute-start(bf16[160,1024]{1,0:T(8,128)(2,1)S(1)} %copy-done.59), channel_id=1, source_target_pairs={{0,2},{1,3},{2,0},{3,1},{4,6},{5,7},{6,4},{7,5},{8,10},{9,11},{10,... | collective-permute-start | bytes 983048 | tf_op jit(solution)/shard_map/ppermute | solution.py:864
  78.7 27.2 %collective-permute-start.22 = (bf16[1024,512]{1,0:T(8,128)(2,1)}, bf16[1024,512]{1,0:T(8,128)(2,1)}, u32[]{:S(2)}, u32[]{:S(2)}) collective-permute-start(bf16[1024,512]{1,0:T(8,128)(2,1)} %collective-permute-done.4), channel_id=1, source_target_pairs={{8,0},{9,1},{10,2},{11,3},{12,4},{13,5},{14,6},{15,7},{16,24},{17,... | collective-permute-start | bytes 3145736 | tf_op jit(solution)/shard_map/ppermute | solution.py:873
  91.7 25.7 %collective-permute-start.19 = (bf16[2,512,512]{2,1,0:T(8,128)(2,1)S(1)}, bf16[2,512,512]{2,1,0:T(8,128)(2,1)}, u32[]{:S(2)}, u32[]{:S(2)}) collective-permute-start(bf16[2,512,512]{2,1,0:T(8,128)(2,1)S(1)} %pad_maximum_fusion.9.refs_5_.refs_6_.refs_21_.refs_22_.refs_20_.refs_23_.refs_4_.refs_9_), channel_id=1, source_target_pairs={{0,2},{1,3},{2,0},{3,1},{4,6},{5,7},{6,4},{7,5},{8,10},{9,11},{10,... | collective-permute-start | bytes 3145736 | tf_op jit(solution)/shard_map/ppermute | solution.py:864
  92.8 24.6 %collective-permute-start.20 = (bf16[2,512,512]{2,1,0:T(8,128)(2,1)S(1)}, bf16[2,512,512]{2,1,0:T(8,128)(2,1)}, u32[]{:S(2)}, u32[]{:S(2)}) collective-permute-start(bf16[2,512,512]{2,1,0:T(8,128)(2,1)S(1)} %pad_maximum_fusion.8.refs_3_.refs_4_.refs_19_.refs_20_.refs_18_.refs_21_.refs_2_.refs_7_), channel_id=1, source_target_pairs={{0,1},{1,0},{2,3},{3,2},{4,5},{5,4},{6,7},{7,6},{8,9},{9,8},{10,11... | collective-permute-start | bytes 3145736 | tf_op jit(solution)/shard_map/ppermute | solution.py:864
  93.0 25.5 %collective-permute-start.18 = (bf16[2,512,512]{2,1,0:T(8,128)(2,1)S(1)}, bf16[2,512,512]{2,1,0:T(8,128)(2,1)}, u32[]{:S(2)}, u32[]{:S(2)}) collective-permute-start(bf16[2,512,512]{2,1,0:T(8,128)(2,1)S(1)} %pad_maximum_fusion.8.refs_3_.refs_4_.refs_19_.refs_20_.refs_18_.refs_21_.refs_2_.refs_7_), channel_id=1, source_target_pairs={{0,4},{1,5},{2,6},{3,7},{4,0},{5,1},{6,2},{7,3},{8,12},{9,13},{10,... | collective-permute-start | bytes 3145736 | tf_op jit(solution)/shard_map/ppermute | solution.py:864
  140.8 25.6 %collective-permute-start.28 = (bf16[2,512,512]{2,1,0:T(8,128)(2,1)S(1)}, bf16[2,512,512]{2,1,0:T(8,128)(2,1)S(1)}, u32[]{:S(2)}, u32[]{:S(2)}) collective-permute-start(bf16[2,512,512]{2,1,0:T(8,128)(2,1)S(1)} %pad_maximum_fusion.11.refs_5_.refs_6_.refs_7_.refs_4_), channel_id=1, source_target_pairs={{0,2},{1,3},{2,0},{3,1},{4,6},{5,7},{6,4},{7,5},{8,10},{9,11},{10,... | collective-permute-start | bytes 3145736 | tf_op jit(solution)/shard_map/ppermute | solution.py:864
  142.0 24.4 %collective-permute-start.29 = (bf16[2,512,512]{2,1,0:T(8,128)(2,1)S(1)}, bf16[2,512,512]{2,1,0:T(8,128)(2,1)}, u32[]{:S(2)}, u32[]{:S(2)}) collective-permute-start(bf16[2,512,512]{2,1,0:T(8,128)(2,1)S(1)} %pad_maximum_fusion.10.refs_3_.refs_4_.refs_5_.refs_2_), channel_id=1, source_target_pairs={{0,1},{1,0},{2,3},{3,2},{4,5},{5,4},{6,7},{7,6},{8,9},{9,8},{10,11... | collective-permute-start | bytes 3145736 | tf_op jit(solution)/shard_map/ppermute | solution.py:864
  142.2 25.5 %collective-permute-start.27 = (bf16[2,512,512]{2,1,0:T(8,128)(2,1)S(1)}, bf16[2,512,512]{2,1,0:T(8,128)(2,1)}, u32[]{:S(2)}, u32[]{:S(2)}) collective-permute-start(bf16[2,512,512]{2,1,0:T(8,128)(2,1)S(1)} %pad_maximum_fusion.10.refs_3_.refs_4_.refs_5_.refs_2_), channel_id=1, source_target_pairs={{0,4},{1,5},{2,6},{3,7},{4,0},{5,1},{6,2},{7,3},{8,12},{9,13},{10,... | collective-permute-start | bytes 3145736 | tf_op jit(solution)/shard_map/ppermute | solution.py:864
  170.7 23.9 %collective-permute-start.11 = (bf16[512,512]{1,0:T(8,128)(2,1)}, bf16[512,512]{1,0:T(8,128)(2,1)}, u32[]{:S(2)}, u32[]{:S(2)}) collective-permute-start(bf16[512,512]{1,0:T(8,128)(2,1)} %get-tuple-element.491), channel_id=1, source_target_pairs={{0,4},{1,5},{2,6},{3,7},{4,0},{5,1},{6,2},{7,3},{8,12},{9,13},{10,... | collective-permute-start | bytes 1572872 | tf_op jit(solution)/shard_map/ppermute | solution.py:864
  171.4 23.2 %collective-permute-start.10 = (bf16[512,512]{1,0:T(8,128)(2,1)}, bf16[512,512]{1,0:T(8,128)(2,1)}, u32[]{:S(2)}, u32[]{:S(2)}) collective-permute-start(bf16[512,512]{1,0:T(8,128)(2,1)} %get-tuple-element.492), channel_id=1, source_target_pairs={{0,2},{1,3},{2,0},{3,1},{4,6},{5,7},{6,4},{7,5},{8,10},{9,11},{10,... | collective-permute-start | bytes 1572872 | tf_op jit(solution)/shard_map/ppermute | solution.py:864
  195.8 32.4 %collective-permute-start.36 = (bf16[2,512,512]{2,1,0:T(8,128)(2,1)S(1)}, bf16[2,512,512]{2,1,0:T(8,128)(2,1)}, u32[]{:S(2)}, u32[]{:S(2)}) collective-permute-start(bf16[2,512,512]{2,1,0:T(8,128)(2,1)S(1)} %pad_maximum_fusion.13.refs_15_.refs_19_), channel_id=1, source_target_pairs={{0,1},{1,0},{2,3},{3,2},{4,5},{5,4},{6,7},{7,6},{8,9},{9,8},{10,11... | collective-permute-start | bytes 3145736 | tf_op jit(solution)/shard_map/ppermute | solution.py:864
  195.9 32.4 %collective-permute-start.34 = (bf16[2,512,512]{2,1,0:T(8,128)(2,1)S(1)}, bf16[2,512,512]{2,1,0:T(8,128)(2,1)S(1)}, u32[]{:S(2)}, u32[]{:S(2)}) collective-permute-start(bf16[2,512,512]{2,1,0:T(8,128)(2,1)S(1)} %pad_maximum_fusion.13.refs_15_.refs_19_), channel_id=1, source_target_pairs={{0,2},{1,3},{2,0},{3,1},{4,6},{5,7},{6,4},{7,5},{8,10},{9,11},{10,... | collective-permute-start | bytes 3145736 | tf_op jit(solution)/shard_map/ppermute | solution.py:864
  197.9 30.3 %collective-permute-start.35 = (bf16[2,512,512]{2,1,0:T(8,128)(2,1)S(1)}, bf16[2,512,512]{2,1,0:T(8,128)(2,1)}, u32[]{:S(2)}, u32[]{:S(2)}) collective-permute-start(bf16[2,512,512]{2,1,0:T(8,128)(2,1)S(1)} %pad_maximum_fusion.12.refs_13_.refs_17_), channel_id=1, source_target_pairs={{0,1},{1,0},{2,3},{3,2},{4,5},{5,4},{6,7},{7,6},{8,9},{9,8},{10,11... | collective-permute-start | bytes 3145736 | tf_op jit(solution)/shard_map/ppermute | solution.py:864
  198.1 30.1 %collective-permute-start.33 = (bf16[2,512,512]{2,1,0:T(8,128)(2,1)S(1)}, bf16[2,512,512]{2,1,0:T(8,128)(2,1)}, u32[]{:S(2)}, u32[]{:S(2)}) collective-permute-start(bf16[2,512,512]{2,1,0:T(8,128)(2,1)S(1)} %pad_maximum_fusion.12.refs_13_.refs_17_), channel_id=1, source_target_pairs={{0,4},{1,5},{2,6},{3,7},{4,0},{5,1},{6,2},{7,3},{8,12},{9,13},{10,... | collective-permute-start | bytes 3145736 | tf_op jit(solution)/shard_map/ppermute | solution.py:864
  284.2 37.7 %collective-permute-start.39 = (bf16[4,1024,512]{2,1,0:T(8,128)(2,1)}, bf16[4,1024,512]{2,1,0:T(8,128)(2,1)}, u32[]{:S(2)}, u32[]{:S(2)}) collective-permute-start(bf16[4,1024,512]{2,1,0:T(8,128)(2,1)} %get-tuple-element.302), channel_id=1, source_target_pairs={{0,1},{1,0},{2,3},{3,2},{4,5},{5,4},{6,7},{7,6},{8,9},{9,8},{10,11... | collective-permute-start | bytes 12582920 | tf_op jit(solution)/shard_map/ppermute | solution.py:864
  284.3 37.6 %collective-permute-start.40 = (bf16[4,1024,512]{2,1,0:T(8,128)(2,1)}, bf16[4,1024,512]{2,1,0:T(8,128)(2,1)}, u32[]{:S(2)}, u32[]{:S(2)}) collective-permute-start(bf16[4,1024,512]{2,1,0:T(8,128)(2,1)} %get-tuple-element.303), channel_id=1, source_target_pairs={{0,1},{1,0},{2,3},{3,2},{4,5},{5,4},{6,7},{7,6},{8,9},{9,8},{10,11... | collective-permute-start | bytes 12582920 | tf_op jit(solution)/shard_map/ppermute | solution.py:864
  327.8 63.4 %collective-permute-start.41 = (bf16[2,2,512,512]{3,2,1,0:T(8,128)(2,1)}, bf16[2,2,512,512]{3,2,1,0:T(8,128)(2,1)}, u32[]{:S(2)}, u32[]{:S(2)}) collective-permute-start(bf16[2,2,512,512]{3,2,1,0:T(8,128)(2,1)} %get-tuple-element.318), channel_id=1, source_target_pairs={{0,4},{1,5},{2,6},{3,7},{4,0},{5,1},{6,2},{7,3},{8,12},{9,13},{10,... | collective-permute-start | bytes 6291464 | tf_op jit(solution)/shard_map/ppermute | solution.py:864
  328.5 62.7 %collective-permute-start.42 = (bf16[2,2,512,512]{3,2,1,0:T(8,128)(2,1)}, bf16[2,2,512,512]{3,2,1,0:T(8,128)(2,1)}, u32[]{:S(2)}, u32[]{:S(2)}) collective-permute-start(bf16[2,2,512,512]{3,2,1,0:T(8,128)(2,1)} %get-tuple-element.319), channel_id=1, source_target_pairs={{0,2},{1,3},{2,0},{3,1},{4,6},{5,7},{6,4},{7,5},{8,10},{9,11},{10,... | collective-permute-start | bytes 6291464 | tf_op jit(solution)/shard_map/ppermute | solution.py:864
  402.0 51.4 %collective-permute-start.45 = (bf16[4,1024,512]{2,1,0:T(8,128)(2,1)}, bf16[4,1024,512]{2,1,0:T(8,128)(2,1)}, u32[]{:S(2)}, u32[]{:S(2)}) collective-permute-start(bf16[4,1024,512]{2,1,0:T(8,128)(2,1)} %pad_maximum_fusion), channel_id=1, source_target_pairs={{0,1},{1,0},{2,3},{3,2},{4,5},{5,4},{6,7},{7,6},{8,9},{9,8},{10,11... | collective-permute-start | bytes 12582920 | tf_op jit(solution)/shard_map/ppermute | solution.py:864
  413.7 78.4 %collective-permute-start.51 = (bf16[160,1024]{1,0:T(8,128)(2,1)}, bf16[160,1024]{1,0:T(8,128)(2,1)}, u32[]{:S(2)}, u32[]{:S(2)}) collective-permute-start(bf16[160,1024]{1,0:T(8,128)(2,1)} %get-tuple-element.481), channel_id=1, source_target_pairs={{0,3},{1,2},{2,1},{3,0},{4,7},{5,6},{6,5},{7,4},{8,11},{9,10},{10,... | collective-permute-start | bytes 983048 | tf_op jit(solution)/shard_map/ppermute | solution.py:864
  414.7 80.4 %collective-permute-start.50 = (bf16[160,1024]{1,0:T(8,128)(2,1)}, bf16[160,1024]{1,0:T(8,128)(2,1)}, u32[]{:S(2)}, u32[]{:S(2)}) collective-permute-start(bf16[160,1024]{1,0:T(8,128)(2,1)} %get-tuple-element.482), channel_id=1, source_target_pairs={{0,2},{1,3},{2,0},{3,1},{4,6},{5,7},{6,4},{7,5},{8,10},{9,11},{10,... | collective-permute-start | bytes 983048 | tf_op jit(solution)/shard_map/ppermute | solution.py:864
  422.1 31.3 %collective-permute-start.43 = (bf16[2,1,512,512]{3,2,1,0:T(8,128)(2,1)}, bf16[2,1,512,512]{3,2,1,0:T(8,128)(2,1)S(1)}, u32[]{:S(2)}, u32[]{:S(2)}) collective-permute-start(bf16[2,1,512,512]{3,2,1,0:T(8,128)(2,1)} %get-tuple-element.338), channel_id=1, source_target_pairs={{0,2},{1,3},{2,0},{3,1},{4,6},{5,7},{6,4},{7,5},{8,10},{9,11},{10,... | collective-permute-start | bytes 3145736 | tf_op jit(solution)/shard_map/ppermute | solution.py:864
  422.9 30.5 %collective-permute-start.44 = (bf16[2,1,512,512]{3,2,1,0:T(8,128)(2,1)}, bf16[2,1,512,512]{3,2,1,0:T(8,128)(2,1)}, u32[]{:S(2)}, u32[]{:S(2)}) collective-permute-start(bf16[2,1,512,512]{3,2,1,0:T(8,128)(2,1)} %get-tuple-element.339), channel_id=1, source_target_pairs={{0,4},{1,5},{2,6},{3,7},{4,0},{5,1},{6,2},{7,3},{8,12},{9,13},{10,... | collective-permute-start | bytes 3145736 | tf_op jit(solution)/shard_map/ppermute | solution.py:864
  465.0 30.1 %collective-permute-start.46 = (bf16[1024,512]{1,0:T(8,128)(2,1)}, bf16[1024,512]{1,0:T(8,128)(2,1)S(1)}, u32[]{:S(2)}, u32[]{:S(2)}) collective-permute-start(bf16[1024,512]{1,0:T(8,128)(2,1)} %get-tuple-element.361), channel_id=1, source_target_pairs={{0,8},{1,9},{2,10},{3,11},{4,12},{5,13},{6,14},{7,15},{8,0},{9,1},... | collective-permute-start | bytes 3145736 | tf_op jit(solution)/shard_map/ppermute | solution.py:873
  466.7 28.4 %collective-permute-start.47 = (bf16[1,2,512,512]{3,2,1,0:T(8,128)(2,1)}, bf16[1,2,512,512]{3,2,1,0:T(8,128)(2,1)S(1)}, u32[]{:S(2)}, u32[]{:S(2)}) collective-permute-start(bf16[1,2,512,512]{3,2,1,0:T(8,128)(2,1)} %get-tuple-element.362), channel_id=1, source_target_pairs={{0,4},{1,5},{2,6},{3,7},{4,0},{5,1},{6,2},{7,3},{8,12},{9,13},{10,... | collective-permute-start | bytes 3145736 | tf_op jit(solution)/shard_map/ppermute | solution.py:864
  467.9 27.2 %collective-permute-start.48 = (bf16[1,2,512,512]{3,2,1,0:T(8,128)(2,1)}, bf16[1,2,512,512]{3,2,1,0:T(8,128)(2,1)S(1)}, u32[]{:S(2)}, u32[]{:S(2)}) collective-permute-start(bf16[1,2,512,512]{3,2,1,0:T(8,128)(2,1)} %get-tuple-element.363), channel_id=1, source_target_pairs={{0,2},{1,3},{2,0},{3,1},{4,6},{5,7},{6,4},{7,5},{8,10},{9,11},{10,... | collective-permute-start | bytes 3145736 | tf_op jit(solution)/shard_map/ppermute | solution.py:864
  495.1 36.1 %collective-permute-start.52 = (bf16[4,1024,512]{2,1,0:T(8,128)(2,1)}, bf16[4,1024,512]{2,1,0:T(8,128)(2,1)}, u32[]{:S(2)}, u32[]{:S(2)}) collective-permute-start(bf16[4,1024,512]{2,1,0:T(8,128)(2,1)} %pad_maximum_fusion.2), channel_id=1, source_target_pairs={{0,1},{1,0},{2,3},{3,2},{4,5},{5,4},{6,7},{7,6},{8,9},{9,8},{10,11... | collective-permute-start | bytes 12582920 | tf_op jit(solution)/shard_map/ppermute | solution.py:864
  503.9 27.3 %collective-permute-start.53 = (bf16[1,1,512,512]{3,2,1,0:T(8,128)(2,1)}, bf16[1,1,512,512]{3,2,1,0:T(8,128)(2,1)S(1)}, u32[]{:S(2)}, u32[]{:S(2)}) collective-permute-start(bf16[1,1,512,512]{3,2,1,0:T(8,128)(2,1)} %get-tuple-element.387), channel_id=1, source_target_pairs={{0,2},{1,3},{2,0},{3,1},{4,6},{5,7},{6,4},{7,5},{8,10},{9,11},{10,... | collective-permute-start | bytes 1572872 | tf_op jit(solution)/shard_map/ppermute | solution.py:864
  505.0 26.2 %collective-permute-start.54 = (bf16[1,1,512,512]{3,2,1,0:T(8,128)(2,1)}, bf16[1,1,512,512]{3,2,1,0:T(8,128)(2,1)S(1)}, u32[]{:S(2)}, u32[]{:S(2)}) collective-permute-start(bf16[1,1,512,512]{3,2,1,0:T(8,128)(2,1)} %get-tuple-element.388), channel_id=1, source_target_pairs={{0,4},{1,5},{2,6},{3,7},{4,0},{5,1},{6,2},{7,3},{8,12},{9,13},{10,... | collective-permute-start | bytes 1572872 | tf_op jit(solution)/shard_map/ppermute | solution.py:864
  535.2 26.8 %collective-permute-start.55 = (bf16[1,2,512,512]{3,2,1,0:T(8,128)(2,1)}, bf16[1,2,512,512]{3,2,1,0:T(8,128)(2,1)S(1)}, u32[]{:S(2)}, u32[]{:S(2)}) collective-permute-start(bf16[1,2,512,512]{3,2,1,0:T(8,128)(2,1)} %get-tuple-element.403), channel_id=1, source_target_pairs={{0,4},{1,5},{2,6},{3,7},{4,0},{5,1},{6,2},{7,3},{8,12},{9,13},{10,... | collective-permute-start | bytes 3145736 | tf_op jit(solution)/shard_map/ppermute | solution.py:864
  536.4 25.6 %collective-permute-start.56 = (bf16[1,2,512,512]{3,2,1,0:T(8,128)(2,1)}, bf16[1,2,512,512]{3,2,1,0:T(8,128)(2,1)}, u32[]{:S(2)}, u32[]{:S(2)}) collective-permute-start(bf16[1,2,512,512]{3,2,1,0:T(8,128)(2,1)} %get-tuple-element.404), channel_id=1, source_target_pairs={{0,2},{1,3},{2,0},{3,1},{4,6},{5,7},{6,4},{7,5},{8,10},{9,11},{10,... | collective-permute-start | bytes 3145736 | tf_op jit(solution)/shard_map/ppermute | solution.py:864
  562.0 38.8 %collective-permute-start.62 = (bf16[1024,512]{1,0:T(8,128)(2,1)}, bf16[1024,512]{1,0:T(8,128)(2,1)}, u32[]{:S(2)}, u32[]{:S(2)}) collective-permute-start(bf16[1024,512]{1,0:T(8,128)(2,1)} %get-tuple-element.442), channel_id=1, source_target_pairs={{0,8},{1,9},{2,10},{3,11},{4,12},{5,13},{6,14},{7,15},{24,16},{25,... | collective-permute-start | bytes 3145736 | tf_op jit(solution)/shard_map/ppermute | solution.py:873
  569.8 21.9 %collective-permute-start.57 = (bf16[1,1,512,512]{3,2,1,0:T(8,128)(2,1)}, bf16[1,1,512,512]{3,2,1,0:T(8,128)(2,1)S(1)}, u32[]{:S(2)}, u32[]{:S(2)}) collective-permute-start(bf16[1,1,512,512]{3,2,1,0:T(8,128)(2,1)} %get-tuple-element.430), channel_id=1, source_target_pairs={{0,2},{1,3},{2,0},{3,1},{4,6},{5,7},{6,4},{7,5},{8,10},{9,11},{10,... | collective-permute-start | bytes 1572872 | tf_op jit(solution)/shard_map/ppermute | solution.py:864
  570.8 20.9 %collective-permute-start.58 = (bf16[1,1,512,512]{3,2,1,0:T(8,128)(2,1)}, bf16[1,1,512,512]{3,2,1,0:T(8,128)(2,1)S(1)}, u32[]{:S(2)}, u32[]{:S(2)}) collective-permute-start(bf16[1,1,512,512]{3,2,1,0:T(8,128)(2,1)} %get-tuple-element.431), channel_id=1, source_target_pairs={{0,4},{1,5},{2,6},{3,7},{4,0},{5,1},{6,2},{7,3},{8,12},{9,13},{10,... | collective-permute-start | bytes 1572872 | tf_op jit(solution)/shard_map/ppermute | solution.py:864
  586.0 39.6 %collective-permute-start.64 = (bf16[1024,512]{1,0:T(8,128)(2,1)}, bf16[1024,512]{1,0:T(8,128)(2,1)}, u32[]{:S(2)}, u32[]{:S(2)}) collective-permute-start(bf16[1024,512]{1,0:T(8,128)(2,1)} %fusion), channel_id=1, source_target_pairs={{0,16},{1,17},{2,18},{3,19},{4,20},{5,21},{6,22},{7,23},{8,24},{9,... | collective-permute-start | bytes 3145736 | tf_op jit(solution)/shard_map/ppermute | solution.py:873
  598.6 29.5 %collective-permute-start.61 = (bf16[1024,512]{1,0:T(8,128)(2,1)}, bf16[1024,512]{1,0:T(8,128)(2,1)S(1)}, u32[]{:S(2)}, u32[]{:S(2)}) collective-permute-start(bf16[1024,512]{1,0:T(8,128)(2,1)} %get-tuple-element.440), channel_id=1, source_target_pairs={{8,0},{9,1},{10,2},{11,3},{12,4},{13,5},{14,6},{15,7},{24,16},{25,... | collective-permute-start | bytes 3145736 | tf_op jit(solution)/shard_map/ppermute | solution.py:873
  604.2 24.0 %collective-permute-start.63 = (bf16[1024,512]{1,0:T(8,128)(2,1)}, bf16[1024,512]{1,0:T(8,128)(2,1)}, u32[]{:S(2)}, u32[]{:S(2)}) collective-permute-start(bf16[1024,512]{1,0:T(8,128)(2,1)} %fusion.1), channel_id=1, source_target_pairs={{16,8},{17,9},{18,10},{19,11},{20,12},{21,13},{22,14},{23,15}} | collective-permute-start | bytes 3145736 | tf_op jit(solution)/shard_map/ppermute | solution.py:873
  631.6 23.6 %collective-permute-start.67 = (bf16[1024,512]{1,0:T(8,128)(2,1)S(1)}, bf16[1024,512]{1,0:T(8,128)(2,1)S(1)}, u32[]{:S(2)}, u32[]{:S(2)}) collective-permute-start(bf16[1024,512]{1,0:T(8,128)(2,1)S(1)} %add_convert_fusion), channel_id=1, source_target_pairs={{16,0},{17,1},{18,2},{19,3},{20,4},{21,5},{22,6},{23,7}} | collective-permute-start | bytes 3145736 | tf_op jit(solution)/shard_map/ppermute | solution.py:873
  (108 other events, 1078.8 us)

commit v7 on v6

--- a/solution.py
+++ b/solution.py
@@ -369,15 +369,18 @@
                 (chunk % 2 == 0, evens, lower_place, 1),
                 (chunk % 2 == 1, odds, lower_place, 1),
             )
-            for condition, array, index, part in copies:
-
-                @pl.when(wanted & condition)
-                def _(array=array, index=index, part=part):
-                    pltpu.make_async_copy(
-                        array.at[index],
-                        buffer.at[turn, pl.ds(part * half, half), :],
-                        semaphores.at[turn, part],
-                    ).start()
+
+            @pl.when(wanted)
+            def _(copies=copies):
+                for condition, array, index, part in copies:
+
+                    @pl.when(condition)
+                    def _(array=array, index=index, part=part):
+                        pltpu.make_async_copy(
+                            array.at[index],
+                            buffer.at[turn, pl.ds(part * half, half), :],
+                            semaphores.at[turn, part],
+                        ).start()
 
 
 def wait_fetch(source, refs, buffer, semaphores, turn):
@@ -390,9 +393,7 @@
         ).wait()
 
 
-def fetched(source, refs, buffer, semaphores, plane, order, item, count):
-    turn = item % 2
-
+def start_fetches(source, refs, buffer, semaphores, plane, order, item, count):
     @pl.when(item == 0)
     def _():
         side, chunk = order(0)
@@ -403,8 +404,10 @@
         side, chunk = order(item + 1)
         start_fetch(source, refs, buffer, semaphores, plane, side, chunk, (item + 1) % 2)
 
-    wait_fetch(source, refs, buffer, semaphores, turn)
-    return buffer.at[turn]
+
+def fetched(source, refs, buffer, semaphores, item):
+    wait_fetch(source, refs, buffer, semaphores, item % 2)
+    return buffer.at[item % 2]
 
 
 def vector_part(vectors_ref, row, first, width):
@@ -435,7 +438,7 @@
     refs = refs[len(down_refs) :]
     out_ref, back_ref, grad_up_ref, grad_down_ref, grad_bias_ref = refs[:5]
     low_ref = refs[5] if norm else values_ref
-    low_turned, grad_turned, active_ref, hidden_ref = refs[-8:-4]
+    out_total, back_total, low_turned, grad_turned, active_ref, hidden_ref = refs[-10:-4]
     up_buffer, up_semaphores, down_buffer, down_semaphores = refs[-4:]
     plane = place_ref[PLACE_PLANE]
     step = pl.program_id(0)
@@ -444,8 +447,8 @@
     def order(item):
         return 0, item
 
-    up_chunk = fetched(up_source, up_refs, up_buffer, up_semaphores, plane, order, step, count)
-    down_chunk = fetched(
+    start_fetches(up_source, up_refs, up_buffer, up_semaphores, plane, order, step, count)
+    start_fetches(
         down_source, down_refs, down_buffer, down_semaphores, plane, order, step, count
     )
 
@@ -459,11 +462,11 @@
                 ).astype(BF16)
         low_turned[...] = low_ref[...].T
         grad_turned[...] = grad_ref[...].T
-        out_ref[...] = jnp.zeros_like(out_ref)
-        back_ref[...] = jnp.zeros_like(back_ref)
-
-    up = up_chunk[...]
-    down = down_chunk[...]
+        out_total[...] = jnp.zeros_like(out_total)
+        back_total[...] = jnp.zeros_like(back_total)
+
+    up = fetched(up_source, up_refs, up_buffer, up_semaphores, step)[...]
+    down = fetched(down_source, down_refs, down_buffer, down_semaphores, step)[...]
     total = jnp.zeros((1, up.shape[1]), F32)
     pieces = low_ref.shape[0] // FEED_ROWS
     for piece in range(pieces):
@@ -474,13 +477,18 @@
         active_ref[rows, :] = active_low
         hidden_ref[rows, :] = hidden_low
         total = total + jnp.sum(hidden_low.astype(F32), axis=0, keepdims=True)
-        out_ref[rows, :] += dot_last(active_low, down)
-        back_ref[rows, :] += dot_last(hidden_low, up)
+        out_total[rows, :] += dot_last(active_low, down)
+        back_total[rows, :] += dot_last(hidden_low, up)
     grad_bias_ref[0] = total
     for piece in range(low_turned.shape[0] // FEED_ROWS):
         rows = slice(piece * FEED_ROWS, (piece + 1) * FEED_ROWS)
         grad_down_ref[0, rows, :] = dot(grad_turned[rows, :], active_ref[...]).astype(BF16)
         grad_up_ref[0, rows, :] = dot(low_turned[rows, :], hidden_ref[...]).astype(BF16)
+
+    @pl.when(step == count - 1)
+    def _():
+        out_ref[...] = out_total[...].astype(BF16)
+        back_ref[...] = back_total[...].astype(BF16)
 
 
 def feed_half(place, values, grad, vectors, bias, slots, side, norm):
@@ -503,8 +511,8 @@
         pl.BlockSpec((1, 1, width), lambda step, place: (step ^ place[1], 0, 0)),
     ]
     out_shape = [
-        jax.ShapeDtypeStruct((row_count, model), F32),
-        jax.ShapeDtypeStruct((row_count, model), F32),
+        jax.ShapeDtypeStruct((row_count, model), BF16),
+        jax.ShapeDtypeStruct((row_count, model), BF16),
         jax.ShapeDtypeStruct((steps, model, width), BF16),
         jax.ShapeDtypeStruct((steps, model, width), BF16),
         jax.ShapeDtypeStruct((steps, 1, width), F32),
@@ -531,6 +539,8 @@
             + down_source.specs(),
             out_specs=out_specs,
             scratch_shapes=[
+                pltpu.VMEM((row_count, model), F32),
+                pltpu.VMEM((row_count, model), F32),
                 pltpu.VMEM((model, row_count), BF16),
                 pltpu.VMEM((model, row_count), BF16),
                 pltpu.VMEM((row_count, width), BF16),
@@ -569,9 +579,9 @@
     values_ref, vectors_ref, stream_ref = refs[:3]
     grad_refs = refs[3 : 3 + count]
     out_ref, low_ref, sums_ref = refs[3 + count :]
-    grad = grad_refs[0][...]
+    grad = grad_refs[0][...].astype(F32)
     for grad_ref in grad_refs[1:]:
-        grad = grad + grad_ref[...]
+        grad = grad + grad_ref[...].astype(F32)
     result, normal = norm_back_rows(
         values_ref[...], grad, vectors_ref[row : row + 1, :], stream_ref[...]
     )
@@ -615,8 +625,11 @@
     source_refs = refs[: len(source.operands)]
     refs = refs[len(source_refs) :]
     out_ref = refs.pop(0)
-    low_ref = refs.pop(0) if norm is not None else values_ref
-    buffer, semaphores = refs
+    low_ref = refs.pop(0) if norm is not None else None
+    buffer, semaphores, held_ref, load_semaphore = refs
+    load = pltpu.make_async_copy(values_ref, held_ref, load_semaphore)
+    values_ref = held_ref
+    low_ref = held_ref if low_ref is None else low_ref
     model = values_ref.shape[1]
     width = out_ref.shape[1]
     parts = model // (2 * width)
@@ -626,13 +639,18 @@
     def order(item):
         return item % 2, (block * parts + item // 2) ^ place_ref[1]
 
-    columns_ref = fetched(
+    @pl.when(item == 0)
+    def _():
+        load.start()
+
+    start_fetches(
         source, source_refs, buffer, semaphores, place_ref[PLACE_PLANE], order, item, count
     )
-    if norm is not None:
-
-        @pl.when(item == 0)
-        def _():
+
+    @pl.when(item == 0)
+    def _():
+        load.wait()
+        if norm is not None:
             for first in range(0, values_ref.shape[0], QUERY_ROWS):
                 rows = slice(first, first + QUERY_ROWS)
                 low_ref[rows, :] = normalize(
@@ -641,6 +659,7 @@
                     vectors_ref[norm + 1 : norm + 2, :],
                 ).astype(BF16)
 
+    columns_ref = fetched(source, source_refs, buffer, semaphores, item)
     inside = item // 2 % parts
     column = (2 * inside + (item % 2 ^ place_ref[0])) * width
     row_count = values_ref.shape[0]
@@ -677,7 +696,7 @@
         (row_count, width),
         lambda item, place: (0, 2 * (item // 2) + (item % 2 ^ place[0])),
     )
-    in_specs = [whole((row_count, model)), whole((VECTOR_ROWS, model))]
+    in_specs = [pl.BlockSpec(memory_space=pl.ANY), whole((VECTOR_ROWS, model))]
     operands = [values, vectors]
     if residual is not None:
         in_specs.append(panel)
@@ -701,7 +720,8 @@
             grid=(2 * parts * len(lines),),
             in_specs=in_specs + source.specs(),
             out_specs=out_specs,
-            scratch_shapes=source.scratch(),
+            scratch_shapes=source.scratch()
+            + [pltpu.VMEM(values.shape, values.dtype), pltpu.SemaphoreType.DMA],
         ),
         out_shape=out_shape,
         compiler_params=pltpu.CompilerParams(vmem_limit_bytes=60 << 20),
@@ -734,7 +754,7 @@
     def order(item):
         return item % 2, (block * parts + item // 2) ^ place_ref[1]
 
-    columns_ref = fetched(
+    start_fetches(
         source, source_refs, buffer, semaphores, place_ref[PLACE_PLANE], order, item, steps
     )
     if row is not None:
@@ -750,6 +770,7 @@
                 load.start()
         total_ref[...] = jnp.zeros_like(total_ref)
 
+    columns_ref = fetched(source, source_refs, buffer, semaphores, item)
     for number, grad_ref in enumerate(grad_refs):
 
         @pl.when(item // (2 * parts) == number)
@@ -1282,11 +1303,45 @@
     return padded.reshape(device_count, tiles * sublanes, LANES)
 
 
-def vector_send(pieces, device, bit):
-    halves = pieces.reshape((2, -1) + pieces.shape[1:])
+def vector_kernel(one_ref, two_ref, three_ref, self_ref, cross_ref, up_ref, out_ref):
+    rows = (
+        (one_ref, 0),
+        (one_ref, 1),
+        (two_ref, 0),
+        (two_ref, 1),
+        (three_ref, 0),
+        (three_ref, 1),
+        (self_ref, 0),
+        (self_ref, 1),
+        (two_ref, 2),
+        (cross_ref, 0),
+        (cross_ref, 1),
+        (three_ref, 2),
+        (three_ref, 3),
+        (up_ref, 0),
+        (up_ref, 1),
+        (up_ref, 2),
+        (up_ref, 3),
+    )
+    out_ref[...] = jnp.zeros_like(out_ref)
+    for number, (source, row) in enumerate(rows):
+        out_ref[number : number + 1, :] = source[row : row + 1, :]
+
+
+def vector_table(sums_one, sums_two, sums_three, self_sums, cross_sums, up_bias):
+    return pl.pallas_call(
+        vector_kernel,
+        out_shape=jax.ShapeDtypeStruct((VECTOR_ROWS, sums_one.shape[1]), F32),
+        compiler_params=pltpu.CompilerParams(vmem_limit_bytes=60 << 20),
+        cost_estimate=SMALL,
+    )(sums_one, sums_two, sums_three, self_sums, cross_sums, up_bias)
+
+
+def vector_send(terms, device, bit):
+    half = terms.shape[1] // 2
     mine = (device // bit) % 2
-    kept = lax.dynamic_index_in_dim(halves, mine, 0, keepdims=False)
-    sent = lax.dynamic_index_in_dim(halves, 1 - mine, 0, keepdims=False)
+    kept = lax.dynamic_slice_in_dim(terms, mine * half, half, 1)
+    sent = lax.dynamic_slice_in_dim(terms, (1 - mine) * half, half, 1)
     return kept, sent
 
 
@@ -1339,34 +1394,24 @@
     )
     parts = spread_begin(own)
     got = spread_swaps(parts, 0, device_count)
-    first, got, vector_pieces, own = pinned(first, got, vector_pieces, own)
+    first, got, vector_pieces, own, memory_parts = pinned(
+        first, got, vector_pieces, own, memory_parts
+    )
     held = jnp.where((plane == 0) | (plane == 3), own, first)
     near = move_planes(held, NEAR, plane_size)
     middle = move_planes(own, ((1, 2), (2, 1)), plane_size)
     parts, got = spread_on(parts, got, device_count)
-    near, middle, first, got, memory_parts = pinned(near, middle, first, got, memory_parts)
+    near, middle, first, got = pinned(near, middle, first, got)
     slot_zero = flat_slot(parts, got)
     even = plane % 2 == 0
     parts_one = spread_begin(jnp.where(even, first, near))
     got_one = spread_swaps(parts_one, 0, device_count)
     last = move_planes(middle, ((1, 0), (2, 3)), plane_size)
     zero_away = swap_cores(slot_zero, device_count)
-    got_one, zero_away = pinned(got_one, zero_away)
-    vector_rows = jnp.swapaxes(vector_pieces, 0, 1).reshape(vector_shape[0], model).astype(F32)
-    table = jnp.pad(vector_rows, ((0, VECTOR_ROWS - vector_shape[0]), (0, 0)))
-    parts_one, got_one = spread_on(parts_one, got_one, device_count)
-    one_away = swap_cores(parts_one, device_count)
-    got_one, one_away, last, vector_rows, table = pinned(
-        got_one, one_away, last, vector_rows, table
-    )
-    got_one_away = swap_cores(got_one, device_count)
-    parts_two = spread_begin(jnp.where((plane == 1) | (plane == 2), middle, last))
-    got_two = spread_swaps(parts_two, 0, device_count)
-    slots = [
-        (slot_zero, tuple(zero_away)),
-        (flat_slot(parts_one, got_one), flat_slot(one_away, got_one_away)),
-    ]
-
+    got_one, zero_away, memory_parts, near, first, upstream, slot_masks = pinned(
+        got_one, zero_away, memory_parts, near, first, upstream, slot_masks
+    )
+    parts_three = spread_begin(jnp.where(even, near, first))
     memory_here = jnp.concatenate(memory_parts, axis=0)
     live_rows = (jnp.arange(row_count) < page_lengths[0]).astype(F32)[:, None]
     slots_here = lax.dynamic_slice_in_dim(slot_masks, member, 1, 0).reshape(group_size, quarter)
@@ -1375,6 +1420,24 @@
     slot_bias = jnp.broadcast_to(
         jnp.where(slots_here > 0, 0.0, MASKED).astype(F32), (group_size * SLOT_PAD, LANES)
     )
+    grad_low_three = (upstream.astype(F32) * live_rows).astype(BF16)
+    vector_rows = jnp.swapaxes(vector_pieces, 0, 1).reshape(vector_shape[0], model).astype(F32)
+    table = jnp.pad(vector_rows, ((0, VECTOR_ROWS - vector_shape[0]), (0, 0)))
+    parts_one, got_one = spread_on(parts_one, got_one, device_count)
+    one_away = swap_cores(parts_one, device_count)
+    bias_up = vector_rows[13:17].reshape(-1, 1, width)
+    last, table, bias_up, slot_bias, grad_low_three, memory_here, parts_three = pinned(
+        last, table, bias_up, slot_bias, grad_low_three, memory_here, parts_three
+    )
+    parts_two = spread_begin(jnp.where((plane == 1) | (plane == 2), middle, last))
+    got_one, one_away, parts_two, table = pinned(got_one, one_away, parts_two, table)
+    got_one_away = swap_cores(got_one, device_count)
+    got_two = spread_swaps(parts_two, 0, device_count)
+    slots = [
+        (slot_zero, tuple(zero_away)),
+        (flat_slot(parts_one, got_one), flat_slot(one_away, got_one_away)),
+    ]
+
     pairs = HEADS // 2
     self_firsts = (0, pairs, 2 * pairs)
     cross_firsts = (0, 0, pairs)
@@ -1388,7 +1451,6 @@
     attended, self_log = attention_forward(self_low, self_low, self_low, self_firsts)
     got_two, two_away, attended = pinned(got_two, two_away, attended)
     got_two_away = swap_cores(got_two, device_count)
-    parts_three = spread_begin(jnp.where(even, near, first))
     got_three = spread_swaps(parts_three, 0, device_count)
     after_self = project(
         here, attended, table, slots, 0, 3, ((8, 1.0),), residual=tokens, out_type=F32
@@ -1410,13 +1472,11 @@
     after_cross = project(
         here, merged, table, slots, 1, 3, ((11, 1.0),), residual=after_self, out_type=F32
     )
-    grad_low_three = (upstream.astype(F32) * live_rows).astype(BF16)
     got_three_away, after_cross, grad_low_three = pinned(
         got_three_away, after_cross, grad_low_three
     )
     slots.append((flat_slot(parts_three, got_three), flat_slot(three_away, got_three_away)))
 
-    bias_up = vector_rows[13:17].reshape(-1, 1, width)
     out_a, back_a, up_sent, down_sent, bias_sent, low_three = feed_half(
         away, after_cross, grad_low_three, table, bias_up, slots, 1, True
     )
@@ -1540,7 +1600,8 @@
     feed_sent, cross_sends, self_whole = pinned(
         feed_kept.astype(BF16), cross_sends, self_whole
     )
-    feed_got = move_planes(feed_sent, ((0, 2), (1, 3)), plane_size)
+    feed_middle = model // 2
+    feed_upper = move_planes(feed_sent[:feed_middle], ((0, 2), (1, 3)), plane_size)
     cross_swaps = stage_swaps(cross_sends, cross_sum, device_count)
     self_whole, (queries_own, keys_own, values_own) = attention_backward(
         here, width, *self_operands, self_whole
@@ -1575,36 +1636,19 @@
     sums_one, cross_swaps = pinned(sums_one, cross_sum.swaps)
     cross_sum.swaps = list(cross_swaps)
     cross_total, cross_sent = plane_totals(here, cross_sum)
-    self_swaps, cross_sent, sums_one = pinned(self_swaps, cross_sent, sums_one)
+    self_swaps, cross_sent, sums_one, feed_upper, feed_sent = pinned(
+        self_swaps, cross_sent, sums_one, feed_upper, feed_sent
+    )
+    feed_lower = move_planes(feed_sent[feed_middle:], ((0, 2), (1, 3)), plane_size)
     cross_got = move_planes(cross_sent, ((0, 1), (3, 2)), plane_size)
     self_sum = self_sum.joined(self_swaps)
     self_sends = stage_sends(here, self_sum, device_count)
     self_sends, sums_one = pinned(self_sends, sums_one)
     self_swaps = stage_swaps(self_sends, self_sum, device_count)
-    vector_head = jnp.stack(
-        [
-            sums_one[0],
-            sums_one[1],
-            sums_two[0],
-            sums_two[1],
-            sums_three[0],
-            sums_three[1],
-            self_sums[0],
-            self_sums[1],
-            sums_two[2],
-            cross_sums[0],
-            cross_sums[1],
-            sums_three[2],
-            sums_three[3],
-        ],
-        axis=0,
-    )
-    vector_terms = jnp.concatenate([vector_head, grad_bias_up], axis=0)
-    vector_terms = jnp.swapaxes(
-        vector_terms.reshape(vector_shape[0], device_count, vector_shape[1]), 0, 1
+    vector_terms = vector_table(
+        sums_one, sums_two, sums_three, self_sums, cross_sums, grad_bias_up
     )
     vector_bits = [1 << number for number in reversed(range(device_count.bit_length() - 1))]
-    vector_terms = pad_vectors(vector_terms.reshape(device_count, -1), 8)
     vector_kept, vector_sent = vector_send(vector_terms, device, vector_bits[0])
     vector_got = swap_bit(vector_sent, device_count, vector_bits[0])
 
@@ -1618,16 +1662,18 @@
     self_sent, vector_got = pinned(self_sent, vector_got)
     self_got = move_planes(self_sent, ((1, 0), (3, 2)), plane_size)
     vector_kept, vector_got = vector_next(vector_kept, vector_got, 1)
-    result = (after_cross + (out_a + out_b) + vector_rows[12]) * live_rows
+    branch = out_a.astype(F32) + out_b.astype(F32)
+    result = (after_cross + branch + vector_rows[12]) * live_rows
     mixed = result.astype(BF16)
     mixed, vector_got = pinned(mixed, vector_got)
     vector_kept, vector_got = vector_next(vector_kept, vector_got, 2)
     cross_total = cross_total + cross_got.astype(F32)
     cross_got = move_planes(cross_total.astype(BF16), ((2, 1),), plane_size)
 
-    self_got, cross_got, feed_got, vector_got = pinned(
-        self_got, cross_got, feed_got, vector_got
-    )
+    self_got, cross_got, feed_lower, vector_got = pinned(
+        self_got, cross_got, feed_lower, vector_got
+    )
+    feed_got = jnp.concatenate([feed_upper, feed_lower], axis=0)
     self_sent = (self_total + self_got.astype(F32)).astype(BF16)
     self_sent, cross_got, feed_got, memory_back, vector_got = pinned(
         self_sent, cross_got, feed_got, memory_back, vector_got
@@ -1645,7 +1691,7 @@
     for number in range(4, len(vector_bits)):
         vector_kept, vector_got = vector_next(vector_kept, vector_got, number)
     group_other, self_far, vector_got = pinned(group_other, self_far, vector_got)
-    vector_grad = (vector_kept + vector_got).reshape(-1)[: vectors.size].reshape(vector_shape)
+    vector_grad = (vector_kept + vector_got)[: vector_shape[0]]
     (
         weight_grad,
         weight_first,

time: 691 us -> 682 us (0.987)
  local copies, waits for them, and re-layouts: 49.1 us -> 32.3 us
    ppermute x59, waiting for transfers between devices: 71.2 us -> 51 us  [swap_bit(): lax.ppermute(values, AXES, [(item, item ^ bit) for item in range(device_c...]
    ppermute x10 -> x11, waiting for transfers between devices: 18.6 us -> 36 us  [move_planes(): return lax.ppermute(values, AXES, pairs)]
    concatenate x16 -> x0, local copies, waits for them, and re-layouts: 8.57 us -> none  [local(): vector_terms = jnp.concatenate([vector_head, grad_bias_up], axis=0)]
    all_to_all x1, waiting for transfers between devices: 15.5 us -> 23.2 us  [exchange_vectors(): got = lax.all_to_all(padded, AXES, split_axis=0, concat_axis=0, tiled=True)]
    ppermute x10 -> x11, starting transfers between devices: 21.8 us -> 26.9 us  [move_planes(): return lax.ppermute(values, AXES, pairs)]
  transfers between devices with their start and end apart: 70 -> 71, of which waited for: 13 -> 18; matrix products, arithmetic and copies ran while one was open for 16% -> 14% of each run, Pallas kernels for 43% -> 43%
where the time goes in v7:
time: 682 us; the launch traced here: 676 us
  Pallas kernels  369 us (54%)
  waiting for transfers between devices  110 us (16%)
  starting transfers between devices  71.8 us (11%)
  other arithmetic  54.1 us (8%)
  matrix products  34.8 us (5%)
  local copies, waits for them, and re-layouts  32.3 us (5%)
    pallas_call x2, Pallas kernels, feed_half(): pl.pallas_call(functools.partial(feed_kernel, norm=norm, up_source=up_sou...  76.8 us
    pallas_call x4, Pallas kernels, attention_backward(): pl.pallas_call(functools.partial(attention_backward_kernel, causal=causal...  70 us
    pallas_call x5, Pallas kernels, project_back(): pl.pallas_call(functools.partial(project_back_kernel, source=source, bloc...  55.2 us
    ppermute x59, waiting for transfers between devices, swap_bit(): lax.ppermute(values, AXES, [(item, item ^ bit) for item in range(device_c...  51 us
    pallas_call x5, Pallas kernels, project(): pl.pallas_call(functools.partial(project_kernel, source=source, block=blo...  49.3 us
    ppermute x59, starting transfers between devices, swap_bit(): lax.ppermute(values, AXES, [(item, item ^ bit) for item in range(device_c...  42.4 us
    pallas_call x2, Pallas kernels, attention_forward(): pl.pallas_call(functools.partial(attention_forward_kernel, causal=causal)...  36.6 us
    ppermute x11, waiting for transfers between devices, move_planes(): return lax.ppermute(values, AXES, pairs)  36 us
  transfers between devices with their start and end apart: 71, of which 18 were waited for; matrix products, arithmetic and copies ran while one was open for 14% of the time, Pallas kernels for 43%

profile of v7, /device:TPU:0, one launch (start us, length us, event | category | flops | bytes accessed | tf_op | source)
XLA Modules:
  0.0 675.7 jit_solution(8115128678953527772)
XLA Ops:
  3.5 4.0 collective-permute-start
  19.1 23.2 %all-to-all-done = bf16[32,16,128]{2,1,0:T(8,128)(2,1)S(1)} async-done(((bf16[32,16,128]{2,1,0:T(8,128)(2,1)}), bf16[32,16,128]{2,1,0:T(8,128)(2,1)S(1)}, u32[]{:S(2)}, u32[]{:S(2)}) %all-to-all-start) | async-done | bytes 131104 | tf_op jit(solution)/shard_map/all_to_all | solution.py:1294
  52.0 20.4 %collective-permute-done.6 = bf16[1024,512]{1,0:T(8,128)(2,1)} collective-permute-done((bf16[1024,512]{1,0:T(8,128)(2,1)}, bf16[1024,512]{1,0:T(8,128)(2,1)}, u32[]{:S(2)}, u32[]{:S(2)}) %collective-permute-start.6) | collective-permute-done | bytes 1048608 | tf_op jit(solution)/shard_map/ppermute | solution.py:894
  86.3 6.0 collective-permute-done.11
  105.3 6.4 collective-permute-done.10
  115.0 3.7 collective-permute-done.19.refs_4_.refs_5_.refs_20_.refs_21_.refs_19_.refs_22_.refs_3_.refs_8_
  118.7 4.6 collective-permute-done.20.refs_6_.refs_7_.refs_22_.refs_23_.refs_21_.refs_24_.refs_5_.refs_10_
  128.7 15.1 %shard_map.286 = (bf16[1024,3072]{1,0:T(8,128)(2,1)}, bf16[1024,1024]{1,0:T(8,128)(2,1)}) custom-call(s32[4]{0:T(128)} %add_add_fusion.refs_0_.place_ref, bf16[1024,1024]{1,0:T(8,128)(2,1)} %refs_4_.1, f32[24,1024]{1,0:T(8,128)} %pad.24.refs_2_.refs_3_.refs_1_.refs_4_.refs_6_, bf16[2,512,512]{2,1,0:T(8,128)(2,1)} %copy-done.5, ...), custom_call_target="tpu_custom_call" | custom-call | flops 1048576 | bytes 65536 | tf_op jit(solution)/shard_map/pallas_call | solution.py:709
  148.8 17.7 %shard_map.287 = (bf16[1024,1024]{1,0:T(8,128)(2,1)}, f32[8,8,1024]{2,1,0:T(8,128)}) custom-call(bf16[1024,3072]{1,0:T(8,128)(2,1)} %get-tuple-element.306.refs_0_.refs_1_.refs_2_.refs_3_, bf16[1024,3072]{1,0:T(8,128)(2,1)} %get-tuple-element.306.refs_0_.refs_1_.refs_2_.refs_3_, bf16[1024,3072]{1,0:T(8,128)(2,1)} %get-tuple-element.306.refs_0_.refs_1_.refs_2_.refs_3_), custom_call_target="tpu_custom_call" | custom-call | flops 1048576 | bytes 65536 | tf_op jit(solution)/shard_map/pallas_call | solution.py:234
  166.5 3.8 collective-permute-done.27.refs_4_.refs_5_.refs_6_.refs_3_
  174.5 7.8 %shard_map.288.refs_1_.refs_3_.refs_2_ = f32[1024,1024]{1,0:T(8,128)} custom-call(s32[4]{0:T(128)} %add_add_fusion.refs_0_.place_ref, bf16[1024,1024]{1,0:T(8,128)(2,1)} %get-tuple-element.310.refs_1_.refs_5_, f32[24,1024]{1,0:T(8,128)} %pad.24.refs_2_.refs_3_.refs_1_.refs_4_.refs_6_, bf16[1024,1024]{1,0:T(8,128)(2,1)} %refs_4_.1, ...), custom_call_target="tpu_custom_call" | custom-call | flops 1048576 | bytes 65536 | tf_op jit(solution)/shard_map/pallas_call | solution.py:709
  184.3 9.4 %shard_map.289 = (bf16[1024,1024]{1,0:T(8,128)(2,1)}, bf16[1024,1024]{1,0:T(8,128)(2,1)}) custom-call(s32[4]{0:T(128)} %add_add_fusion.refs_0_.place_ref, f32[1024,1024]{1,0:T(8,128)} %shard_map.288.refs_1_.refs_3_.refs_2_, f32[24,1024]{1,0:T(8,128)} %pad.24.refs_2_.refs_3_.refs_1_.refs_4_.refs_6_, bf16[2,512,512]{2,1,0:T(8,128)(2,1)} %copy-done.10, ...), custom_call_target="tpu_custom_call" | custom-call | flops 1048576 | bytes 65536 | tf_op jit(solution)/shard_map/pallas_call | solution.py:709
  199.2 8.6 %shard_map.290.refs_1_.refs_2_.refs_3_ = bf16[640,2048]{1,0:T(8,128)(2,1)} custom-call(s32[4]{0:T(128)} %add_add_fusion.refs_0_.place_ref, bf16[640,1024]{1,0:T(8,128)(2,1)} %pad_maximum_fusion.4.refs_1_, f32[24,1024]{1,0:T(8,128)} %pad.24.refs_2_.refs_3_.refs_1_.refs_4_.refs_6_, bf16[2,512,512]{2,1,0:T(8,128)(2,1)} %copy-done.10, ...), custom_call_target="tpu_custom_call" | custom-call | flops 1048576 | bytes 65536 | tf_op jit(solution)/shard_map/pallas_call | solution.py:709
  207.9 18.9 %shard_map.291 = (bf16[1024,1024]{1,0:T(8,128)(2,1)}, f32[8,8,1024]{2,1,0:T(8,128)}) custom-call(bf16[1024,1024]{1,0:T(8,128)(2,1)} %get-tuple-element.320.refs_0_.refs_1_, bf16[640,2048]{1,0:T(8,128)(2,1)} %shard_map.290.refs_1_.refs_2_.refs_3_, bf16[640,2048]{1,0:T(8,128)(2,1)} %shard_map.290.refs_1_.refs_2_.refs_3_, ...), custom_call_target="tpu_custom_call" | custom-call | flops 1048576 | bytes 65536 | tf_op jit(solution)/shard_map/pallas_call | solution.py:234
  228.0 8.3 %shard_map.292.refs_1_.refs_0_ = f32[1024,1024]{1,0:T(8,128)} custom-call(s32[4]{0:T(128)} %add_add_fusion.refs_0_.place_ref, bf16[1024,1024]{1,0:T(8,128)(2,1)} %get-tuple-element.326.refs_1_.refs_5_, f32[24,1024]{1,0:T(8,128)} %pad.24.refs_2_.refs_3_.refs_1_.refs_4_.refs_6_, f32[1024,1024]{1,0:T(8,128)} %shard_map.288.refs_1_.refs_3_.refs_2_, ...), custom_call_target="tpu_custom_call" | custom-call | flops 1048576 | bytes 65536 | tf_op jit(solution)/shard_map/pallas_call | solution.py:709
  237.4 39.3 %shard_map.293 = (bf16[1024,1024]{1,0:T(8,128)(2,1)}, bf16[1024,1024]{1,0:T(8,128)(2,1)}, bf16[4,1024,512]{2,1,0:T(8,128)(2,1)}, bf16[4,1024,512]{2,1,0:T(8,128)...) custom-call(s32[4]{0:T(128)} %add_add_fusion.1.refs_0_, f32[1024,1024]{1,0:T(8,128)} %shard_map.292.refs_1_.refs_0_, ...), custom_call_target="tpu_custom_call" | custom-call | flops 1048576 | bytes 65536 | tf_op jit(solution)/shard_map/pallas_call | solution.py:523
  277.3 37.5 %shard_map.294 = (bf16[1024,1024]{1,0:T(8,128)(2,1)}, bf16[1024,1024]{1,0:T(8,128)(2,1)}, bf16[4,1024,512]{2,1,0:T(8,128)(2,1)}, bf16[4,1024,512]{2,1,0:T(8,128)(2,1)}, f32[4,1,512]{2,1,0:T(1,128)}) custom-call(s32[4]{0:T(128)} %add_add_fusion.refs_0_.place_ref, bf16[1024,1024]{1,0:T(8,128)(2,1)} %get-tuple-element.339.refs_1_, ...), custom_call_target="tpu_custom_call" | custom-call | flops 1048576 | bytes 65536 | tf_op jit(solution)/shard_map/pallas_call | solution.py:523
  314.9 5.9 shard_map.295
  322.5 9.7 %shard_map.296 = (f32[1024,1024]{1,0:T(8,128)}, bf16[1024,1024]{1,0:T(8,128)(2,1)}, f32[8,1024]{1,0:T(8,128)}) custom-call(f32[1024,1024]{1,0:T(8,128)} %shard_map.292.refs_1_.refs_0_, f32[24,1024]{1,0:T(8,128)} %pad.24.refs_2_.refs_3_.refs_1_.refs_4_.refs_6_, bf16[1024,1024]{1,0:T(8,128)(2,1)} %multiply_convert_fusion.1.refs_2_, ...), custom_call_target="tpu_custom_call" | custom-call | flops 1048576 | bytes 65536 | tf_op jit(solution)/shard_map/pallas_call | solution.py:603
  332.2 7.5 %shard_map.297.refs_4_ = bf16[1024,1024]{1,0:T(8,128)(2,1)} custom-call(s32[4]{0:T(128)} %add_add_fusion.refs_0_.place_ref, bf16[1024,1024]{1,0:T(8,128)(2,1)} %get-tuple-element.356.refs_1_, bf16[2,512,512]{2,1,0:T(8,128)(2,1)} %copy-done.10, bf16[2,512,512]{2,1,0:T(8,128)(2,1)} %copy-done.13, bf16[2,512,512]{2,1,0:T(8,128)(2,1)} %copy-done.11, ...), custom_call_target="tpu_custom_call" | custom-call | flops 1048576 | bytes 65536 | tf_op jit(solution)/shard_map/pallas_call | solution.py:859
  339.8 17.9 %shard_map.298 = (bf16[1024,1024]{1,0:T(8,128)(2,1)}, bf16[640,1024]{1,0:T(8,128)(2,1)}, bf16[640,1024]{1,0:T(8,128)(2,1)}, f32[8,1024]{1,0:T(8,128)}, bf16[1024...) custom-call(s32[4]{0:T(128)} %add_add_fusion.1.refs_0_, ...), custom_call_target="tpu_custom_call" | custom-call | flops 1048576 | bytes 65536 | tf_op jit(solution)/shard_map/pallas_call | solution.py:289
  357.7 17.8 %shard_map.299 = (bf16[1024,1024]{1,0:T(8,128)(2,1)}, bf16[640,1024]{1,0:T(8,128)(2,1)}, bf16[640,1024]{1,0:T(8,128)(2,1)}, f32[8,1024]{1,0:T(8,128)}, bf16[1024...) custom-call(s32[4]{0:T(128)} %add_add_fusion.refs_0_.place_ref, ...), custom_call_target="tpu_custom_call", output_to_operand_aliasing={{0}: (8, {}), {1}: (9, {}), {2}: (10, {}), {3}: (11, {})} | custom-call | flops 1048576 | bytes 65536 | tf_op jit(solution)/shard_map/pallas_call | solution.py:289
  382.4 5.2 shard_map.300
  393.2 9.0 %shard_map.306 = bf16[640,1024]{1,0:T(8,128)(2,1)} custom-call(s32[4]{0:T(128)} %add_add_fusion.refs_0_.place_ref, bf16[640,1024]{1,0:T(8,128)(2,1)} %get-tuple-element.408.refs_1_, bf16[640,1024]{1,0:T(8,128)(2,1)} %get-tuple-element.409.refs_2_, bf16[2,512,512]{2,1,0:T(8,128)(2,1)} %copy-done.10, bf16[2,512,512]{2,1,0:T(8,128)(2,1)} %copy-done.13, ...), custom_call_target="tpu_custom_call" | custom-call | flops 1048576 | bytes 65536 | tf_op jit(solution)/shard_map/pallas_call | solution.py:859
  414.3 11.8 %shard_map.301 = (f32[1024,1024]{1,0:T(8,128)}, bf16[1024,1024]{1,0:T(8,128)(2,1)}, f32[8,1024]{1,0:T(8,128)}) custom-call(s32[4]{0:T(128)} %add_add_fusion.refs_0_.place_ref, bf16[1024,1024]{1,0:T(8,128)(2,1)} %get-tuple-element.384.refs_1_, f32[1024,1024]{1,0:T(8,128)} %shard_map.288.refs_1_.refs_3_.refs_2_, f32[1024,1024]{1,0:T(8,128)} %get-tuple-element.385.refs_3_, ...), custom_call_target="tpu_custom_call" | custom-call | flops 1048576 | bytes 65536 | tf_op jit(solution)/shard_map/pallas_call | solution.py:859
  426.2 8.0 %shard_map.302.refs_4_ = bf16[1024,1024]{1,0:T(8,128)(2,1)} custom-call(s32[4]{0:T(128)} %add_add_fusion.refs_0_.place_ref, bf16[1024,1024]{1,0:T(8,128)(2,1)} %get-tuple-element.386.refs_1_, bf16[2,512,512]{2,1,0:T(8,128)(2,1)} %copy-done.5, bf16[2,512,512]{2,1,0:T(8,128)(2,1)} %copy-done.7, bf16[2,512,512]{2,1,0:T(8,128)(2,1)} %copy-done.6, ...), custom_call_target="tpu_custom_call" | custom-call | flops 1048576 | bytes 65536 | tf_op jit(solution)/shard_map/pallas_call | solution.py:859
  434.2 3.7 fusion.13
  443.0 6.6 shard_map.303
  449.5 4.0 shard_map.304
  457.7 17.2 %shard_map.305 = (bf16[1024,1024]{1,0:T(8,128)(2,1)}, bf16[1024,1024]{1,0:T(8,128)(2,1)}, bf16[1024,1024]{1,0:T(8,128)(2,1)}, f32[8,1024]{1,0:T(8,128)}, bf16[10...) custom-call(s32[4]{0:T(128)} %add_add_fusion.1.refs_0_, ...), custom_call_target="tpu_custom_call" | custom-call | flops 1048576 | bytes 65536 | tf_op jit(solution)/shard_map/pallas_call | solution.py:289
  483.5 6.3 collective-permute-done.51
  493.5 3.8 shard_map.307
  501.2 17.2 %shard_map.308 = (bf16[1024,1024]{1,0:T(8,128)(2,1)}, bf16[1024,1024]{1,0:T(8,128)(2,1)}, bf16[1024,1024]{1,0:T(8,128)(2,1)}, f32[8,1024]{1,0:T(8,128)}, bf16[10...) custom-call(s32[4]{0:T(128)} %add_add_fusion.refs_0_.place_ref, ...), custom_call_target="tpu_custom_call", output_to_operand_aliasing={{0}: (7, {}), {1}: (8, {}), {2}: (9, {}), {3}: (10, {})} | custom-call | flops 1048576 | bytes 65536 | tf_op jit(solution)/shard_map/pallas_call | solution.py:289
  526.6 4.0 shard_map.309
  532.6 3.4 collective-permute-start.57
  536.0 18.8 %shard_map.310 = (f32[1024,1024]{1,0:T(8,128)}, bf16[1024,1024]{1,0:T(8,128)(2,1)}, f32[8,1024]{1,0:T(8,128)}) custom-call(s32[4]{0:T(128)} %add_add_fusion.refs_0_.place_ref, bf16[1024,1024]{1,0:T(8,128)(2,1)} %get-tuple-element.439.refs_1_, bf16[1024,1024]{1,0:T(8,128)(2,1)} %get-tuple-element.440.refs_2_, bf16[1024,1024]{1,0:T(8,128)(2,1)} %get-tuple-element.441.refs_3_, ...), custom_call_target="tpu_custom_call" | custom-call | flops 1048576 | bytes 65536 | tf_op jit(solution)/shard_map/pallas_call | solution.py:859
  554.8 5.3 shard_map.311
  560.1 4.1 collective-permute-start.63
  564.3 3.8 shard_map.312
  575.0 5.6 collective-permute-start.65
  580.7 7.5 %collective-permute-done.60 = f32[24,512]{1,0:T(8,128)} collective-permute-done((f32[24,512]{1,0:T(8,128)S(1)}, f32[24,512]{1,0:T(8,128)}, u32[]{:S(2)}, u32[]{:S(2)}) %collective-permute-start.60) | collective-permute-done | bytes 49184 | tf_op jit(solution)/shard_map/ppermute | solution.py:885
  588.2 5.4 shard_map.314
  594.9 3.3 fusion.1
  603.2 4.4 multiply_convert_fusion
  607.6 8.7 %collective-permute-done.61 = f32[24,256]{1,0:T(8,128)S(1)} collective-permute-done((f32[24,256]{1,0:T(8,128)S(1)}, f32[24,256]{1,0:T(8,128)S(1)}, u32[]{:S(2)}, u32[]{:S(2)}) %collective-permute-start.61) | collective-permute-done | bytes 24608 | tf_op jit(solution)/shard_map/ppermute | solution.py:885
  630.1 3.8 add_select_fusion.other_ref
  638.2 9.1 %collective-permute-done.68.far_ref = bf16[1024,512]{1,0:T(8,128)(2,1)S(1)} collective-permute-done((bf16[1024,512]{1,0:T(8,128)(2,1)S(1)}, bf16[1024,512]{1,0:T(8,128)(2,1)S(1)}, u32[]{:S(2)}, u32[]{:S(2)}) %collective-permute-start.68) | collective-permute-done | bytes 1048608 | tf_op jit(solution)/shard_map/ppermute | solution.py:894
  649.2 26.3 %shard_map.315 = (f32[1024,512]{1,0:T(8,128)}, f32[1024,512]{1,0:T(8,128)}, f32[1024,512]{1,0:T(8,128)}, f32[1024,512]{1,0:T(8,128)}, f32[1024,512]{1,0:T(8,128)...) custom-call(s32[4]{0:T(128)} %add_add_fusion.refs_0_.place_ref, ...), custom_call_target="tpu_custom_call" | custom-call | flops 1048576 | bytes 65536 | tf_op jit(solution)/shard_map/pallas_call | solution.py:1259
  (387 shorter events, 172.5 us)
Async XLA Ops:
  3.5 39.7 %collective-permute-start = (bf16[1024,512]{1,0:T(8,128)(2,1)}, bf16[1024,512]{1,0:T(8,128)(2,1)S(1)}, u32[]{:S(2)}, u32[]{:S(2)}) collective-permute-start(bf16[1024,512]{1,0:T(8,128)(2,1)} %convert_element_type.124), channel_id=1, source_target_pairs={{0,16},{1,17},{2,18},{3,19},{4,20},{5,21},{6,22},{7,23},{8,0},{9,1... | collective-permute-start | bytes 3145736 | tf_op jit(solution)/shard_map/ppermute | solution.py:894
  11.3 31.8 %collective-permute-start.1 = (bf16[512,512]{1,0:T(8,128)(2,1)}, bf16[512,512]{1,0:T(8,128)(2,1)S(1)}, u32[]{:S(2)}, u32[]{:S(2)}) collective-permute-start(bf16[512,512]{1,0:T(8,128)(2,1)} %get-tuple-element.534), channel_id=1, source_target_pairs={{0,2},{1,3},{2,0},{3,1},{4,6},{5,7},{6,4},{7,5},{8,10},{9,11},{10,... | collective-permute-start | bytes 1572872 | tf_op jit(solution)/shard_map/ppermute | solution.py:885
  12.8 30.4 %collective-permute-start.2 = (bf16[512,512]{1,0:T(8,128)(2,1)}, bf16[512,512]{1,0:T(8,128)(2,1)S(1)}, u32[]{:S(2)}, u32[]{:S(2)}) collective-permute-start(bf16[512,512]{1,0:T(8,128)(2,1)} %get-tuple-element.533), channel_id=1, source_target_pairs={{0,4},{1,5},{2,6},{3,7},{4,0},{5,1},{6,2},{7,3},{8,12},{9,13},{10,... | collective-permute-start | bytes 1572872 | tf_op jit(solution)/shard_map/ppermute | solution.py:885
  14.3 28.8 %collective-permute-start.4 = (bf16[160,1024]{1,0:T(8,128)(2,1)}, bf16[160,1024]{1,0:T(8,128)(2,1)}, u32[]{:S(2)}, u32[]{:S(2)}) collective-permute-start(bf16[160,1024]{1,0:T(8,128)(2,1)} %get-tuple-element.521), channel_id=1, source_target_pairs={{0,2},{1,3},{2,0},{3,1},{4,6},{5,7},{6,4},{7,5},{8,10},{9,11},{10,... | collective-permute-start | bytes 983048 | tf_op jit(solution)/shard_map/ppermute | solution.py:885
  15.0 28.2 %collective-permute-start.5 = (bf16[160,1024]{1,0:T(8,128)(2,1)}, bf16[160,1024]{1,0:T(8,128)(2,1)}, u32[]{:S(2)}, u32[]{:S(2)}) collective-permute-start(bf16[160,1024]{1,0:T(8,128)(2,1)} %get-tuple-element.519), channel_id=1, source_target_pairs={{0,3},{1,2},{2,1},{3,0},{4,7},{5,6},{6,5},{7,4},{8,11},{9,10},{10,... | collective-permute-start | bytes 983048 | tf_op jit(solution)/shard_map/ppermute | solution.py:885
  16.4 25.8 %all-to-all-start = ((bf16[32,16,128]{2,1,0:T(8,128)(2,1)}), bf16[32,16,128]{2,1,0:T(8,128)(2,1)S(1)}, u32[]{:S(2)}, u32[]{:S(2)}) async-start(bf16[32,16,128]{2,1,0:T(8,128)(2,1)} %pad.22), calls=%async_computation | async-start | bytes 262144 | tf_op jit(solution)/shard_map/all_to_all | solution.py:1294
  43.2 29.2 %collective-permute-start.7 = (bf16[1024,512]{1,0:T(8,128)(2,1)}, bf16[1024,512]{1,0:T(8,128)(2,1)}, u32[]{:S(2)}, u32[]{:S(2)}) collective-permute-start(bf16[1024,512]{1,0:T(8,128)(2,1)} %convert_element_type.124), channel_id=1, source_target_pairs={{8,16},{9,17},{10,18},{11,19},{12,20},{13,21},{14,22},{15,23},{16,... | collective-permute-start | bytes 3145736 | tf_op jit(solution)/shard_map/ppermute | solution.py:894
  47.3 25.1 %collective-permute-start.6 = (bf16[1024,512]{1,0:T(8,128)(2,1)}, bf16[1024,512]{1,0:T(8,128)(2,1)}, u32[]{:S(2)}, u32[]{:S(2)}) collective-permute-start(bf16[1024,512]{1,0:T(8,128)(2,1)} %broadcast_select_fusion.3), channel_id=1, source_target_pairs={{0,8},{1,9},{2,10},{3,11},{4,12},{5,13},{6,14},{7,15},{8,0},{9,1},... | collective-permute-start | bytes 3145736 | tf_op jit(solution)/shard_map/ppermute | solution.py:894
  49.8 24.3 %collective-permute-start.8 = (bf16[2,512,512]{2,1,0:T(8,128)(2,1)S(1)}, bf16[2,512,512]{2,1,0:T(8,128)(2,1)S(1)}, u32[]{:S(2)}, u32[]{:S(2)}) collective-permute-start(bf16[2,512,512]{2,1,0:T(8,128)(2,1)S(1)} %pad_maximum_fusion.6.refs_11_.refs_12_.refs_9_.refs_21_.refs_10_.refs_13_.refs_15_), channel_id=1, source_target_pairs={{0,4},{1,5},{2,6},{3,7},{4,0},{5,1},{6,2},{7,3},{8,12},{9,13},{10,... | collective-permute-start | bytes 3145736 | tf_op jit(solution)/shard_map/ppermute | solution.py:885
  50.4 24.5 %collective-permute-start.9 = (bf16[2,512,512]{2,1,0:T(8,128)(2,1)S(1)}, bf16[2,512,512]{2,1,0:T(8,128)(2,1)}, u32[]{:S(2)}, u32[]{:S(2)}) collective-permute-start(bf16[2,512,512]{2,1,0:T(8,128)(2,1)S(1)} %pad_maximum_fusion.7.refs_13_.refs_14_.refs_11_.refs_23_.refs_12_.refs_15_.refs_17_), channel_id=1, source_target_pairs={{0,2},{1,3},{2,0},{3,1},{4,6},{5,7},{6,4},{7,5},{8,10},{9,11},{10,... | collective-permute-start | bytes 3145736 | tf_op jit(solution)/shard_map/ppermute | solution.py:885
  52.0 27.7 %collective-permute-start.13 = (bf16[2,512,512]{2,1,0:T(8,128)(2,1)S(1)}, bf16[2,512,512]{2,1,0:T(8,128)(2,1)}, u32[]{:S(2)}, u32[]{:S(2)}) collective-permute-start(bf16[2,512,512]{2,1,0:T(8,128)(2,1)S(1)} %pad_maximum_fusion.6.refs_11_.refs_12_.refs_9_.refs_21_.refs_10_.refs_13_.refs_15_), channel_id=1, source_target_pairs={{0,1},{1,0},{2,3},{3,2},{4,5},{5,4},{6,7},{7,6},{8,9},{9,8},{10,11... | collective-permute-start | bytes 3145736 | tf_op jit(solution)/shard_map/ppermute | solution.py:885
  85.0 26.7 %collective-permute-start.10 = (bf16[1024,512]{1,0:T(8,128)(2,1)}, bf16[1024,512]{1,0:T(8,128)(2,1)}, u32[]{:S(2)}, u32[]{:S(2)}) collective-permute-start(bf16[1024,512]{1,0:T(8,128)(2,1)} %collective-permute-done.7), channel_id=1, source_target_pairs={{8,0},{9,1},{10,2},{11,3},{12,4},{13,5},{14,6},{15,7},{16,24},{17,... | collective-permute-start | bytes 3145736 | tf_op jit(solution)/shard_map/ppermute | solution.py:894
  94.7 24.0 %collective-permute-start.19 = (bf16[2,512,512]{2,1,0:T(8,128)(2,1)S(1)}, bf16[2,512,512]{2,1,0:T(8,128)(2,1)S(1)}, u32[]{:S(2)}, u32[]{:S(2)}) collective-permute-start(bf16[2,512,512]{2,1,0:T(8,128)(2,1)S(1)} %pad_maximum_fusion.8.refs_3_.refs_4_.refs_19_.refs_20_.refs_18_.refs_21_.refs_2_.refs_7_), channel_id=1, source_target_pairs={{0,4},{1,5},{2,6},{3,7},{4,0},{5,1},{6,2},{7,3},{8,12},{9,13},{10,... | collective-permute-start | bytes 3145736 | tf_op jit(solution)/shard_map/ppermute | solution.py:885
  96.2 27.1 %collective-permute-start.21 = (bf16[2,512,512]{2,1,0:T(8,128)(2,1)S(1)}, bf16[2,512,512]{2,1,0:T(8,128)(2,1)}, u32[]{:S(2)}, u32[]{:S(2)}) collective-permute-start(bf16[2,512,512]{2,1,0:T(8,128)(2,1)S(1)} %pad_maximum_fusion.8.refs_3_.refs_4_.refs_19_.refs_20_.refs_18_.refs_21_.refs_2_.refs_7_), channel_id=1, source_target_pairs={{0,1},{1,0},{2,3},{3,2},{4,5},{5,4},{6,7},{7,6},{8,9},{9,8},{10,11... | collective-permute-start | bytes 3145736 | tf_op jit(solution)/shard_map/ppermute | solution.py:885
  97.5 25.7 %collective-permute-start.20 = (bf16[2,512,512]{2,1,0:T(8,128)(2,1)S(1)}, bf16[2,512,512]{2,1,0:T(8,128)(2,1)}, u32[]{:S(2)}, u32[]{:S(2)}) collective-permute-start(bf16[2,512,512]{2,1,0:T(8,128)(2,1)S(1)} %pad_maximum_fusion.9.refs_5_.refs_6_.refs_21_.refs_22_.refs_20_.refs_23_.refs_4_.refs_9_), channel_id=1, source_target_pairs={{0,2},{1,3},{2,0},{3,1},{4,6},{5,7},{6,4},{7,5},{8,10},{9,11},{10,... | collective-permute-start | bytes 3145736 | tf_op jit(solution)/shard_map/ppermute | solution.py:885
  98.0 25.3 %collective-permute-start.22 = (bf16[2,512,512]{2,1,0:T(8,128)(2,1)S(1)}, bf16[2,512,512]{2,1,0:T(8,128)(2,1)}, u32[]{:S(2)}, u32[]{:S(2)}) collective-permute-start(bf16[2,512,512]{2,1,0:T(8,128)(2,1)S(1)} %pad_maximum_fusion.9.refs_5_.refs_6_.refs_21_.refs_22_.refs_20_.refs_23_.refs_4_.refs_9_), channel_id=1, source_target_pairs={{0,1},{1,0},{2,3},{3,2},{4,5},{5,4},{6,7},{7,6},{8,9},{9,8},{10,11... | collective-permute-start | bytes 3145736 | tf_op jit(solution)/shard_map/ppermute | solution.py:885
  145.1 25.3 %collective-permute-start.27 = (bf16[2,512,512]{2,1,0:T(8,128)(2,1)S(1)}, bf16[2,512,512]{2,1,0:T(8,128)(2,1)S(1)}, u32[]{:S(2)}, u32[]{:S(2)}) collective-permute-start(bf16[2,512,512]{2,1,0:T(8,128)(2,1)S(1)} %pad_maximum_fusion.10.refs_3_.refs_4_.refs_5_.refs_2_), channel_id=1, source_target_pairs={{0,4},{1,5},{2,6},{3,7},{4,0},{5,1},{6,2},{7,3},{8,12},{9,13},{10,... | collective-permute-start | bytes 3145736 | tf_op jit(solution)/shard_map/ppermute | solution.py:885
  147.1 25.1 %collective-permute-start.28 = (bf16[2,512,512]{2,1,0:T(8,128)(2,1)S(1)}, bf16[2,512,512]{2,1,0:T(8,128)(2,1)}, u32[]{:S(2)}, u32[]{:S(2)}) collective-permute-start(bf16[2,512,512]{2,1,0:T(8,128)(2,1)S(1)} %pad_maximum_fusion.11.refs_5_.refs_6_.refs_7_.refs_4_), channel_id=1, source_target_pairs={{0,2},{1,3},{2,0},{3,1},{4,6},{5,7},{6,4},{7,5},{8,10},{9,11},{10,... | collective-permute-start | bytes 3145736 | tf_op jit(solution)/shard_map/ppermute | solution.py:885
  148.3 23.9 %collective-permute-start.29 = (bf16[2,512,512]{2,1,0:T(8,128)(2,1)S(1)}, bf16[2,512,512]{2,1,0:T(8,128)(2,1)}, u32[]{:S(2)}, u32[]{:S(2)}) collective-permute-start(bf16[2,512,512]{2,1,0:T(8,128)(2,1)S(1)} %pad_maximum_fusion.10.refs_3_.refs_4_.refs_5_.refs_2_), channel_id=1, source_target_pairs={{0,1},{1,0},{2,3},{3,2},{4,5},{5,4},{6,7},{7,6},{8,9},{9,8},{10,11... | collective-permute-start | bytes 3145736 | tf_op jit(solution)/shard_map/ppermute | solution.py:885
  148.3 23.9 %collective-permute-start.30 = (bf16[2,512,512]{2,1,0:T(8,128)(2,1)S(1)}, bf16[2,512,512]{2,1,0:T(8,128)(2,1)}, u32[]{:S(2)}, u32[]{:S(2)}) collective-permute-start(bf16[2,512,512]{2,1,0:T(8,128)(2,1)S(1)} %pad_maximum_fusion.11.refs_5_.refs_6_.refs_7_.refs_4_), channel_id=1, source_target_pairs={{0,1},{1,0},{2,3},{3,2},{4,5},{5,4},{6,7},{7,6},{8,9},{9,8},{10,11... | collective-permute-start | bytes 3145736 | tf_op jit(solution)/shard_map/ppermute | solution.py:885
  172.7 21.1 %collective-permute-start.17 = (bf16[512,512]{1,0:T(8,128)(2,1)}, bf16[512,512]{1,0:T(8,128)(2,1)}, u32[]{:S(2)}, u32[]{:S(2)}) collective-permute-start(bf16[512,512]{1,0:T(8,128)(2,1)} %get-tuple-element.286), channel_id=1, source_target_pairs={{0,2},{1,3},{2,0},{3,1},{4,6},{5,7},{6,4},{7,5},{8,10},{9,11},{10,... | collective-permute-start | bytes 1572872 | tf_op jit(solution)/shard_map/ppermute | solution.py:885
  195.1 31.7 %collective-permute-start.33 = (bf16[2,512,512]{2,1,0:T(8,128)(2,1)S(1)}, bf16[2,512,512]{2,1,0:T(8,128)(2,1)S(1)}, u32[]{:S(2)}, u32[]{:S(2)}) collective-permute-start(bf16[2,512,512]{2,1,0:T(8,128)(2,1)S(1)} %pad_maximum_fusion.12.refs_13_.refs_17_), channel_id=1, source_target_pairs={{0,4},{1,5},{2,6},{3,7},{4,0},{5,1},{6,2},{7,3},{8,12},{9,13},{10,... | collective-permute-start | bytes 3145736 | tf_op jit(solution)/shard_map/ppermute | solution.py:885
  197.1 29.7 %collective-permute-start.34 = (bf16[2,512,512]{2,1,0:T(8,128)(2,1)S(1)}, bf16[2,512,512]{2,1,0:T(8,128)(2,1)}, u32[]{:S(2)}, u32[]{:S(2)}) collective-permute-start(bf16[2,512,512]{2,1,0:T(8,128)(2,1)S(1)} %pad_maximum_fusion.13.refs_15_.refs_19_), channel_id=1, source_target_pairs={{0,2},{1,3},{2,0},{3,1},{4,6},{5,7},{6,4},{7,5},{8,10},{9,11},{10,... | collective-permute-start | bytes 3145736 | tf_op jit(solution)/shard_map/ppermute | solution.py:885
  198.7 28.1 %collective-permute-start.35 = (bf16[2,512,512]{2,1,0:T(8,128)(2,1)S(1)}, bf16[2,512,512]{2,1,0:T(8,128)(2,1)}, u32[]{:S(2)}, u32[]{:S(2)}) collective-permute-start(bf16[2,512,512]{2,1,0:T(8,128)(2,1)S(1)} %pad_maximum_fusion.12.refs_13_.refs_17_), channel_id=1, source_target_pairs={{0,1},{1,0},{2,3},{3,2},{4,5},{5,4},{6,7},{7,6},{8,9},{9,8},{10,11... | collective-permute-start | bytes 3145736 | tf_op jit(solution)/shard_map/ppermute | solution.py:885
  198.7 28.1 %collective-permute-start.36 = (bf16[2,512,512]{2,1,0:T(8,128)(2,1)S(1)}, bf16[2,512,512]{2,1,0:T(8,128)(2,1)}, u32[]{:S(2)}, u32[]{:S(2)}) collective-permute-start(bf16[2,512,512]{2,1,0:T(8,128)(2,1)S(1)} %pad_maximum_fusion.13.refs_15_.refs_19_), channel_id=1, source_target_pairs={{0,1},{1,0},{2,3},{3,2},{4,5},{5,4},{6,7},{7,6},{8,9},{9,8},{10,11... | collective-permute-start | bytes 3145736 | tf_op jit(solution)/shard_map/ppermute | solution.py:885
  276.7 38.1 %collective-permute-start.39 = (bf16[4,1024,512]{2,1,0:T(8,128)(2,1)}, bf16[4,1024,512]{2,1,0:T(8,128)(2,1)}, u32[]{:S(2)}, u32[]{:S(2)}) collective-permute-start(bf16[4,1024,512]{2,1,0:T(8,128)(2,1)} %get-tuple-element.336), channel_id=1, source_target_pairs={{0,1},{1,0},{2,3},{3,2},{4,5},{5,4},{6,7},{7,6},{8,9},{9,8},{10,11... | collective-permute-start | bytes 12582920 | tf_op jit(solution)/shard_map/ppermute | solution.py:885
  276.9 38.0 %collective-permute-start.40 = (bf16[4,1024,512]{2,1,0:T(8,128)(2,1)}, bf16[4,1024,512]{2,1,0:T(8,128)(2,1)}, u32[]{:S(2)}, u32[]{:S(2)}) collective-permute-start(bf16[4,1024,512]{2,1,0:T(8,128)(2,1)} %get-tuple-element.337), channel_id=1, source_target_pairs={{0,1},{1,0},{2,3},{3,2},{4,5},{5,4},{6,7},{7,6},{8,9},{9,8},{10,11... | collective-permute-start | bytes 12582920 | tf_op jit(solution)/shard_map/ppermute | solution.py:885
  320.8 61.6 %collective-permute-start.41 = (bf16[2,2,512,512]{3,2,1,0:T(8,128)(2,1)}, bf16[2,2,512,512]{3,2,1,0:T(8,128)(2,1)}, u32[]{:S(2)}, u32[]{:S(2)}) collective-permute-start(bf16[2,2,512,512]{3,2,1,0:T(8,128)(2,1)} %get-tuple-element.352), channel_id=1, source_target_pairs={{0,4},{1,5},{2,6},{3,7},{4,0},{5,1},{6,2},{7,3},{8,12},{9,13},{10,... | collective-permute-start | bytes 6291464 | tf_op jit(solution)/shard_map/ppermute | solution.py:885
  322.2 60.2 %collective-permute-start.42 = (bf16[2,2,512,512]{3,2,1,0:T(8,128)(2,1)}, bf16[2,2,512,512]{3,2,1,0:T(8,128)(2,1)}, u32[]{:S(2)}, u32[]{:S(2)}) collective-permute-start(bf16[2,2,512,512]{3,2,1,0:T(8,128)(2,1)} %get-tuple-element.353), channel_id=1, source_target_pairs={{0,2},{1,3},{2,0},{3,1},{4,6},{5,7},{6,4},{7,5},{8,10},{9,11},{10,... | collective-permute-start | bytes 6291464 | tf_op jit(solution)/shard_map/ppermute | solution.py:885
  393.2 48.8 %collective-permute-start.45 = (bf16[4,1024,512]{2,1,0:T(8,128)(2,1)}, bf16[4,1024,512]{2,1,0:T(8,128)(2,1)}, u32[]{:S(2)}, u32[]{:S(2)}) collective-permute-start(bf16[4,1024,512]{2,1,0:T(8,128)(2,1)} %pad_maximum_fusion), channel_id=1, source_target_pairs={{0,1},{1,0},{2,3},{3,2},{4,5},{5,4},{6,7},{7,6},{8,9},{9,8},{10,11... | collective-permute-start | bytes 12582920 | tf_op jit(solution)/shard_map/ppermute | solution.py:885
  404.7 76.1 %collective-permute-start.49 = (bf16[160,1024]{1,0:T(8,128)(2,1)}, bf16[160,1024]{1,0:T(8,128)(2,1)}, u32[]{:S(2)}, u32[]{:S(2)}) collective-permute-start(bf16[160,1024]{1,0:T(8,128)(2,1)} %get-tuple-element.517), channel_id=1, source_target_pairs={{0,1},{1,0},{2,3},{3,2},{4,5},{5,4},{6,7},{7,6},{8,9},{9,8},{10,11... | collective-permute-start | bytes 983048 | tf_op jit(solution)/shard_map/ppermute | solution.py:885
  405.2 78.3 %collective-permute-start.50 = (bf16[160,1024]{1,0:T(8,128)(2,1)}, bf16[160,1024]{1,0:T(8,128)(2,1)}, u32[]{:S(2)}, u32[]{:S(2)}) collective-permute-start(bf16[160,1024]{1,0:T(8,128)(2,1)} %get-tuple-element.516), channel_id=1, source_target_pairs={{0,2},{1,3},{2,0},{3,1},{4,6},{5,7},{6,4},{7,5},{8,10},{9,11},{10,... | collective-permute-start | bytes 983048 | tf_op jit(solution)/shard_map/ppermute | solution.py:885
  413.3 28.7 %collective-permute-start.43 = (bf16[2,1,512,512]{3,2,1,0:T(8,128)(2,1)}, bf16[2,1,512,512]{3,2,1,0:T(8,128)(2,1)S(1)}, u32[]{:S(2)}, u32[]{:S(2)}) collective-permute-start(bf16[2,1,512,512]{3,2,1,0:T(8,128)(2,1)} %get-tuple-element.372), channel_id=1, source_target_pairs={{0,2},{1,3},{2,0},{3,1},{4,6},{5,7},{6,4},{7,5},{8,10},{9,11},{10,... | collective-permute-start | bytes 3145736 | tf_op jit(solution)/shard_map/ppermute | solution.py:885
  413.6 28.4 %collective-permute-start.44 = (bf16[2,1,512,512]{3,2,1,0:T(8,128)(2,1)}, bf16[2,1,512,512]{3,2,1,0:T(8,128)(2,1)}, u32[]{:S(2)}, u32[]{:S(2)}) collective-permute-start(bf16[2,1,512,512]{3,2,1,0:T(8,128)(2,1)} %get-tuple-element.373), channel_id=1, source_target_pairs={{0,4},{1,5},{2,6},{3,7},{4,0},{5,1},{6,2},{7,3},{8,12},{9,13},{10,... | collective-permute-start | bytes 3145736 | tf_op jit(solution)/shard_map/ppermute | solution.py:885
  453.6 36.3 %collective-permute-start.46 = (bf16[1024,512]{1,0:T(8,128)(2,1)}, bf16[1024,512]{1,0:T(8,128)(2,1)S(1)}, u32[]{:S(2)}, u32[]{:S(2)}) collective-permute-start(bf16[1024,512]{1,0:T(8,128)(2,1)} %get-tuple-element.395), channel_id=1, source_target_pairs={{0,8},{1,9},{2,10},{3,11},{4,12},{5,13},{6,14},{7,15},{8,0},{9,1},... | collective-permute-start | bytes 3145736 | tf_op jit(solution)/shard_map/ppermute | solution.py:894
  454.7 35.1 %collective-permute-start.47 = (bf16[1,2,512,512]{3,2,1,0:T(8,128)(2,1)}, bf16[1,2,512,512]{3,2,1,0:T(8,128)(2,1)S(1)}, u32[]{:S(2)}, u32[]{:S(2)}) collective-permute-start(bf16[1,2,512,512]{3,2,1,0:T(8,128)(2,1)} %get-tuple-element.396), channel_id=1, source_target_pairs={{0,4},{1,5},{2,6},{3,7},{4,0},{5,1},{6,2},{7,3},{8,12},{9,13},{10,... | collective-permute-start | bytes 3145736 | tf_op jit(solution)/shard_map/ppermute | solution.py:885
  456.0 33.9 %collective-permute-start.48 = (bf16[1,2,512,512]{3,2,1,0:T(8,128)(2,1)}, bf16[1,2,512,512]{3,2,1,0:T(8,128)(2,1)S(1)}, u32[]{:S(2)}, u32[]{:S(2)}) collective-permute-start(bf16[1,2,512,512]{3,2,1,0:T(8,128)(2,1)} %get-tuple-element.397), channel_id=1, source_target_pairs={{0,2},{1,3},{2,0},{3,1},{4,6},{5,7},{6,4},{7,5},{8,10},{9,11},{10,... | collective-permute-start | bytes 3145736 | tf_op jit(solution)/shard_map/ppermute | solution.py:885
  489.9 36.8 %collective-permute-start.52 = (bf16[4,1024,512]{2,1,0:T(8,128)(2,1)}, bf16[4,1024,512]{2,1,0:T(8,128)(2,1)}, u32[]{:S(2)}, u32[]{:S(2)}) collective-permute-start(bf16[4,1024,512]{2,1,0:T(8,128)(2,1)} %pad_maximum_fusion.2), channel_id=1, source_target_pairs={{0,1},{1,0},{2,3},{3,2},{4,5},{5,4},{6,7},{7,6},{8,9},{9,8},{10,11... | collective-permute-start | bytes 12582920 | tf_op jit(solution)/shard_map/ppermute | solution.py:885
  499.0 27.7 %collective-permute-start.53 = (bf16[1,1,512,512]{3,2,1,0:T(8,128)(2,1)}, bf16[1,1,512,512]{3,2,1,0:T(8,128)(2,1)S(1)}, u32[]{:S(2)}, u32[]{:S(2)}) collective-permute-start(bf16[1,1,512,512]{3,2,1,0:T(8,128)(2,1)} %get-tuple-element.421), channel_id=1, source_target_pairs={{0,2},{1,3},{2,0},{3,1},{4,6},{5,7},{6,4},{7,5},{8,10},{9,11},{10,... | collective-permute-start | bytes 1572872 | tf_op jit(solution)/shard_map/ppermute | solution.py:885
  500.3 26.4 %collective-permute-start.54 = (bf16[1,1,512,512]{3,2,1,0:T(8,128)(2,1)}, bf16[1,1,512,512]{3,2,1,0:T(8,128)(2,1)}, u32[]{:S(2)}, u32[]{:S(2)}) collective-permute-start(bf16[1,1,512,512]{3,2,1,0:T(8,128)(2,1)} %get-tuple-element.422), channel_id=1, source_target_pairs={{0,4},{1,5},{2,6},{3,7},{4,0},{5,1},{6,2},{7,3},{8,12},{9,13},{10,... | collective-permute-start | bytes 1572872 | tf_op jit(solution)/shard_map/ppermute | solution.py:885
  530.6 29.4 %collective-permute-start.55 = (bf16[1,2,512,512]{3,2,1,0:T(8,128)(2,1)}, bf16[1,2,512,512]{3,2,1,0:T(8,128)(2,1)}, u32[]{:S(2)}, u32[]{:S(2)}) collective-permute-start(bf16[1,2,512,512]{3,2,1,0:T(8,128)(2,1)} %get-tuple-element.437), channel_id=1, source_target_pairs={{0,4},{1,5},{2,6},{3,7},{4,0},{5,1},{6,2},{7,3},{8,12},{9,13},{10,... | collective-permute-start | bytes 3145736 | tf_op jit(solution)/shard_map/ppermute | solution.py:885
  531.8 28.3 %collective-permute-start.56 = (bf16[1,2,512,512]{3,2,1,0:T(8,128)(2,1)}, bf16[1,2,512,512]{3,2,1,0:T(8,128)(2,1)}, u32[]{:S(2)}, u32[]{:S(2)}) collective-permute-start(bf16[1,2,512,512]{3,2,1,0:T(8,128)(2,1)} %get-tuple-element.438), channel_id=1, source_target_pairs={{0,2},{1,3},{2,0},{3,1},{4,6},{5,7},{6,4},{7,5},{8,10},{9,11},{10,... | collective-permute-start | bytes 3145736 | tf_op jit(solution)/shard_map/ppermute | solution.py:885
  532.6 27.5 %collective-permute-start.57 = (bf16[512,512]{1,0:T(8,128)(2,1)S(1)}, bf16[512,512]{1,0:T(8,128)(2,1)}, u32[]{:S(2)}, u32[]{:S(2)}) collective-permute-start(bf16[512,512]{1,0:T(8,128)(2,1)S(1)} %slice.91), channel_id=1, source_target_pairs={{0,16},{1,17},{2,18},{3,19},{4,20},{5,21},{6,22},{7,23},{8,24},{9,... | collective-permute-start | bytes 1572872 | tf_op jit(solution)/shard_map/ppermute | solution.py:894
  560.1 34.8 %collective-permute-start.63 = (bf16[1024,512]{1,0:T(8,128)(2,1)}, bf16[1024,512]{1,0:T(8,128)(2,1)}, u32[]{:S(2)}, u32[]{:S(2)}) collective-permute-start(bf16[1024,512]{1,0:T(8,128)(2,1)} %get-tuple-element.477), channel_id=1, source_target_pairs={{0,8},{1,9},{2,10},{3,11},{4,12},{5,13},{6,14},{7,15},{24,16},{25,... | collective-permute-start | bytes 3145736 | tf_op jit(solution)/shard_map/ppermute | solution.py:894
  575.0 42.4 %collective-permute-start.65 = (bf16[512,512]{1,0:T(8,128)(2,1)}, bf16[512,512]{1,0:T(8,128)(2,1)}, u32[]{:S(2)}, u32[]{:S(2)}) collective-permute-start(bf16[512,512]{1,0:T(8,128)(2,1)} %slice.92), channel_id=1, source_target_pairs={{0,16},{1,17},{2,18},{3,19},{4,20},{5,21},{6,22},{7,23},{8,24},{9,... | collective-permute-start | bytes 1572872 | tf_op jit(solution)/shard_map/ppermute | solution.py:894
  593.6 26.4 %collective-permute-start.62 = (bf16[1024,512]{1,0:T(8,128)(2,1)}, bf16[1024,512]{1,0:T(8,128)(2,1)S(1)}, u32[]{:S(2)}, u32[]{:S(2)}) collective-permute-start(bf16[1024,512]{1,0:T(8,128)(2,1)} %get-tuple-element.475), channel_id=1, source_target_pairs={{8,0},{9,1},{10,2},{11,3},{12,4},{13,5},{14,6},{15,7},{24,16},{25,... | collective-permute-start | bytes 3145736 | tf_op jit(solution)/shard_map/ppermute | solution.py:894
  598.3 21.8 %collective-permute-start.64 = (bf16[1024,512]{1,0:T(8,128)(2,1)}, bf16[1024,512]{1,0:T(8,128)(2,1)}, u32[]{:S(2)}, u32[]{:S(2)}) collective-permute-start(bf16[1024,512]{1,0:T(8,128)(2,1)} %fusion.1), channel_id=1, source_target_pairs={{16,8},{17,9},{18,10},{19,11},{20,12},{21,13},{22,14},{23,15}} | collective-permute-start | bytes 3145736 | tf_op jit(solution)/shard_map/ppermute | solution.py:894
  625.8 21.5 %collective-permute-start.68 = (bf16[1024,512]{1,0:T(8,128)(2,1)S(1)}, bf16[1024,512]{1,0:T(8,128)(2,1)S(1)}, u32[]{:S(2)}, u32[]{:S(2)}) collective-permute-start(bf16[1024,512]{1,0:T(8,128)(2,1)S(1)} %add_convert_fusion), channel_id=1, source_target_pairs={{16,0},{17,1},{18,2},{19,3},{20,4},{21,5},{22,6},{23,7}} | collective-permute-start | bytes 3145736 | tf_op jit(solution)/shard_map/ppermute | solution.py:894
  (104 other events, 985.3 us)

commit v8 on v7

--- a/solution.py
+++ b/solution.py
@@ -1590,8 +1590,8 @@
         ),
         width,
     )
-    feed_got, cross_swaps, self_sent, self_whole, memory_back = pinned(
-        feed_got, cross_swaps, self_sent, self_whole, memory_back
+    feed_got, cross_swaps, self_sent, self_whole = pinned(
+        feed_got, cross_swaps, self_sent, self_whole
     )
     self_got = swap_bit(self_sent, device_count, 1)
     feed_kept = feed_kept + feed_got.astype(F32)
@@ -1636,15 +1636,15 @@
     sums_one, cross_swaps = pinned(sums_one, cross_sum.swaps)
     cross_sum.swaps = list(cross_swaps)
     cross_total, cross_sent = plane_totals(here, cross_sum)
-    self_swaps, cross_sent, sums_one, feed_upper, feed_sent = pinned(
-        self_swaps, cross_sent, sums_one, feed_upper, feed_sent
+    self_swaps, cross_sent, sums_one, feed_upper, feed_sent, memory_back = pinned(
+        self_swaps, cross_sent, sums_one, feed_upper, feed_sent, memory_back
     )
     feed_lower = move_planes(feed_sent[feed_middle:], ((0, 2), (1, 3)), plane_size)
-    cross_got = move_planes(cross_sent, ((0, 1), (3, 2)), plane_size)
     self_sum = self_sum.joined(self_swaps)
     self_sends = stage_sends(here, self_sum, device_count)
-    self_sends, sums_one = pinned(self_sends, sums_one)
+    self_sends, sums_one, cross_sent = pinned(self_sends, sums_one, cross_sent)
     self_swaps = stage_swaps(self_sends, self_sum, device_count)
+    cross_got = move_planes(cross_sent, ((0, 1), (3, 2)), plane_size)
     vector_terms = vector_table(
         sums_one, sums_two, sums_three, self_sums, cross_sums, grad_bias_up
     )
@@ -1656,10 +1656,9 @@
         kept, sent = vector_send(kept + got, device, vector_bits[number])
         return kept, swap_bit(sent, device_count, vector_bits[number])
 
-    self_swaps, vector_got = pinned(self_swaps, vector_got)
+    self_swaps, vector_sent = pinned(self_swaps, vector_sent)
     self_sum = finish_stages(here, self_sum.joined(self_swaps), device_count)
     self_total, self_sent = plane_totals(here, self_sum)
-    self_sent, vector_got = pinned(self_sent, vector_got)
     self_got = move_planes(self_sent, ((1, 0), (3, 2)), plane_size)
     vector_kept, vector_got = vector_next(vector_kept, vector_got, 1)
     branch = out_a.astype(F32) + out_b.astype(F32)

time: 682 us -> 681 us (level)
  transfers between devices with their start and end apart: 71 -> 71, of which waited for: 18 -> 19; matrix products, arithmetic and copies ran while one was open for 14% -> 14% of each run, Pallas kernels for 43% -> 41%
where the time goes in v8:
time: 681 us; the launch traced here: 674 us
  Pallas kernels  369 us (54%)
  waiting for transfers between devices  110 us (16%)
  starting transfers between devices  69.2 us (10%)
  other arithmetic  53.3 us (8%)
  matrix products  36 us (5%)
  local copies, waits for them, and re-layouts  33.5 us (5%)
    pallas_call x2, Pallas kernels, feed_half(): pl.pallas_call(functools.partial(feed_kernel, norm=norm, up_source=up_sou...  76.9 us
    pallas_call x4, Pallas kernels, attention_backward(): pl.pallas_call(functools.partial(attention_backward_kernel, causal=causal...  70.2 us
    pallas_call x5, Pallas kernels, project_back(): pl.pallas_call(functools.partial(project_back_kernel, source=source, bloc...  54.6 us
    pallas_call x5, Pallas kernels, project(): pl.pallas_call(functools.partial(project_kernel, source=source, block=blo...  49.3 us
    ppermute x59, waiting for transfers between devices, swap_bit(): lax.ppermute(values, AXES, [(item, item ^ bit) for item in range(device_c...  45.6 us
    ppermute x11, waiting for transfers between devices, move_planes(): return lax.ppermute(values, AXES, pairs)  41.1 us
    ppermute x59, starting transfers between devices, swap_bit(): lax.ppermute(values, AXES, [(item, item ^ bit) for item in range(device_c...  39.9 us
    pallas_call x2, Pallas kernels, attention_forward(): pl.pallas_call(functools.partial(attention_forward_kernel, causal=causal)...  36.6 us
  transfers between devices with their start and end apart: 71, of which 19 were waited for; matrix products, arithmetic and copies ran while one was open for 14% of the time, Pallas kernels for 41%

profile of v8, /device:TPU:0, one launch (start us, length us, event | category | flops | bytes accessed | tf_op | source)
XLA Modules:
  0.0 674.4 jit_solution(18408265187274061113)
XLA Ops:
  3.5 4.0 collective-permute-start
  19.1 23.2 %all-to-all-done = bf16[32,16,128]{2,1,0:T(8,128)(2,1)S(1)} async-done(((bf16[32,16,128]{2,1,0:T(8,128)(2,1)}), bf16[32,16,128]{2,1,0:T(8,128)(2,1)S(1)}, u32[]{:S(2)}, u32[]{:S(2)}) %all-to-all-start) | async-done | bytes 131104 | tf_op jit(solution)/shard_map/all_to_all | solution.py:1294
  52.0 20.4 %collective-permute-done.6 = bf16[1024,512]{1,0:T(8,128)(2,1)} collective-permute-done((bf16[1024,512]{1,0:T(8,128)(2,1)}, bf16[1024,512]{1,0:T(8,128)(2,1)}, u32[]{:S(2)}, u32[]{:S(2)}) %collective-permute-start.6) | collective-permute-done | bytes 1048608 | tf_op jit(solution)/shard_map/ppermute | solution.py:894
  86.3 6.0 collective-permute-done.11
  105.3 6.4 collective-permute-done.10
  115.0 3.7 collective-permute-done.19.refs_4_.refs_5_.refs_20_.refs_21_.refs_19_.refs_22_.refs_3_.refs_8_
  118.7 4.6 collective-permute-done.20.refs_6_.refs_7_.refs_22_.refs_23_.refs_21_.refs_24_.refs_5_.refs_10_
  128.7 15.1 %shard_map.286 = (bf16[1024,3072]{1,0:T(8,128)(2,1)}, bf16[1024,1024]{1,0:T(8,128)(2,1)}) custom-call(s32[4]{0:T(128)} %add_add_fusion.refs_0_.place_ref, bf16[1024,1024]{1,0:T(8,128)(2,1)} %refs_4_.1, f32[24,1024]{1,0:T(8,128)} %pad.24.refs_2_.refs_3_.refs_1_.refs_4_.refs_6_, bf16[2,512,512]{2,1,0:T(8,128)(2,1)} %copy-done.5, ...), custom_call_target="tpu_custom_call" | custom-call | flops 1048576 | bytes 65536 | tf_op jit(solution)/shard_map/pallas_call | solution.py:709
  148.8 17.7 %shard_map.287 = (bf16[1024,1024]{1,0:T(8,128)(2,1)}, f32[8,8,1024]{2,1,0:T(8,128)}) custom-call(bf16[1024,3072]{1,0:T(8,128)(2,1)} %get-tuple-element.304.refs_0_.refs_1_.refs_2_.refs_3_, bf16[1024,3072]{1,0:T(8,128)(2,1)} %get-tuple-element.304.refs_0_.refs_1_.refs_2_.refs_3_, bf16[1024,3072]{1,0:T(8,128)(2,1)} %get-tuple-element.304.refs_0_.refs_1_.refs_2_.refs_3_), custom_call_target="tpu_custom_call" | custom-call | flops 1048576 | bytes 65536 | tf_op jit(solution)/shard_map/pallas_call | solution.py:234
  166.5 3.8 collective-permute-done.27.refs_4_.refs_5_.refs_6_.refs_3_
  174.5 7.9 %shard_map.288.refs_1_.refs_3_.refs_2_ = f32[1024,1024]{1,0:T(8,128)} custom-call(s32[4]{0:T(128)} %add_add_fusion.refs_0_.place_ref, bf16[1024,1024]{1,0:T(8,128)(2,1)} %get-tuple-element.308.refs_1_.refs_5_, f32[24,1024]{1,0:T(8,128)} %pad.24.refs_2_.refs_3_.refs_1_.refs_4_.refs_6_, bf16[1024,1024]{1,0:T(8,128)(2,1)} %refs_4_.1, ...), custom_call_target="tpu_custom_call" | custom-call | flops 1048576 | bytes 65536 | tf_op jit(solution)/shard_map/pallas_call | solution.py:709
  184.4 9.4 %shard_map.289 = (bf16[1024,1024]{1,0:T(8,128)(2,1)}, bf16[1024,1024]{1,0:T(8,128)(2,1)}) custom-call(s32[4]{0:T(128)} %add_add_fusion.refs_0_.place_ref, f32[1024,1024]{1,0:T(8,128)} %shard_map.288.refs_1_.refs_3_.refs_2_, f32[24,1024]{1,0:T(8,128)} %pad.24.refs_2_.refs_3_.refs_1_.refs_4_.refs_6_, bf16[2,512,512]{2,1,0:T(8,128)(2,1)} %copy-done.10, ...), custom_call_target="tpu_custom_call" | custom-call | flops 1048576 | bytes 65536 | tf_op jit(solution)/shard_map/pallas_call | solution.py:709
  199.3 8.6 %shard_map.290.refs_1_.refs_2_.refs_3_ = bf16[640,2048]{1,0:T(8,128)(2,1)} custom-call(s32[4]{0:T(128)} %add_add_fusion.refs_0_.place_ref, bf16[640,1024]{1,0:T(8,128)(2,1)} %pad_maximum_fusion.4.refs_1_, f32[24,1024]{1,0:T(8,128)} %pad.24.refs_2_.refs_3_.refs_1_.refs_4_.refs_6_, bf16[2,512,512]{2,1,0:T(8,128)(2,1)} %copy-done.10, ...), custom_call_target="tpu_custom_call" | custom-call | flops 1048576 | bytes 65536 | tf_op jit(solution)/shard_map/pallas_call | solution.py:709
  208.0 18.9 %shard_map.291 = (bf16[1024,1024]{1,0:T(8,128)(2,1)}, f32[8,8,1024]{2,1,0:T(8,128)}) custom-call(bf16[1024,1024]{1,0:T(8,128)(2,1)} %get-tuple-element.318.refs_0_.refs_1_, bf16[640,2048]{1,0:T(8,128)(2,1)} %shard_map.290.refs_1_.refs_2_.refs_3_, bf16[640,2048]{1,0:T(8,128)(2,1)} %shard_map.290.refs_1_.refs_2_.refs_3_, ...), custom_call_target="tpu_custom_call" | custom-call | flops 1048576 | bytes 65536 | tf_op jit(solution)/shard_map/pallas_call | solution.py:234
  228.1 8.4 %shard_map.292.refs_1_.refs_0_ = f32[1024,1024]{1,0:T(8,128)} custom-call(s32[4]{0:T(128)} %add_add_fusion.refs_0_.place_ref, bf16[1024,1024]{1,0:T(8,128)(2,1)} %get-tuple-element.324.refs_1_.refs_5_, f32[24,1024]{1,0:T(8,128)} %pad.24.refs_2_.refs_3_.refs_1_.refs_4_.refs_6_, f32[1024,1024]{1,0:T(8,128)} %shard_map.288.refs_1_.refs_3_.refs_2_, ...), custom_call_target="tpu_custom_call" | custom-call | flops 1048576 | bytes 65536 | tf_op jit(solution)/shard_map/pallas_call | solution.py:709
  237.5 39.4 %shard_map.293 = (bf16[1024,1024]{1,0:T(8,128)(2,1)}, bf16[1024,1024]{1,0:T(8,128)(2,1)}, bf16[4,1024,512]{2,1,0:T(8,128)(2,1)}, bf16[4,1024,512]{2,1,0:T(8,128)...) custom-call(s32[4]{0:T(128)} %add_add_fusion.1.refs_0_, f32[1024,1024]{1,0:T(8,128)} %shard_map.292.refs_1_.refs_0_, ...), custom_call_target="tpu_custom_call" | custom-call | flops 1048576 | bytes 65536 | tf_op jit(solution)/shard_map/pallas_call | solution.py:523
  277.5 37.5 %shard_map.294 = (bf16[1024,1024]{1,0:T(8,128)(2,1)}, bf16[1024,1024]{1,0:T(8,128)(2,1)}, bf16[4,1024,512]{2,1,0:T(8,128)(2,1)}, bf16[4,1024,512]{2,1,0:T(8,128)(2,1)}, f32[4,1,512]{2,1,0:T(1,128)}) custom-call(s32[4]{0:T(128)} %add_add_fusion.refs_0_.place_ref, bf16[1024,1024]{1,0:T(8,128)(2,1)} %get-tuple-element.337.refs_1_, ...), custom_call_target="tpu_custom_call" | custom-call | flops 1048576 | bytes 65536 | tf_op jit(solution)/shard_map/pallas_call | solution.py:523
  315.0 5.9 shard_map.295
  322.6 9.8 %shard_map.296 = (f32[1024,1024]{1,0:T(8,128)}, bf16[1024,1024]{1,0:T(8,128)(2,1)}, f32[8,1024]{1,0:T(8,128)}) custom-call(f32[1024,1024]{1,0:T(8,128)} %shard_map.292.refs_1_.refs_0_, f32[24,1024]{1,0:T(8,128)} %pad.24.refs_2_.refs_3_.refs_1_.refs_4_.refs_6_, bf16[1024,1024]{1,0:T(8,128)(2,1)} %multiply_convert_fusion.1.refs_2_, ...), custom_call_target="tpu_custom_call" | custom-call | flops 1048576 | bytes 65536 | tf_op jit(solution)/shard_map/pallas_call | solution.py:603
  332.4 7.5 %shard_map.297.refs_4_ = bf16[1024,1024]{1,0:T(8,128)(2,1)} custom-call(s32[4]{0:T(128)} %add_add_fusion.refs_0_.place_ref, bf16[1024,1024]{1,0:T(8,128)(2,1)} %get-tuple-element.354.refs_1_, bf16[2,512,512]{2,1,0:T(8,128)(2,1)} %copy-done.10, bf16[2,512,512]{2,1,0:T(8,128)(2,1)} %copy-done.13, bf16[2,512,512]{2,1,0:T(8,128)(2,1)} %copy-done.11, ...), custom_call_target="tpu_custom_call" | custom-call | flops 1048576 | bytes 65536 | tf_op jit(solution)/shard_map/pallas_call | solution.py:859
  339.9 17.8 %shard_map.298 = (bf16[1024,1024]{1,0:T(8,128)(2,1)}, bf16[640,1024]{1,0:T(8,128)(2,1)}, bf16[640,1024]{1,0:T(8,128)(2,1)}, f32[8,1024]{1,0:T(8,128)}, bf16[1024...) custom-call(s32[4]{0:T(128)} %add_add_fusion.1.refs_0_, ...), custom_call_target="tpu_custom_call" | custom-call | flops 1048576 | bytes 65536 | tf_op jit(solution)/shard_map/pallas_call | solution.py:289
  357.8 17.8 %shard_map.299 = (bf16[1024,1024]{1,0:T(8,128)(2,1)}, bf16[640,1024]{1,0:T(8,128)(2,1)}, bf16[640,1024]{1,0:T(8,128)(2,1)}, f32[8,1024]{1,0:T(8,128)}, bf16[1024...) custom-call(s32[4]{0:T(128)} %add_add_fusion.refs_0_.place_ref, ...), custom_call_target="tpu_custom_call", output_to_operand_aliasing={{0}: (8, {}), {1}: (9, {}), {2}: (10, {}), {3}: (11, {})} | custom-call | flops 1048576 | bytes 65536 | tf_op jit(solution)/shard_map/pallas_call | solution.py:289
  382.5 5.2 shard_map.300
  387.8 3.3 fusion.2
  403.5 11.8 %shard_map.301 = (f32[1024,1024]{1,0:T(8,128)}, bf16[1024,1024]{1,0:T(8,128)(2,1)}, f32[8,1024]{1,0:T(8,128)}) custom-call(s32[4]{0:T(128)} %add_add_fusion.refs_0_.place_ref, bf16[1024,1024]{1,0:T(8,128)(2,1)} %get-tuple-element.382.refs_1_, f32[1024,1024]{1,0:T(8,128)} %shard_map.288.refs_1_.refs_3_.refs_2_, f32[1024,1024]{1,0:T(8,128)} %get-tuple-element.383.refs_3_, ...), custom_call_target="tpu_custom_call" | custom-call | flops 1048576 | bytes 65536 | tf_op jit(solution)/shard_map/pallas_call | solution.py:859
  415.3 7.6 %shard_map.302.refs_4_ = bf16[1024,1024]{1,0:T(8,128)(2,1)} custom-call(s32[4]{0:T(128)} %add_add_fusion.refs_0_.place_ref, bf16[1024,1024]{1,0:T(8,128)(2,1)} %get-tuple-element.384.refs_1_, bf16[2,512,512]{2,1,0:T(8,128)(2,1)} %copy-done.5, bf16[2,512,512]{2,1,0:T(8,128)(2,1)} %copy-done.7, bf16[2,512,512]{2,1,0:T(8,128)(2,1)} %copy-done.6, ...), custom_call_target="tpu_custom_call" | custom-call | flops 1048576 | bytes 65536 | tf_op jit(solution)/shard_map/pallas_call | solution.py:859
  423.0 3.7 fusion.13
  431.7 6.9 %shard_map.303 = (f32[1024,512]{1,0:T(8,128)}, bf16[1024,512]{1,0:T(8,128)(2,1)}) custom-call(s32[4]{0:T(128)} %add_add_fusion.refs_0_.place_ref, bf16[4,1024,512]{2,1,0:T(8,128)(2,1)} %get-tuple-element.343.refs_1_.refs_5_.refs_6_, bf16[4,1024,512]{2,1,0:T(8,128)(2,1)} %collective-permute-done.39.refs_2_.refs_6_.refs_7_, ...), custom_call_target="tpu_custom_call" | custom-call | flops 1048576 | bytes 65536 | tf_op jit(solution)/shard_map/pallas_call | solution.py:1095
  438.7 4.0 shard_map.304
  445.6 17.2 %shard_map.305 = (bf16[1024,1024]{1,0:T(8,128)(2,1)}, bf16[1024,1024]{1,0:T(8,128)(2,1)}, bf16[1024,1024]{1,0:T(8,128)(2,1)}, f32[8,1024]{1,0:T(8,128)}, bf16[10...) custom-call(s32[4]{0:T(128)} %add_add_fusion.1.refs_0_, ...), custom_call_target="tpu_custom_call" | custom-call | flops 1048576 | bytes 65536 | tf_op jit(solution)/shard_map/pallas_call | solution.py:289
  475.5 3.8 shard_map.306
  483.3 17.4 %shard_map.307 = (bf16[1024,1024]{1,0:T(8,128)(2,1)}, bf16[1024,1024]{1,0:T(8,128)(2,1)}, bf16[1024,1024]{1,0:T(8,128)(2,1)}, f32[8,1024]{1,0:T(8,128)}, bf16[10...) custom-call(s32[4]{0:T(128)} %add_add_fusion.refs_0_.place_ref, ...), custom_call_target="tpu_custom_call", output_to_operand_aliasing={{0}: (7, {}), {1}: (8, {}), {2}: (9, {}), {3}: (10, {})} | custom-call | flops 1048576 | bytes 65536 | tf_op jit(solution)/shard_map/pallas_call | solution.py:289
  500.7 3.3 fusion.16
  509.0 4.0 shard_map.308
  514.7 8.8 %shard_map.311 = bf16[640,1024]{1,0:T(8,128)(2,1)} custom-call(s32[4]{0:T(128)} %add_add_fusion.refs_0_.place_ref, bf16[640,1024]{1,0:T(8,128)(2,1)} %get-tuple-element.449.refs_1_, bf16[640,1024]{1,0:T(8,128)(2,1)} %get-tuple-element.450.refs_2_, bf16[2,512,512]{2,1,0:T(8,128)(2,1)} %copy-done.10, bf16[2,512,512]{2,1,0:T(8,128)(2,1)} %copy-done.13, ...), custom_call_target="tpu_custom_call" | custom-call | flops 1048576 | bytes 65536 | tf_op jit(solution)/shard_map/pallas_call | solution.py:859
  525.9 3.4 collective-permute-start.54
  531.7 18.8 %shard_map.309 = (f32[1024,1024]{1,0:T(8,128)}, bf16[1024,1024]{1,0:T(8,128)(2,1)}, f32[8,1024]{1,0:T(8,128)}) custom-call(s32[4]{0:T(128)} %add_add_fusion.refs_0_.place_ref, bf16[1024,1024]{1,0:T(8,128)(2,1)} %get-tuple-element.435.refs_1_, bf16[1024,1024]{1,0:T(8,128)(2,1)} %get-tuple-element.436.refs_2_, bf16[1024,1024]{1,0:T(8,128)(2,1)} %get-tuple-element.437.refs_3_, ...), custom_call_target="tpu_custom_call" | custom-call | flops 1048576 | bytes 65536 | tf_op jit(solution)/shard_map/pallas_call | solution.py:859
  550.5 5.3 shard_map.310
  555.8 3.8 shard_map.312
  559.6 4.2 collective-permute-start.63
  570.7 5.6 collective-permute-start.65
  579.5 5.4 shard_map.314
  586.6 3.3 fusion.1
  593.9 4.4 multiply_convert_fusion
  598.3 13.5 %collective-permute-done.59 = f32[24,256]{1,0:T(8,128)S(1)} collective-permute-done((f32[24,256]{1,0:T(8,128)S(1)}, f32[24,256]{1,0:T(8,128)S(1)}, u32[]{:S(2)}, u32[]{:S(2)}) %collective-permute-start.59) | collective-permute-done | bytes 24608 | tf_op jit(solution)/shard_map/ppermute | solution.py:885
  624.3 3.8 add_select_fusion.other_ref
  632.3 13.9 %collective-permute-done.68.far_ref = bf16[1024,512]{1,0:T(8,128)(2,1)} collective-permute-done((bf16[1024,512]{1,0:T(8,128)(2,1)S(1)}, bf16[1024,512]{1,0:T(8,128)(2,1)}, u32[]{:S(2)}, u32[]{:S(2)}) %collective-permute-start.68) | collective-permute-done | bytes 1048608 | tf_op jit(solution)/shard_map/ppermute | solution.py:894
  648.0 26.2 %shard_map.315 = (f32[1024,512]{1,0:T(8,128)}, f32[1024,512]{1,0:T(8,128)}, f32[1024,512]{1,0:T(8,128)}, f32[1024,512]{1,0:T(8,128)}, f32[1024,512]{1,0:T(8,128)...) custom-call(s32[4]{0:T(128)} %add_add_fusion.refs_0_.place_ref, ...), custom_call_target="tpu_custom_call" | custom-call | flops 1048576 | bytes 65536 | tf_op jit(solution)/shard_map/pallas_call | solution.py:1259
  (383 shorter events, 169.0 us)
Async XLA Ops:
  3.5 39.7 %collective-permute-start = (bf16[1024,512]{1,0:T(8,128)(2,1)}, bf16[1024,512]{1,0:T(8,128)(2,1)S(1)}, u32[]{:S(2)}, u32[]{:S(2)}) collective-permute-start(bf16[1024,512]{1,0:T(8,128)(2,1)} %convert_element_type.124), channel_id=1, source_target_pairs={{0,16},{1,17},{2,18},{3,19},{4,20},{5,21},{6,22},{7,23},{8,0},{9,1... | collective-permute-start | bytes 3145736 | tf_op jit(solution)/shard_map/ppermute | solution.py:894
  11.3 31.8 %collective-permute-start.1 = (bf16[512,512]{1,0:T(8,128)(2,1)}, bf16[512,512]{1,0:T(8,128)(2,1)S(1)}, u32[]{:S(2)}, u32[]{:S(2)}) collective-permute-start(bf16[512,512]{1,0:T(8,128)(2,1)} %get-tuple-element.530), channel_id=1, source_target_pairs={{0,2},{1,3},{2,0},{3,1},{4,6},{5,7},{6,4},{7,5},{8,10},{9,11},{10,... | collective-permute-start | bytes 1572872 | tf_op jit(solution)/shard_map/ppermute | solution.py:885
  12.8 30.4 %collective-permute-start.2 = (bf16[512,512]{1,0:T(8,128)(2,1)}, bf16[512,512]{1,0:T(8,128)(2,1)S(1)}, u32[]{:S(2)}, u32[]{:S(2)}) collective-permute-start(bf16[512,512]{1,0:T(8,128)(2,1)} %get-tuple-element.529), channel_id=1, source_target_pairs={{0,4},{1,5},{2,6},{3,7},{4,0},{5,1},{6,2},{7,3},{8,12},{9,13},{10,... | collective-permute-start | bytes 1572872 | tf_op jit(solution)/shard_map/ppermute | solution.py:885
  14.3 28.8 %collective-permute-start.4 = (bf16[160,1024]{1,0:T(8,128)(2,1)}, bf16[160,1024]{1,0:T(8,128)(2,1)}, u32[]{:S(2)}, u32[]{:S(2)}) collective-permute-start(bf16[160,1024]{1,0:T(8,128)(2,1)} %get-tuple-element.517), channel_id=1, source_target_pairs={{0,2},{1,3},{2,0},{3,1},{4,6},{5,7},{6,4},{7,5},{8,10},{9,11},{10,... | collective-permute-start | bytes 983048 | tf_op jit(solution)/shard_map/ppermute | solution.py:885
  15.0 28.2 %collective-permute-start.5 = (bf16[160,1024]{1,0:T(8,128)(2,1)}, bf16[160,1024]{1,0:T(8,128)(2,1)}, u32[]{:S(2)}, u32[]{:S(2)}) collective-permute-start(bf16[160,1024]{1,0:T(8,128)(2,1)} %get-tuple-element.515), channel_id=1, source_target_pairs={{0,3},{1,2},{2,1},{3,0},{4,7},{5,6},{6,5},{7,4},{8,11},{9,10},{10,... | collective-permute-start | bytes 983048 | tf_op jit(solution)/shard_map/ppermute | solution.py:885
  16.4 25.8 %all-to-all-start = ((bf16[32,16,128]{2,1,0:T(8,128)(2,1)}), bf16[32,16,128]{2,1,0:T(8,128)(2,1)S(1)}, u32[]{:S(2)}, u32[]{:S(2)}) async-start(bf16[32,16,128]{2,1,0:T(8,128)(2,1)} %pad.22), calls=%async_computation | async-start | bytes 262144 | tf_op jit(solution)/shard_map/all_to_all | solution.py:1294
  43.2 29.2 %collective-permute-start.7 = (bf16[1024,512]{1,0:T(8,128)(2,1)}, bf16[1024,512]{1,0:T(8,128)(2,1)}, u32[]{:S(2)}, u32[]{:S(2)}) collective-permute-start(bf16[1024,512]{1,0:T(8,128)(2,1)} %convert_element_type.124), channel_id=1, source_target_pairs={{8,16},{9,17},{10,18},{11,19},{12,20},{13,21},{14,22},{15,23},{16,... | collective-permute-start | bytes 3145736 | tf_op jit(solution)/shard_map/ppermute | solution.py:894
  47.3 25.1 %collective-permute-start.6 = (bf16[1024,512]{1,0:T(8,128)(2,1)}, bf16[1024,512]{1,0:T(8,128)(2,1)}, u32[]{:S(2)}, u32[]{:S(2)}) collective-permute-start(bf16[1024,512]{1,0:T(8,128)(2,1)} %broadcast_select_fusion.3), channel_id=1, source_target_pairs={{0,8},{1,9},{2,10},{3,11},{4,12},{5,13},{6,14},{7,15},{8,0},{9,1},... | collective-permute-start | bytes 3145736 | tf_op jit(solution)/shard_map/ppermute | solution.py:894
  49.8 24.3 %collective-permute-start.8 = (bf16[2,512,512]{2,1,0:T(8,128)(2,1)S(1)}, bf16[2,512,512]{2,1,0:T(8,128)(2,1)S(1)}, u32[]{:S(2)}, u32[]{:S(2)}) collective-permute-start(bf16[2,512,512]{2,1,0:T(8,128)(2,1)S(1)} %pad_maximum_fusion.6.refs_11_.refs_12_.refs_9_.refs_21_.refs_10_.refs_13_.refs_15_), channel_id=1, source_target_pairs={{0,4},{1,5},{2,6},{3,7},{4,0},{5,1},{6,2},{7,3},{8,12},{9,13},{10,... | collective-permute-start | bytes 3145736 | tf_op jit(solution)/shard_map/ppermute | solution.py:885
  50.4 24.5 %collective-permute-start.9 = (bf16[2,512,512]{2,1,0:T(8,128)(2,1)S(1)}, bf16[2,512,512]{2,1,0:T(8,128)(2,1)}, u32[]{:S(2)}, u32[]{:S(2)}) collective-permute-start(bf16[2,512,512]{2,1,0:T(8,128)(2,1)S(1)} %pad_maximum_fusion.7.refs_13_.refs_14_.refs_11_.refs_23_.refs_12_.refs_15_.refs_17_), channel_id=1, source_target_pairs={{0,2},{1,3},{2,0},{3,1},{4,6},{5,7},{6,4},{7,5},{8,10},{9,11},{10,... | collective-permute-start | bytes 3145736 | tf_op jit(solution)/shard_map/ppermute | solution.py:885
  52.0 27.7 %collective-permute-start.13 = (bf16[2,512,512]{2,1,0:T(8,128)(2,1)S(1)}, bf16[2,512,512]{2,1,0:T(8,128)(2,1)}, u32[]{:S(2)}, u32[]{:S(2)}) collective-permute-start(bf16[2,512,512]{2,1,0:T(8,128)(2,1)S(1)} %pad_maximum_fusion.6.refs_11_.refs_12_.refs_9_.refs_21_.refs_10_.refs_13_.refs_15_), channel_id=1, source_target_pairs={{0,1},{1,0},{2,3},{3,2},{4,5},{5,4},{6,7},{7,6},{8,9},{9,8},{10,11... | collective-permute-start | bytes 3145736 | tf_op jit(solution)/shard_map/ppermute | solution.py:885
  85.0 26.7 %collective-permute-start.10 = (bf16[1024,512]{1,0:T(8,128)(2,1)}, bf16[1024,512]{1,0:T(8,128)(2,1)}, u32[]{:S(2)}, u32[]{:S(2)}) collective-permute-start(bf16[1024,512]{1,0:T(8,128)(2,1)} %collective-permute-done.7), channel_id=1, source_target_pairs={{8,0},{9,1},{10,2},{11,3},{12,4},{13,5},{14,6},{15,7},{16,24},{17,... | collective-permute-start | bytes 3145736 | tf_op jit(solution)/shard_map/ppermute | solution.py:894
  94.7 24.0 %collective-permute-start.19 = (bf16[2,512,512]{2,1,0:T(8,128)(2,1)S(1)}, bf16[2,512,512]{2,1,0:T(8,128)(2,1)S(1)}, u32[]{:S(2)}, u32[]{:S(2)}) collective-permute-start(bf16[2,512,512]{2,1,0:T(8,128)(2,1)S(1)} %pad_maximum_fusion.8.refs_3_.refs_4_.refs_19_.refs_20_.refs_18_.refs_21_.refs_2_.refs_7_), channel_id=1, source_target_pairs={{0,4},{1,5},{2,6},{3,7},{4,0},{5,1},{6,2},{7,3},{8,12},{9,13},{10,... | collective-permute-start | bytes 3145736 | tf_op jit(solution)/shard_map/ppermute | solution.py:885
  96.2 27.1 %collective-permute-start.21 = (bf16[2,512,512]{2,1,0:T(8,128)(2,1)S(1)}, bf16[2,512,512]{2,1,0:T(8,128)(2,1)}, u32[]{:S(2)}, u32[]{:S(2)}) collective-permute-start(bf16[2,512,512]{2,1,0:T(8,128)(2,1)S(1)} %pad_maximum_fusion.8.refs_3_.refs_4_.refs_19_.refs_20_.refs_18_.refs_21_.refs_2_.refs_7_), channel_id=1, source_target_pairs={{0,1},{1,0},{2,3},{3,2},{4,5},{5,4},{6,7},{7,6},{8,9},{9,8},{10,11... | collective-permute-start | bytes 3145736 | tf_op jit(solution)/shard_map/ppermute | solution.py:885
  97.5 25.7 %collective-permute-start.20 = (bf16[2,512,512]{2,1,0:T(8,128)(2,1)S(1)}, bf16[2,512,512]{2,1,0:T(8,128)(2,1)}, u32[]{:S(2)}, u32[]{:S(2)}) collective-permute-start(bf16[2,512,512]{2,1,0:T(8,128)(2,1)S(1)} %pad_maximum_fusion.9.refs_5_.refs_6_.refs_21_.refs_22_.refs_20_.refs_23_.refs_4_.refs_9_), channel_id=1, source_target_pairs={{0,2},{1,3},{2,0},{3,1},{4,6},{5,7},{6,4},{7,5},{8,10},{9,11},{10,... | collective-permute-start | bytes 3145736 | tf_op jit(solution)/shard_map/ppermute | solution.py:885
  98.0 25.3 %collective-permute-start.22 = (bf16[2,512,512]{2,1,0:T(8,128)(2,1)S(1)}, bf16[2,512,512]{2,1,0:T(8,128)(2,1)}, u32[]{:S(2)}, u32[]{:S(2)}) collective-permute-start(bf16[2,512,512]{2,1,0:T(8,128)(2,1)S(1)} %pad_maximum_fusion.9.refs_5_.refs_6_.refs_21_.refs_22_.refs_20_.refs_23_.refs_4_.refs_9_), channel_id=1, source_target_pairs={{0,1},{1,0},{2,3},{3,2},{4,5},{5,4},{6,7},{7,6},{8,9},{9,8},{10,11... | collective-permute-start | bytes 3145736 | tf_op jit(solution)/shard_map/ppermute | solution.py:885
  145.1 25.3 %collective-permute-start.27 = (bf16[2,512,512]{2,1,0:T(8,128)(2,1)S(1)}, bf16[2,512,512]{2,1,0:T(8,128)(2,1)S(1)}, u32[]{:S(2)}, u32[]{:S(2)}) collective-permute-start(bf16[2,512,512]{2,1,0:T(8,128)(2,1)S(1)} %pad_maximum_fusion.10.refs_3_.refs_4_.refs_5_.refs_2_), channel_id=1, source_target_pairs={{0,4},{1,5},{2,6},{3,7},{4,0},{5,1},{6,2},{7,3},{8,12},{9,13},{10,... | collective-permute-start | bytes 3145736 | tf_op jit(solution)/shard_map/ppermute | solution.py:885
  147.1 25.1 %collective-permute-start.28 = (bf16[2,512,512]{2,1,0:T(8,128)(2,1)S(1)}, bf16[2,512,512]{2,1,0:T(8,128)(2,1)}, u32[]{:S(2)}, u32[]{:S(2)}) collective-permute-start(bf16[2,512,512]{2,1,0:T(8,128)(2,1)S(1)} %pad_maximum_fusion.11.refs_5_.refs_6_.refs_7_.refs_4_), channel_id=1, source_target_pairs={{0,2},{1,3},{2,0},{3,1},{4,6},{5,7},{6,4},{7,5},{8,10},{9,11},{10,... | collective-permute-start | bytes 3145736 | tf_op jit(solution)/shard_map/ppermute | solution.py:885
  148.3 23.9 %collective-permute-start.29 = (bf16[2,512,512]{2,1,0:T(8,128)(2,1)S(1)}, bf16[2,512,512]{2,1,0:T(8,128)(2,1)}, u32[]{:S(2)}, u32[]{:S(2)}) collective-permute-start(bf16[2,512,512]{2,1,0:T(8,128)(2,1)S(1)} %pad_maximum_fusion.10.refs_3_.refs_4_.refs_5_.refs_2_), channel_id=1, source_target_pairs={{0,1},{1,0},{2,3},{3,2},{4,5},{5,4},{6,7},{7,6},{8,9},{9,8},{10,11... | collective-permute-start | bytes 3145736 | tf_op jit(solution)/shard_map/ppermute | solution.py:885
  148.3 23.9 %collective-permute-start.30 = (bf16[2,512,512]{2,1,0:T(8,128)(2,1)S(1)}, bf16[2,512,512]{2,1,0:T(8,128)(2,1)}, u32[]{:S(2)}, u32[]{:S(2)}) collective-permute-start(bf16[2,512,512]{2,1,0:T(8,128)(2,1)S(1)} %pad_maximum_fusion.11.refs_5_.refs_6_.refs_7_.refs_4_), channel_id=1, source_target_pairs={{0,1},{1,0},{2,3},{3,2},{4,5},{5,4},{6,7},{7,6},{8,9},{9,8},{10,11... | collective-permute-start | bytes 3145736 | tf_op jit(solution)/shard_map/ppermute | solution.py:885
  195.2 31.7 %collective-permute-start.33 = (bf16[2,512,512]{2,1,0:T(8,128)(2,1)S(1)}, bf16[2,512,512]{2,1,0:T(8,128)(2,1)S(1)}, u32[]{:S(2)}, u32[]{:S(2)}) collective-permute-start(bf16[2,512,512]{2,1,0:T(8,128)(2,1)S(1)} %pad_maximum_fusion.12.refs_13_.refs_17_), channel_id=1, source_target_pairs={{0,4},{1,5},{2,6},{3,7},{4,0},{5,1},{6,2},{7,3},{8,12},{9,13},{10,... | collective-permute-start | bytes 3145736 | tf_op jit(solution)/shard_map/ppermute | solution.py:885
  197.2 29.7 %collective-permute-start.34 = (bf16[2,512,512]{2,1,0:T(8,128)(2,1)S(1)}, bf16[2,512,512]{2,1,0:T(8,128)(2,1)}, u32[]{:S(2)}, u32[]{:S(2)}) collective-permute-start(bf16[2,512,512]{2,1,0:T(8,128)(2,1)S(1)} %pad_maximum_fusion.13.refs_15_.refs_19_), channel_id=1, source_target_pairs={{0,2},{1,3},{2,0},{3,1},{4,6},{5,7},{6,4},{7,5},{8,10},{9,11},{10,... | collective-permute-start | bytes 3145736 | tf_op jit(solution)/shard_map/ppermute | solution.py:885
  198.8 28.1 %collective-permute-start.35 = (bf16[2,512,512]{2,1,0:T(8,128)(2,1)S(1)}, bf16[2,512,512]{2,1,0:T(8,128)(2,1)}, u32[]{:S(2)}, u32[]{:S(2)}) collective-permute-start(bf16[2,512,512]{2,1,0:T(8,128)(2,1)S(1)} %pad_maximum_fusion.12.refs_13_.refs_17_), channel_id=1, source_target_pairs={{0,1},{1,0},{2,3},{3,2},{4,5},{5,4},{6,7},{7,6},{8,9},{9,8},{10,11... | collective-permute-start | bytes 3145736 | tf_op jit(solution)/shard_map/ppermute | solution.py:885
  198.8 28.1 %collective-permute-start.36 = (bf16[2,512,512]{2,1,0:T(8,128)(2,1)S(1)}, bf16[2,512,512]{2,1,0:T(8,128)(2,1)}, u32[]{:S(2)}, u32[]{:S(2)}) collective-permute-start(bf16[2,512,512]{2,1,0:T(8,128)(2,1)S(1)} %pad_maximum_fusion.13.refs_15_.refs_19_), channel_id=1, source_target_pairs={{0,1},{1,0},{2,3},{3,2},{4,5},{5,4},{6,7},{7,6},{8,9},{9,8},{10,11... | collective-permute-start | bytes 3145736 | tf_op jit(solution)/shard_map/ppermute | solution.py:885
  277.0 38.1 %collective-permute-start.39 = (bf16[4,1024,512]{2,1,0:T(8,128)(2,1)}, bf16[4,1024,512]{2,1,0:T(8,128)(2,1)}, u32[]{:S(2)}, u32[]{:S(2)}) collective-permute-start(bf16[4,1024,512]{2,1,0:T(8,128)(2,1)} %get-tuple-element.334), channel_id=1, source_target_pairs={{0,1},{1,0},{2,3},{3,2},{4,5},{5,4},{6,7},{7,6},{8,9},{9,8},{10,11... | collective-permute-start | bytes 12582920 | tf_op jit(solution)/shard_map/ppermute | solution.py:885
  277.0 38.0 %collective-permute-start.40 = (bf16[4,1024,512]{2,1,0:T(8,128)(2,1)}, bf16[4,1024,512]{2,1,0:T(8,128)(2,1)}, u32[]{:S(2)}, u32[]{:S(2)}) collective-permute-start(bf16[4,1024,512]{2,1,0:T(8,128)(2,1)} %get-tuple-element.335), channel_id=1, source_target_pairs={{0,1},{1,0},{2,3},{3,2},{4,5},{5,4},{6,7},{7,6},{8,9},{9,8},{10,11... | collective-permute-start | bytes 12582920 | tf_op jit(solution)/shard_map/ppermute | solution.py:885
  320.9 61.6 %collective-permute-start.41 = (bf16[2,2,512,512]{3,2,1,0:T(8,128)(2,1)}, bf16[2,2,512,512]{3,2,1,0:T(8,128)(2,1)}, u32[]{:S(2)}, u32[]{:S(2)}) collective-permute-start(bf16[2,2,512,512]{3,2,1,0:T(8,128)(2,1)} %get-tuple-element.350), channel_id=1, source_target_pairs={{0,4},{1,5},{2,6},{3,7},{4,0},{5,1},{6,2},{7,3},{8,12},{9,13},{10,... | collective-permute-start | bytes 6291464 | tf_op jit(solution)/shard_map/ppermute | solution.py:885
  322.3 60.2 %collective-permute-start.42 = (bf16[2,2,512,512]{3,2,1,0:T(8,128)(2,1)}, bf16[2,2,512,512]{3,2,1,0:T(8,128)(2,1)}, u32[]{:S(2)}, u32[]{:S(2)}) collective-permute-start(bf16[2,2,512,512]{3,2,1,0:T(8,128)(2,1)} %get-tuple-element.351), channel_id=1, source_target_pairs={{0,2},{1,3},{2,0},{3,1},{4,6},{5,7},{6,4},{7,5},{8,10},{9,11},{10,... | collective-permute-start | bytes 6291464 | tf_op jit(solution)/shard_map/ppermute | solution.py:885
  393.5 37.3 %collective-permute-start.45 = (bf16[4,1024,512]{2,1,0:T(8,128)(2,1)}, bf16[4,1024,512]{2,1,0:T(8,128)(2,1)}, u32[]{:S(2)}, u32[]{:S(2)}) collective-permute-start(bf16[4,1024,512]{2,1,0:T(8,128)(2,1)} %pad_maximum_fusion), channel_id=1, source_target_pairs={{0,1},{1,0},{2,3},{3,2},{4,5},{5,4},{6,7},{7,6},{8,9},{9,8},{10,11... | collective-permute-start | bytes 12582920 | tf_op jit(solution)/shard_map/ppermute | solution.py:885
  401.1 29.6 %collective-permute-start.43 = (bf16[2,1,512,512]{3,2,1,0:T(8,128)(2,1)}, bf16[2,1,512,512]{3,2,1,0:T(8,128)(2,1)S(1)}, u32[]{:S(2)}, u32[]{:S(2)}) collective-permute-start(bf16[2,1,512,512]{3,2,1,0:T(8,128)(2,1)} %get-tuple-element.370), channel_id=1, source_target_pairs={{0,2},{1,3},{2,0},{3,1},{4,6},{5,7},{6,4},{7,5},{8,10},{9,11},{10,... | collective-permute-start | bytes 3145736 | tf_op jit(solution)/shard_map/ppermute | solution.py:885
  402.9 27.9 %collective-permute-start.44 = (bf16[2,1,512,512]{3,2,1,0:T(8,128)(2,1)}, bf16[2,1,512,512]{3,2,1,0:T(8,128)(2,1)}, u32[]{:S(2)}, u32[]{:S(2)}) collective-permute-start(bf16[2,1,512,512]{3,2,1,0:T(8,128)(2,1)} %get-tuple-element.371), channel_id=1, source_target_pairs={{0,4},{1,5},{2,6},{3,7},{4,0},{5,1},{6,2},{7,3},{8,12},{9,13},{10,... | collective-permute-start | bytes 3145736 | tf_op jit(solution)/shard_map/ppermute | solution.py:885
  442.7 28.5 %collective-permute-start.46 = (bf16[1024,512]{1,0:T(8,128)(2,1)}, bf16[1024,512]{1,0:T(8,128)(2,1)S(1)}, u32[]{:S(2)}, u32[]{:S(2)}) collective-permute-start(bf16[1024,512]{1,0:T(8,128)(2,1)} %get-tuple-element.393), channel_id=1, source_target_pairs={{0,8},{1,9},{2,10},{3,11},{4,12},{5,13},{6,14},{7,15},{8,0},{9,1},... | collective-permute-start | bytes 3145736 | tf_op jit(solution)/shard_map/ppermute | solution.py:894
  443.8 27.4 %collective-permute-start.47 = (bf16[1,2,512,512]{3,2,1,0:T(8,128)(2,1)}, bf16[1,2,512,512]{3,2,1,0:T(8,128)(2,1)S(1)}, u32[]{:S(2)}, u32[]{:S(2)}) collective-permute-start(bf16[1,2,512,512]{3,2,1,0:T(8,128)(2,1)} %get-tuple-element.394), channel_id=1, source_target_pairs={{0,4},{1,5},{2,6},{3,7},{4,0},{5,1},{6,2},{7,3},{8,12},{9,13},{10,... | collective-permute-start | bytes 3145736 | tf_op jit(solution)/shard_map/ppermute | solution.py:885
  445.2 25.9 %collective-permute-start.48 = (bf16[1,2,512,512]{3,2,1,0:T(8,128)(2,1)}, bf16[1,2,512,512]{3,2,1,0:T(8,128)(2,1)S(1)}, u32[]{:S(2)}, u32[]{:S(2)}) collective-permute-start(bf16[1,2,512,512]{3,2,1,0:T(8,128)(2,1)} %get-tuple-element.395), channel_id=1, source_target_pairs={{0,2},{1,3},{2,0},{3,1},{4,6},{5,7},{6,4},{7,5},{8,10},{9,11},{10,... | collective-permute-start | bytes 3145736 | tf_op jit(solution)/shard_map/ppermute | solution.py:885
  471.2 37.8 %collective-permute-start.49 = (bf16[4,1024,512]{2,1,0:T(8,128)(2,1)}, bf16[4,1024,512]{2,1,0:T(8,128)(2,1)}, u32[]{:S(2)}, u32[]{:S(2)}) collective-permute-start(bf16[4,1024,512]{2,1,0:T(8,128)(2,1)} %pad_maximum_fusion.2), channel_id=1, source_target_pairs={{0,1},{1,0},{2,3},{3,2},{4,5},{5,4},{6,7},{7,6},{8,9},{9,8},{10,11... | collective-permute-start | bytes 12582920 | tf_op jit(solution)/shard_map/ppermute | solution.py:885
  481.0 28.0 %collective-permute-start.50 = (bf16[1,1,512,512]{3,2,1,0:T(8,128)(2,1)}, bf16[1,1,512,512]{3,2,1,0:T(8,128)(2,1)S(1)}, u32[]{:S(2)}, u32[]{:S(2)}) collective-permute-start(bf16[1,1,512,512]{3,2,1,0:T(8,128)(2,1)} %get-tuple-element.417), channel_id=1, source_target_pairs={{0,2},{1,3},{2,0},{3,1},{4,6},{5,7},{6,4},{7,5},{8,10},{9,11},{10,... | collective-permute-start | bytes 1572872 | tf_op jit(solution)/shard_map/ppermute | solution.py:885
  482.7 26.3 %collective-permute-start.51 = (bf16[1,1,512,512]{3,2,1,0:T(8,128)(2,1)}, bf16[1,1,512,512]{3,2,1,0:T(8,128)(2,1)}, u32[]{:S(2)}, u32[]{:S(2)}) collective-permute-start(bf16[1,1,512,512]{3,2,1,0:T(8,128)(2,1)} %get-tuple-element.418), channel_id=1, source_target_pairs={{0,4},{1,5},{2,6},{3,7},{4,0},{5,1},{6,2},{7,3},{8,12},{9,13},{10,... | collective-permute-start | bytes 1572872 | tf_op jit(solution)/shard_map/ppermute | solution.py:885
  513.0 42.8 %collective-permute-start.52 = (bf16[1,2,512,512]{3,2,1,0:T(8,128)(2,1)}, bf16[1,2,512,512]{3,2,1,0:T(8,128)(2,1)}, u32[]{:S(2)}, u32[]{:S(2)}) collective-permute-start(bf16[1,2,512,512]{3,2,1,0:T(8,128)(2,1)} %get-tuple-element.433), channel_id=1, source_target_pairs={{0,4},{1,5},{2,6},{3,7},{4,0},{5,1},{6,2},{7,3},{8,12},{9,13},{10,... | collective-permute-start | bytes 3145736 | tf_op jit(solution)/shard_map/ppermute | solution.py:885
  514.4 41.4 %collective-permute-start.53 = (bf16[1,2,512,512]{3,2,1,0:T(8,128)(2,1)}, bf16[1,2,512,512]{3,2,1,0:T(8,128)(2,1)}, u32[]{:S(2)}, u32[]{:S(2)}) collective-permute-start(bf16[1,2,512,512]{3,2,1,0:T(8,128)(2,1)} %get-tuple-element.434), channel_id=1, source_target_pairs={{0,2},{1,3},{2,0},{3,1},{4,6},{5,7},{6,4},{7,5},{8,10},{9,11},{10,... | collective-permute-start | bytes 3145736 | tf_op jit(solution)/shard_map/ppermute | solution.py:885
  525.9 29.9 %collective-permute-start.54 = (bf16[512,512]{1,0:T(8,128)(2,1)S(1)}, bf16[512,512]{1,0:T(8,128)(2,1)}, u32[]{:S(2)}, u32[]{:S(2)}) collective-permute-start(bf16[512,512]{1,0:T(8,128)(2,1)S(1)} %slice.87), channel_id=1, source_target_pairs={{0,16},{1,17},{2,18},{3,19},{4,20},{5,21},{6,22},{7,23},{8,24},{9,... | collective-permute-start | bytes 1572872 | tf_op jit(solution)/shard_map/ppermute | solution.py:894
  529.2 26.6 %collective-permute-start.56 = (bf16[160,1024]{1,0:T(8,128)(2,1)}, bf16[160,1024]{1,0:T(8,128)(2,1)}, u32[]{:S(2)}, u32[]{:S(2)}) collective-permute-start(bf16[160,1024]{1,0:T(8,128)(2,1)} %get-tuple-element.512), channel_id=1, source_target_pairs={{0,2},{1,3},{2,0},{3,1},{4,6},{5,7},{6,4},{7,5},{8,10},{9,11},{10,... | collective-permute-start | bytes 983048 | tf_op jit(solution)/shard_map/ppermute | solution.py:885
  531.7 24.1 %collective-permute-start.57 = (bf16[160,1024]{1,0:T(8,128)(2,1)}, bf16[160,1024]{1,0:T(8,128)(2,1)}, u32[]{:S(2)}, u32[]{:S(2)}) collective-permute-start(bf16[160,1024]{1,0:T(8,128)(2,1)} %get-tuple-element.511), channel_id=1, source_target_pairs={{0,3},{1,2},{2,1},{3,0},{4,7},{5,6},{6,5},{7,4},{8,11},{9,10},{10,... | collective-permute-start | bytes 983048 | tf_op jit(solution)/shard_map/ppermute | solution.py:885
  559.6 27.0 %collective-permute-start.63 = (bf16[1024,512]{1,0:T(8,128)(2,1)}, bf16[1024,512]{1,0:T(8,128)(2,1)}, u32[]{:S(2)}, u32[]{:S(2)}) collective-permute-start(bf16[1024,512]{1,0:T(8,128)(2,1)} %get-tuple-element.473), channel_id=1, source_target_pairs={{0,8},{1,9},{2,10},{3,11},{4,12},{5,13},{6,14},{7,15},{24,16},{25,... | collective-permute-start | bytes 3145736 | tf_op jit(solution)/shard_map/ppermute | solution.py:894
  569.9 21.7 %collective-permute-start.58 = (f32[24,512]{1,0:T(8,128)S(1)}, f32[24,512]{1,0:T(8,128)S(1)}, u32[]{:S(2)}, u32[]{:S(2)}) collective-permute-start(f32[24,512]{1,0:T(8,128)S(1)} %constant_dynamic-slice_fusion.4), channel_id=1, source_target_pairs={{0,16},{1,17},{2,18},{3,19},{4,20},{5,21},{6,22},{7,23},{8,24},{9,... | collective-permute-start | bytes 147464 | tf_op jit(solution)/shard_map/ppermute | solution.py:885
  570.7 44.8 %collective-permute-start.65 = (bf16[512,512]{1,0:T(8,128)(2,1)}, bf16[512,512]{1,0:T(8,128)(2,1)}, u32[]{:S(2)}, u32[]{:S(2)}) collective-permute-start(bf16[512,512]{1,0:T(8,128)(2,1)} %slice.92), channel_id=1, source_target_pairs={{0,16},{1,17},{2,18},{3,19},{4,20},{5,21},{6,22},{7,23},{8,24},{9,... | collective-permute-start | bytes 1572872 | tf_op jit(solution)/shard_map/ppermute | solution.py:894
  584.9 30.6 %collective-permute-start.62 = (bf16[1024,512]{1,0:T(8,128)(2,1)}, bf16[1024,512]{1,0:T(8,128)(2,1)S(1)}, u32[]{:S(2)}, u32[]{:S(2)}) collective-permute-start(bf16[1024,512]{1,0:T(8,128)(2,1)} %get-tuple-element.471), channel_id=1, source_target_pairs={{8,0},{9,1},{10,2},{11,3},{12,4},{13,5},{14,6},{15,7},{24,16},{25,... | collective-permute-start | bytes 3145736 | tf_op jit(solution)/shard_map/ppermute | solution.py:894
  589.9 25.6 %collective-permute-start.64 = (bf16[1024,512]{1,0:T(8,128)(2,1)}, bf16[1024,512]{1,0:T(8,128)(2,1)}, u32[]{:S(2)}, u32[]{:S(2)}) collective-permute-start(bf16[1024,512]{1,0:T(8,128)(2,1)} %fusion.1), channel_id=1, source_target_pairs={{16,8},{17,9},{18,10},{19,11},{20,12},{21,13},{22,14},{23,15}} | collective-permute-start | bytes 3145736 | tf_op jit(solution)/shard_map/ppermute | solution.py:894
  620.0 26.1 %collective-permute-start.68 = (bf16[1024,512]{1,0:T(8,128)(2,1)S(1)}, bf16[1024,512]{1,0:T(8,128)(2,1)}, u32[]{:S(2)}, u32[]{:S(2)}) collective-permute-start(bf16[1024,512]{1,0:T(8,128)(2,1)S(1)} %add_convert_fusion), channel_id=1, source_target_pairs={{16,0},{17,1},{18,2},{19,3},{20,4},{21,5},{22,6},{23,7}} | collective-permute-start | bytes 3145736 | tf_op jit(solution)/shard_map/ppermute | solution.py:894
  (102 other events, 987.8 us)
